TPU v7x, 32 devices: a whole 2x2x4 slice. The times are simulated.
32 devices in a mesh: chan: 16 (over z, y, x), tm: 2 (over core).
Axes of the slice: x: 2, y: 2, z: 4, core: 2. Of those that a mesh axis runs over, the one named last changes fastest.
Arguments:
- traces: float32 [2048, 8192], P('chan', 'tm'), may hold values from -600 to 600
- channel_ok: int32 [2048], P('chan'), may hold values 0 or 1
- time_taps: float32 [33], replicated, may hold values from -4 to 4
- space_taps: float32 [5], replicated, may hold values from -4 to 4
- pair_blocks: int32 [256, 2], P('chan'), may hold values from 0 to 15, as said below
- pair_count: int32 [16], P('chan'), may hold values from 4 to 16, as said below
Outputs:
- stacks: float32 [256, 201, 128], P(('chan', 'tm'))
Inputs may be any that keep to these rules, and one draw needn't show every extreme that they name: `pair_blocks`: a != b, |a - b| <= 4, and both a and b lie within 4 of the owner's index p. Owner p uses its first pair_count[p] slots; the other slots' pairs are ignored. Some owner uses all 16 slots.
All inputs are finite; a program needn't handle non-finite values. No bound on the sum of `channel_ok` on one device may be relied on, other than what follows from the above.
Results may differ from a plain program's by a relative error of at most 0.0049.
Values may be sent and summed in bfloat16 or wider, within the bound.
No kernel may reach another device: no remote copies, remote signals or barrier semaphores. Data moves between devices by JAX's collectives and lax.ppermute only.
A program may use at most 128 MiB of HBM per device.

v0:
```python
import math

import jax
import jax.numpy as jnp
from jax import lax
from jax.sharding import PartitionSpec as P

SEG = 256
MAXLAG = 100
TAPS = 33
STAPS = 5
CUT = 4
SLOTS = 16
NFFT = 510
LAGS = 201


def padded_2(cells, sides, width):
    for axis, dim in sides:
        count = lax.axis_size(axis)
        ends = count - 1
        head = lax.slice_in_dim(cells, 0, width, axis=dim)
        tail = lax.slice_in_dim(cells, cells.shape[dim] - width, cells.shape[dim], axis=dim)
        cells = jnp.concatenate(
            [
                lax.ppermute(tail, axis, [(i, (i + 1) % count) for i in range(ends)]),
                cells,
                lax.ppermute(head, axis, [((i + 1) % count, i) for i in range(ends)]),
            ],
            axis=dim,
        )
    return cells


def passed_along(block, axis, distance):
    devices = range(lax.axis_size(axis))
    route = [(i - distance, i) for i in devices if i - distance in devices]
    return lax.ppermute(block, axis, route)


def forward_table():
    sample_pos = lax.broadcasted_iota(jnp.int32, (SEG, SEG), 0)
    bin_pos = lax.broadcasted_iota(jnp.int32, (SEG, SEG), 1)
    phase_angle = (sample_pos * bin_pos % NFFT).astype(jnp.float32) * (2.0 * math.pi / NFFT)
    return jnp.concatenate([jnp.cos(phase_angle), -jnp.sin(phase_angle)], axis=1).astype(
        jnp.bfloat16
    )


def inverse_table():
    lag_values = lax.broadcasted_iota(jnp.int32, (LAGS, SEG), 0) - MAXLAG
    bin_pos = lax.broadcasted_iota(jnp.int32, (LAGS, SEG), 1)
    phase_angle = (lag_values * bin_pos % NFFT).astype(jnp.float32) * (2.0 * math.pi / NFFT)
    weight = jnp.where((bin_pos == 0) | (bin_pos == SEG - 1), 1.0, 2.0) / NFFT
    return jnp.concatenate([weight * jnp.cos(phase_angle), -weight * jnp.sin(phase_angle)], axis=1)


def transform(segment_rows, dft_table):
    flat_rows = segment_rows.reshape(-1, SEG)
    spectrum = jnp.dot(flat_rows, dft_table, preferred_element_type=jnp.float32)
    return spectrum.astype(jnp.bfloat16).reshape(segment_rows.shape[:-1] + (2 * SEG,))


def to_lags(spectra_rows, lag_table):
    slot_rows, chan_rows, width = spectra_rows.shape
    flat_rows = spectra_rows.reshape(slot_rows * chan_rows, width)
    lagged = jnp.dot(
        flat_rows,
        jnp.transpose(lag_table),
        precision=lax.Precision.HIGHEST,
        preferred_element_type=jnp.float32,
    )
    return jnp.transpose(lagged.reshape(slot_rows, chan_rows, lag_table.shape[0]), (0, 2, 1))


def local(traces, channel_ok, time_taps, space_taps, pair_blocks, pair_count):
    chan_width, samples = traces.shape
    local_segs = samples // SEG
    masked = traces * channel_ok.astype(jnp.float32)[:, None]
    half_taps = (TAPS - 1) // 2
    padded = padded_2(masked, (("tm", 1),), half_taps)
    time_filtered = time_taps[0] * padded[:, 0:samples]
    for tap_index in range(1, TAPS):
        time_filtered = (
            time_filtered + time_taps[tap_index] * padded[:, tap_index : tap_index + samples]
        )
    half_space = (STAPS - 1) // 2
    rim_rows = padded_2(time_filtered, (("chan", 0),), half_space)
    filtered = space_taps[0] * rim_rows[0:chan_width]
    for tap_index in range(1, STAPS):
        filtered = filtered + space_taps[tap_index] * rim_rows[tap_index : tap_index + chan_width]
    segment_view = filtered.reshape(chan_width, local_segs, SEG)
    seg_power = jnp.mean(segment_view * segment_view, axis=2, keepdims=True)
    whitened = (segment_view / jnp.sqrt(seg_power + 1e-05)).astype(jnp.bfloat16)
    dft_table = forward_table()
    own_spec = transform(whitened, dft_table)
    pieces = []
    for offset in range(-CUT, CUT + 1):
        if offset == 0:
            pieces.append(own_spec)
        else:
            pieces.append(passed_along(own_spec, "chan", -offset))
    window = jnp.stack(pieces)
    owner_index = lax.axis_index("chan")

    def correlate(pair_item):
        first_block, second, alive = pair_item
        left_spec = lax.dynamic_index_in_dim(
            window, first_block - owner_index + CUT, 0, keepdims=False
        ).astype(jnp.float32)
        right_spec = lax.dynamic_index_in_dim(
            window, second - owner_index + CUT, 0, keepdims=False
        ).astype(jnp.float32)
        left_re, left_im = (left_spec[..., :SEG], left_spec[..., SEG:])
        right_re, right_im = (right_spec[..., :SEG], right_spec[..., SEG:])
        cross_re = jnp.sum(left_re * right_re + left_im * right_im, axis=1)
        cross_im = jnp.sum(left_im * right_re - left_re * right_im, axis=1)
        return jnp.concatenate([cross_re, cross_im], axis=1) * alive

    slot_index = jnp.arange(SLOTS, dtype=jnp.int32)
    alive_flag = (slot_index < pair_count[0]).astype(jnp.float32)
    cross_spec = lax.map(correlate, (pair_blocks[:, 0], pair_blocks[:, 1], alive_flag))
    lag_table = inverse_table()
    stack_scale = 1.0 / math.sqrt(local_segs * lax.axis_size("tm") * SEG)
    lagged_all = to_lags(cross_spec, lag_table)
    lagged = lax.psum_scatter(lagged_all, "tm", scatter_dimension=0, tiled=True)
    return lagged * stack_scale


def solution(mesh):
    return jax.shard_map(
        local,
        mesh=mesh,
        in_specs=(P("chan", "tm"), P("chan"), P(), P(), P("chan", None), P("chan")),
        out_specs=P(("chan", "tm"), None, None),
        check_vma=False,
    )
```

profile of v0, /device:TPU:16, one launch (start us, length us, event | category | flops | bytes accessed | tf_op | source)
XLA Modules:
  0.0 520.9 jit_solution(5859440511149969195)
XLA Ops:
  7.2 1.9 broadcast_multiply_fusion
  14.8 43.2 %fusion.12 = f32[128,4096]{1,0:T(8,128)S(1)} fusion(f32[128,16]{1,0:T(8,128)S(1)} %collective-permute-done.1, f32[128,16]{1,0:T(8,128)S(1)} %collective-permute-done, f32[128,4096]{1,0:T(8,128)S(1)} %broadcast_multiply_fusion, f32[]{:T(128)} %bitcast.43, f32[]{:T(128)} %bitcast.42, f32[]{:T(128)} %bitcast.41, f32[]{:T(128)} %bitcast.40, f32[]{:T(128)} %bitcast.39, ...), kind=kLoop, calls=%fused_computation.52 | loop fusion | flops 50855936 | bytes 4210820 | tf_op jit(solution)/shard_map/add | solution.py:85
  58.1 3.4 collective-permute-start.2
  61.5 4.2 collective-permute-start.3
  67.5 4.6 fusion.126
  72.1 2.0 copy.10
  74.1 1.9 reduce_sum.35
  77.7 2.4 convolution_convert_fusion
  80.1 3.5 collective-permute-start.4
  83.6 4.6 collective-permute-start.5
  88.2 1.9 collective-permute-start.6
  90.1 2.5 collective-permute-start.7
  92.6 5.2 collective-permute-start.8
  98.4 31.0 %collective-permute-done.4 = bf16[128,16,512]{2,1,0:T(8,128)(2,1)S(1)} collective-permute-done((bf16[128,16,512]{2,1,0:T(8,128)(2,1)S(1)}, bf16[128,16,512]{2,1,0:T(8,128)(2,1)S(1)}, u32[]{:S(2)}, u32[]{:S(2)}) %collective-permute-start.4) | collective-permute-done | bytes 2097184 | tf_op jit(solution)/shard_map/ppermute | solution.py:38
  130.8 4.3 collective-permute-start.9
  136.1 115.2 %collective-permute-done.5 = bf16[128,16,512]{2,1,0:T(8,128)(2,1)} collective-permute-done((bf16[128,16,512]{2,1,0:T(8,128)(2,1)S(1)}, bf16[128,16,512]{2,1,0:T(8,128)(2,1)}, u32[]{:S(2)}, u32[]{:S(2)}) %collective-permute-start.5) | collective-permute-done | bytes 2097184 | tf_op jit(solution)/shard_map/ppermute | solution.py:38
  251.3 1.9 collective-permute-start.10
  253.2 1.8 bitcast_dynamic-update-slice_fusion.7
  255.0 14.9 %collective-permute-done.6 = bf16[128,16,512]{2,1,0:T(8,128)(2,1)} collective-permute-done((bf16[128,16,512]{2,1,0:T(8,128)(2,1)S(1)}, bf16[128,16,512]{2,1,0:T(8,128)(2,1)}, u32[]{:S(2)}, u32[]{:S(2)}) %collective-permute-start.6) | collective-permute-done | bytes 2097184 | tf_op jit(solution)/shard_map/ppermute | solution.py:38
  269.9 4.1 collective-permute-start.11
  274.1 1.8 bitcast_dynamic-update-slice_fusion.6
  275.9 1.8 bitcast_dynamic-update-slice_fusion.5
  277.6 28.4 %collective-permute-done.7 = bf16[128,16,512]{2,1,0:T(8,128)(2,1)} collective-permute-done((bf16[128,16,512]{2,1,0:T(8,128)(2,1)S(1)}, bf16[128,16,512]{2,1,0:T(8,128)(2,1)}, u32[]{:S(2)}, u32[]{:S(2)}) %collective-permute-start.7) | collective-permute-done | bytes 2097184 | tf_op jit(solution)/shard_map/ppermute | solution.py:38
  306.0 1.8 bitcast_dynamic-update-slice_fusion.4
  307.9 1.8 bitcast_dynamic-update-slice_fusion.3
  309.7 1.8 bitcast_dynamic-update-slice_fusion.2
  311.5 34.1 %collective-permute-done.10 = bf16[128,16,512]{2,1,0:T(8,128)(2,1)S(1)} collective-permute-done((bf16[128,16,512]{2,1,0:T(8,128)(2,1)S(1)}, bf16[128,16,512]{2,1,0:T(8,128)(2,1)S(1)}, u32[]{:S(2)}, u32[]{:S(2)}) %collective-permute-start.10) | collective-permute-done | bytes 2097184 | tf_op jit(solution)/shard_map/ppermute | solution.py:38
  346.0 6.5 %copy-done = bf16[9,128,16,512]{3,2,1,0:T(8,128)(2,1)} copy-done((bf16[9,128,16,512]{3,2,1,0:T(8,128)(2,1)}, bf16[9,128,16,512]{3,2,1,0:T(8,128)(2,1)S(1)}, u32[]{:S(2)}) %copy-start) | copy-done | bytes 18874392
  352.4 142.9 %while.13 = (s32[]{:T(128)}, f32[16,128,512]{2,1,0:T(8,128)}, s32[16]{0:T(128)S(1)}, s32[]{:T(128)}, bf16[9,128,16,512]{3,2,1,0:T(8,128)(2,1)}, /*index=5*/s32[1...) while((s32[]{:T(128)}, f32[16,128,512]{2,1,0:T(8,128)}, ...), condition=%wide.region_4.5_spmd, body=%wide.region_1.4_spmd.sunk | while | flops 6357004 | bytes 21759244 | solution.py:122
  354.7 3.4 bitcast_convert_fusion.3
  363.7 3.4 bitcast_convert_fusion.3
  372.6 3.4 bitcast_convert_fusion.3
  381.6 3.4 bitcast_convert_fusion.3
  390.5 3.4 bitcast_convert_fusion.3
  399.4 3.4 bitcast_convert_fusion.3
  408.3 3.4 bitcast_convert_fusion.3
  417.2 3.4 bitcast_convert_fusion.3
  426.2 3.4 bitcast_convert_fusion.3
  435.1 3.4 bitcast_convert_fusion.3
  444.1 3.4 bitcast_convert_fusion.3
  453.0 3.4 bitcast_convert_fusion.3
  461.9 3.4 bitcast_convert_fusion.3
  470.8 3.4 bitcast_convert_fusion.3
  479.8 3.4 bitcast_convert_fusion.3
  488.7 3.4 bitcast_convert_fusion.3
  495.3 6.1 %fusion.106 = f32[16,128,201]{1,2,0:T(8,128)S(1)} fusion(f32[16,128,512]{2,1,0:T(8,128)} %get-tuple-element.114, f32[201,256]{1,0:T(8,128)S(1)} %get-tuple-element.140, f32[201,256]{1,0:T(8,128)S(1)} %get-tuple-element.139), kind=kOutput, calls=%fused_computation.186 | convolution fusion | flops 2529268224 | bytes 6252544 | tf_op jit(solution)/shard_map/dot_general | solution.py:67
  503.2 8.8 %reduce-scatter.2.cloned.1.call-done = f32[8,201,128]{2,0,1:T(8,128)} async-done(((f32[16,201,128]{2,0,1:T(8,128)}), f32[8,201,128]{2,0,1:T(8,128)}) %reduce-scatter.2.cloned.1.call-update) | async-done | bytes 823312 | tf_op jit(solution)/shard_map/reduce_scatter | solution.py:126
  511.9 2.1 broadcast_multiply_fusion.1
  (120 shorter events, 84.5 us)
Async XLA Ops:
  6.5 505.4 %reduce-scatter.2.cloned.1.call-start = ((), (), s32[]{:S(2)}) async-start(), calls=%async_computation.1 | async-start | bytes 2469888 | tf_op jit(solution)/shard_map/reduce_scatter | solution.py:126
  7.2 6.2 %copy-start.2 = (f32[33]{0:T(128)S(1)}, f32[33]{0:T(128)}, u32[]{:S(2)}) copy-start(f32[33]{0:T(128)} %param.10) | copy-start | bytes 400
  9.2 5.6 %collective-permute-start = (f32[128,16]{1,0:T(8,128)S(1)}, f32[128,16]{1,0:T(8,128)S(1)}, u32[]{:S(2)}, u32[]{:S(2)}) collective-permute-start(f32[128,16]{1,0:T(8,128)S(1)} %get-tuple-element.137), channel_id=1, source_target_pairs={{0,1},{2,3},{4,5},{6,7},{8,9},{10,11},{12,13},{14,15},{16,17},{18,... | collective-permute-start | bytes 24584 | tf_op jit(solution)/shard_map/ppermute | solution.py:26
  10.9 3.9 collective-permute-start.1
  14.8 50.9 %copy-start.3 = (f32[5]{0:T(128)S(1)}, f32[5]{0:T(128)}, u32[]{:S(2)}) copy-start(f32[5]{0:T(128)} %param.11) | copy-start | bytes 64
  58.1 8.3 %collective-permute-start.2 = (f32[2,4096]{1,0:T(2,128)S(1)}, f32[2,4096]{1,0:T(2,128)S(1)}, u32[]{:S(2)}, u32[]{:S(2)}) collective-permute-start(f32[2,4096]{1,0:T(2,128)S(1)} %get-tuple-element.135), channel_id=1, source_target_pairs={{0,2},{2,4},{4,6},{6,8},{8,10},{10,12},{12,14},{14,16},{16,18},{18... | collective-permute-start | bytes 98312 | tf_op jit(solution)/shard_map/ppermute | solution.py:26
  61.5 6.0 %collective-permute-start.3 = (f32[2,4096]{1,0:T(2,128)S(1)}, f32[2,4096]{1,0:T(2,128)S(1)}, u32[]{:S(2)}, u32[]{:S(2)}) collective-permute-start(f32[2,4096]{1,0:T(2,128)S(1)} %get-tuple-element.136), channel_id=1, source_target_pairs={{2,0},{4,2},{6,4},{8,6},{10,8},{12,10},{14,12},{16,14},{18,16},{20... | collective-permute-start | bytes 98312 | tf_op jit(solution)/shard_map/ppermute | solution.py:28
  77.7 20.7 %copy-start.4 = (s32[16,2]{0,1:T(2,128)S(1)}, s32[16,2]{0,1:T(2,128)}, u32[]{:S(2)}) copy-start(s32[16,2]{0,1:T(2,128)} %param.12) | copy-start | bytes 388
  80.1 49.4 %collective-permute-start.4 = (bf16[128,16,512]{2,1,0:T(8,128)(2,1)S(1)}, bf16[128,16,512]{2,1,0:T(8,128)(2,1)S(1)}, u32[]{:S(2)}, u32[]{:S(2)}) collective-permute-start(bf16[128,16,512]{2,1,0:T(8,128)(2,1)S(1)} %bitcast.99), channel_id=1, source_target_pairs={{0,8},{2,10},{4,12},{6,14},{8,16},{10,18},{12,20},{14,22},{16,24},... | collective-permute-start | bytes 6291464 | tf_op jit(solution)/shard_map/ppermute | solution.py:38
  83.6 167.8 %collective-permute-start.5 = (bf16[128,16,512]{2,1,0:T(8,128)(2,1)S(1)}, bf16[128,16,512]{2,1,0:T(8,128)(2,1)}, u32[]{:S(2)}, u32[]{:S(2)}) collective-permute-start(bf16[128,16,512]{2,1,0:T(8,128)(2,1)S(1)} %bitcast.100), channel_id=1, source_target_pairs={{0,6},{2,8},{4,10},{6,12},{8,14},{10,16},{12,18},{14,20},{16,22},{... | collective-permute-start | bytes 6291464 | tf_op jit(solution)/shard_map/ppermute | solution.py:38
  88.2 181.8 %collective-permute-start.6 = (bf16[128,16,512]{2,1,0:T(8,128)(2,1)S(1)}, bf16[128,16,512]{2,1,0:T(8,128)(2,1)}, u32[]{:S(2)}, u32[]{:S(2)}) collective-permute-start(bf16[128,16,512]{2,1,0:T(8,128)(2,1)S(1)} %bitcast.101), channel_id=1, source_target_pairs={{0,4},{2,6},{4,8},{6,10},{8,12},{10,14},{12,16},{14,18},{16,20},{1... | collective-permute-start | bytes 6291464 | tf_op jit(solution)/shard_map/ppermute | solution.py:38
  90.1 215.9 %collective-permute-start.7 = (bf16[128,16,512]{2,1,0:T(8,128)(2,1)S(1)}, bf16[128,16,512]{2,1,0:T(8,128)(2,1)}, u32[]{:S(2)}, u32[]{:S(2)}) collective-permute-start(bf16[128,16,512]{2,1,0:T(8,128)(2,1)S(1)} %bitcast.102), channel_id=1, source_target_pairs={{0,2},{2,4},{4,6},{6,8},{8,10},{10,12},{12,14},{14,16},{16,18},{18... | collective-permute-start | bytes 6291464 | tf_op jit(solution)/shard_map/ppermute | solution.py:38
  92.6 215.3 %collective-permute-start.8 = (bf16[128,16,512]{2,1,0:T(8,128)(2,1)S(1)}, bf16[128,16,512]{2,1,0:T(8,128)(2,1)}, u32[]{:S(2)}, u32[]{:S(2)}) collective-permute-start(bf16[128,16,512]{2,1,0:T(8,128)(2,1)S(1)} %bitcast.103), channel_id=1, source_target_pairs={{2,0},{4,2},{6,4},{8,6},{10,8},{12,10},{14,12},{16,14},{18,16},{20... | collective-permute-start | bytes 6291464 | tf_op jit(solution)/shard_map/ppermute | solution.py:38
  129.5 1.3 copy-start.1
  130.8 178.9 %collective-permute-start.9 = (bf16[128,16,512]{2,1,0:T(8,128)(2,1)S(1)}, bf16[128,16,512]{2,1,0:T(8,128)(2,1)}, u32[]{:S(2)}, u32[]{:S(2)}) collective-permute-start(bf16[128,16,512]{2,1,0:T(8,128)(2,1)S(1)} %bitcast.104), channel_id=1, source_target_pairs={{4,0},{6,2},{8,4},{10,6},{12,8},{14,10},{16,12},{18,14},{20,16},{2... | collective-permute-start | bytes 6291464 | tf_op jit(solution)/shard_map/ppermute | solution.py:38
  251.3 94.3 %collective-permute-start.10 = (bf16[128,16,512]{2,1,0:T(8,128)(2,1)S(1)}, bf16[128,16,512]{2,1,0:T(8,128)(2,1)S(1)}, u32[]{:S(2)}, u32[]{:S(2)}) collective-permute-start(bf16[128,16,512]{2,1,0:T(8,128)(2,1)S(1)} %bitcast.105), channel_id=1, source_target_pairs={{6,0},{8,2},{10,4},{12,6},{14,8},{16,10},{18,12},{20,14},{22,16},{... | collective-permute-start | bytes 6291464 | tf_op jit(solution)/shard_map/ppermute | solution.py:38
  269.9 75.8 %collective-permute-start.11 = (bf16[128,16,512]{2,1,0:T(8,128)(2,1)S(1)}, bf16[128,16,512]{2,1,0:T(8,128)(2,1)S(1)}, u32[]{:S(2)}, u32[]{:S(2)}) collective-permute-start(bf16[128,16,512]{2,1,0:T(8,128)(2,1)S(1)} %bitcast.106), channel_id=1, source_target_pairs={{8,0},{10,2},{12,4},{14,6},{16,8},{18,10},{20,12},{22,14},{24,16},... | collective-permute-start | bytes 6291464 | tf_op jit(solution)/shard_map/ppermute | solution.py:38
  346.0 6.5 %copy-start = (bf16[9,128,16,512]{3,2,1,0:T(8,128)(2,1)}, bf16[9,128,16,512]{3,2,1,0:T(8,128)(2,1)S(1)}, u32[]{:S(2)}) copy-start(bf16[9,128,16,512]{3,2,1,0:T(8,128)(2,1)S(1)} %bitcast_dynamic-update-slice_fusion) | copy-start | bytes 56623108
Sparse Core Ops, SparseCore 0:
  503.3 8.5 reduce-scatter.1
where the time goes:
time: 524 us; the launch traced here: 521 us
  waiting for transfers between devices  234 us (45%)
  other arithmetic  153 us (29%)
  local copies, waits for them, and re-layouts  54.1 us (10%)
  starting transfers between devices  38.6 us (7%)
  loops' own time  18.8 us (4%)
  between operations  14.4 us (3%)
  matrix products  8.49 us (2%)
    ppermute x8, waiting for transfers between devices, passed_along(): return lax.ppermute(block, axis, route)  224 us
    convert_element_type x16, other arithmetic, correlate(): left_spec = lax.dynamic_index_in_dim(window, first_block - owner_index +...  53.9 us
    add x1, other arithmetic, local(): time_filtered + time_taps[tap_index] * padded[:, tap_index:tap_index + sa...  43.2 us
    ppermute x8, starting transfers between devices, passed_along(): return lax.ppermute(block, axis, route)  28 us
    dynamic_slice x48, local copies, waits for them, and re-layouts, local(): lax.map(correlate, (pair_blocks[:, 0], pair_blocks[:, 1], alive_flag))  27.8 us
    reduce_sum x16, other arithmetic, correlate(): cross_re = jnp.sum(left_re * right_re + left_im * right_im, axis=1)  21.7 us
    dynamic_update_slice x16, other arithmetic, local(): lax.map(correlate, (pair_blocks[:, 0], pair_blocks[:, 1], alive_flag))  20.7 us
    unnamed x19, local copies, waits for them, and re-layouts  20.7 us
  transfers between devices with their start and end apart: 13, of which 7 were waited for; matrix products, arithmetic and copies ran while one was open for 3% of the time, Pallas kernels for 0%

commit v1 on v0

v1 whole, which is shorter than its diff:
```python
import math

import jax
import jax.numpy as jnp
import ml_dtypes
import numpy as np
from jax import lax
from jax.experimental import pallas as pl
from jax.experimental.pallas import tpu as pltpu
from jax.sharding import PartitionSpec as P

SEG = 256
MAXLAG = 100
TAPS = 33
STAPS = 5
SLOTS = 16
NFFT = 510
LAGS = 201
LAG_ROWS = 208
PLANE = 4
QG = 16
BOTH = ("chan", "tm")
F32 = jnp.float32
BF16 = jnp.bfloat16
VMEM_LIMIT = 56 * 1024 * 1024
PAIR_LIST = (
    [(2, 3), (2, 4), (2, 5), (3, 4), (3, 5), (4, 5)]
    + [(2, 6), (3, 6), (4, 6), (5, 6), (3, 7), (4, 7), (5, 7)]
    + [(0, 4), (1, 4), (1, 5)]
)
N_PAIRS = len(PAIR_LIST)


def split_np(table):
    high = table.astype(np.float32).astype(ml_dtypes.bfloat16)
    low = (table - high.astype(np.float64)).astype(np.float32).astype(ml_dtypes.bfloat16)
    return high, low


def forward_np():
    sample = np.arange(SEG)[:, None]
    bins = np.arange(SEG)[None, :]
    angle = (sample * bins % NFFT) * (2.0 * math.pi / NFFT)
    table = np.concatenate([np.cos(angle), -np.sin(angle)], axis=1)
    return table.astype(np.float32).astype(ml_dtypes.bfloat16)


def inverse_np(scale):
    lag = np.arange(LAG_ROWS)[:, None] - MAXLAG
    bins = np.arange(SEG)[None, :]
    angle = (lag * bins % NFFT) * (2.0 * math.pi / NFFT)
    weight = np.where((bins == 0) | (bins == SEG - 1), 1.0, 2.0) / NFFT * scale
    table = np.concatenate([weight * np.cos(angle), -weight * np.sin(angle)], axis=1)
    table[LAGS:] = 0.0
    return split_np(table)


def reverse_np():
    rows = np.arange(LAG_ROWS)
    table = (rows[:, None] + rows[None, :] == LAGS - 1).astype(np.float32)
    return table.astype(ml_dtypes.bfloat16)


def split_terms(value):
    high = value.astype(BF16)
    low = (value - high.astype(F32)).astype(BF16)
    return high, low


def mxu(a, b):
    return jnp.dot(a, b, preferred_element_type=F32)


def my_place():
    return lax.axis_index("chan") % PLANE, lax.axis_index("tm")


def pair_id(first, second, plane):
    low, high = jnp.minimum(first, second), jnp.maximum(first, second)
    low_plane, low_at = low // PLANE, low % PLANE
    high_plane, high_at = high // PLANE, high % PLANE
    near = (low_plane == high_plane) | (high_at < 2)
    handler = jnp.where(near, low_plane, high_plane)
    left = jnp.where(near, low_at + 2, low_at - 2)
    right = jnp.where(low_plane == high_plane, high_at + 2, jnp.where(near, high_at + 6, high_at + 2))
    index = jnp.int32(0)
    for k, (a, b) in enumerate(PAIR_LIST):
        index = jnp.where((left == a) & (right == b), k, index)
    return (handler - plane + 1) * N_PAIRS + index


def prepare_kernel(taps, pairs, t_high, t_low, pid):
    plane = lax.axis_index("chan") // PLANE
    tap = (
        lax.broadcasted_iota(jnp.int32, (2 * SEG, SEG), 0)
        - lax.broadcasted_iota(jnp.int32, (2 * SEG, SEG), 1)
        - (SEG // 2 - (TAPS - 1) // 2)
    )
    table = jnp.zeros((2 * SEG, SEG), F32)
    for j in range(TAPS):
        table = jnp.where(tap == j, taps[j], table)
    t_high[...], t_low[...] = split_terms(table)
    slot = lax.broadcasted_iota(jnp.int32, pid.shape, 1) >> 4
    ids = jnp.zeros(pid.shape, jnp.int32)
    for s in range(SLOTS):
        ids = jnp.where(slot == s, pair_id(pairs[s, 0], pairs[s, 1], plane), ids)
    pid[...] = ids.astype(F32).astype(BF16)


def filter_kernel(
    space, own, other, halo_own, halo_other, ok, t_high, t_low, pid,
    out_0, out_1, out_2, out_3, x_high, x_low, edge, white, ok_column,
):
    member, core = my_place()
    half = own.shape[1]
    rows = own.shape[0] // 2
    pad = SEG // 2
    first_row = pl.multiple_of(core * rows, rows)
    edge_row = pl.multiple_of(rows - 8 + 8 * (1 - core), 8)
    zeros = jnp.zeros((rows + 16, pad), BF16)
    total = 2 * half
    for buf in (x_high, x_low):
        buf[:, 0:pad] = zeros
        buf[:, pad + total : 2 * pad + total] = zeros
    width = ok.shape[1]
    diagonal = lax.broadcasted_iota(jnp.int32, (width, width), 0) == lax.broadcasted_iota(
        jnp.int32, (width, width), 1
    )
    spread = jnp.where(diagonal, ok[...].astype(F32), 0.0)
    ok_column[...] = jnp.broadcast_to(jnp.sum(spread, axis=1, keepdims=True), ok_column.shape)
    ok_rows = ok_column[pl.ds(first_row, rows), 0:1]
    ok_edge = ok_column[pl.ds(edge_row, 8), 0:1]
    for source, halo, slot in ((own, halo_own, core), (other, halo_other, 1 - core)):
        lanes = pl.ds(pl.multiple_of(pad + slot * half, pad), half)
        high, low = split_terms(source[pl.ds(first_row, rows), :] * ok_rows)
        x_high[0:rows, lanes] = high
        x_low[0:rows, lanes] = low
        for k in range(4):
            edge[2 * k : 2 * k + 2, :] = halo[...]
        near = source[pl.ds(edge_row, 8), :] * ok_edge
        far = edge[...]
        is_low = core == 0
        tile = jnp.concatenate([jnp.where(is_low, far, near), jnp.where(is_low, near, far)], axis=0)
        high, low = split_terms(tile)
        x_high[rows : rows + 16, lanes] = high
        x_low[rows : rows + 16, lanes] = low
    segs = total // SEG
    chunk = 8
    height = rows + 16

    def body(step, carry):
        seg0 = step * chunk
        high = jnp.concatenate(
            [x_high[:, pl.ds(pl.multiple_of((seg0 + s) * SEG, SEG), 2 * SEG)] for s in range(chunk)], axis=0
        )
        low = jnp.concatenate(
            [x_low[:, pl.ds(pl.multiple_of((seg0 + s) * SEG, SEG), 2 * SEG)] for s in range(chunk)], axis=0
        )
        y = mxu(high, t_high[...]) + mxu(low, t_high[...]) + mxu(high, t_low[...])
        for s in range(chunk):
            block = y[s * height : (s + 1) * height]
            ext = jnp.concatenate(
                [block[rows : rows + 8], block[0:rows], block[rows + 8 : rows + 16]], axis=0
            )
            filtered = space[0] * ext[6 : 6 + rows]
            for j in range(1, STAPS):
                filtered = filtered + space[j] * ext[6 + j : 6 + j + rows]
            power = jnp.mean(filtered * filtered, axis=1, keepdims=True)
            white[seg0 + s] = (filtered * (1.0 / jnp.sqrt(power + 1e-5))).astype(BF16)
        return carry

    lax.fori_loop(0, segs // chunk, body, 0)
    for rel, out in enumerate((out_0, out_1, out_2, out_3)):
        row = pl.multiple_of((member ^ rel) * QG, QG)
        out[0:segs] = white[:, pl.ds(row, QG), :]
        out[segs] = pid[...]


def pair_kernel(b0, b1, b2, b3, z0, z1, z2, z3, table, l_high, l_low, out, spec, cross):
    member, _ = my_place()
    segs = spec.shape[1]
    for rel, ref in enumerate((b0, b1, b2, b3)):
        slot = 2 + (member ^ rel)
        value = mxu(ref[0:segs].reshape(segs * QG, SEG), table[...])
        spec[slot] = value.astype(BF16).astype(F32).reshape(segs, QG, 2 * SEG)
    for rel, ref in enumerate((z0, z1, z2, z3)):
        block = member ^ rel
        slot = jnp.where(block < 2, block + 6, block - 2)
        value = mxu(ref[0:segs].reshape(segs * QG, SEG), table[...])
        spec[slot] = value.astype(BF16).astype(F32).reshape(segs, QG, 2 * SEG)
    for q8 in range(QG // 8):
        for part in range(SEG // 128):
            rows = slice(q8 * 8, q8 * 8 + 8)
            re_lanes = slice(part * 128, part * 128 + 128)
            im_lanes = slice(SEG + part * 128, SEG + part * 128 + 128)

            def body(seg, sums):
                real = [spec[w, seg, rows, re_lanes] for w in range(8)]
                imag = [spec[w, seg, rows, im_lanes] for w in range(8)]
                out_sums = []
                for index, (a, b) in enumerate(PAIR_LIST):
                    out_sums.append(sums[2 * index] + (real[a] * real[b] + imag[a] * imag[b]))
                    out_sums.append(sums[2 * index + 1] + (imag[a] * real[b] - real[a] * imag[b]))
                return tuple(out_sums)

            zero = jnp.zeros((8, 128), F32)
            sums = lax.fori_loop(0, segs, body, (zero,) * (2 * N_PAIRS), unroll=2)
            for index in range(N_PAIRS):
                at = slice(index * QG + q8 * 8, index * QG + q8 * 8 + 8)
                cross[at, re_lanes] = sums[2 * index]
                cross[at, im_lanes] = sums[2 * index + 1]
    high, low = split_terms(cross[...])

    def turned(left, right):
        return lax.dot_general(left, right, (((1,), (1,)), ((), ())), preferred_element_type=F32)

    lagged = turned(l_high[...], high) + turned(l_high[...], low) + turned(l_low[...], high)
    out[...] = lagged.astype(BF16)


def select_kernel(below, here, above, pid_0, pid_1, pid_2, pid_3, *refs):
    outs, picked = refs[:8], refs[8]
    _, core = my_place()
    width = N_PAIRS * QG
    row_id = lax.broadcasted_iota(jnp.int32, (3 * width, SLOTS * QG), 0)
    col_id = lax.broadcasted_iota(jnp.int32, (3 * width, SLOTS * QG), 1)
    row_pair = (row_id >> 4).astype(F32)
    same_q = (row_id & 15) == (col_id & 15)
    row_key = jnp.where(same_q, row_pair, -1.0)
    lags = jnp.concatenate([below[...], here[...], above[...]], axis=1)
    for rel, pid in enumerate((pid_0, pid_1, pid_2, pid_3)):
        ids = pid[0].astype(F32)[0:1, :]
        chosen = jnp.where(row_key == ids, 1.0, 0.0).astype(BF16)
        picked[...] = mxu(lags, chosen).astype(BF16)
        for side in range(2):
            lane = pl.multiple_of((core ^ side) * 128, 128)
            outs[2 * rel + side][...] = picked[:, pl.ds(lane, 128)]


def finish_kernel(pairs, count, *refs):
    pieces, table, out, stage, flat, done, sems = refs[:8], *refs[8:14]
    member, core = my_place()
    for rel in range(4):
        for side in range(2):
            spot = (core ^ side) * 4 + (member ^ rel)
            stage[spot] = pieces[2 * rel + side][...].astype(F32)
    group = lax.broadcasted_iota(jnp.int32, (LAG_ROWS, 128), 1) >> 4
    for s in range(SLOTS // 2):
        value = jnp.zeros((LAG_ROWS, 128), F32)
        for m in range(8):
            shift = ((m - s) * QG) % 128
            piece = stage[m]
            moved = pltpu.roll(piece, shift, 1) if shift else piece
            value = jnp.where(group == m, moved, value)
        flat[:, s * 128 : (s + 1) * 128] = value
    back = mxu(table[...], flat[...].astype(BF16))
    copies = []
    for s in range(SLOTS // 2):
        lanes = slice(s * 128, (s + 1) * 128)
        slot = core * (SLOTS // 2) + s
        value = jnp.where(pairs[slot, 0] > pairs[slot, 1], back[:, lanes], flat[:, lanes])
        done[s] = jnp.where(slot < count[0], value, 0.0)[0:LAGS]
        copies.append(pltpu.make_async_copy(done.at[s], out.at[s], sems.at[s]))
        copies[-1].start()
    for copy in copies:
        copy.wait()


VM = pl.BlockSpec(memory_space=pltpu.VMEM)
SM = pl.BlockSpec(memory_space=pltpu.SMEM)
PARAMS = pltpu.CompilerParams(vmem_limit_bytes=VMEM_LIMIT)


def shape(dims, kind):
    return jax.ShapeDtypeStruct(dims, kind)


def local(traces, channel_ok, time_taps, space_taps, pair_blocks, pair_count):
    n_chan = lax.axis_size("chan")
    chan_width, half = traces.shape
    segs = 2 * half // SEG
    core = lax.axis_index("tm")

    def to_core(x):
        return lax.ppermute(x, "tm", [(0, 1), (1, 0)])

    def in_plane(x, rel, side=0):
        if rel == 0 and side == 0:
            return x
        route = [(k, k ^ (2 * rel + side)) for k in range(2 * n_chan)]
        return lax.ppermute(x, BOTH, route)

    def to_next_plane(x, rel):
        route = []
        for c in range(n_chan):
            target = c - PLANE if (c ^ rel) % PLANE < 2 else c + PLANE
            if 0 <= target < n_chan:
                route.append((c, target))
        return lax.ppermute(x, "chan", route)

    other = to_core(traces)
    ok = channel_ok.astype(F32)
    head = traces[0:2] * ok[0:2, None]
    tail = traces[chan_width - 2 :] * ok[chan_width - 2 :, None]
    same_half, cross_half = [], []
    for c in range(n_chan):
        if c + 1 < n_chan:
            same_half.append((2 * c, 2 * c + 2))
            cross_half.append((2 * c + 1, 2 * c + 2))
        if c > 0:
            same_half.append((2 * c + 1, 2 * c - 1))
            cross_half.append((2 * c, 2 * c - 1))
    halo_own = lax.ppermute(jnp.where(core == 0, tail, head), BOTH, same_half)
    halo_other = lax.ppermute(jnp.where(core == 0, head, tail), BOTH, cross_half)
    table = shape((2 * SEG, SEG), BF16)
    t_high, t_low, pid = pl.pallas_call(
        prepare_kernel,
        out_shape=[table, table, shape((QG, SLOTS * QG), BF16)],
        in_specs=[SM, SM],
        out_specs=[VM] * 3,
        compiler_params=PARAMS,
        name="prepare",
    )(time_taps, pair_blocks)
    block = shape((segs + 1, QG, SEG), BF16)
    rows = chan_width // 2
    sent = pl.pallas_call(
        filter_kernel,
        out_shape=[block] * 4,
        in_specs=[SM] + [VM] * 8,
        out_specs=[VM] * 4,
        scratch_shapes=[
            pltpu.VMEM((rows + 16, 2 * half + SEG), BF16),
            pltpu.VMEM((rows + 16, 2 * half + SEG), BF16),
            pltpu.VMEM((8, half), F32),
            pltpu.VMEM((segs, rows, SEG), BF16),
            pltpu.VMEM((chan_width, 128), F32),
        ],
        compiler_params=PARAMS,
        name="filter_whiten",
    )(space_taps, traces, other, halo_own, halo_other, channel_ok[None, :], t_high, t_low, pid)
    blocks = [in_plane(x, rel) for rel, x in enumerate(sent)]
    far = [to_next_plane(x, rel) for rel, x in enumerate(blocks)]
    scale = 1.0 / math.sqrt(segs * SEG)
    l_high, l_low = inverse_np(scale)
    lags = pl.pallas_call(
        pair_kernel,
        out_shape=shape((LAG_ROWS, N_PAIRS * QG), BF16),
        in_specs=[VM] * 11,
        out_specs=VM,
        scratch_shapes=[
            pltpu.VMEM((8, segs, QG, 2 * SEG), F32),
            pltpu.VMEM((N_PAIRS * QG, 2 * SEG), F32),
        ],
        compiler_params=PARAMS,
        name="pair_lags",
    )(*blocks, *far, jnp.asarray(forward_np()), jnp.asarray(l_high), jnp.asarray(l_low))
    below = lax.ppermute(lags, "chan", [(c, c + PLANE) for c in range(n_chan - PLANE)])
    above = lax.ppermute(lags, "chan", [(c + PLANE, c) for c in range(n_chan - PLANE)])
    pid_spec = pl.BlockSpec((1, QG, SEG), lambda step: (segs, 0, 0))
    picked = pl.pallas_call(
        select_kernel,
        grid=(1,),
        out_shape=[shape((LAG_ROWS, 128), BF16)] * 8,
        in_specs=[VM] * 3 + [pid_spec] * 4,
        out_specs=[VM] * 8,
        scratch_shapes=[pltpu.VMEM((LAG_ROWS, SLOTS * QG), BF16)],
        compiler_params=PARAMS,
        name="select_slots",
    )(below, lags, above, *blocks)
    pieces = [in_plane(x, k // 2, k % 2) for k, x in enumerate(picked)]
    return pl.pallas_call(
        finish_kernel,
        out_shape=shape((SLOTS // 2, LAGS, chan_width), F32),
        in_specs=[SM] * 2 + [VM] * 9,
        out_specs=pl.BlockSpec(memory_space=pl.ANY),
        scratch_shapes=[
            pltpu.VMEM((8, LAG_ROWS, 128), F32),
            pltpu.VMEM((LAG_ROWS, SLOTS // 2 * 128), F32),
            pltpu.VMEM((SLOTS // 2, LAGS, 128), F32),
            pltpu.SemaphoreType.DMA((SLOTS // 2,)),
        ],
        compiler_params=PARAMS,
        name="finish_slots",
    )(pair_blocks, pair_count, *pieces, jnp.asarray(reverse_np()))


def solution(mesh):
    return jax.shard_map(
        local,
        mesh=mesh,
        in_specs=(P("chan", "tm"), P("chan"), P(), P(), P("chan", None), P("chan")),
        out_specs=P(("chan", "tm"), None, None),
        check_vma=False,
    )
```

time: 524 us -> 93.7 us (0.18)
  the two profiles are of different devices: /device:TPU:16 before, /device:TPU:0 now
where the time goes in v1:
time: 93.7 us; the launch traced here: 93.1 us
  starting transfers between devices  33.2 us (35%)
  waiting for transfers between devices  25.8 us (28%)
  Pallas kernels  24.4 us (26%)
  local copies, waits for them, and re-layouts  7.07 us (8%)
  other arithmetic  1.72 us (2%)
    ppermute x10, waiting for transfers between devices, in_plane(): return lax.ppermute(x, BOTH, route)  13 us
    ppermute x10, starting transfers between devices, in_plane(): return lax.ppermute(x, BOTH, route)  11.5 us
    ppermute x4, starting transfers between devices, to_next_plane(): return lax.ppermute(x, 'chan', route)  10.5 us
    pallas_call x1, Pallas kernels, local(): pl.pallas_call(filter_kernel, out_shape=[block] * 4, in_specs=[SM] + [VM]...  8.87 us
    ppermute x4, waiting for transfers between devices, to_next_plane(): return lax.ppermute(x, 'chan', route)  7.34 us
    pallas_call x1, Pallas kernels, local(): pl.pallas_call(pair_kernel, out_shape=shape((LAG_ROWS, N_PAIRS * QG), BF1...  7.22 us
    unnamed x39, local copies, waits for them, and re-layouts  4.68 us
    ppermute x1, starting transfers between devices, local(): halo_own = lax.ppermute(jnp.where(core == 0, tail, head), BOTH, same_half)  4.39 us
  transfers between devices with their start and end apart: 19, of which 9 were waited for; matrix products, arithmetic and copies ran while one was open for 3% of the time, Pallas kernels for 2%

profile of v1, /device:TPU:0, one launch (start us, length us, event | category | flops | bytes accessed | tf_op | source)
XLA Modules:
  0.0 93.1 jit_solution(9000742275063133463)
XLA Ops:
  0.0 0.5 collective-permute-start
  0.5 0.7 convert_element_type.3
  1.1 0.1 fusion
  1.2 1.1 %broadcast_select_fusion = (f32[2,4096]{1,0:T(2,128)S(1)}, f32[2,4096]{1,0:T(2,128)S(1)}) fusion(pred[]{:T(512)S(6)} %eq.4, f32[128,4096]{1,0:T(8,128)} %own.1, f32[2]{0:T(128)S(1)} %get-tuple-element.38, f32[2]{0:T(128)S(1)} %get-tuple-element.37), kind=kLoop, calls=%fused_computation.2 | loop fusion | flops 32768 | bytes 131089 | tf_op jit(solution)/shard_map/jit(_where)/select_n | solution.py:314
  2.2 4.4 %collective-permute-start.1 = (f32[2,4096]{1,0:T(2,128)S(1)}, f32[2,4096]{1,0:T(2,128)S(1)}, u32[]{:S(2)}, u32[]{:S(2)}) collective-permute-start(f32[2,4096]{1,0:T(2,128)S(1)} %get-tuple-element.36), channel_id=1, source_target_pairs={{0,2},{2,4},{3,1},{4,6},{5,3},{6,8},{7,5},{8,10},{9,7},{10,12},{11... | collective-permute-start | bytes 98312 | tf_op jit(solution)/shard_map/ppermute | solution.py:313
  6.7 0.7 collective-permute-start.2
  7.3 1.4 %copy.12.pairs = s32[16,2]{1,0:T(8,128)} copy(s32[16,2]{0,1:T(2,128)} %param.14) | data formatting | bytes 256 | tf_op args[4]
  8.7 2.1 %prepare.1 = (bf16[512,256]{1,0:T(8,128)(2,1)}, bf16[512,256]{1,0:T(8,128)(2,1)}, bf16[16,256]{1,0:T(8,128)(2,1)}) custom-call(f32[33]{0:T(128)} %taps.1, s32[16,2]{1,0:T(8,128)} %copy.12.pairs), custom_call_target="tpu_custom_call" | custom-call | tf_op jit(solution)/shard_map/prepare/pallas_call | solution.py:316
  10.8 0.0 collective-permute-done.1.halo_own
  10.8 0.0 collective-permute-done.2.halo_other
  10.9 0.6 copy-done.17
  11.4 0.0 copy-done.18
  11.4 0.8 copy-done
  12.2 8.9 %filter_whiten.1 = (bf16[33,16,256]{2,1,0:T(8,128)(2,1)}, bf16[33,16,256]{2,1,0:T(8,128)(2,1)}, bf16[33,16,256]{2,1,0:T(8,128)(2,1)}, bf16[33,16,256]{2,1,0:T(8,128)(2,1)}) custom-call(f32[5]{0:T(128)} %space.1, f32[128,4096]{1,0:T(8,128)} %own.1, f32[128,4096]{1,0:T(8,128)} %copy-done, f32[2,4096]{1,0:T(2,128)} %copy-done.17, f32[2,4096]{1,0:T(2,128)} %copy-done.18, ...), custom_call_target="tpu_custom_call" | custom-call | tf_op jit(solution)/shard_map/filter_whiten/pallas_call | solution.py:326
  21.1 2.8 %collective-permute-start.3 = (bf16[33,16,256]{2,1,0:T(8,128)(2,1)}, bf16[33,16,256]{2,1,0:T(8,128)(2,1)S(1)}, u32[]{:S(2)}, u32[]{:S(2)}) collective-permute-start(bf16[33,16,256]{2,1,0:T(8,128)(2,1)} %get-tuple-element.24), channel_id=1, source_target_pairs={{0,2},{1,3},{2,0},{3,1},{4,6},{5,7},{6,4},{7,5},{8,10},{9,11},{10,... | collective-permute-start | bytes 811016 | tf_op jit(solution)/shard_map/ppermute | solution.py:291
  23.8 1.8 %collective-permute-start.4 = (bf16[33,16,256]{2,1,0:T(8,128)(2,1)}, bf16[33,16,256]{2,1,0:T(8,128)(2,1)S(1)}, u32[]{:S(2)}, u32[]{:S(2)}) collective-permute-start(bf16[33,16,256]{2,1,0:T(8,128)(2,1)} %get-tuple-element.25), channel_id=1, source_target_pairs={{0,4},{1,5},{2,6},{3,7},{4,0},{5,1},{6,2},{7,3},{8,12},{9,13},{10,... | collective-permute-start | bytes 811016 | tf_op jit(solution)/shard_map/ppermute | solution.py:291
  25.7 0.4 collective-permute-start.5
  26.0 1.3 %collective-permute-start.6 = (bf16[33,16,256]{2,1,0:T(8,128)(2,1)}, bf16[33,16,256]{2,1,0:T(8,128)(2,1)S(1)}, u32[]{:S(2)}, u32[]{:S(2)}) collective-permute-start(bf16[33,16,256]{2,1,0:T(8,128)(2,1)} %get-tuple-element.23.b0.pid_0), channel_id=1, source_target_pairs={{4,12},{6,14},{8,0},{10,2},{12,20},{14,22},{16,8},{18,10},{20,28},... | collective-permute-start | bytes 811016 | tf_op jit(solution)/shard_map/ppermute | solution.py:299
  27.3 3.2 %collective-permute-done.3.b1.pid_1 = bf16[33,16,256]{2,1,0:T(8,128)(2,1)S(1)} collective-permute-done((bf16[33,16,256]{2,1,0:T(8,128)(2,1)}, bf16[33,16,256]{2,1,0:T(8,128)(2,1)S(1)}, u32[]{:S(2)}, u32[]{:S(2)}) %collective-permute-start.3) | collective-permute-done | bytes 270368 | tf_op jit(solution)/shard_map/ppermute | solution.py:291
  30.5 1.3 %collective-permute-start.7 = (bf16[33,16,256]{2,1,0:T(8,128)(2,1)S(1)}, bf16[33,16,256]{2,1,0:T(8,128)(2,1)S(1)}, u32[]{:S(2)}, u32[]{:S(2)}) collective-permute-start(bf16[33,16,256]{2,1,0:T(8,128)(2,1)S(1)} %collective-permute-done.3.b1.pid_1), channel_id=1, source_target_pairs={{4,12},{6,14},{8,0},{10,2},{12,20},{14,22},{16,8},{18,10},{20,28},... | collective-permute-start | bytes 811016 | tf_op jit(solution)/shard_map/ppermute | solution.py:299
  31.8 6.8 %collective-permute-done.4.b2.pid_2 = bf16[33,16,256]{2,1,0:T(8,128)(2,1)S(1)} collective-permute-done((bf16[33,16,256]{2,1,0:T(8,128)(2,1)}, bf16[33,16,256]{2,1,0:T(8,128)(2,1)S(1)}, u32[]{:S(2)}, u32[]{:S(2)}) %collective-permute-start.4) | collective-permute-done | bytes 270368 | tf_op jit(solution)/shard_map/ppermute | solution.py:291
  38.6 4.5 %collective-permute-start.8 = (bf16[33,16,256]{2,1,0:T(8,128)(2,1)S(1)}, bf16[33,16,256]{2,1,0:T(8,128)(2,1)S(1)}, u32[]{:S(2)}, u32[]{:S(2)}) collective-permute-start(bf16[33,16,256]{2,1,0:T(8,128)(2,1)S(1)} %collective-permute-done.4.b2.pid_2), channel_id=1, source_target_pairs={{0,8},{2,10},{8,16},{10,18},{12,4},{14,6},{16,24},{18,26},{20,12},... | collective-permute-start | bytes 811016 | tf_op jit(solution)/shard_map/ppermute | solution.py:299
  43.1 3.5 %collective-permute-start.9 = (bf16[33,16,256]{2,1,0:T(8,128)(2,1)S(1)}, bf16[33,16,256]{2,1,0:T(8,128)(2,1)S(1)}, u32[]{:S(2)}, u32[]{:S(2)}) collective-permute-start(bf16[33,16,256]{2,1,0:T(8,128)(2,1)S(1)} %collective-permute-done.5.b3.pid_3), channel_id=1, source_target_pairs={{0,8},{2,10},{8,16},{10,18},{12,4},{14,6},{16,24},{18,26},{20,12},... | collective-permute-start | bytes 811016 | tf_op jit(solution)/shard_map/ppermute | solution.py:299
  46.6 0.0 collective-permute-done.6.z0
  46.6 0.0 collective-permute-done.7.z1
  46.6 3.4 %collective-permute-done.8.z2 = bf16[33,16,256]{2,1,0:T(8,128)(2,1)S(1)} collective-permute-done((bf16[33,16,256]{2,1,0:T(8,128)(2,1)S(1)}, bf16[33,16,256]{2,1,0:T(8,128)(2,1)S(1)}, u32[]{:S(2)}, u32[]{:S(2)}) %collective-permute-start.8) | collective-permute-done | bytes 270368 | tf_op jit(solution)/shard_map/ppermute | solution.py:299
  50.0 4.0 %collective-permute-done.9.z3 = bf16[33,16,256]{2,1,0:T(8,128)(2,1)S(1)} collective-permute-done((bf16[33,16,256]{2,1,0:T(8,128)(2,1)S(1)}, bf16[33,16,256]{2,1,0:T(8,128)(2,1)S(1)}, u32[]{:S(2)}, u32[]{:S(2)}) %collective-permute-start.9) | collective-permute-done | bytes 270368 | tf_op jit(solution)/shard_map/ppermute | solution.py:299
  54.0 0.7 copy-done.7
  54.7 7.2 %pair_lags.1.here = bf16[208,256]{1,0:T(8,128)(2,1)} custom-call(bf16[33,16,256]{2,1,0:T(8,128)(2,1)} %get-tuple-element.23.b0.pid_0, bf16[33,16,256]{2,1,0:T(8,128)(2,1)} %copy-done.1, bf16[33,16,256]{2,1,0:T(8,128)(2,1)} %copy-done.2, bf16[33,16,256]{2,1,0:T(8,128)(2,1)} %copy-done.3, bf16[33,16,256]{2,1,0:T(8,128)(2,1)} %copy-done.4, ...), custom_call_target="tpu_custom_call" | custom-call | tf_op jit(solution)/shard_map/pair_lags/pallas_call | solution.py:345
  61.9 4.4 %collective-permute-start.10 = (bf16[208,256]{1,0:T(8,128)(2,1)}, bf16[208,256]{1,0:T(8,128)(2,1)S(1)}, u32[]{:S(2)}, u32[]{:S(2)}) collective-permute-start(bf16[208,256]{1,0:T(8,128)(2,1)} %pair_lags.1.here), channel_id=1, source_target_pairs={{0,8},{2,10},{4,12},{6,14},{8,16},{10,18},{12,20},{14,22},{16,24},... | collective-permute-start | bytes 319496 | tf_op jit(solution)/shard_map/ppermute | solution.py:357
  66.3 1.3 %collective-permute-start.11 = (bf16[208,256]{1,0:T(8,128)(2,1)}, bf16[208,256]{1,0:T(8,128)(2,1)S(1)}, u32[]{:S(2)}, u32[]{:S(2)}) collective-permute-start(bf16[208,256]{1,0:T(8,128)(2,1)} %pair_lags.1.here), channel_id=1, source_target_pairs={{8,0},{10,2},{12,4},{14,6},{16,8},{18,10},{20,12},{22,14},{24,16},... | collective-permute-start | bytes 319496 | tf_op jit(solution)/shard_map/ppermute | solution.py:358
  67.6 1.3 %collective-permute-done.10.below = bf16[208,256]{1,0:T(8,128)(2,1)S(1)} collective-permute-done((bf16[208,256]{1,0:T(8,128)(2,1)}, bf16[208,256]{1,0:T(8,128)(2,1)S(1)}, u32[]{:S(2)}, u32[]{:S(2)}) %collective-permute-start.10) | collective-permute-done | bytes 106528 | tf_op jit(solution)/shard_map/ppermute | solution.py:357
  68.9 4.2 %collective-permute-done.11.above = bf16[208,256]{1,0:T(8,128)(2,1)S(1)} collective-permute-done((bf16[208,256]{1,0:T(8,128)(2,1)}, bf16[208,256]{1,0:T(8,128)(2,1)S(1)}, u32[]{:S(2)}, u32[]{:S(2)}) %collective-permute-start.11) | collective-permute-done | bytes 106528 | tf_op jit(solution)/shard_map/ppermute | solution.py:358
  73.2 0.6 copy-done.9
  73.8 2.4 %select_slots.1 = (bf16[208,128]{1,0:T(8,128)(2,1)}, bf16[208,128]{1,0:T(8,128)(2,1)}, bf16[208,128]{1,0:T(8,128)(2,1)}, bf16[208,128]{1,0:T(8,128)(2,1)}, bf16[...) custom-call(bf16[208,256]{1,0:T(8,128)(2,1)} %copy-done.8, ...), custom_call_target="tpu_custom_call" | custom-call | tf_op jit(solution)/shard_map/select_slots/pallas_call | solution.py:360
  76.2 0.0 collective-permute-start.12
  76.2 0.1 collective-permute-start.13
  76.2 1.8 %collective-permute-start.14 = (bf16[208,128]{1,0:T(8,128)(2,1)}, bf16[208,128]{1,0:T(8,128)(2,1)S(1)}, u32[]{:S(2)}, u32[]{:S(2)}) collective-permute-start(bf16[208,128]{1,0:T(8,128)(2,1)} %get-tuple-element.30), channel_id=1, source_target_pairs={{0,3},{1,2},{2,1},{3,0},{4,7},{5,6},{6,5},{7,4},{8,11},{9,10},{10,... | collective-permute-start | bytes 159752 | tf_op jit(solution)/shard_map/ppermute | solution.py:291
  78.0 2.3 %collective-permute-start.15 = (bf16[208,128]{1,0:T(8,128)(2,1)}, bf16[208,128]{1,0:T(8,128)(2,1)S(1)}, u32[]{:S(2)}, u32[]{:S(2)}) collective-permute-start(bf16[208,128]{1,0:T(8,128)(2,1)} %get-tuple-element.31), channel_id=1, source_target_pairs={{0,4},{1,5},{2,6},{3,7},{4,0},{5,1},{6,2},{7,3},{8,12},{9,13},{10,... | collective-permute-start | bytes 159752 | tf_op jit(solution)/shard_map/ppermute | solution.py:291
  80.4 0.0 collective-permute-start.16
  80.4 1.2 %collective-permute-start.17 = (bf16[208,128]{1,0:T(8,128)(2,1)}, bf16[208,128]{1,0:T(8,128)(2,1)S(1)}, u32[]{:S(2)}, u32[]{:S(2)}) collective-permute-start(bf16[208,128]{1,0:T(8,128)(2,1)} %get-tuple-element.33), channel_id=1, source_target_pairs={{0,6},{1,7},{2,4},{3,5},{4,2},{5,3},{6,0},{7,1},{8,14},{9,15},{10,... | collective-permute-start | bytes 159752 | tf_op jit(solution)/shard_map/ppermute | solution.py:291
  81.6 1.2 %collective-permute-start.18 = (bf16[208,128]{1,0:T(8,128)(2,1)}, bf16[208,128]{1,0:T(8,128)(2,1)S(1)}, u32[]{:S(2)}, u32[]{:S(2)}) collective-permute-start(bf16[208,128]{1,0:T(8,128)(2,1)} %get-tuple-element.34), channel_id=1, source_target_pairs={{0,7},{1,6},{2,5},{3,4},{4,3},{5,2},{6,1},{7,0},{8,15},{9,14},{10,... | collective-permute-start | bytes 159752 | tf_op jit(solution)/shard_map/ppermute | solution.py:291
  83.4 1.6 %collective-permute-done.16.refs_5_ = bf16[208,128]{1,0:T(8,128)(2,1)S(1)} collective-permute-done((bf16[208,128]{1,0:T(8,128)(2,1)}, bf16[208,128]{1,0:T(8,128)(2,1)S(1)}, u32[]{:S(2)}, u32[]{:S(2)}) %collective-permute-start.16) | collective-permute-done | bytes 53280 | tf_op jit(solution)/shard_map/ppermute | solution.py:291
  85.0 0.7 collective-permute-done.17.refs_6_
  85.7 0.7 collective-permute-done.18.refs_7_
  86.5 0.6 copy-done.16
  87.0 3.8 %finish_slots.1 = f32[8,201,128]{2,1,0:T(8,128)} custom-call(s32[16,2]{1,0:T(8,128)} %copy.12.pairs, s32[1]{0:T(128)S(6)} %copy.14.count, bf16[208,128]{1,0:T(8,128)(2,1)} %get-tuple-element.27.refs_0_, bf16[208,128]{1,0:T(8,128)(2,1)} %copy-done.10, bf16[208,128]{1,0:T(8,128)(2,1)} %copy-done.11, bf16[208,128]{1,0:T(8,128)(2,1)} %copy-done.12, ...), custom_call_target="tpu_custom_call" | custom-call | tf_op jit(solution)/shard_map/finish_slots/pallas_call | solution.py:371
  90.8 2.3 %copy.13 = f32[8,201,128]{2,0,1:T(8,128)} copy(f32[8,201,128]{2,1,0:T(8,128)} %finish_slots.1) | data formatting | bytes 1646592 | tf_op jit(solution)/shard_map/finish_slots/pallas_call | solution.py:371
  (38 shorter events, 0.1 us)
Async XLA Ops:
  0.0 10.8 %collective-permute-start = (f32[128,4096]{1,0:T(8,128)}, f32[128,4096]{1,0:T(8,128)S(1)}, u32[]{:S(2)}, u32[]{:S(2)}) collective-permute-start(f32[128,4096]{1,0:T(8,128)} %own.1), channel_id=1, source_target_pairs={{0,1},{1,0},{2,3},{3,2},{4,5},{5,4},{6,7},{7,6},{8,9},{9,8},{10,11... | collective-permute-start | bytes 6291464 | tf_op jit(solution)/shard_map/ppermute | solution.py:285
  2.2 8.6 %collective-permute-start.1 = (f32[2,4096]{1,0:T(2,128)S(1)}, f32[2,4096]{1,0:T(2,128)S(1)}, u32[]{:S(2)}, u32[]{:S(2)}) collective-permute-start(f32[2,4096]{1,0:T(2,128)S(1)} %get-tuple-element.36), channel_id=1, source_target_pairs={{0,2},{2,4},{3,1},{4,6},{5,3},{6,8},{7,5},{8,10},{9,7},{10,12},{11... | collective-permute-start | bytes 98312 | tf_op jit(solution)/shard_map/ppermute | solution.py:313
  6.7 4.2 %collective-permute-start.2 = (f32[2,4096]{1,0:T(2,128)S(1)}, f32[2,4096]{1,0:T(2,128)S(1)}, u32[]{:S(2)}, u32[]{:S(2)}) collective-permute-start(f32[2,4096]{1,0:T(2,128)S(1)} %get-tuple-element.35), channel_id=1, source_target_pairs={{1,2},{3,4},{2,1},{5,6},{4,3},{7,8},{6,5},{9,10},{8,7},{11,12},{10... | collective-permute-start | bytes 98312 | tf_op jit(solution)/shard_map/ppermute | solution.py:314
  10.8 0.6 copy-start.17
  10.8 0.6 copy-start.18
  10.9 1.4 %copy-start = (f32[128,4096]{1,0:T(8,128)}, f32[128,4096]{1,0:T(8,128)S(1)}, u32[]{:S(2)}) copy-start(f32[128,4096]{1,0:T(8,128)S(1)} %collective-permute-done.other) | copy-start | bytes 6291460
  21.1 9.4 %collective-permute-start.3 = (bf16[33,16,256]{2,1,0:T(8,128)(2,1)}, bf16[33,16,256]{2,1,0:T(8,128)(2,1)S(1)}, u32[]{:S(2)}, u32[]{:S(2)}) collective-permute-start(bf16[33,16,256]{2,1,0:T(8,128)(2,1)} %get-tuple-element.24), channel_id=1, source_target_pairs={{0,2},{1,3},{2,0},{3,1},{4,6},{5,7},{6,4},{7,5},{8,10},{9,11},{10,... | collective-permute-start | bytes 811016 | tf_op jit(solution)/shard_map/ppermute | solution.py:291
  23.8 14.8 %collective-permute-start.4 = (bf16[33,16,256]{2,1,0:T(8,128)(2,1)}, bf16[33,16,256]{2,1,0:T(8,128)(2,1)S(1)}, u32[]{:S(2)}, u32[]{:S(2)}) collective-permute-start(bf16[33,16,256]{2,1,0:T(8,128)(2,1)} %get-tuple-element.25), channel_id=1, source_target_pairs={{0,4},{1,5},{2,6},{3,7},{4,0},{5,1},{6,2},{7,3},{8,12},{9,13},{10,... | collective-permute-start | bytes 811016 | tf_op jit(solution)/shard_map/ppermute | solution.py:291
  25.7 17.4 %collective-permute-start.5 = (bf16[33,16,256]{2,1,0:T(8,128)(2,1)}, bf16[33,16,256]{2,1,0:T(8,128)(2,1)S(1)}, u32[]{:S(2)}, u32[]{:S(2)}) collective-permute-start(bf16[33,16,256]{2,1,0:T(8,128)(2,1)} %get-tuple-element.26), channel_id=1, source_target_pairs={{0,6},{1,7},{2,4},{3,5},{4,2},{5,3},{6,0},{7,1},{8,14},{9,15},{10,... | collective-permute-start | bytes 811016 | tf_op jit(solution)/shard_map/ppermute | solution.py:291
  26.0 20.6 %collective-permute-start.6 = (bf16[33,16,256]{2,1,0:T(8,128)(2,1)}, bf16[33,16,256]{2,1,0:T(8,128)(2,1)S(1)}, u32[]{:S(2)}, u32[]{:S(2)}) collective-permute-start(bf16[33,16,256]{2,1,0:T(8,128)(2,1)} %get-tuple-element.23.b0.pid_0), channel_id=1, source_target_pairs={{4,12},{6,14},{8,0},{10,2},{12,20},{14,22},{16,8},{18,10},{20,28},... | collective-permute-start | bytes 811016 | tf_op jit(solution)/shard_map/ppermute | solution.py:299
  30.5 23.5 %copy-start.1 = (bf16[33,16,256]{2,1,0:T(8,128)(2,1)}, bf16[33,16,256]{2,1,0:T(8,128)(2,1)S(1)}, u32[]{:S(2)}) copy-start(bf16[33,16,256]{2,1,0:T(8,128)(2,1)S(1)} %collective-permute-done.3.b1.pid_1) | copy-start | bytes 811012
  30.5 16.1 %collective-permute-start.7 = (bf16[33,16,256]{2,1,0:T(8,128)(2,1)S(1)}, bf16[33,16,256]{2,1,0:T(8,128)(2,1)S(1)}, u32[]{:S(2)}, u32[]{:S(2)}) collective-permute-start(bf16[33,16,256]{2,1,0:T(8,128)(2,1)S(1)} %collective-permute-done.3.b1.pid_1), channel_id=1, source_target_pairs={{4,12},{6,14},{8,0},{10,2},{12,20},{14,22},{16,8},{18,10},{20,28},... | collective-permute-start | bytes 811016 | tf_op jit(solution)/shard_map/ppermute | solution.py:299
  38.6 15.4 %copy-start.2 = (bf16[33,16,256]{2,1,0:T(8,128)(2,1)}, bf16[33,16,256]{2,1,0:T(8,128)(2,1)S(1)}, u32[]{:S(2)}) copy-start(bf16[33,16,256]{2,1,0:T(8,128)(2,1)S(1)} %collective-permute-done.4.b2.pid_2) | copy-start | bytes 811012
  38.6 11.4 %collective-permute-start.8 = (bf16[33,16,256]{2,1,0:T(8,128)(2,1)S(1)}, bf16[33,16,256]{2,1,0:T(8,128)(2,1)S(1)}, u32[]{:S(2)}, u32[]{:S(2)}) collective-permute-start(bf16[33,16,256]{2,1,0:T(8,128)(2,1)S(1)} %collective-permute-done.4.b2.pid_2), channel_id=1, source_target_pairs={{0,8},{2,10},{8,16},{10,18},{12,4},{14,6},{16,24},{18,26},{20,12},... | collective-permute-start | bytes 811016 | tf_op jit(solution)/shard_map/ppermute | solution.py:299
  43.1 10.9 %copy-start.3 = (bf16[33,16,256]{2,1,0:T(8,128)(2,1)}, bf16[33,16,256]{2,1,0:T(8,128)(2,1)S(1)}, u32[]{:S(2)}) copy-start(bf16[33,16,256]{2,1,0:T(8,128)(2,1)S(1)} %collective-permute-done.5.b3.pid_3) | copy-start | bytes 811012
  43.1 10.9 %collective-permute-start.9 = (bf16[33,16,256]{2,1,0:T(8,128)(2,1)S(1)}, bf16[33,16,256]{2,1,0:T(8,128)(2,1)S(1)}, u32[]{:S(2)}, u32[]{:S(2)}) collective-permute-start(bf16[33,16,256]{2,1,0:T(8,128)(2,1)S(1)} %collective-permute-done.5.b3.pid_3), channel_id=1, source_target_pairs={{0,8},{2,10},{8,16},{10,18},{12,4},{14,6},{16,24},{18,26},{20,12},... | collective-permute-start | bytes 811016 | tf_op jit(solution)/shard_map/ppermute | solution.py:299
  46.6 7.4 %copy-start.4 = (bf16[33,16,256]{2,1,0:T(8,128)(2,1)}, bf16[33,16,256]{2,1,0:T(8,128)(2,1)S(1)}, u32[]{:S(2)}) copy-start(bf16[33,16,256]{2,1,0:T(8,128)(2,1)S(1)} %collective-permute-done.6.z0) | copy-start | bytes 811012
  46.6 7.4 %copy-start.5 = (bf16[33,16,256]{2,1,0:T(8,128)(2,1)}, bf16[33,16,256]{2,1,0:T(8,128)(2,1)S(1)}, u32[]{:S(2)}) copy-start(bf16[33,16,256]{2,1,0:T(8,128)(2,1)S(1)} %collective-permute-done.7.z1) | copy-start | bytes 811012
  50.0 4.0 %copy-start.6 = (bf16[33,16,256]{2,1,0:T(8,128)(2,1)}, bf16[33,16,256]{2,1,0:T(8,128)(2,1)S(1)}, u32[]{:S(2)}) copy-start(bf16[33,16,256]{2,1,0:T(8,128)(2,1)S(1)} %collective-permute-done.8.z2) | copy-start | bytes 811012
  54.0 0.7 copy-start.7
  61.9 7.0 %collective-permute-start.10 = (bf16[208,256]{1,0:T(8,128)(2,1)}, bf16[208,256]{1,0:T(8,128)(2,1)S(1)}, u32[]{:S(2)}, u32[]{:S(2)}) collective-permute-start(bf16[208,256]{1,0:T(8,128)(2,1)} %pair_lags.1.here), channel_id=1, source_target_pairs={{0,8},{2,10},{4,12},{6,14},{8,16},{10,18},{12,20},{14,22},{16,24},... | collective-permute-start | bytes 319496 | tf_op jit(solution)/shard_map/ppermute | solution.py:357
  66.3 6.8 %collective-permute-start.11 = (bf16[208,256]{1,0:T(8,128)(2,1)}, bf16[208,256]{1,0:T(8,128)(2,1)S(1)}, u32[]{:S(2)}, u32[]{:S(2)}) collective-permute-start(bf16[208,256]{1,0:T(8,128)(2,1)} %pair_lags.1.here), channel_id=1, source_target_pairs={{8,0},{10,2},{12,4},{14,6},{16,8},{18,10},{20,12},{22,14},{24,16},... | collective-permute-start | bytes 319496 | tf_op jit(solution)/shard_map/ppermute | solution.py:358
  68.9 4.2 %copy-start.8 = (bf16[208,256]{1,0:T(8,128)(2,1)}, bf16[208,256]{1,0:T(8,128)(2,1)S(1)}, u32[]{:S(2)}) copy-start(bf16[208,256]{1,0:T(8,128)(2,1)S(1)} %collective-permute-done.10.below) | copy-start | bytes 319492
  73.2 0.6 copy-start.9
  76.2 4.2 %collective-permute-start.12 = (bf16[208,128]{1,0:T(8,128)(2,1)}, bf16[208,128]{1,0:T(8,128)(2,1)S(1)}, u32[]{:S(2)}, u32[]{:S(2)}) collective-permute-start(bf16[208,128]{1,0:T(8,128)(2,1)} %get-tuple-element.28), channel_id=1, source_target_pairs={{0,1},{1,0},{2,3},{3,2},{4,5},{5,4},{6,7},{7,6},{8,9},{9,8},{10,11... | collective-permute-start | bytes 159752 | tf_op jit(solution)/shard_map/ppermute | solution.py:291
  76.2 5.4 %collective-permute-start.13 = (bf16[208,128]{1,0:T(8,128)(2,1)}, bf16[208,128]{1,0:T(8,128)(2,1)S(1)}, u32[]{:S(2)}, u32[]{:S(2)}) collective-permute-start(bf16[208,128]{1,0:T(8,128)(2,1)} %get-tuple-element.29), channel_id=1, source_target_pairs={{0,2},{1,3},{2,0},{3,1},{4,6},{5,7},{6,4},{7,5},{8,10},{9,11},{10,... | collective-permute-start | bytes 159752 | tf_op jit(solution)/shard_map/ppermute | solution.py:291
  76.2 7.2 %collective-permute-start.14 = (bf16[208,128]{1,0:T(8,128)(2,1)}, bf16[208,128]{1,0:T(8,128)(2,1)S(1)}, u32[]{:S(2)}, u32[]{:S(2)}) collective-permute-start(bf16[208,128]{1,0:T(8,128)(2,1)} %get-tuple-element.30), channel_id=1, source_target_pairs={{0,3},{1,2},{2,1},{3,0},{4,7},{5,6},{6,5},{7,4},{8,11},{9,10},{10,... | collective-permute-start | bytes 159752 | tf_op jit(solution)/shard_map/ppermute | solution.py:291
  78.0 5.4 %collective-permute-start.15 = (bf16[208,128]{1,0:T(8,128)(2,1)}, bf16[208,128]{1,0:T(8,128)(2,1)S(1)}, u32[]{:S(2)}, u32[]{:S(2)}) collective-permute-start(bf16[208,128]{1,0:T(8,128)(2,1)} %get-tuple-element.31), channel_id=1, source_target_pairs={{0,4},{1,5},{2,6},{3,7},{4,0},{5,1},{6,2},{7,3},{8,12},{9,13},{10,... | collective-permute-start | bytes 159752 | tf_op jit(solution)/shard_map/ppermute | solution.py:291
  80.4 4.7 %collective-permute-start.16 = (bf16[208,128]{1,0:T(8,128)(2,1)}, bf16[208,128]{1,0:T(8,128)(2,1)S(1)}, u32[]{:S(2)}, u32[]{:S(2)}) collective-permute-start(bf16[208,128]{1,0:T(8,128)(2,1)} %get-tuple-element.32), channel_id=1, source_target_pairs={{0,5},{1,4},{2,7},{3,6},{4,1},{5,0},{6,3},{7,2},{8,13},{9,12},{10,... | collective-permute-start | bytes 159752 | tf_op jit(solution)/shard_map/ppermute | solution.py:291
  80.4 6.1 %copy-start.10 = (bf16[208,128]{1,0:T(8,128)(2,1)}, bf16[208,128]{1,0:T(8,128)(2,1)S(1)}, u32[]{:S(2)}) copy-start(bf16[208,128]{1,0:T(8,128)(2,1)S(1)} %collective-permute-done.12.refs_1_) | copy-start | bytes 159748
  80.4 5.4 %collective-permute-start.17 = (bf16[208,128]{1,0:T(8,128)(2,1)}, bf16[208,128]{1,0:T(8,128)(2,1)S(1)}, u32[]{:S(2)}, u32[]{:S(2)}) collective-permute-start(bf16[208,128]{1,0:T(8,128)(2,1)} %get-tuple-element.33), channel_id=1, source_target_pairs={{0,6},{1,7},{2,4},{3,5},{4,2},{5,3},{6,0},{7,1},{8,14},{9,15},{10,... | collective-permute-start | bytes 159752 | tf_op jit(solution)/shard_map/ppermute | solution.py:291
  81.6 4.8 %copy-start.11 = (bf16[208,128]{1,0:T(8,128)(2,1)}, bf16[208,128]{1,0:T(8,128)(2,1)S(1)}, u32[]{:S(2)}) copy-start(bf16[208,128]{1,0:T(8,128)(2,1)S(1)} %collective-permute-done.13.refs_2_) | copy-start | bytes 159748
  81.6 4.8 %collective-permute-start.18 = (bf16[208,128]{1,0:T(8,128)(2,1)}, bf16[208,128]{1,0:T(8,128)(2,1)S(1)}, u32[]{:S(2)}, u32[]{:S(2)}) collective-permute-start(bf16[208,128]{1,0:T(8,128)(2,1)} %get-tuple-element.34), channel_id=1, source_target_pairs={{0,7},{1,6},{2,5},{3,4},{4,3},{5,2},{6,1},{7,0},{8,15},{9,14},{10,... | collective-permute-start | bytes 159752 | tf_op jit(solution)/shard_map/ppermute | solution.py:291
  83.4 3.0 %copy-start.12 = (bf16[208,128]{1,0:T(8,128)(2,1)}, bf16[208,128]{1,0:T(8,128)(2,1)S(1)}, u32[]{:S(2)}) copy-start(bf16[208,128]{1,0:T(8,128)(2,1)S(1)} %collective-permute-done.14.refs_3_) | copy-start | bytes 159748
  83.4 3.0 %copy-start.13 = (bf16[208,128]{1,0:T(8,128)(2,1)}, bf16[208,128]{1,0:T(8,128)(2,1)S(1)}, u32[]{:S(2)}) copy-start(bf16[208,128]{1,0:T(8,128)(2,1)S(1)} %collective-permute-done.15.refs_4_) | copy-start | bytes 159748
  85.0 1.4 %copy-start.14 = (bf16[208,128]{1,0:T(8,128)(2,1)}, bf16[208,128]{1,0:T(8,128)(2,1)S(1)}, u32[]{:S(2)}) copy-start(bf16[208,128]{1,0:T(8,128)(2,1)S(1)} %collective-permute-done.16.refs_5_) | copy-start | bytes 159748
  85.7 0.7 copy-start.15
  86.4 0.6 copy-start.16

commit v2 on v1

v2 whole, which is shorter than its diff:
```python
import math

import jax
import jax.numpy as jnp
import ml_dtypes
import numpy as np
from jax import lax
from jax.experimental import pallas as pl
from jax.experimental.pallas import tpu as pltpu
from jax.sharding import PartitionSpec as P

SEG = 256
MAXLAG = 100
TAPS = 33
STAPS = 5
SLOTS = 16
NFFT = 510
LAGS = 201
LAG_ROWS = 208
PLANE = 4
QG = 16
BOTH = ("chan", "tm")
F32 = jnp.float32
BF16 = jnp.bfloat16
VMEM_LIMIT = 56 * 1024 * 1024
INNER = [(0, 1), (0, 2), (0, 3), (1, 2), (1, 3), (2, 3)]
CROSS = [(i, j) for i in range(PLANE) for j in range(i + 1)]
N_IN, N_CROSS = len(INNER), len(CROSS)
N_OWN = N_CROSS + N_IN + N_CROSS
N_SENT = N_IN + N_CROSS
N_ALL = N_OWN + 2 * N_SENT


def split_np(table):
    high = table.astype(np.float32).astype(ml_dtypes.bfloat16)
    low = (table - high.astype(np.float64)).astype(np.float32).astype(ml_dtypes.bfloat16)
    return high, low


def forward_np():
    sample = np.arange(SEG)[:, None]
    bins = np.arange(SEG)[None, :]
    angle = (sample * bins % NFFT) * (2.0 * math.pi / NFFT)
    table = np.concatenate([np.cos(angle), -np.sin(angle)], axis=1)
    return table.astype(np.float32).astype(ml_dtypes.bfloat16)


def inverse_np(scale):
    lag = np.arange(LAG_ROWS)[:, None] - MAXLAG
    bins = np.arange(SEG)[None, :]
    angle = (lag * bins % NFFT) * (2.0 * math.pi / NFFT)
    weight = np.where((bins == 0) | (bins == SEG - 1), 1.0, 2.0) / NFFT * scale
    table = np.concatenate([weight * np.cos(angle), -weight * np.sin(angle)], axis=1)
    table[LAGS:] = 0.0
    return split_np(table)


def reverse_np():
    rows = np.arange(LAG_ROWS)
    table = (rows[:, None] + rows[None, :] == LAGS - 1).astype(np.float32)
    return table.astype(ml_dtypes.bfloat16)


def split_terms(value):
    high = value.astype(BF16)
    low = (value - high.astype(F32)).astype(BF16)
    return high, low


def mxu(a, b):
    return jnp.dot(a, b, preferred_element_type=F32)


def my_place():
    chan = lax.axis_index("chan")
    return chan % PLANE, lax.axis_index("tm"), (chan // PLANE) % 2


def pair_ids(first, second, plane):
    low, high = jnp.minimum(first, second), jnp.maximum(first, second)
    low_plane, low_at = low // PLANE - plane, low % PLANE
    high_plane, high_at = high // PLANE - plane, high % PLANE
    inner = jnp.int32(0)
    for k, (i, j) in enumerate(INNER):
        inner = jnp.where((low_at == i) & (high_at == j), k, inner)
    cross = low_at * (low_at + 1) // 2 + high_at
    one = jnp.where(
        low_plane == 0,
        jnp.where(high_plane == 0, N_CROSS + inner, N_CROSS + N_IN + cross),
        jnp.where(
            low_plane > 0,
            N_OWN + N_SENT + N_CROSS + inner,
            jnp.where(high_plane == 0, cross, N_OWN + inner),
        ),
    )
    two = jnp.where(
        low_plane == high_plane,
        N_ALL,
        jnp.where(low_plane == 0, N_OWN + N_SENT + cross, N_OWN + N_IN + cross),
    )
    return one, two


def prepare_kernel(taps, pairs, t_high, t_low, pid):
    plane = lax.axis_index("chan") // PLANE
    tap = (
        lax.broadcasted_iota(jnp.int32, (2 * SEG, SEG), 0)
        - lax.broadcasted_iota(jnp.int32, (2 * SEG, SEG), 1)
        - (SEG // 2 - (TAPS - 1) // 2)
    )
    table = jnp.zeros((2 * SEG, SEG), F32)
    for j in range(TAPS):
        table = jnp.where(tap == j, taps[j], table)
    t_high[...], t_low[...] = split_terms(table)
    slot = lax.broadcasted_iota(jnp.int32, pid.shape, 1) >> 4
    upper = lax.broadcasted_iota(jnp.int32, pid.shape, 0) < 8
    ids = jnp.zeros(pid.shape, jnp.int32)
    for s in range(SLOTS):
        one, two = pair_ids(pairs[0, s], pairs[1, s], plane)
        ids = jnp.where(slot == s, jnp.where(upper, one, two), ids)
    pid[...] = ids.astype(F32).astype(BF16)


def filter_kernel(
    space, own, other, halos, ok, t_high, t_low, pid,
    out_first, out_second, out_1, out_2, out_3, x_high, x_low, edge, white, ok_column,
):
    member, core, odd = my_place()
    half = own.shape[1]
    rows = own.shape[0] // 2
    pad = SEG // 2
    first_row = pl.multiple_of(core * rows, rows)
    edge_row = pl.multiple_of(rows - 8 + 8 * (1 - core), 8)
    zeros = jnp.zeros((rows + 16, pad), BF16)
    total = 2 * half
    for buf in (x_high, x_low):
        buf[:, 0:pad] = zeros
        buf[:, pad + total : 2 * pad + total] = zeros
    width = ok.shape[1]
    diagonal = lax.broadcasted_iota(jnp.int32, (width, width), 0) == lax.broadcasted_iota(
        jnp.int32, (width, width), 1
    )
    spread = jnp.where(diagonal, ok[...].astype(F32), 0.0)
    ok_column[...] = jnp.broadcast_to(jnp.sum(spread, axis=1, keepdims=True), ok_column.shape)
    ok_rows = ok_column[pl.ds(first_row, rows), 0:1]
    ok_edge = ok_column[pl.ds(edge_row, 8), 0:1]
    for source, halo, slot in ((own, halos[2:4], core), (other, halos[0:2], 1 - core)):
        lanes = pl.ds(pl.multiple_of(pad + slot * half, pad), half)
        high, low = split_terms(source[pl.ds(first_row, rows), :] * ok_rows)
        x_high[0:rows, lanes] = high
        x_low[0:rows, lanes] = low
        for k in range(4):
            edge[2 * k : 2 * k + 2, :] = halo
        near = source[pl.ds(edge_row, 8), :] * ok_edge
        far = edge[...]
        is_low = core == 0
        tile = jnp.concatenate([jnp.where(is_low, far, near), jnp.where(is_low, near, far)], axis=0)
        high, low = split_terms(tile)
        x_high[rows : rows + 16, lanes] = high
        x_low[rows : rows + 16, lanes] = low
    segs = total // SEG
    chunk = 8
    height = rows + 16

    def body(step, carry):
        seg0 = step * chunk
        high = jnp.concatenate(
            [x_high[:, pl.ds(pl.multiple_of((seg0 + s) * SEG, SEG), 2 * SEG)] for s in range(chunk)], axis=0
        )
        low = jnp.concatenate(
            [x_low[:, pl.ds(pl.multiple_of((seg0 + s) * SEG, SEG), 2 * SEG)] for s in range(chunk)], axis=0
        )
        y = mxu(high, t_high[...]) + mxu(low, t_high[...]) + mxu(high, t_low[...])
        for s in range(chunk):
            block = y[s * height : (s + 1) * height]
            ext = jnp.concatenate(
                [block[rows : rows + 8], block[0:rows], block[rows + 8 : rows + 16]], axis=0
            )
            filtered = space[0] * ext[6 : 6 + rows]
            for j in range(1, STAPS):
                filtered = filtered + space[j] * ext[6 + j : 6 + j + rows]
            power = jnp.mean(filtered * filtered, axis=1, keepdims=True)
            white[seg0 + s] = (filtered * (1.0 / jnp.sqrt(power + 1e-5))).astype(BF16)
        return carry

    lax.fori_loop(0, segs // chunk, body, 0)
    own_row = pl.multiple_of(member * QG, QG)
    part = segs // 2
    out_first[...] = white[pl.ds((1 - odd) * part, part), pl.ds(own_row, QG), :]
    out_second[...] = white[pl.ds(odd * part, part), pl.ds(own_row, QG), :]
    for rel, out in ((1, out_1), (2, out_2), (3, out_3)):
        row = pl.multiple_of((member ^ rel) * QG, QG)
        out[0:segs] = white[:, pl.ds(row, QG), :]
        out[segs] = pid[...]


def pair_kernel(
    first, second, b1, b2, b3, near_0, far_0, near_1, far_1, near_2, far_2, near_3, far_3, table, l_high, l_low,
    out, out_first, out_second, spec, spec_z, cross,
):
    member, _, odd = my_place()
    segs = spec.shape[1]
    part = segs // 2

    def transform(block):
        value = mxu(block.reshape(block.shape[0] * QG, SEG), table[...])
        return value.astype(BF16).astype(F32).reshape(block.shape[0], QG, 2 * SEG)

    spec[member, pl.ds((1 - odd) * part, part)] = transform(first[...])
    spec[member, pl.ds(odd * part, part)] = transform(second[...])
    for rel, ref in ((1, b1), (2, b2), (3, b3)):
        spec[member ^ rel] = transform(ref[0:segs])
    for side, refs in ((odd, (near_0, near_1, near_2, near_3)), (1 - odd, (far_0, far_1, far_2, far_3))):
        for rel, ref in enumerate(refs):
            spec_z[side, member ^ rel] = transform(ref[...])
    for q8 in range(QG // 8):
        for lanes in range(SEG // 128):
            rows = slice(q8 * 8, q8 * 8 + 8)
            re_lanes = slice(lanes * 128, lanes * 128 + 128)
            im_lanes = slice(SEG + lanes * 128, SEG + lanes * 128 + 128)

            def add(sums, index, left, right):
                re = sums[2 * index] + (left[0] * right[0] + left[1] * right[1])
                im = sums[2 * index + 1] + (left[1] * right[0] - left[0] * right[1])
                return [re, im]

            def sweep(side, sums):
                def body(seg, sums):
                    at = seg + side * part
                    mine = [(spec[w, at, rows, re_lanes], spec[w, at, rows, im_lanes]) for w in range(PLANE)]
                    theirs = [
                        (spec_z[side, w, seg, rows, re_lanes], spec_z[side, w, seg, rows, im_lanes])
                        for w in range(PLANE)
                    ]
                    low, high = (theirs, mine) if side else (mine, theirs)
                    result = []
                    for k, (i, j) in enumerate(INNER):
                        result += add(sums, k, mine[i], mine[j])
                    for k, (i, j) in enumerate(CROSS):
                        result += add(sums, N_IN + k, low[i], high[j])
                    return tuple(result)

                return lax.fori_loop(0, part, body, sums, unroll=2)

            zero = jnp.zeros((8, 128), F32)
            up = sweep(0, (zero,) * (2 * N_SENT))
            down = sweep(1, up[: 2 * N_IN] + (zero,) * (2 * N_CROSS))
            order = down[2 * N_IN :] + down[: 2 * N_IN] + up[2 * N_IN :]
            for index in range(N_OWN):
                at = slice(index * QG + q8 * 8, index * QG + q8 * 8 + 8)
                cross[at, re_lanes] = order[2 * index]
                cross[at, im_lanes] = order[2 * index + 1]
    high, low = split_terms(cross[...])

    def turned(left, right):
        return lax.dot_general(left, right, (((1,), (1,)), ((), ())), preferred_element_type=F32)

    lagged = turned(l_high[...], high) + turned(l_high[...], low) + turned(l_low[...], high)
    out[...] = lagged.astype(BF16)
    to_above = lagged[:, N_CROSS * QG :]
    to_below = lagged[:, : N_SENT * QG]
    out_first[...] = jnp.where(odd == 1, to_below, to_above).astype(BF16)
    out_second[...] = jnp.where(odd == 1, to_above, to_below).astype(BF16)


def select_kernel(*refs):
    mine, swapped, pids, outs = refs[0:3], refs[3:6], refs[6:10], refs[10:14]
    chosen, lags = refs[14:16]
    _, core, odd = my_place()
    own, sent = N_OWN * QG, N_SENT * QG
    row_id = lax.broadcasted_iota(jnp.int32, (N_ALL * QG, 128), 0)
    col_id = lax.broadcasted_iota(jnp.int32, (N_ALL * QG, 128), 1)
    row_key = jnp.where((row_id & 15) == (col_id & 15), (row_id >> 4).astype(F32), -1.0)
    lane = pl.multiple_of(core * 128, 128)
    for rel, pid in enumerate(pids):
        ids = pid[0, :, pl.ds(lane, 128)].astype(F32)
        match = (row_key == ids[0:1, :]) | (row_key == ids[8:9, :])
        chosen[:, rel * 128 : (rel + 1) * 128] = jnp.where(match, 1.0, 0.0).astype(BF16)
    for side, (here, first, second) in enumerate((mine, swapped)):
        at = slice(side * LAG_ROWS, (side + 1) * LAG_ROWS)
        below = jnp.where(odd == 1, first[...].astype(F32), second[...].astype(F32)).astype(BF16)
        above = jnp.where(odd == 1, second[...].astype(F32), first[...].astype(F32)).astype(BF16)
        lags[at, 0:own] = here[...]
        lags[at, own : own + sent] = below
        lags[at, own + sent : own + 2 * sent] = above
    picked = mxu(lags[...], chosen[...]).astype(BF16)
    for rel in range(4):
        for side in range(2):
            outs[rel][side] = picked[side * LAG_ROWS : (side + 1) * LAG_ROWS, rel * 128 : (rel + 1) * 128]


def finish_kernel(pairs, count, *refs):
    pieces, table, out, stage, flat = refs[:4], *refs[4:8]
    member, core, _ = my_place()
    for rel in range(4):
        for side in range(2):
            stage[(core ^ side) * 4 + (member ^ rel)] = pieces[rel][side].astype(F32)
    group = lax.broadcasted_iota(jnp.int32, (LAG_ROWS, 128), 1) >> 4
    for s in range(SLOTS // 2):
        value = jnp.zeros((LAG_ROWS, 128), F32)
        for m in range(8):
            shift = ((m - s) * QG) % 128
            piece = stage[m]
            moved = pltpu.roll(piece, shift, 1) if shift else piece
            value = jnp.where(group == m, moved, value)
        flat[:, s * 128 : (s + 1) * 128] = value
    back = mxu(table[...], flat[...].astype(BF16))
    for s in range(SLOTS // 2):
        lanes = slice(s * 128, (s + 1) * 128)
        slot = core * (SLOTS // 2) + s
        value = jnp.where(pairs[0, slot] > pairs[1, slot], back[:, lanes], flat[:, lanes])
        out[:, s, :] = jnp.where(slot < count[0], value, 0.0)[0:LAGS]


VM = pl.BlockSpec(memory_space=pltpu.VMEM)
SM = pl.BlockSpec(memory_space=pltpu.SMEM)
PARAMS = pltpu.CompilerParams(vmem_limit_bytes=VMEM_LIMIT)


def shape(dims, kind):
    return jax.ShapeDtypeStruct(dims, kind)


def local(traces, channel_ok, time_taps, space_taps, pair_blocks, pair_count):
    n_chan = lax.axis_size("chan")
    n_plane = n_chan // PLANE
    chan_width, half = traces.shape
    segs = 2 * half // SEG
    part = segs // 2
    core = lax.axis_index("tm")
    odd = (lax.axis_index("chan") // PLANE) % 2
    pairs = jnp.transpose(pair_blocks)

    def to_core(x):
        return lax.ppermute(x, "tm", [(0, 1), (1, 0)])

    def in_plane(x, rel):
        return lax.ppermute(x, "chan", [(c, c ^ rel) for c in range(n_chan)])

    def plane_swap(x, start):
        route = []
        for p in range(start, n_plane - 1, 2):
            for k in range(PLANE):
                low, high = p * PLANE + k, (p + 1) * PLANE + k
                route += [(low, high), (high, low)]
        return lax.ppermute(x, "chan", route)

    ok = channel_ok.astype(F32)
    head = traces[0:2] * ok[0:2, None]
    tail = traces[chan_width - 2 :] * ok[chan_width - 2 :, None]
    got = to_core(jnp.where(core == 0, tail, head))
    mine = jnp.where(core == 0, head, tail)
    got, late = lax.optimization_barrier((got, traces))
    route = []
    for c in range(n_chan - 1):
        route += [(2 * c + 1, 2 * c + 2), (2 * c + 2, 2 * c + 1)]
    halos = lax.ppermute(jnp.concatenate([mine, got], axis=0), BOTH, route)
    other = to_core(late)
    table = shape((2 * SEG, SEG), BF16)
    t_high, t_low, pid = pl.pallas_call(
        prepare_kernel,
        out_shape=[table, table, shape((QG, SLOTS * QG), BF16)],
        in_specs=[SM, SM],
        out_specs=[VM] * 3,
        compiler_params=PARAMS,
        name="prepare",
    )(time_taps, pairs)
    block = shape((segs + 1, QG, SEG), BF16)
    short = shape((part, QG, SEG), BF16)
    rows = chan_width // 2
    first, second, *sent = pl.pallas_call(
        filter_kernel,
        out_shape=[short] * 2 + [block] * 3,
        in_specs=[SM] + [VM] * 7,
        out_specs=[VM] * 5,
        scratch_shapes=[
            pltpu.VMEM((rows + 16, 2 * half + SEG), BF16),
            pltpu.VMEM((rows + 16, 2 * half + SEG), BF16),
            pltpu.VMEM((8, half), F32),
            pltpu.VMEM((segs, rows, SEG), BF16),
            pltpu.VMEM((chan_width, 128), F32),
        ],
        compiler_params=PARAMS,
        name="filter_whiten",
    )(space_taps, traces, other, halos, channel_ok[None, :], t_high, t_low, pid)
    b1, b2, b3 = [in_plane(x, rel + 1) for rel, x in enumerate(sent)]

    def halves(x):
        near = lax.dynamic_slice_in_dim(x, (1 - odd) * part, part, axis=0)
        far = lax.dynamic_slice_in_dim(x, odd * part, part, axis=0)
        return near, far

    near_0, far_0 = plane_swap(first, 0), plane_swap(second, 1)
    b1, near_0, far_0 = lax.optimization_barrier((b1, near_0, far_0))
    (near_1, far_1), (near_2, far_2), (near_3, far_3) = halves(b1), halves(b2), halves(b3)
    near_1, far_1 = plane_swap(near_1, 0), plane_swap(far_1, 1)
    near_2, far_2 = plane_swap(near_2, 0), plane_swap(far_2, 1)
    near_3, far_3 = plane_swap(near_3, 0), plane_swap(far_3, 1)
    scale = 1.0 / math.sqrt(segs * SEG)
    l_high, l_low = inverse_np(scale)
    sent_shape = shape((LAG_ROWS, N_SENT * QG), BF16)
    lags, lags_first, lags_second = pl.pallas_call(
        pair_kernel,
        out_shape=[shape((LAG_ROWS, N_OWN * QG), BF16), sent_shape, sent_shape],
        in_specs=[VM] * 16,
        out_specs=[VM] * 3,
        scratch_shapes=[
            pltpu.VMEM((PLANE, segs, QG, 2 * SEG), F32),
            pltpu.VMEM((2, PLANE, part, QG, 2 * SEG), F32),
            pltpu.VMEM((N_OWN * QG, 2 * SEG), F32),
        ],
        compiler_params=PARAMS,
        name="pair_lags",
    )(
        first, second, b1, b2, b3, near_0, far_0, near_1, far_1, near_2, far_2, near_3, far_3,
        jnp.asarray(forward_np()), jnp.asarray(l_high), jnp.asarray(l_low),
    )
    from_first, from_second = plane_swap(lags_first, 0), plane_swap(lags_second, 1)
    known = [lags, from_first, from_second]
    pid_spec = pl.BlockSpec((1, QG, SEG), lambda step: (segs, 0, 0))
    own_spec = pl.BlockSpec((1, QG, SEG), lambda step: (0, 0, 0))
    slots_shape = shape((2, LAG_ROWS, 128), BF16)
    picked = pl.pallas_call(
        select_kernel,
        grid=(1,),
        out_shape=[slots_shape] * 4,
        in_specs=[VM] * 6 + [own_spec] + [pid_spec] * 3,
        out_specs=[VM] * 4,
        scratch_shapes=[
            pltpu.VMEM((N_ALL * QG, 512), BF16),
            pltpu.VMEM((2 * LAG_ROWS, N_ALL * QG), BF16),
        ],
        compiler_params=PARAMS,
        name="select_slots",
    )(*known, *[to_core(x) for x in known], pid[None], b1, b2, b3)
    pieces = [picked[0]] + [in_plane(x, rel + 1) for rel, x in enumerate(picked[1:])]
    out = pl.pallas_call(
        finish_kernel,
        out_shape=shape((LAGS, SLOTS // 2, chan_width), F32),
        in_specs=[SM] * 2 + [VM] * 5,
        out_specs=VM,
        scratch_shapes=[
            pltpu.VMEM((8, LAG_ROWS, 128), F32),
            pltpu.VMEM((LAG_ROWS, SLOTS // 2 * 128), F32),
        ],
        compiler_params=PARAMS,
        name="finish_slots",
    )(pairs, pair_count, *pieces, jnp.asarray(reverse_np()))
    return jnp.transpose(out, (1, 0, 2))


def solution(mesh):
    return jax.shard_map(
        local,
        mesh=mesh,
        in_specs=(P("chan", "tm"), P("chan"), P(), P(), P("chan", None), P("chan")),
        out_specs=P(("chan", "tm"), None, None),
        check_vma=False,
    )
```

time: 93.7 us -> 82.8 us (0.88)
  the two profiles are of different devices: /device:TPU:0 before, /device:TPU:16 now
where the time goes in v2:
time: 82.8 us; the launch traced here: 82 us
  starting transfers between devices  28.2 us (34%)
  Pallas kernels  25.2 us (30%)
  waiting for transfers between devices  22.4 us (27%)
  local copies, waits for them, and re-layouts  3.47 us (4%)
  other arithmetic  1.75 us (2%)
  between operations  0.99 us (1%)
    ppermute x10, starting transfers between devices, plane_swap(): return lax.ppermute(x, 'chan', route)  16.7 us
    ppermute x6, waiting for transfers between devices, in_plane(): return lax.ppermute(x, 'chan', [(c, c ^ rel) for c in range(n_chan)])  10.6 us
    pallas_call x1, Pallas kernels, local(): pl.pallas_call(filter_kernel, out_shape=[short] * 2 + [block] * 3, in_spe...  8.83 us
    ppermute x10, waiting for transfers between devices, plane_swap(): return lax.ppermute(x, 'chan', route)  8.05 us
    pallas_call x1, Pallas kernels, local(): pl.pallas_call(pair_kernel, out_shape=[shape((LAG_ROWS, N_OWN * QG), BF16...  7.31 us
    ppermute x6, starting transfers between devices, in_plane(): return lax.ppermute(x, 'chan', [(c, c ^ rel) for c in range(n_chan)])  6.98 us
    ppermute x1, starting transfers between devices, local(): halos = lax.ppermute(jnp.concatenate([mine, got], axis=0), BOTH, route)  4.19 us
    pallas_call x1, Pallas kernels, local(): pl.pallas_call(finish_kernel, out_shape=shape((LAGS, SLOTS // 2, chan_wid...  4.07 us
  transfers between devices with their start and end apart: 22, of which 13 were waited for; matrix products, arithmetic and copies ran while one was open for 0% of the time, Pallas kernels for 2%

profile of v2, /device:TPU:16, one launch (start us, length us, event | category | flops | bytes accessed | tf_op | source)
XLA Modules:
  0.0 82.0 jit_solution(14679319411144077265)
XLA Ops:
  0.0 0.7 convert_element_type.3
  0.7 0.1 fusion
  0.7 1.1 %broadcast_select_fusion = (f32[2,4096]{1,0:T(2,128)S(1)}, f32[2,4096]{1,0:T(2,128)S(1)}) fusion(pred[]{:T(512)S(6)} %eq.6, f32[128,4096]{1,0:T(8,128)} %own.1, f32[2]{0:T(128)S(1)} %get-tuple-element.54, f32[2]{0:T(128)S(1)} %get-tuple-element.53), kind=kLoop, calls=%fused_computation.3 | loop fusion | flops 32768 | bytes 131089 | tf_op jit(solution)/shard_map/jit(_where)/select_n | solution.py:352
  1.8 0.1 collective-permute-start
  1.9 1.2 %collective-permute-done = f32[2,4096]{1,0:T(2,128)S(1)} collective-permute-done((f32[2,4096]{1,0:T(2,128)S(1)}, f32[2,4096]{1,0:T(2,128)S(1)}, u32[]{:S(2)}, u32[]{:S(2)}) %collective-permute-start) | collective-permute-done | bytes 32800 | tf_op jit(solution)/shard_map/ppermute | solution.py:335
  3.1 0.2 collective-permute-start.1
  3.3 4.2 %collective-permute-start.2 = (f32[4,4096]{1,0:T(4,128)S(1)}, f32[4,4096]{1,0:T(4,128)S(1)}, u32[]{:S(2)}, u32[]{:S(2)}) collective-permute-start(f32[4,4096]{1,0:T(4,128)S(1)} %pad_maximum_fusion), channel_id=1, source_target_pairs={{1,2},{2,1},{3,4},{4,3},{5,6},{6,5},{7,8},{8,7},{9,10},{10,9},{11,... | collective-permute-start | bytes 196616 | tf_op jit(solution)/shard_map/ppermute | solution.py:357
  7.5 2.0 %prepare.1 = (bf16[512,256]{1,0:T(8,128)(2,1)}, bf16[512,256]{1,0:T(8,128)(2,1)}, bf16[16,256]{1,0:T(8,128)(2,1)}) custom-call(f32[33]{0:T(128)} %taps.1, s32[2,16]{1,0:T(2,128)} %bitcast.5), custom_call_target="tpu_custom_call" | custom-call | tf_op jit(solution)/shard_map/prepare/pallas_call | solution.py:360
  9.5 1.3 %collective-permute-done.2.halos = f32[4,4096]{1,0:T(4,128)S(1)} collective-permute-done((f32[4,4096]{1,0:T(4,128)S(1)}, f32[4,4096]{1,0:T(4,128)S(1)}, u32[]{:S(2)}, u32[]{:S(2)}) %collective-permute-start.2) | collective-permute-done | bytes 65568 | tf_op jit(solution)/shard_map/ppermute | solution.py:357
  10.8 0.0 collective-permute-done.1.other
  10.8 0.6 copy-done.20
  11.4 0.7 copy-done.3
  12.1 8.8 %filter_whiten.1 = (bf16[16,16,256]{2,1,0:T(8,128)(2,1)}, bf16[16,16,256]{2,1,0:T(8,128)(2,1)}, bf16[33,16,256]{2,1,0:T(8,128)(2,1)}, bf16[33,16,256]{2,1,0:T(8,128)(2,1)}, bf16[33,16,256]{2,1,0:T(8,128)(2,1)}) custom-call(f32[5]{0:T(128)} %space.1, f32[128,4096]{1,0:T(8,128)} %own.1, f32[128,4096]{1,0:T(8,128)} %copy-done.3, f32[4,4096]{1,0:T(4,128)} %copy-done.20, ...), custom_call_target="tpu_custom_call" | custom-call | tf_op jit(solution)/shard_map/filter_whiten/pallas_call | solution.py:371
  20.9 0.8 %collective-permute-start.7 = (bf16[33,16,256]{2,1,0:T(8,128)(2,1)}, bf16[33,16,256]{2,1,0:T(8,128)(2,1)S(1)}, u32[]{:S(2)}, u32[]{:S(2)}) collective-permute-start(bf16[33,16,256]{2,1,0:T(8,128)(2,1)} %get-tuple-element.35), channel_id=1, source_target_pairs={{0,6},{2,4},{4,2},{6,0},{8,14},{10,12},{12,10},{14,8},{16,22},{18,... | collective-permute-start | bytes 811016 | tf_op jit(solution)/shard_map/ppermute | solution.py:338
  21.8 0.2 collective-permute-start.6
  22.0 2.4 %collective-permute-start.3 = (bf16[33,16,256]{2,1,0:T(8,128)(2,1)}, bf16[33,16,256]{2,1,0:T(8,128)(2,1)S(1)}, u32[]{:S(2)}, u32[]{:S(2)}) collective-permute-start(bf16[33,16,256]{2,1,0:T(8,128)(2,1)} %get-tuple-element.32), channel_id=1, source_target_pairs={{0,2},{2,0},{4,6},{6,4},{8,10},{10,8},{12,14},{14,12},{16,18},{18,... | collective-permute-start | bytes 811016 | tf_op jit(solution)/shard_map/ppermute | solution.py:338
  24.4 1.6 %collective-permute-start.4 = (bf16[16,16,256]{2,1,0:T(8,128)(2,1)}, bf16[16,16,256]{2,1,0:T(8,128)(2,1)S(1)}, u32[]{:S(2)}, u32[]{:S(2)}) collective-permute-start(bf16[16,16,256]{2,1,0:T(8,128)(2,1)} %get-tuple-element.30.first), channel_id=1, source_target_pairs={{0,8},{8,0},{2,10},{10,2},{4,12},{12,4},{6,14},{14,6},{16,24},{24,... | collective-permute-start | bytes 393224 | tf_op jit(solution)/shard_map/ppermute | solution.py:346
  26.0 1.9 %collective-permute-start.5 = (bf16[16,16,256]{2,1,0:T(8,128)(2,1)}, bf16[16,16,256]{2,1,0:T(8,128)(2,1)S(1)}, u32[]{:S(2)}, u32[]{:S(2)}) collective-permute-start(bf16[16,16,256]{2,1,0:T(8,128)(2,1)} %get-tuple-element.31.second), channel_id=1, source_target_pairs={{8,16},{16,8},{10,18},{18,10},{12,20},{20,12},{14,22},{22,14},{9,1... | collective-permute-start | bytes 393224 | tf_op jit(solution)/shard_map/ppermute | solution.py:346
  27.9 3.5 %collective-permute-done.7.b3.refs_9_ = bf16[33,16,256]{2,1,0:T(8,128)(2,1)S(1)} collective-permute-done((bf16[33,16,256]{2,1,0:T(8,128)(2,1)}, bf16[33,16,256]{2,1,0:T(8,128)(2,1)S(1)}, u32[]{:S(2)}, u32[]{:S(2)}) %collective-permute-start.7) | collective-permute-done | bytes 270368 | tf_op jit(solution)/shard_map/ppermute | solution.py:338
  31.5 1.7 %collective-permute-start.12 = (bf16[16,16,256]{2,1,0:T(8,128)(2,1)S(1)}, bf16[16,16,256]{2,1,0:T(8,128)(2,1)S(1)}, u32[]{:S(2)}, u32[]{:S(2)}) collective-permute-start(bf16[16,16,256]{2,1,0:T(8,128)(2,1)S(1)} %get-tuple-element.48), channel_id=1, source_target_pairs={{0,8},{8,0},{2,10},{10,2},{4,12},{12,4},{6,14},{14,6},{16,24},{24,... | collective-permute-start | bytes 393224 | tf_op jit(solution)/shard_map/ppermute | solution.py:346
  33.2 3.0 %collective-permute-done.6.b2.refs_8_ = bf16[33,16,256]{2,1,0:T(8,128)(2,1)S(1)} collective-permute-done((bf16[33,16,256]{2,1,0:T(8,128)(2,1)}, bf16[33,16,256]{2,1,0:T(8,128)(2,1)S(1)}, u32[]{:S(2)}, u32[]{:S(2)}) %collective-permute-start.6) | collective-permute-done | bytes 270368 | tf_op jit(solution)/shard_map/ppermute | solution.py:338
  36.2 2.3 %collective-permute-start.13 = (bf16[16,16,256]{2,1,0:T(8,128)(2,1)S(1)}, bf16[16,16,256]{2,1,0:T(8,128)(2,1)S(1)}, u32[]{:S(2)}, u32[]{:S(2)}) collective-permute-start(bf16[16,16,256]{2,1,0:T(8,128)(2,1)S(1)} %get-tuple-element.47), channel_id=1, source_target_pairs={{8,16},{16,8},{10,18},{18,10},{12,20},{20,12},{14,22},{22,14},{9,1... | collective-permute-start | bytes 393224 | tf_op jit(solution)/shard_map/ppermute | solution.py:346
  38.6 0.0 collective-permute-done.4.near_0
  38.6 0.1 collective-permute-start.10
  38.7 3.5 %collective-permute-start.11 = (bf16[16,16,256]{2,1,0:T(8,128)(2,1)S(1)}, bf16[16,16,256]{2,1,0:T(8,128)(2,1)S(1)}, u32[]{:S(2)}, u32[]{:S(2)}) collective-permute-start(bf16[16,16,256]{2,1,0:T(8,128)(2,1)S(1)} %get-tuple-element.49), channel_id=1, source_target_pairs={{8,16},{16,8},{10,18},{18,10},{12,20},{20,12},{14,22},{22,14},{9,1... | collective-permute-start | bytes 393224 | tf_op jit(solution)/shard_map/ppermute | solution.py:346
  42.2 0.0 copy-start.2
  42.3 0.1 collective-permute-start.8
  42.4 2.6 %collective-permute-start.9 = (bf16[16,16,256]{2,1,0:T(8,128)(2,1)S(1)}, bf16[16,16,256]{2,1,0:T(8,128)(2,1)S(1)}, u32[]{:S(2)}, u32[]{:S(2)}) collective-permute-start(bf16[16,16,256]{2,1,0:T(8,128)(2,1)S(1)} %get-tuple-element.51), channel_id=1, source_target_pairs={{8,16},{16,8},{10,18},{18,10},{12,20},{20,12},{14,22},{22,14},{9,1... | collective-permute-start | bytes 393224 | tf_op jit(solution)/shard_map/ppermute | solution.py:346
  45.1 1.4 %collective-permute-done.11.far_2 = bf16[16,16,256]{2,1,0:T(8,128)(2,1)S(1)} collective-permute-done((bf16[16,16,256]{2,1,0:T(8,128)(2,1)S(1)}, bf16[16,16,256]{2,1,0:T(8,128)(2,1)S(1)}, u32[]{:S(2)}, u32[]{:S(2)}) %collective-permute-start.11) | collective-permute-done | bytes 131104 | tf_op jit(solution)/shard_map/ppermute | solution.py:346
  46.5 0.9 %collective-permute-done.8.near_1 = bf16[16,16,256]{2,1,0:T(8,128)(2,1)S(1)} collective-permute-done((bf16[16,16,256]{2,1,0:T(8,128)(2,1)S(1)}, bf16[16,16,256]{2,1,0:T(8,128)(2,1)S(1)}, u32[]{:S(2)}, u32[]{:S(2)}) %collective-permute-start.8) | collective-permute-done | bytes 131104 | tf_op jit(solution)/shard_map/ppermute | solution.py:346
  47.4 1.9 %collective-permute-done.9.far_1 = bf16[16,16,256]{2,1,0:T(8,128)(2,1)S(1)} collective-permute-done((bf16[16,16,256]{2,1,0:T(8,128)(2,1)S(1)}, bf16[16,16,256]{2,1,0:T(8,128)(2,1)S(1)}, u32[]{:S(2)}, u32[]{:S(2)}) %collective-permute-start.9) | collective-permute-done | bytes 131104 | tf_op jit(solution)/shard_map/ppermute | solution.py:346
  49.4 0.6 copy-done.12
  50.0 7.3 %pair_lags.1 = (bf16[208,416]{1,0:T(8,128)(2,1)}, bf16[208,256]{1,0:T(8,128)(2,1)}, bf16[208,256]{1,0:T(8,128)(2,1)}) custom-call(bf16[16,16,256]{2,1,0:T(8,128)(2,1)} %get-tuple-element.30.first, bf16[16,16,256]{2,1,0:T(8,128)(2,1)} %get-tuple-element.31.second, bf16[33,16,256]{2,1,0:T(8,128)(2,1)} %copy-done.2, bf16[33,16,256]{2,1,0:T(8,128)(2,1)} %copy-done.1, ...), custom_call_target="tpu_custom_call" | custom-call | tf_op jit(solution)/shard_map/pair_lags/pallas_call | solution.py:402
  57.3 2.9 %collective-permute-start.15 = (bf16[208,256]{1,0:T(8,128)(2,1)}, bf16[208,256]{1,0:T(8,128)(2,1)S(1)}, u32[]{:S(2)}, u32[]{:S(2)}) collective-permute-start(bf16[208,256]{1,0:T(8,128)(2,1)} %get-tuple-element.40), channel_id=1, source_target_pairs={{8,16},{16,8},{10,18},{18,10},{12,20},{20,12},{14,22},{22,14},{9,1... | collective-permute-start | bytes 319496 | tf_op jit(solution)/shard_map/ppermute | solution.py:346
  60.3 0.1 collective-permute-start.16
  60.3 1.9 %collective-permute-done.14.refs_1_ = bf16[208,256]{1,0:T(8,128)(2,1)S(1)} collective-permute-done((bf16[208,256]{1,0:T(8,128)(2,1)}, bf16[208,256]{1,0:T(8,128)(2,1)S(1)}, u32[]{:S(2)}, u32[]{:S(2)}) %collective-permute-start.14) | collective-permute-done | bytes 106528 | tf_op jit(solution)/shard_map/ppermute | solution.py:346
  62.3 1.9 %collective-permute-done.15.refs_2_ = bf16[208,256]{1,0:T(8,128)(2,1)S(1)} collective-permute-done((bf16[208,256]{1,0:T(8,128)(2,1)}, bf16[208,256]{1,0:T(8,128)(2,1)S(1)}, u32[]{:S(2)}, u32[]{:S(2)}) %collective-permute-start.15) | collective-permute-done | bytes 106528 | tf_op jit(solution)/shard_map/ppermute | solution.py:346
  64.2 1.3 %collective-permute-done.18.refs_5_ = bf16[208,256]{1,0:T(8,128)(2,1)S(1)} collective-permute-done((bf16[208,256]{1,0:T(8,128)(2,1)S(1)}, bf16[208,256]{1,0:T(8,128)(2,1)S(1)}, u32[]{:S(2)}, u32[]{:S(2)}) %collective-permute-start.18) | collective-permute-done | bytes 106528 | tf_op jit(solution)/shard_map/ppermute | solution.py:335
  65.5 0.6 copy-done.17
  66.1 3.0 %select_slots.1 = (bf16[2,208,128]{2,1,0:T(8,128)(2,1)}, bf16[2,208,128]{2,1,0:T(8,128)(2,1)}, bf16[2,208,128]{2,1,0:T(8,128)(2,1)}, bf16[2,208,128]{2,1,0:T(8,128)(2,1)}) custom-call(bf16[208,416]{1,0:T(8,128)(2,1)} %get-tuple-element.38.refs_0_, bf16[208,256]{1,0:T(8,128)(2,1)} %copy-done.13, bf16[208,256]{1,0:T(8,128)(2,1)} %copy-done.14, ...), custom_call_target="tpu_custom_call" | custom-call | tf_op jit(solution)/shard_map/select_slots/pallas_call | solution.py:423
  69.1 0.5 collective-permute-start.19
  69.6 1.8 %collective-permute-start.20 = (bf16[2,208,128]{2,1,0:T(8,128)(2,1)}, bf16[2,208,128]{2,1,0:T(8,128)(2,1)S(1)}, u32[]{:S(2)}, u32[]{:S(2)}) collective-permute-start(bf16[2,208,128]{2,1,0:T(8,128)(2,1)} %get-tuple-element.43), channel_id=1, source_target_pairs={{0,4},{2,6},{4,0},{6,2},{8,12},{10,14},{12,8},{14,10},{16,20},{18,... | collective-permute-start | bytes 319496 | tf_op jit(solution)/shard_map/ppermute | solution.py:338
  71.4 1.2 %collective-permute-start.21 = (bf16[2,208,128]{2,1,0:T(8,128)(2,1)}, bf16[2,208,128]{2,1,0:T(8,128)(2,1)S(1)}, u32[]{:S(2)}, u32[]{:S(2)}) collective-permute-start(bf16[2,208,128]{2,1,0:T(8,128)(2,1)} %get-tuple-element.44), channel_id=1, source_target_pairs={{0,6},{2,4},{4,2},{6,0},{8,14},{10,12},{12,10},{14,8},{16,22},{18,... | collective-permute-start | bytes 319496 | tf_op jit(solution)/shard_map/ppermute | solution.py:338
  73.2 1.9 %collective-permute-done.19.refs_1_ = bf16[2,208,128]{2,1,0:T(8,128)(2,1)S(1)} collective-permute-done((bf16[2,208,128]{2,1,0:T(8,128)(2,1)}, bf16[2,208,128]{2,1,0:T(8,128)(2,1)S(1)}, u32[]{:S(2)}, u32[]{:S(2)}) %collective-permute-start.19) | collective-permute-done | bytes 106528 | tf_op jit(solution)/shard_map/ppermute | solution.py:338
  75.2 1.2 %collective-permute-done.20.refs_2_ = bf16[2,208,128]{2,1,0:T(8,128)(2,1)S(1)} collective-permute-done((bf16[2,208,128]{2,1,0:T(8,128)(2,1)}, bf16[2,208,128]{2,1,0:T(8,128)(2,1)S(1)}, u32[]{:S(2)}, u32[]{:S(2)}) %collective-permute-start.20) | collective-permute-done | bytes 106528 | tf_op jit(solution)/shard_map/ppermute | solution.py:338
  76.3 0.9 %collective-permute-done.21.refs_3_ = bf16[2,208,128]{2,1,0:T(8,128)(2,1)S(1)} collective-permute-done((bf16[2,208,128]{2,1,0:T(8,128)(2,1)}, bf16[2,208,128]{2,1,0:T(8,128)(2,1)S(1)}, u32[]{:S(2)}, u32[]{:S(2)}) %collective-permute-start.21) | collective-permute-done | bytes 106528 | tf_op jit(solution)/shard_map/ppermute | solution.py:338
  77.3 0.6 copy-done.19
  77.9 4.1 %finish_slots.1 = f32[201,8,128]{2,1,0:T(8,128)} custom-call(s32[2,16]{1,0:T(2,128)} %bitcast.6, s32[1]{0:T(128)S(6)} %copy.11.count, bf16[2,208,128]{2,1,0:T(8,128)(2,1)} %get-tuple-element.41.refs_0_, bf16[2,208,128]{2,1,0:T(8,128)(2,1)} %copy-done.16, bf16[2,208,128]{2,1,0:T(8,128)(2,1)} %copy-done.18, bf16[2,208,128]{2,1,0:T(8,128)(2,1)} %copy-done.19, ...), custom_call_target="tpu_custom_call" | custom-call | tf_op jit(solution)/shard_map/finish_slots/pallas_call | solution.py:437
  (50 shorter events, 0.2 us)
Async XLA Ops:
  1.8 1.3 %collective-permute-start = (f32[2,4096]{1,0:T(2,128)S(1)}, f32[2,4096]{1,0:T(2,128)S(1)}, u32[]{:S(2)}, u32[]{:S(2)}) collective-permute-start(f32[2,4096]{1,0:T(2,128)S(1)} %get-tuple-element.46), channel_id=1, source_target_pairs={{0,1},{1,0},{2,3},{3,2},{4,5},{5,4},{6,7},{7,6},{8,9},{9,8},{10,11... | collective-permute-start | bytes 98312 | tf_op jit(solution)/shard_map/ppermute | solution.py:335
  3.1 7.7 %collective-permute-start.1 = (f32[128,4096]{1,0:T(8,128)}, f32[128,4096]{1,0:T(8,128)S(1)}, u32[]{:S(2)}, u32[]{:S(2)}) collective-permute-start(f32[128,4096]{1,0:T(8,128)} %own.1), channel_id=1, source_target_pairs={{0,1},{1,0},{2,3},{3,2},{4,5},{5,4},{6,7},{7,6},{8,9},{9,8},{10,11... | collective-permute-start | bytes 6291464 | tf_op jit(solution)/shard_map/ppermute | solution.py:335
  3.3 7.5 %collective-permute-start.2 = (f32[4,4096]{1,0:T(4,128)S(1)}, f32[4,4096]{1,0:T(4,128)S(1)}, u32[]{:S(2)}, u32[]{:S(2)}) collective-permute-start(f32[4,4096]{1,0:T(4,128)S(1)} %pad_maximum_fusion), channel_id=1, source_target_pairs={{1,2},{2,1},{3,4},{4,3},{5,6},{6,5},{7,8},{8,7},{9,10},{10,9},{11,... | collective-permute-start | bytes 196616 | tf_op jit(solution)/shard_map/ppermute | solution.py:357
  10.8 0.6 copy-start.20
  10.8 1.4 %copy-start.3 = (f32[128,4096]{1,0:T(8,128)}, f32[128,4096]{1,0:T(8,128)S(1)}, u32[]{:S(2)}) copy-start(f32[128,4096]{1,0:T(8,128)S(1)} %collective-permute-done.1.other) | copy-start | bytes 6291460
  20.9 10.5 %collective-permute-start.7 = (bf16[33,16,256]{2,1,0:T(8,128)(2,1)}, bf16[33,16,256]{2,1,0:T(8,128)(2,1)S(1)}, u32[]{:S(2)}, u32[]{:S(2)}) collective-permute-start(bf16[33,16,256]{2,1,0:T(8,128)(2,1)} %get-tuple-element.35), channel_id=1, source_target_pairs={{0,6},{2,4},{4,2},{6,0},{8,14},{10,12},{12,10},{14,8},{16,22},{18,... | collective-permute-start | bytes 811016 | tf_op jit(solution)/shard_map/ppermute | solution.py:338
  21.8 14.4 %collective-permute-start.6 = (bf16[33,16,256]{2,1,0:T(8,128)(2,1)}, bf16[33,16,256]{2,1,0:T(8,128)(2,1)S(1)}, u32[]{:S(2)}, u32[]{:S(2)}) collective-permute-start(bf16[33,16,256]{2,1,0:T(8,128)(2,1)} %get-tuple-element.34), channel_id=1, source_target_pairs={{0,4},{2,6},{4,0},{6,2},{8,12},{10,14},{12,8},{14,10},{16,20},{18,... | collective-permute-start | bytes 811016 | tf_op jit(solution)/shard_map/ppermute | solution.py:338
  22.0 20.2 %collective-permute-start.3 = (bf16[33,16,256]{2,1,0:T(8,128)(2,1)}, bf16[33,16,256]{2,1,0:T(8,128)(2,1)S(1)}, u32[]{:S(2)}, u32[]{:S(2)}) collective-permute-start(bf16[33,16,256]{2,1,0:T(8,128)(2,1)} %get-tuple-element.32), channel_id=1, source_target_pairs={{0,2},{2,0},{4,6},{6,4},{8,10},{10,8},{12,14},{14,12},{16,18},{18,... | collective-permute-start | bytes 811016 | tf_op jit(solution)/shard_map/ppermute | solution.py:338
  24.4 14.2 %collective-permute-start.4 = (bf16[16,16,256]{2,1,0:T(8,128)(2,1)}, bf16[16,16,256]{2,1,0:T(8,128)(2,1)S(1)}, u32[]{:S(2)}, u32[]{:S(2)}) collective-permute-start(bf16[16,16,256]{2,1,0:T(8,128)(2,1)} %get-tuple-element.30.first), channel_id=1, source_target_pairs={{0,8},{8,0},{2,10},{10,2},{4,12},{12,4},{6,14},{14,6},{16,24},{24,... | collective-permute-start | bytes 393224 | tf_op jit(solution)/shard_map/ppermute | solution.py:346
  26.0 12.7 %collective-permute-start.5 = (bf16[16,16,256]{2,1,0:T(8,128)(2,1)}, bf16[16,16,256]{2,1,0:T(8,128)(2,1)S(1)}, u32[]{:S(2)}, u32[]{:S(2)}) collective-permute-start(bf16[16,16,256]{2,1,0:T(8,128)(2,1)} %get-tuple-element.31.second), channel_id=1, source_target_pairs={{8,16},{16,8},{10,18},{18,10},{12,20},{20,12},{14,22},{22,14},{9,1... | collective-permute-start | bytes 393224 | tf_op jit(solution)/shard_map/ppermute | solution.py:346
  31.4 17.9 %copy-start = (bf16[33,16,256]{2,1,0:T(8,128)(2,1)}, bf16[33,16,256]{2,1,0:T(8,128)(2,1)S(1)}, u32[]{:S(2)}) copy-start(bf16[33,16,256]{2,1,0:T(8,128)(2,1)S(1)} %collective-permute-done.7.b3.refs_9_) | copy-start | bytes 811012
  31.5 10.9 %collective-permute-start.12 = (bf16[16,16,256]{2,1,0:T(8,128)(2,1)S(1)}, bf16[16,16,256]{2,1,0:T(8,128)(2,1)S(1)}, u32[]{:S(2)}, u32[]{:S(2)}) collective-permute-start(bf16[16,16,256]{2,1,0:T(8,128)(2,1)S(1)} %get-tuple-element.48), channel_id=1, source_target_pairs={{0,8},{8,0},{2,10},{10,2},{4,12},{12,4},{6,14},{14,6},{16,24},{24,... | collective-permute-start | bytes 393224 | tf_op jit(solution)/shard_map/ppermute | solution.py:346
  36.2 13.1 %copy-start.1 = (bf16[33,16,256]{2,1,0:T(8,128)(2,1)}, bf16[33,16,256]{2,1,0:T(8,128)(2,1)S(1)}, u32[]{:S(2)}) copy-start(bf16[33,16,256]{2,1,0:T(8,128)(2,1)S(1)} %collective-permute-done.6.b2.refs_8_) | copy-start | bytes 811012
  36.2 8.8 %collective-permute-start.13 = (bf16[16,16,256]{2,1,0:T(8,128)(2,1)S(1)}, bf16[16,16,256]{2,1,0:T(8,128)(2,1)S(1)}, u32[]{:S(2)}, u32[]{:S(2)}) collective-permute-start(bf16[16,16,256]{2,1,0:T(8,128)(2,1)S(1)} %get-tuple-element.47), channel_id=1, source_target_pairs={{8,16},{16,8},{10,18},{18,10},{12,20},{20,12},{14,22},{22,14},{9,1... | collective-permute-start | bytes 393224 | tf_op jit(solution)/shard_map/ppermute | solution.py:346
  38.6 10.7 %copy-start.5 = (bf16[16,16,256]{2,1,0:T(8,128)(2,1)}, bf16[16,16,256]{2,1,0:T(8,128)(2,1)S(1)}, u32[]{:S(2)}) copy-start(bf16[16,16,256]{2,1,0:T(8,128)(2,1)S(1)} %collective-permute-done.4.near_0) | copy-start | bytes 393220
  38.6 6.4 %collective-permute-start.10 = (bf16[16,16,256]{2,1,0:T(8,128)(2,1)S(1)}, bf16[16,16,256]{2,1,0:T(8,128)(2,1)S(1)}, u32[]{:S(2)}, u32[]{:S(2)}) collective-permute-start(bf16[16,16,256]{2,1,0:T(8,128)(2,1)S(1)} %get-tuple-element.50), channel_id=1, source_target_pairs={{0,8},{8,0},{2,10},{10,2},{4,12},{12,4},{6,14},{14,6},{16,24},{24,... | collective-permute-start | bytes 393224 | tf_op jit(solution)/shard_map/ppermute | solution.py:346
  38.7 10.6 %copy-start.6 = (bf16[16,16,256]{2,1,0:T(8,128)(2,1)}, bf16[16,16,256]{2,1,0:T(8,128)(2,1)S(1)}, u32[]{:S(2)}) copy-start(bf16[16,16,256]{2,1,0:T(8,128)(2,1)S(1)} %collective-permute-done.5.far_0) | copy-start | bytes 393220
  38.7 7.8 %collective-permute-start.11 = (bf16[16,16,256]{2,1,0:T(8,128)(2,1)S(1)}, bf16[16,16,256]{2,1,0:T(8,128)(2,1)S(1)}, u32[]{:S(2)}, u32[]{:S(2)}) collective-permute-start(bf16[16,16,256]{2,1,0:T(8,128)(2,1)S(1)} %get-tuple-element.49), channel_id=1, source_target_pairs={{8,16},{16,8},{10,18},{18,10},{12,20},{20,12},{14,22},{22,14},{9,1... | collective-permute-start | bytes 393224 | tf_op jit(solution)/shard_map/ppermute | solution.py:346
  42.2 7.1 %copy-start.2 = (bf16[33,16,256]{2,1,0:T(8,128)(2,1)}, bf16[33,16,256]{2,1,0:T(8,128)(2,1)S(1)}, u32[]{:S(2)}) copy-start(bf16[33,16,256]{2,1,0:T(8,128)(2,1)S(1)} %collective-permute-done.3.b1.refs_7_) | copy-start | bytes 811012
  42.3 5.1 %collective-permute-start.8 = (bf16[16,16,256]{2,1,0:T(8,128)(2,1)S(1)}, bf16[16,16,256]{2,1,0:T(8,128)(2,1)S(1)}, u32[]{:S(2)}, u32[]{:S(2)}) collective-permute-start(bf16[16,16,256]{2,1,0:T(8,128)(2,1)S(1)} %get-tuple-element.52), channel_id=1, source_target_pairs={{0,8},{8,0},{2,10},{10,2},{4,12},{12,4},{6,14},{14,6},{16,24},{24,... | collective-permute-start | bytes 393224 | tf_op jit(solution)/shard_map/ppermute | solution.py:346
  42.4 7.0 %copy-start.7 = (bf16[16,16,256]{2,1,0:T(8,128)(2,1)}, bf16[16,16,256]{2,1,0:T(8,128)(2,1)S(1)}, u32[]{:S(2)}) copy-start(bf16[16,16,256]{2,1,0:T(8,128)(2,1)S(1)} %collective-permute-done.12.near_3) | copy-start | bytes 393220
  42.4 6.9 %collective-permute-start.9 = (bf16[16,16,256]{2,1,0:T(8,128)(2,1)S(1)}, bf16[16,16,256]{2,1,0:T(8,128)(2,1)S(1)}, u32[]{:S(2)}, u32[]{:S(2)}) collective-permute-start(bf16[16,16,256]{2,1,0:T(8,128)(2,1)S(1)} %get-tuple-element.51), channel_id=1, source_target_pairs={{8,16},{16,8},{10,18},{18,10},{12,20},{20,12},{14,22},{22,14},{9,1... | collective-permute-start | bytes 393224 | tf_op jit(solution)/shard_map/ppermute | solution.py:346
  45.0 4.3 %copy-start.8 = (bf16[16,16,256]{2,1,0:T(8,128)(2,1)}, bf16[16,16,256]{2,1,0:T(8,128)(2,1)S(1)}, u32[]{:S(2)}) copy-start(bf16[16,16,256]{2,1,0:T(8,128)(2,1)S(1)} %collective-permute-done.13.far_3) | copy-start | bytes 393220
  45.0 4.3 %copy-start.9 = (bf16[16,16,256]{2,1,0:T(8,128)(2,1)}, bf16[16,16,256]{2,1,0:T(8,128)(2,1)S(1)}, u32[]{:S(2)}) copy-start(bf16[16,16,256]{2,1,0:T(8,128)(2,1)S(1)} %collective-permute-done.10.near_2) | copy-start | bytes 393220
  46.5 2.9 %copy-start.10 = (bf16[16,16,256]{2,1,0:T(8,128)(2,1)}, bf16[16,16,256]{2,1,0:T(8,128)(2,1)S(1)}, u32[]{:S(2)}) copy-start(bf16[16,16,256]{2,1,0:T(8,128)(2,1)S(1)} %collective-permute-done.11.far_2) | copy-start | bytes 393220
  47.4 2.0 %copy-start.11 = (bf16[16,16,256]{2,1,0:T(8,128)(2,1)}, bf16[16,16,256]{2,1,0:T(8,128)(2,1)S(1)}, u32[]{:S(2)}) copy-start(bf16[16,16,256]{2,1,0:T(8,128)(2,1)S(1)} %collective-permute-done.8.near_1) | copy-start | bytes 393220
  49.4 0.6 copy-start.12
  57.3 4.9 %collective-permute-start.14 = (bf16[208,256]{1,0:T(8,128)(2,1)}, bf16[208,256]{1,0:T(8,128)(2,1)S(1)}, u32[]{:S(2)}, u32[]{:S(2)}) collective-permute-start(bf16[208,256]{1,0:T(8,128)(2,1)} %get-tuple-element.39), channel_id=1, source_target_pairs={{0,8},{8,0},{2,10},{10,2},{4,12},{12,4},{6,14},{14,6},{16,24},{24,... | collective-permute-start | bytes 319496 | tf_op jit(solution)/shard_map/ppermute | solution.py:346
  57.3 6.8 %collective-permute-start.15 = (bf16[208,256]{1,0:T(8,128)(2,1)}, bf16[208,256]{1,0:T(8,128)(2,1)S(1)}, u32[]{:S(2)}, u32[]{:S(2)}) collective-permute-start(bf16[208,256]{1,0:T(8,128)(2,1)} %get-tuple-element.40), channel_id=1, source_target_pairs={{8,16},{16,8},{10,18},{18,10},{12,20},{20,12},{14,22},{22,14},{9,1... | collective-permute-start | bytes 319496 | tf_op jit(solution)/shard_map/ppermute | solution.py:346
  60.3 3.9 %collective-permute-start.16 = (bf16[208,416]{1,0:T(8,128)(2,1)}, bf16[208,416]{1,0:T(8,128)(2,1)S(1)}, u32[]{:S(2)}, u32[]{:S(2)}) collective-permute-start(bf16[208,416]{1,0:T(8,128)(2,1)} %get-tuple-element.38.refs_0_), channel_id=1, source_target_pairs={{0,1},{1,0},{2,3},{3,2},{4,5},{5,4},{6,7},{7,6},{8,9},{9,8},{10,11... | collective-permute-start | bytes 519176 | tf_op jit(solution)/shard_map/ppermute | solution.py:335
  62.3 3.2 %copy-start.13 = (bf16[208,256]{1,0:T(8,128)(2,1)}, bf16[208,256]{1,0:T(8,128)(2,1)S(1)}, u32[]{:S(2)}) copy-start(bf16[208,256]{1,0:T(8,128)(2,1)S(1)} %collective-permute-done.14.refs_1_) | copy-start | bytes 319492
  62.3 1.9 %collective-permute-start.17 = (bf16[208,256]{1,0:T(8,128)(2,1)S(1)}, bf16[208,256]{1,0:T(8,128)(2,1)S(1)}, u32[]{:S(2)}, u32[]{:S(2)}) collective-permute-start(bf16[208,256]{1,0:T(8,128)(2,1)S(1)} %collective-permute-done.14.refs_1_), channel_id=1, source_target_pairs={{0,1},{1,0},{2,3},{3,2},{4,5},{5,4},{6,7},{7,6},{8,9},{9,8},{10,11... | collective-permute-start | bytes 319496 | tf_op jit(solution)/shard_map/ppermute | solution.py:335
  64.1 1.3 %copy-start.14 = (bf16[208,256]{1,0:T(8,128)(2,1)}, bf16[208,256]{1,0:T(8,128)(2,1)S(1)}, u32[]{:S(2)}) copy-start(bf16[208,256]{1,0:T(8,128)(2,1)S(1)} %collective-permute-done.15.refs_2_) | copy-start | bytes 319492
  64.2 1.3 %collective-permute-start.18 = (bf16[208,256]{1,0:T(8,128)(2,1)S(1)}, bf16[208,256]{1,0:T(8,128)(2,1)S(1)}, u32[]{:S(2)}, u32[]{:S(2)}) collective-permute-start(bf16[208,256]{1,0:T(8,128)(2,1)S(1)} %collective-permute-done.15.refs_2_), channel_id=1, source_target_pairs={{0,1},{1,0},{2,3},{3,2},{4,5},{5,4},{6,7},{7,6},{8,9},{9,8},{10,11... | collective-permute-start | bytes 319496 | tf_op jit(solution)/shard_map/ppermute | solution.py:335
  64.2 1.3 %copy-start.4 = (bf16[208,416]{1,0:T(8,128)(2,1)}, bf16[208,416]{1,0:T(8,128)(2,1)S(1)}, u32[]{:S(2)}) copy-start(bf16[208,416]{1,0:T(8,128)(2,1)S(1)} %collective-permute-done.16.refs_3_) | copy-start | bytes 519172
  64.2 1.3 %copy-start.15 = (bf16[208,256]{1,0:T(8,128)(2,1)}, bf16[208,256]{1,0:T(8,128)(2,1)S(1)}, u32[]{:S(2)}) copy-start(bf16[208,256]{1,0:T(8,128)(2,1)S(1)} %collective-permute-done.17.refs_4_) | copy-start | bytes 319492
  65.5 0.6 copy-start.17
  69.1 6.1 %collective-permute-start.19 = (bf16[2,208,128]{2,1,0:T(8,128)(2,1)}, bf16[2,208,128]{2,1,0:T(8,128)(2,1)S(1)}, u32[]{:S(2)}, u32[]{:S(2)}) collective-permute-start(bf16[2,208,128]{2,1,0:T(8,128)(2,1)} %get-tuple-element.42), channel_id=1, source_target_pairs={{0,2},{2,0},{4,6},{6,4},{8,10},{10,8},{12,14},{14,12},{16,18},{18,... | collective-permute-start | bytes 319496 | tf_op jit(solution)/shard_map/ppermute | solution.py:338
  69.6 6.7 %collective-permute-start.20 = (bf16[2,208,128]{2,1,0:T(8,128)(2,1)}, bf16[2,208,128]{2,1,0:T(8,128)(2,1)S(1)}, u32[]{:S(2)}, u32[]{:S(2)}) collective-permute-start(bf16[2,208,128]{2,1,0:T(8,128)(2,1)} %get-tuple-element.43), channel_id=1, source_target_pairs={{0,4},{2,6},{4,0},{6,2},{8,12},{10,14},{12,8},{14,10},{16,20},{18,... | collective-permute-start | bytes 319496 | tf_op jit(solution)/shard_map/ppermute | solution.py:338
  71.4 5.8 %collective-permute-start.21 = (bf16[2,208,128]{2,1,0:T(8,128)(2,1)}, bf16[2,208,128]{2,1,0:T(8,128)(2,1)S(1)}, u32[]{:S(2)}, u32[]{:S(2)}) collective-permute-start(bf16[2,208,128]{2,1,0:T(8,128)(2,1)} %get-tuple-element.44), channel_id=1, source_target_pairs={{0,6},{2,4},{4,2},{6,0},{8,14},{10,12},{12,10},{14,8},{16,22},{18,... | collective-permute-start | bytes 319496 | tf_op jit(solution)/shard_map/ppermute | solution.py:338
  75.2 2.1 %copy-start.16 = (bf16[2,208,128]{2,1,0:T(8,128)(2,1)}, bf16[2,208,128]{2,1,0:T(8,128)(2,1)S(1)}, u32[]{:S(2)}) copy-start(bf16[2,208,128]{2,1,0:T(8,128)(2,1)S(1)} %collective-permute-done.19.refs_1_) | copy-start | bytes 319492
  76.3 0.9 %copy-start.18 = (bf16[2,208,128]{2,1,0:T(8,128)(2,1)}, bf16[2,208,128]{2,1,0:T(8,128)(2,1)S(1)}, u32[]{:S(2)}) copy-start(bf16[2,208,128]{2,1,0:T(8,128)(2,1)S(1)} %collective-permute-done.20.refs_2_) | copy-start | bytes 319492
  77.3 0.6 copy-start.19

commit v3 on v2

--- a/solution.py
+++ b/solution.py
@@ -22,7 +22,7 @@
 BOTH = ("chan", "tm")
 F32 = jnp.float32
 BF16 = jnp.bfloat16
-VMEM_LIMIT = 56 * 1024 * 1024
+VMEM_LIMIT = 20 * 1024 * 1024
 INNER = [(0, 1), (0, 2), (0, 3), (1, 2), (1, 3), (2, 3)]
 CROSS = [(i, j) for i in range(PLANE) for j in range(i + 1)]
 N_IN, N_CROSS = len(INNER), len(CROSS)
@@ -101,89 +101,108 @@
     return one, two
 
 
-def prepare_kernel(taps, pairs, t_high, t_low, pid):
+def tile_rows(own, core):
+    rows = own.shape[0] // 2
+    first_row = pl.multiple_of(core * rows, rows)
+    near_row = pl.multiple_of(rows - 8 + 8 * (1 - core), 8)
+    return pl.ds(first_row, rows), pl.ds(near_row, 8)
+
+
+def prepare_kernel(small, own, t_high, t_low, pid, space, ok, own_high, own_low):
+    _, core, _ = my_place()
     plane = lax.axis_index("chan") // PLANE
-    tap = (
-        lax.broadcasted_iota(jnp.int32, (2 * SEG, SEG), 0)
-        - lax.broadcasted_iota(jnp.int32, (2 * SEG, SEG), 1)
-        - (SEG // 2 - (TAPS - 1) // 2)
-    )
-    table = jnp.zeros((2 * SEG, SEG), F32)
+    t_high[...] = jnp.zeros(t_high.shape, BF16)
+    t_low[...] = jnp.zeros(t_low.shape, BF16)
+    shift = SEG // 2 - (TAPS - 1) // 2
+    height = 128 + TAPS - 1
+    tap = lax.broadcasted_iota(jnp.int32, (height, 128), 0) - lax.broadcasted_iota(
+        jnp.int32, (height, 128), 1
+    )
+    band = jnp.zeros((height, 128), F32)
     for j in range(TAPS):
-        table = jnp.where(tap == j, taps[j], table)
-    t_high[...], t_low[...] = split_terms(table)
+        band = jnp.where(tap == j, small[j], band)
+    high, low = split_terms(band)
+    for lanes in range(SEG // 128):
+        at = (slice(lanes * 128 + shift, lanes * 128 + shift + height), slice(lanes * 128, lanes * 128 + 128))
+        t_high[at] = high
+        t_low[at] = low
+    row = lax.broadcasted_iota(jnp.int32, space.shape, 0)
+    taps = jnp.zeros(space.shape, F32)
+    for j in range(STAPS):
+        taps = jnp.where(row == j, small[TAPS + j], taps)
+    space[...] = taps
     slot = lax.broadcasted_iota(jnp.int32, pid.shape, 1) >> 4
     upper = lax.broadcasted_iota(jnp.int32, pid.shape, 0) < 8
     ids = jnp.zeros(pid.shape, jnp.int32)
     for s in range(SLOTS):
-        one, two = pair_ids(pairs[0, s], pairs[1, s], plane)
+        left = small[TAPS + STAPS + s].astype(jnp.int32)
+        right = small[TAPS + STAPS + SLOTS + s].astype(jnp.int32)
+        one, two = pair_ids(left, right, plane)
         ids = jnp.where(slot == s, jnp.where(upper, one, two), ids)
     pid[...] = ids.astype(F32).astype(BF16)
+    at = lax.broadcasted_iota(jnp.int32, ok.shape, 0)
+    values = jnp.zeros(ok.shape, F32)
+    for k in range(ok.shape[0]):
+        values = jnp.where(at == k, small[TAPS + STAPS + 2 * SLOTS + k], values)
+    ok[...] = values
+    main, near = tile_rows(own, core)
+    own_high[...], own_low[...] = split_terms(own[main, :] * ok[main, 0:1])
 
 
 def filter_kernel(
-    space, own, other, halos, ok, t_high, t_low, pid,
-    out_first, out_second, out_1, out_2, out_3, x_high, x_low, edge, white, ok_column,
+    own, own_high, own_low, other, halos, space, ok, t_high, t_low, pid,
+    out_first, out_second, out_1, out_2, out_3, x_high, x_low, edge, white,
 ):
     member, core, odd = my_place()
     half = own.shape[1]
-    rows = own.shape[0] // 2
+    rows = own_high.shape[0]
+    main, near = tile_rows(own, core)
     pad = SEG // 2
-    first_row = pl.multiple_of(core * rows, rows)
-    edge_row = pl.multiple_of(rows - 8 + 8 * (1 - core), 8)
+    total = 2 * half
     zeros = jnp.zeros((rows + 16, pad), BF16)
-    total = 2 * half
     for buf in (x_high, x_low):
         buf[:, 0:pad] = zeros
         buf[:, pad + total : 2 * pad + total] = zeros
-    width = ok.shape[1]
-    diagonal = lax.broadcasted_iota(jnp.int32, (width, width), 0) == lax.broadcasted_iota(
-        jnp.int32, (width, width), 1
-    )
-    spread = jnp.where(diagonal, ok[...].astype(F32), 0.0)
-    ok_column[...] = jnp.broadcast_to(jnp.sum(spread, axis=1, keepdims=True), ok_column.shape)
-    ok_rows = ok_column[pl.ds(first_row, rows), 0:1]
-    ok_edge = ok_column[pl.ds(edge_row, 8), 0:1]
-    for source, halo, slot in ((own, halos[2:4], core), (other, halos[0:2], 1 - core)):
-        lanes = pl.ds(pl.multiple_of(pad + slot * half, pad), half)
-        high, low = split_terms(source[pl.ds(first_row, rows), :] * ok_rows)
-        x_high[0:rows, lanes] = high
-        x_low[0:rows, lanes] = low
+    own_lanes = pl.ds(pl.multiple_of(pad + core * half, pad), half)
+    other_lanes = pl.ds(pl.multiple_of(pad + (1 - core) * half, pad), half)
+    x_high[0:rows, own_lanes] = own_high[...]
+    x_low[0:rows, own_lanes] = own_low[...]
+    x_high[0:rows, other_lanes], x_low[0:rows, other_lanes] = split_terms(other[main, :] * ok[main, 0:1])
+    ok_near = ok[near, 0:1]
+    for source, halo, lanes in ((own, halos[2:4], own_lanes), (other, halos[0:2], other_lanes)):
         for k in range(4):
             edge[2 * k : 2 * k + 2, :] = halo
-        near = source[pl.ds(edge_row, 8), :] * ok_edge
-        far = edge[...]
-        is_low = core == 0
-        tile = jnp.concatenate([jnp.where(is_low, far, near), jnp.where(is_low, near, far)], axis=0)
-        high, low = split_terms(tile)
+        inside = source[near, :] * ok_near
+        outside = edge[...]
+        above = jnp.where(core == 0, outside, inside)
+        below = jnp.where(core == 0, inside, outside)
+        high, low = split_terms(jnp.concatenate([above, below], axis=0))
         x_high[rows : rows + 16, lanes] = high
         x_low[rows : rows + 16, lanes] = low
     segs = total // SEG
     chunk = 8
     height = rows + 16
+    taps = [space[j : j + 1, :] for j in range(STAPS)]
 
     def body(step, carry):
         seg0 = step * chunk
-        high = jnp.concatenate(
-            [x_high[:, pl.ds(pl.multiple_of((seg0 + s) * SEG, SEG), 2 * SEG)] for s in range(chunk)], axis=0
-        )
-        low = jnp.concatenate(
-            [x_low[:, pl.ds(pl.multiple_of((seg0 + s) * SEG, SEG), 2 * SEG)] for s in range(chunk)], axis=0
-        )
+        spans = [pl.ds(pl.multiple_of((seg0 + s) * SEG, SEG), 2 * SEG) for s in range(chunk)]
+        high = jnp.concatenate([x_high[:, span] for span in spans], axis=0)
+        low = jnp.concatenate([x_low[:, span] for span in spans], axis=0)
         y = mxu(high, t_high[...]) + mxu(low, t_high[...]) + mxu(high, t_low[...])
         for s in range(chunk):
             block = y[s * height : (s + 1) * height]
             ext = jnp.concatenate(
                 [block[rows : rows + 8], block[0:rows], block[rows + 8 : rows + 16]], axis=0
             )
-            filtered = space[0] * ext[6 : 6 + rows]
+            filtered = taps[0] * ext[6 : 6 + rows]
             for j in range(1, STAPS):
-                filtered = filtered + space[j] * ext[6 + j : 6 + j + rows]
+                filtered = filtered + taps[j] * ext[6 + j : 6 + j + rows]
             power = jnp.mean(filtered * filtered, axis=1, keepdims=True)
             white[seg0 + s] = (filtered * (1.0 / jnp.sqrt(power + 1e-5))).astype(BF16)
         return carry
 
-    lax.fori_loop(0, segs // chunk, body, 0)
+    lax.fori_loop(0, segs // chunk, body, 0, unroll=True)
     own_row = pl.multiple_of(member * QG, QG)
     part = segs // 2
     out_first[...] = white[pl.ds((1 - odd) * part, part), pl.ds(own_row, QG), :]
@@ -195,7 +214,7 @@
 
 
 def pair_kernel(
-    first, second, b1, b2, b3, near_0, far_0, near_1, far_1, near_2, far_2, near_3, far_3, table, l_high, l_low,
+    first, second, b1, b2, b3, near_0, far_0, near_12, far_12, near_3, far_3, table, l_high, l_low,
     out, out_first, out_second, spec, spec_z, cross,
 ):
     member, _, odd = my_place()
@@ -210,9 +229,11 @@
     spec[member, pl.ds(odd * part, part)] = transform(second[...])
     for rel, ref in ((1, b1), (2, b2), (3, b3)):
         spec[member ^ rel] = transform(ref[0:segs])
-    for side, refs in ((odd, (near_0, near_1, near_2, near_3)), (1 - odd, (far_0, far_1, far_2, far_3))):
-        for rel, ref in enumerate(refs):
-            spec_z[side, member ^ rel] = transform(ref[...])
+    for side, refs in ((odd, (near_0, near_12, near_3)), (1 - odd, (far_0, far_12, far_3))):
+        spec_z[side, member] = transform(refs[0][...])
+        spec_z[side, member ^ 1] = transform(refs[1][0])
+        spec_z[side, member ^ 2] = transform(refs[1][1])
+        spec_z[side, member ^ 3] = transform(refs[2][...])
     for q8 in range(QG // 8):
         for lanes in range(SEG // 128):
             rows = slice(q8 * 8, q8 * 8 + 8)
@@ -240,7 +261,7 @@
                         result += add(sums, N_IN + k, low[i], high[j])
                     return tuple(result)
 
-                return lax.fori_loop(0, part, body, sums, unroll=2)
+                return lax.fori_loop(0, part, body, sums, unroll=4)
 
             zero = jnp.zeros((8, 128), F32)
             up = sweep(0, (zero,) * (2 * N_SENT))
@@ -345,56 +366,68 @@
                 route += [(low, high), (high, low)]
         return lax.ppermute(x, "chan", route)
 
-    ok = channel_ok.astype(F32)
-    head = traces[0:2] * ok[0:2, None]
-    tail = traces[chan_width - 2 :] * ok[chan_width - 2 :, None]
+    head, tail = traces[0:2], traces[chan_width - 2 :]
     got = to_core(jnp.where(core == 0, tail, head))
     mine = jnp.where(core == 0, head, tail)
-    got, late = lax.optimization_barrier((got, traces))
+    got, late, taps, space, ok, pairs = lax.optimization_barrier(
+        (got, traces, time_taps, space_taps, channel_ok, pairs)
+    )
     route = []
     for c in range(n_chan - 1):
         route += [(2 * c + 1, 2 * c + 2), (2 * c + 2, 2 * c + 1)]
-    halos = lax.ppermute(jnp.concatenate([mine, got], axis=0), BOTH, route)
+    alive = jnp.where(core == 0, channel_ok[0:2], channel_ok[chan_width - 2 :]).astype(F32)[:, None]
+    halos = lax.ppermute(jnp.concatenate([mine * alive, got * alive], axis=0), BOTH, route)
     other = to_core(late)
+    parts = (taps, space, pairs[0].astype(F32), pairs[1].astype(F32), ok.astype(F32))
+    small_size = sum(x.shape[0] for x in parts)
+    small, at = jnp.zeros((small_size,), F32), 0
+    for x in parts:
+        small = small + jnp.pad(x, (at, small_size - at - x.shape[0]))
+        at += x.shape[0]
+    rows = chan_width // 2
     table = shape((2 * SEG, SEG), BF16)
-    t_high, t_low, pid = pl.pallas_call(
+    split = shape((rows, half), BF16)
+    t_high, t_low, pid, space, ok, own_high, own_low = pl.pallas_call(
         prepare_kernel,
-        out_shape=[table, table, shape((QG, SLOTS * QG), BF16)],
-        in_specs=[SM, SM],
-        out_specs=[VM] * 3,
+        out_shape=[
+            table, table, shape((QG, SLOTS * QG), BF16), shape((8, SEG), F32), shape((chan_width, 128), F32),
+            split, split,
+        ],
+        in_specs=[SM, VM],
+        out_specs=[VM] * 7,
         compiler_params=PARAMS,
         name="prepare",
-    )(time_taps, pairs)
+    )(small, late)
     block = shape((segs + 1, QG, SEG), BF16)
     short = shape((part, QG, SEG), BF16)
-    rows = chan_width // 2
     first, second, *sent = pl.pallas_call(
         filter_kernel,
         out_shape=[short] * 2 + [block] * 3,
-        in_specs=[SM] + [VM] * 7,
+        in_specs=[VM] * 10,
         out_specs=[VM] * 5,
         scratch_shapes=[
             pltpu.VMEM((rows + 16, 2 * half + SEG), BF16),
             pltpu.VMEM((rows + 16, 2 * half + SEG), BF16),
             pltpu.VMEM((8, half), F32),
             pltpu.VMEM((segs, rows, SEG), BF16),
-            pltpu.VMEM((chan_width, 128), F32),
         ],
         compiler_params=PARAMS,
         name="filter_whiten",
-    )(space_taps, traces, other, halos, channel_ok[None, :], t_high, t_low, pid)
-    b1, b2, b3 = [in_plane(x, rel + 1) for rel, x in enumerate(sent)]
+    )(late, own_high, own_low, other, halos, space, ok, t_high, t_low, pid)
+    b1, b2 = in_plane(sent[0], 1), in_plane(sent[1], 2)
+    near_0, far_0 = plane_swap(first, 0), plane_swap(second, 1)
+    near_0, far_0, last = lax.optimization_barrier((near_0, far_0, sent[2]))
+    b3 = in_plane(last, 3)
 
     def halves(x):
         near = lax.dynamic_slice_in_dim(x, (1 - odd) * part, part, axis=0)
         far = lax.dynamic_slice_in_dim(x, odd * part, part, axis=0)
         return near, far
 
-    near_0, far_0 = plane_swap(first, 0), plane_swap(second, 1)
-    b1, near_0, far_0 = lax.optimization_barrier((b1, near_0, far_0))
-    (near_1, far_1), (near_2, far_2), (near_3, far_3) = halves(b1), halves(b2), halves(b3)
-    near_1, far_1 = plane_swap(near_1, 0), plane_swap(far_1, 1)
-    near_2, far_2 = plane_swap(near_2, 0), plane_swap(far_2, 1)
+    (near_1, far_1), (near_2, far_2) = halves(b1), halves(b2)
+    near_12 = plane_swap(jnp.stack([near_1, near_2]), 0)
+    far_12 = plane_swap(jnp.stack([far_1, far_2]), 1)
+    near_3, far_3 = halves(b3)
     near_3, far_3 = plane_swap(near_3, 0), plane_swap(far_3, 1)
     scale = 1.0 / math.sqrt(segs * SEG)
     l_high, l_low = inverse_np(scale)
@@ -402,7 +435,7 @@
     lags, lags_first, lags_second = pl.pallas_call(
         pair_kernel,
         out_shape=[shape((LAG_ROWS, N_OWN * QG), BF16), sent_shape, sent_shape],
-        in_specs=[VM] * 16,
+        in_specs=[VM] * 14,
         out_specs=[VM] * 3,
         scratch_shapes=[
             pltpu.VMEM((PLANE, segs, QG, 2 * SEG), F32),
@@ -412,7 +445,7 @@
         compiler_params=PARAMS,
         name="pair_lags",
     )(
-        first, second, b1, b2, b3, near_0, far_0, near_1, far_1, near_2, far_2, near_3, far_3,
+        first, second, b1, b2, b3, near_0, far_0, near_12, far_12, near_3, far_3,
         jnp.asarray(forward_np()), jnp.asarray(l_high), jnp.asarray(l_low),
     )
     from_first, from_second = plane_swap(lags_first, 0), plane_swap(lags_second, 1)

time: 82.8 us -> 68.4 us (0.83)
  Pallas kernels: 25.2 us -> 15.2 us
  waiting for transfers between devices: 22.4 us -> 19.8 us
  other arithmetic: 1.75 us -> 4.18 us
  starting transfers between devices: 28.2 us -> 26.1 us
  local copies, waits for them, and re-layouts: 3.47 us -> 1.74 us
    ppermute x6, waiting for transfers between devices: 10.6 us -> 4.1 us  [in_plane(): return lax.ppermute(x, 'chan', [(c, c ^ rel) for c in range(n_chan)])]
    ppermute x10 -> x8, waiting for transfers between devices: 8.05 us -> 13.2 us  [plane_swap(): return lax.ppermute(x, 'chan', route)]
    pallas_call x1, Pallas kernels: 8.83 us -> 4.57 us  [local(): pl.pallas_call(filter_kernel, out_shape=[short] * 2 + [block] * 3, in_spe...]
    pallas_call x1, Pallas kernels: 7.31 us -> 4.61 us  [local(): pl.pallas_call(pair_kernel, out_shape=[shape((LAG_ROWS, N_OWN * QG), BF16...]
    ppermute x10 -> x8, starting transfers between devices: 16.7 us -> 14.5 us  [plane_swap(): return lax.ppermute(x, 'chan', route)]
    pallas_call x1, Pallas kernels: 2.99 us -> 0.96 us  [local(): pl.pallas_call(select_kernel, grid=(1,), out_shape=[slots_shape] * 4, in_...]
    unnamed x42 -> x14, local copies, waits for them, and re-layouts: 3.32 us -> 1.68 us
    convert_element_type x1 -> x3, other arithmetic: 0.66 us -> 2.22 us  [the longest x1 0.8 us: local(): jnp.where(core == 0, channel_ok[0:2], channel_ok[chan_width - 2:])]
  transfers between devices with their start and end apart: 22 -> 20, of which waited for: 13 -> 14; matrix products, arithmetic and copies ran while one was open for 0% -> 4% of each run, Pallas kernels for 2% -> 2%
where the time goes in v3:
time: 68.4 us; the launch traced here: 67.9 us
  starting transfers between devices  26.1 us (38%)
  waiting for transfers between devices  19.8 us (29%)
  Pallas kernels  15.2 us (22%)
  other arithmetic  4.18 us (6%)
  local copies, waits for them, and re-layouts  1.74 us (3%)
  between operations  0.93 us (1%)
    ppermute x8, starting transfers between devices, plane_swap(): return lax.ppermute(x, 'chan', route)  14.5 us
    ppermute x8, waiting for transfers between devices, plane_swap(): return lax.ppermute(x, 'chan', route)  13.2 us
    ppermute x6, starting transfers between devices, in_plane(): return lax.ppermute(x, 'chan', [(c, c ^ rel) for c in range(n_chan)])  7.1 us
    pallas_call x1, Pallas kernels, local(): pl.pallas_call(pair_kernel, out_shape=[shape((LAG_ROWS, N_OWN * QG), BF16...  4.61 us
    pallas_call x1, Pallas kernels, local(): pl.pallas_call(filter_kernel, out_shape=[short] * 2 + [block] * 3, in_spe...  4.57 us
    ppermute x1, starting transfers between devices, local(): lax.ppermute(jnp.concatenate([mine * alive, got * alive], axis=0), BOTH,...  4.19 us
    ppermute x6, waiting for transfers between devices, in_plane(): return lax.ppermute(x, 'chan', [(c, c ^ rel) for c in range(n_chan)])  4.1 us
    pallas_call x1, Pallas kernels, local(): pl.pallas_call(finish_kernel, out_shape=shape((LAGS, SLOTS // 2, chan_wid...  3.51 us
  transfers between devices with their start and end apart: 20, of which 14 were waited for; matrix products, arithmetic and copies ran while one was open for 4% of the time, Pallas kernels for 2%

profile of v3, /device:TPU:16, one launch (start us, length us, event | category | flops | bytes accessed | tf_op | source)
XLA Modules:
  0.0 67.9 jit_solution(17628769534778053020)
XLA Ops:
  0.0 0.8 %fusion = f32[2]{0:T(128)S(1)} fusion(pred[]{:T(512)S(6)} %eq.4, s32[128]{0:T(128)} %param.11), kind=kLoop, calls=%fused_computation.14 | loop fusion | flops 4 | bytes 25 | tf_op jit(solution)/shard_map/convert_element_type | solution.py:378
  0.8 1.0 %select_multiply_fusion = (f32[2,4096]{1,0:T(2,128)S(1)}, f32[2,4096]{1,0:T(2,128)S(1)}) fusion(pred[]{:T(512)S(6)} %eq.4, f32[128,4096]{1,0:T(8,128)} %own.1, f32[2]{0:T(128)S(1)} %fusion), kind=kLoop, calls=%fused_computation.7 | loop fusion | flops 24576 | bytes 131081 | tf_op jit(solution)/shard_map/mul | solution.py:379
  1.9 0.1 collective-permute-start
  1.9 1.2 %collective-permute-done = f32[2,4096]{1,0:T(2,128)S(1)} collective-permute-done((f32[2,4096]{1,0:T(2,128)S(1)}, f32[2,4096]{1,0:T(2,128)S(1)}, u32[]{:S(2)}, u32[]{:S(2)}) %collective-permute-start) | collective-permute-done | bytes 32800 | tf_op jit(solution)/shard_map/ppermute | solution.py:356
  3.1 0.2 collective-permute-start.1
  3.3 0.7 convert_element_type.32
  3.9 0.1 broadcast_multiply_fusion
  4.1 4.2 %collective-permute-start.2 = (f32[4,4096]{1,0:T(4,128)S(1)}, f32[4,4096]{1,0:T(4,128)S(1)}, u32[]{:S(2)}, u32[]{:S(2)}) collective-permute-start(f32[4,4096]{1,0:T(4,128)S(1)} %pad_maximum_fusion.2), channel_id=1, source_target_pairs={{1,2},{2,1},{3,4},{4,3},{5,6},{6,5},{7,8},{8,7},{9,10},{10,9},{11,... | collective-permute-start | bytes 196616 | tf_op jit(solution)/shard_map/ppermute | solution.py:379
  8.3 0.8 %convert_bitcast_fusion.1 = (f32[16]{0:T(128)S(1)}, f32[16]{0:T(128)S(1)}) fusion(s32[2,16]{1,0:T(2,128)} %bitcast.16), kind=kLoop, calls=%fused_computation.16 | loop fusion | flops 32 | bytes 256 | tf_op jit(solution)/shard_map/convert_element_type | solution.py:381
  9.0 0.7 %pad_add_fusion.small = f32[198]{0:T(256)S(1)} fusion(f32[128]{0:T(128)S(1)} %convert_element_type.32, f32[16]{0:T(128)S(1)} %get-tuple-element.70, f32[16]{0:T(128)S(1)} %get-tuple-element.69, f32[5]{0:T(128)} %param.13, f32[33]{0:T(128)} %param.12), kind=kLoop, calls=%fused_computation.12 | loop fusion | flops 792 | bytes 1584 | tf_op jit(solution)/shard_map/add | solution.py:385
  9.8 1.6 %copy-done = f32[128,4096]{1,0:T(8,128)S(1)} copy-done((f32[128,4096]{1,0:T(8,128)S(1)}, f32[128,4096]{1,0:T(8,128)}, u32[]{:S(2)}) %copy-start) | copy-done | bytes 2097176
  11.4 1.5 %prepare.1 = (bf16[512,256]{1,0:T(8,128)(2,1)S(1)}, bf16[512,256]{1,0:T(8,128)(2,1)S(1)}, bf16[16,256]{1,0:T(8,128)(2,1)S(1)}, f32[8,256]{1,0:T(8,128)S(1)}, f32...) custom-call(f32[198]{0:T(256)S(1)} %pad_add_fusion.small, f32[128,4096]{1,0:T(8,128)S(1)} %copy-done), custom_call_target="tpu_custom_call" | custom-call | tf_op jit(solution)/shard_map/prepare/pallas_call | solution.py:390
  12.9 0.1 copy-done.1
  13.0 4.6 %filter_whiten.1 = (bf16[16,16,256]{2,1,0:T(8,128)(2,1)S(1)}, bf16[16,16,256]{2,1,0:T(8,128)(2,1)S(1)}, bf16[33,16,256]{2,1,0:T(8,128)(2,1)S(1)}, bf16[33,16,256...) custom-call(f32[128,4096]{1,0:T(8,128)S(1)} %copy-done.1, bf16[64,4096]{1,0:T(8,128)(2,1)S(1)} %get-tuple-element.38.own_high, ...), custom_call_target="tpu_custom_call" | custom-call | tf_op jit(solution)/shard_map/filter_whiten/pallas_call | solution.py:403
  17.5 0.0 copy-start.2
  17.6 0.0 copy-start.3
  17.6 0.0 copy-start.4
  17.6 0.1 collective-permute-start.3
  17.7 1.2 %collective-permute-start.4 = (bf16[33,16,256]{2,1,0:T(8,128)(2,1)S(1)}, bf16[33,16,256]{2,1,0:T(8,128)(2,1)S(1)}, u32[]{:S(2)}, u32[]{:S(2)}) collective-permute-start(bf16[33,16,256]{2,1,0:T(8,128)(2,1)S(1)} %get-tuple-element.49), channel_id=1, source_target_pairs={{0,4},{2,6},{4,0},{6,2},{8,12},{10,14},{12,8},{14,10},{16,20},{18,... | collective-permute-start | bytes 811016 | tf_op jit(solution)/shard_map/ppermute | solution.py:359
  18.9 1.6 %collective-permute-start.5 = (bf16[16,16,256]{2,1,0:T(8,128)(2,1)S(1)}, bf16[16,16,256]{2,1,0:T(8,128)(2,1)S(1)}, u32[]{:S(2)}, u32[]{:S(2)}) collective-permute-start(bf16[16,16,256]{2,1,0:T(8,128)(2,1)S(1)} %get-tuple-element.46.first), channel_id=1, source_target_pairs={{0,8},{8,0},{2,10},{10,2},{4,12},{12,4},{6,14},{14,6},{16,24},{24,... | collective-permute-start | bytes 393224 | tf_op jit(solution)/shard_map/ppermute | solution.py:367
  20.4 1.9 %collective-permute-start.6 = (bf16[16,16,256]{2,1,0:T(8,128)(2,1)S(1)}, bf16[16,16,256]{2,1,0:T(8,128)(2,1)S(1)}, u32[]{:S(2)}, u32[]{:S(2)}) collective-permute-start(bf16[16,16,256]{2,1,0:T(8,128)(2,1)S(1)} %get-tuple-element.47.second), channel_id=1, source_target_pairs={{8,16},{16,8},{10,18},{18,10},{12,20},{20,12},{14,22},{22,14},{9,1... | collective-permute-start | bytes 393224 | tf_op jit(solution)/shard_map/ppermute | solution.py:367
  22.4 2.4 %collective-permute-done.5.near_0 = bf16[16,16,256]{2,1,0:T(8,128)(2,1)S(1)} collective-permute-done((bf16[16,16,256]{2,1,0:T(8,128)(2,1)S(1)}, bf16[16,16,256]{2,1,0:T(8,128)(2,1)S(1)}, u32[]{:S(2)}, u32[]{:S(2)}) %collective-permute-start.5) | collective-permute-done | bytes 131104 | tf_op jit(solution)/shard_map/ppermute | solution.py:367
  24.8 2.5 %collective-permute-done.6.far_0 = bf16[16,16,256]{2,1,0:T(8,128)(2,1)S(1)} collective-permute-done((bf16[16,16,256]{2,1,0:T(8,128)(2,1)S(1)}, bf16[16,16,256]{2,1,0:T(8,128)(2,1)S(1)}, u32[]{:S(2)}, u32[]{:S(2)}) %collective-permute-start.6) | collective-permute-done | bytes 131104 | tf_op jit(solution)/shard_map/ppermute | solution.py:367
  27.3 2.3 %collective-permute-start.7 = (bf16[33,16,256]{2,1,0:T(8,128)(2,1)S(1)}, bf16[33,16,256]{2,1,0:T(8,128)(2,1)S(1)}, u32[]{:S(2)}, u32[]{:S(2)}) collective-permute-start(bf16[33,16,256]{2,1,0:T(8,128)(2,1)S(1)} %get-tuple-element.51), channel_id=1, source_target_pairs={{0,6},{2,4},{4,2},{6,0},{8,14},{10,12},{12,10},{14,8},{16,22},{18,... | collective-permute-start | bytes 811016 | tf_op jit(solution)/shard_map/ppermute | solution.py:359
  29.7 1.9 %collective-permute-start.9 = (bf16[2,16,16,256]{3,2,1,0:T(8,128)(2,1)S(1)}, bf16[2,16,16,256]{3,2,1,0:T(8,128)(2,1)S(1)}, u32[]{:S(2)}, u32[]{:S(2)}) collective-permute-start(bf16[2,16,16,256]{3,2,1,0:T(8,128)(2,1)S(1)} %pad_maximum_fusion.1), channel_id=1, source_target_pairs={{8,16},{16,8},{10,18},{18,10},{12,20},{20,12},{14,22},{22,14},{9,1... | collective-permute-start | bytes 786440 | tf_op jit(solution)/shard_map/ppermute | solution.py:367
  31.6 3.2 %collective-permute-start.8 = (bf16[2,16,16,256]{3,2,1,0:T(8,128)(2,1)S(1)}, bf16[2,16,16,256]{3,2,1,0:T(8,128)(2,1)S(1)}, u32[]{:S(2)}, u32[]{:S(2)}) collective-permute-start(bf16[2,16,16,256]{3,2,1,0:T(8,128)(2,1)S(1)} %pad_maximum_fusion), channel_id=1, source_target_pairs={{0,8},{8,0},{2,10},{10,2},{4,12},{12,4},{6,14},{14,6},{16,24},{24,... | collective-permute-start | bytes 786440 | tf_op jit(solution)/shard_map/ppermute | solution.py:367
  34.8 0.1 collective-permute-done.7.b3.refs_9_
  34.9 0.1 collective-permute-start.10
  35.0 2.9 %collective-permute-start.11 = (bf16[16,16,256]{2,1,0:T(8,128)(2,1)S(1)}, bf16[16,16,256]{2,1,0:T(8,128)(2,1)S(1)}, u32[]{:S(2)}, u32[]{:S(2)}) collective-permute-start(bf16[16,16,256]{2,1,0:T(8,128)(2,1)S(1)} %get-tuple-element.63), channel_id=1, source_target_pairs={{8,16},{16,8},{10,18},{18,10},{12,20},{20,12},{14,22},{22,14},{9,1... | collective-permute-start | bytes 393224 | tf_op jit(solution)/shard_map/ppermute | solution.py:367
  37.9 1.0 %collective-permute-done.9.far_12 = bf16[2,16,16,256]{3,2,1,0:T(8,128)(2,1)S(1)} collective-permute-done((bf16[2,16,16,256]{3,2,1,0:T(8,128)(2,1)S(1)}, bf16[2,16,16,256]{3,2,1,0:T(8,128)(2,1)S(1)}, u32[]{:S(2)}, u32[]{:S(2)}) %collective-permute-start.9) | collective-permute-done | bytes 262176 | tf_op jit(solution)/shard_map/ppermute | solution.py:367
  38.8 0.3 collective-permute-done.8.near_12
  39.1 1.4 %collective-permute-done.10.near_3 = bf16[16,16,256]{2,1,0:T(8,128)(2,1)S(1)} collective-permute-done((bf16[16,16,256]{2,1,0:T(8,128)(2,1)S(1)}, bf16[16,16,256]{2,1,0:T(8,128)(2,1)S(1)}, u32[]{:S(2)}, u32[]{:S(2)}) %collective-permute-start.10) | collective-permute-done | bytes 131104 | tf_op jit(solution)/shard_map/ppermute | solution.py:367
  40.5 1.4 %collective-permute-done.11.far_3 = bf16[16,16,256]{2,1,0:T(8,128)(2,1)S(1)} collective-permute-done((bf16[16,16,256]{2,1,0:T(8,128)(2,1)S(1)}, bf16[16,16,256]{2,1,0:T(8,128)(2,1)S(1)}, u32[]{:S(2)}, u32[]{:S(2)}) %collective-permute-start.11) | collective-permute-done | bytes 131104 | tf_op jit(solution)/shard_map/ppermute | solution.py:367
  42.0 4.6 %pair_lags.1 = (bf16[208,416]{1,0:T(8,128)(2,1)S(1)}, bf16[208,256]{1,0:T(8,128)(2,1)S(1)}, bf16[208,256]{1,0:T(8,128)(2,1)S(1)}) custom-call(bf16[16,16,256]{2,1,0:T(8,128)(2,1)S(1)} %get-tuple-element.46.first, bf16[16,16,256]{2,1,0:T(8,128)(2,1)S(1)} %get-tuple-element.47.second, bf16[33,16,256]{2,1,0:T(8,128)(2,1)S(1)} %collective-permute-done.3.b1.refs_7_, ...), custom_call_target="tpu_custom_call" | custom-call | tf_op jit(solution)/shard_map/pair_lags/pallas_call | solution.py:435
  46.6 0.7 collective-permute-start.12
  47.3 2.3 %collective-permute-start.13 = (bf16[208,256]{1,0:T(8,128)(2,1)S(1)}, bf16[208,256]{1,0:T(8,128)(2,1)S(1)}, u32[]{:S(2)}, u32[]{:S(2)}) collective-permute-start(bf16[208,256]{1,0:T(8,128)(2,1)S(1)} %get-tuple-element.56), channel_id=1, source_target_pairs={{8,16},{16,8},{10,18},{18,10},{12,20},{20,12},{14,22},{22,14},{9,1... | collective-permute-start | bytes 319496 | tf_op jit(solution)/shard_map/ppermute | solution.py:367
  49.6 0.1 collective-permute-start.14
  49.7 1.7 %collective-permute-done.12.refs_1_ = bf16[208,256]{1,0:T(8,128)(2,1)S(1)} collective-permute-done((bf16[208,256]{1,0:T(8,128)(2,1)S(1)}, bf16[208,256]{1,0:T(8,128)(2,1)S(1)}, u32[]{:S(2)}, u32[]{:S(2)}) %collective-permute-start.12) | collective-permute-done | bytes 106528 | tf_op jit(solution)/shard_map/ppermute | solution.py:367
  51.4 2.5 %collective-permute-done.13.refs_2_ = bf16[208,256]{1,0:T(8,128)(2,1)S(1)} collective-permute-done((bf16[208,256]{1,0:T(8,128)(2,1)S(1)}, bf16[208,256]{1,0:T(8,128)(2,1)S(1)}, u32[]{:S(2)}, u32[]{:S(2)}) %collective-permute-start.13) | collective-permute-done | bytes 106528 | tf_op jit(solution)/shard_map/ppermute | solution.py:367
  53.9 1.3 %collective-permute-done.16.refs_5_ = bf16[208,256]{1,0:T(8,128)(2,1)S(1)} collective-permute-done((bf16[208,256]{1,0:T(8,128)(2,1)S(1)}, bf16[208,256]{1,0:T(8,128)(2,1)S(1)}, u32[]{:S(2)}, u32[]{:S(2)}) %collective-permute-start.16) | collective-permute-done | bytes 106528 | tf_op jit(solution)/shard_map/ppermute | solution.py:356
  55.2 1.0 %select_slots.1 = (bf16[2,208,128]{2,1,0:T(8,128)(2,1)S(1)}, bf16[2,208,128]{2,1,0:T(8,128)(2,1)S(1)}, bf16[2,208,128]{2,1,0:T(8,128)(2,1)S(1)}, bf16[2,208,128]{2,1,0:T(8,128)(2,1)S(1)}) custom-call(bf16[208,416]{1,0:T(8,128)(2,1)S(1)} %get-tuple-element.54.refs_0_, bf16[208,256]{1,0:T(8,128)(2,1)S(1)} %collective-permute-done.12.refs_1_, ...), custom_call_target="tpu_custom_call" | custom-call | tf_op jit(solution)/shard_map/select_slots/pallas_call | solution.py:456
  56.1 1.1 %collective-permute-start.17 = (bf16[2,208,128]{2,1,0:T(8,128)(2,1)S(1)}, bf16[2,208,128]{2,1,0:T(8,128)(2,1)S(1)}, u32[]{:S(2)}, u32[]{:S(2)}) collective-permute-start(bf16[2,208,128]{2,1,0:T(8,128)(2,1)S(1)} %get-tuple-element.58), channel_id=1, source_target_pairs={{0,2},{2,0},{4,6},{6,4},{8,10},{10,8},{12,14},{14,12},{16,18},{18,... | collective-permute-start | bytes 319496 | tf_op jit(solution)/shard_map/ppermute | solution.py:359
  57.3 1.0 %collective-permute-start.18 = (bf16[2,208,128]{2,1,0:T(8,128)(2,1)S(1)}, bf16[2,208,128]{2,1,0:T(8,128)(2,1)S(1)}, u32[]{:S(2)}, u32[]{:S(2)}) collective-permute-start(bf16[2,208,128]{2,1,0:T(8,128)(2,1)S(1)} %get-tuple-element.59), channel_id=1, source_target_pairs={{0,4},{2,6},{4,0},{6,2},{8,12},{10,14},{12,8},{14,10},{16,20},{18,... | collective-permute-start | bytes 319496 | tf_op jit(solution)/shard_map/ppermute | solution.py:359
  58.3 1.4 %collective-permute-start.19 = (bf16[2,208,128]{2,1,0:T(8,128)(2,1)S(1)}, bf16[2,208,128]{2,1,0:T(8,128)(2,1)S(1)}, u32[]{:S(2)}, u32[]{:S(2)}) collective-permute-start(bf16[2,208,128]{2,1,0:T(8,128)(2,1)S(1)} %get-tuple-element.60), channel_id=1, source_target_pairs={{0,6},{2,4},{4,2},{6,0},{8,14},{10,12},{12,10},{14,8},{16,22},{18,... | collective-permute-start | bytes 319496 | tf_op jit(solution)/shard_map/ppermute | solution.py:359
  60.3 1.2 %collective-permute-done.17.refs_1_ = bf16[2,208,128]{2,1,0:T(8,128)(2,1)S(1)} collective-permute-done((bf16[2,208,128]{2,1,0:T(8,128)(2,1)S(1)}, bf16[2,208,128]{2,1,0:T(8,128)(2,1)S(1)}, u32[]{:S(2)}, u32[]{:S(2)}) %collective-permute-start.17) | collective-permute-done | bytes 106528 | tf_op jit(solution)/shard_map/ppermute | solution.py:359
  61.5 1.3 %collective-permute-done.18.refs_2_ = bf16[2,208,128]{2,1,0:T(8,128)(2,1)S(1)} collective-permute-done((bf16[2,208,128]{2,1,0:T(8,128)(2,1)S(1)}, bf16[2,208,128]{2,1,0:T(8,128)(2,1)S(1)}, u32[]{:S(2)}, u32[]{:S(2)}) %collective-permute-start.18) | collective-permute-done | bytes 106528 | tf_op jit(solution)/shard_map/ppermute | solution.py:359
  62.8 1.5 %collective-permute-done.19.refs_3_ = bf16[2,208,128]{2,1,0:T(8,128)(2,1)S(1)} collective-permute-done((bf16[2,208,128]{2,1,0:T(8,128)(2,1)S(1)}, bf16[2,208,128]{2,1,0:T(8,128)(2,1)S(1)}, u32[]{:S(2)}, u32[]{:S(2)}) %collective-permute-start.19) | collective-permute-done | bytes 106528 | tf_op jit(solution)/shard_map/ppermute | solution.py:359
  64.4 3.5 %finish_slots.1 = f32[201,8,128]{2,1,0:T(8,128)} custom-call(s32[2,16]{1,0:T(2,128)S(1)} %bitcast.17, s32[1]{0:T(128)S(6)} %copy.11.count, bf16[2,208,128]{2,1,0:T(8,128)(2,1)S(1)} %get-tuple-element.57.refs_0_, bf16[2,208,128]{2,1,0:T(8,128)(2,1)S(1)} %collective-permute-done.17.refs_1_, bf16[2,208,128]{2,1,0:T(8,128)(2,1)S(1)} %collective-permute-done.18.refs_2_, ...), custom_call_target="tpu_custom_call" | custom-call | tf_op jit(solution)/shard_map/finish_slots/pallas_call | solution.py:470
  (23 shorter events, 0.2 us)
Async XLA Ops:
  1.9 1.3 %collective-permute-start = (f32[2,4096]{1,0:T(2,128)S(1)}, f32[2,4096]{1,0:T(2,128)S(1)}, u32[]{:S(2)}, u32[]{:S(2)}) collective-permute-start(f32[2,4096]{1,0:T(2,128)S(1)} %get-tuple-element.62), channel_id=1, source_target_pairs={{0,1},{1,0},{2,3},{3,2},{4,5},{5,4},{6,7},{7,6},{8,9},{9,8},{10,11... | collective-permute-start | bytes 98312 | tf_op jit(solution)/shard_map/ppermute | solution.py:356
  3.1 9.8 %collective-permute-start.1 = (f32[128,4096]{1,0:T(8,128)}, f32[128,4096]{1,0:T(8,128)S(1)}, u32[]{:S(2)}, u32[]{:S(2)}) collective-permute-start(f32[128,4096]{1,0:T(8,128)} %own.1), channel_id=1, source_target_pairs={{0,1},{1,0},{2,3},{3,2},{4,5},{5,4},{6,7},{7,6},{8,9},{9,8},{10,11... | collective-permute-start | bytes 6291464 | tf_op jit(solution)/shard_map/ppermute | solution.py:356
  4.1 8.8 %collective-permute-start.2 = (f32[4,4096]{1,0:T(4,128)S(1)}, f32[4,4096]{1,0:T(4,128)S(1)}, u32[]{:S(2)}, u32[]{:S(2)}) collective-permute-start(f32[4,4096]{1,0:T(4,128)S(1)} %pad_maximum_fusion.2), channel_id=1, source_target_pairs={{1,2},{2,1},{3,4},{4,3},{5,6},{6,5},{7,8},{8,7},{9,10},{10,9},{11,... | collective-permute-start | bytes 196616 | tf_op jit(solution)/shard_map/ppermute | solution.py:379
  9.8 1.6 %copy-start = (f32[128,4096]{1,0:T(8,128)S(1)}, f32[128,4096]{1,0:T(8,128)}, u32[]{:S(2)}) copy-start(f32[128,4096]{1,0:T(8,128)} %own.1) | copy-start | bytes 6291460
  11.4 1.6 %copy-start.1 = (f32[128,4096]{1,0:T(8,128)S(1)}, f32[128,4096]{1,0:T(8,128)}, u32[]{:S(2)}) copy-start(f32[128,4096]{1,0:T(8,128)} %own.1) | copy-start | bytes 6291460
  17.5 24.4 %copy-start.2 = (bf16[256,512]{1,0:T(8,128)(2,1)S(1)}, bf16[256,512]{1,0:T(8,128)(2,1)}, u32[]{:S(2)}) copy-start(bf16[256,512]{1,0:T(8,128)(2,1)} %constant.50.clone.table) | copy-start | bytes 786436
  17.6 24.4 %copy-start.3 = (bf16[208,512]{1,0:T(8,128)(2,1)S(1)}, bf16[208,512]{1,0:T(8,128)(2,1)}, u32[]{:S(2)}) copy-start(bf16[208,512]{1,0:T(8,128)(2,1)} %constant.51.clone.l_high) | copy-start | bytes 638980
  17.6 24.4 %copy-start.4 = (bf16[208,512]{1,0:T(8,128)(2,1)S(1)}, bf16[208,512]{1,0:T(8,128)(2,1)}, u32[]{:S(2)}) copy-start(bf16[208,512]{1,0:T(8,128)(2,1)} %constant.52.clone.l_low) | copy-start | bytes 638980
  17.6 12.0 %collective-permute-start.3 = (bf16[33,16,256]{2,1,0:T(8,128)(2,1)S(1)}, bf16[33,16,256]{2,1,0:T(8,128)(2,1)S(1)}, u32[]{:S(2)}, u32[]{:S(2)}) collective-permute-start(bf16[33,16,256]{2,1,0:T(8,128)(2,1)S(1)} %get-tuple-element.48), channel_id=1, source_target_pairs={{0,2},{2,0},{4,6},{6,4},{8,10},{10,8},{12,14},{14,12},{16,18},{18,... | collective-permute-start | bytes 811016 | tf_op jit(solution)/shard_map/ppermute | solution.py:359
  17.7 11.9 %collective-permute-start.4 = (bf16[33,16,256]{2,1,0:T(8,128)(2,1)S(1)}, bf16[33,16,256]{2,1,0:T(8,128)(2,1)S(1)}, u32[]{:S(2)}, u32[]{:S(2)}) collective-permute-start(bf16[33,16,256]{2,1,0:T(8,128)(2,1)S(1)} %get-tuple-element.49), channel_id=1, source_target_pairs={{0,4},{2,6},{4,0},{6,2},{8,12},{10,14},{12,8},{14,10},{16,20},{18,... | collective-permute-start | bytes 811016 | tf_op jit(solution)/shard_map/ppermute | solution.py:359
  18.9 6.0 %collective-permute-start.5 = (bf16[16,16,256]{2,1,0:T(8,128)(2,1)S(1)}, bf16[16,16,256]{2,1,0:T(8,128)(2,1)S(1)}, u32[]{:S(2)}, u32[]{:S(2)}) collective-permute-start(bf16[16,16,256]{2,1,0:T(8,128)(2,1)S(1)} %get-tuple-element.46.first), channel_id=1, source_target_pairs={{0,8},{8,0},{2,10},{10,2},{4,12},{12,4},{6,14},{14,6},{16,24},{24,... | collective-permute-start | bytes 393224 | tf_op jit(solution)/shard_map/ppermute | solution.py:367
  20.4 6.8 %collective-permute-start.6 = (bf16[16,16,256]{2,1,0:T(8,128)(2,1)S(1)}, bf16[16,16,256]{2,1,0:T(8,128)(2,1)S(1)}, u32[]{:S(2)}, u32[]{:S(2)}) collective-permute-start(bf16[16,16,256]{2,1,0:T(8,128)(2,1)S(1)} %get-tuple-element.47.second), channel_id=1, source_target_pairs={{8,16},{16,8},{10,18},{18,10},{12,20},{20,12},{14,22},{22,14},{9,1... | collective-permute-start | bytes 393224 | tf_op jit(solution)/shard_map/ppermute | solution.py:367
  27.3 7.6 %collective-permute-start.7 = (bf16[33,16,256]{2,1,0:T(8,128)(2,1)S(1)}, bf16[33,16,256]{2,1,0:T(8,128)(2,1)S(1)}, u32[]{:S(2)}, u32[]{:S(2)}) collective-permute-start(bf16[33,16,256]{2,1,0:T(8,128)(2,1)S(1)} %get-tuple-element.51), channel_id=1, source_target_pairs={{0,6},{2,4},{4,2},{6,0},{8,14},{10,12},{12,10},{14,8},{16,22},{18,... | collective-permute-start | bytes 811016 | tf_op jit(solution)/shard_map/ppermute | solution.py:359
  29.7 9.2 %collective-permute-start.9 = (bf16[2,16,16,256]{3,2,1,0:T(8,128)(2,1)S(1)}, bf16[2,16,16,256]{3,2,1,0:T(8,128)(2,1)S(1)}, u32[]{:S(2)}, u32[]{:S(2)}) collective-permute-start(bf16[2,16,16,256]{3,2,1,0:T(8,128)(2,1)S(1)} %pad_maximum_fusion.1), channel_id=1, source_target_pairs={{8,16},{16,8},{10,18},{18,10},{12,20},{20,12},{14,22},{22,14},{9,1... | collective-permute-start | bytes 786440 | tf_op jit(solution)/shard_map/ppermute | solution.py:367
  31.6 7.5 %collective-permute-start.8 = (bf16[2,16,16,256]{3,2,1,0:T(8,128)(2,1)S(1)}, bf16[2,16,16,256]{3,2,1,0:T(8,128)(2,1)S(1)}, u32[]{:S(2)}, u32[]{:S(2)}) collective-permute-start(bf16[2,16,16,256]{3,2,1,0:T(8,128)(2,1)S(1)} %pad_maximum_fusion), channel_id=1, source_target_pairs={{0,8},{8,0},{2,10},{10,2},{4,12},{12,4},{6,14},{14,6},{16,24},{24,... | collective-permute-start | bytes 786440 | tf_op jit(solution)/shard_map/ppermute | solution.py:367
  34.9 5.7 %collective-permute-start.10 = (bf16[16,16,256]{2,1,0:T(8,128)(2,1)S(1)}, bf16[16,16,256]{2,1,0:T(8,128)(2,1)S(1)}, u32[]{:S(2)}, u32[]{:S(2)}) collective-permute-start(bf16[16,16,256]{2,1,0:T(8,128)(2,1)S(1)} %get-tuple-element.64), channel_id=1, source_target_pairs={{0,8},{8,0},{2,10},{10,2},{4,12},{12,4},{6,14},{14,6},{16,24},{24,... | collective-permute-start | bytes 393224 | tf_op jit(solution)/shard_map/ppermute | solution.py:367
  35.0 29.4 %copy-start.5 = (bf16[208,208]{1,0:T(8,128)(2,1)S(1)}, bf16[208,208]{1,0:T(8,128)(2,1)}, u32[]{:S(2)}) copy-start(bf16[208,208]{1,0:T(8,128)(2,1)} %constant.53.clone.refs_4_) | copy-start | bytes 259588
  35.0 29.4 %copy-start.6 = (s32[16,2]{0,1:T(2,128)S(1)}, s32[16,2]{0,1:T(2,128)}, u32[]{:S(2)}) copy-start(s32[16,2]{0,1:T(2,128)} %param.14) | copy-start | bytes 388
  35.0 7.0 %collective-permute-start.11 = (bf16[16,16,256]{2,1,0:T(8,128)(2,1)S(1)}, bf16[16,16,256]{2,1,0:T(8,128)(2,1)S(1)}, u32[]{:S(2)}, u32[]{:S(2)}) collective-permute-start(bf16[16,16,256]{2,1,0:T(8,128)(2,1)S(1)} %get-tuple-element.63), channel_id=1, source_target_pairs={{8,16},{16,8},{10,18},{18,10},{12,20},{20,12},{14,22},{22,14},{9,1... | collective-permute-start | bytes 393224 | tf_op jit(solution)/shard_map/ppermute | solution.py:367
  46.6 4.8 %collective-permute-start.12 = (bf16[208,256]{1,0:T(8,128)(2,1)S(1)}, bf16[208,256]{1,0:T(8,128)(2,1)S(1)}, u32[]{:S(2)}, u32[]{:S(2)}) collective-permute-start(bf16[208,256]{1,0:T(8,128)(2,1)S(1)} %get-tuple-element.55), channel_id=1, source_target_pairs={{0,8},{8,0},{2,10},{10,2},{4,12},{12,4},{6,14},{14,6},{16,24},{24,... | collective-permute-start | bytes 319496 | tf_op jit(solution)/shard_map/ppermute | solution.py:367
  47.3 6.6 %collective-permute-start.13 = (bf16[208,256]{1,0:T(8,128)(2,1)S(1)}, bf16[208,256]{1,0:T(8,128)(2,1)S(1)}, u32[]{:S(2)}, u32[]{:S(2)}) collective-permute-start(bf16[208,256]{1,0:T(8,128)(2,1)S(1)} %get-tuple-element.56), channel_id=1, source_target_pairs={{8,16},{16,8},{10,18},{18,10},{12,20},{20,12},{14,22},{22,14},{9,1... | collective-permute-start | bytes 319496 | tf_op jit(solution)/shard_map/ppermute | solution.py:367
  49.6 4.2 %collective-permute-start.14 = (bf16[208,416]{1,0:T(8,128)(2,1)S(1)}, bf16[208,416]{1,0:T(8,128)(2,1)S(1)}, u32[]{:S(2)}, u32[]{:S(2)}) collective-permute-start(bf16[208,416]{1,0:T(8,128)(2,1)S(1)} %get-tuple-element.54.refs_0_), channel_id=1, source_target_pairs={{0,1},{1,0},{2,3},{3,2},{4,5},{5,4},{6,7},{7,6},{8,9},{9,8},{10,11... | collective-permute-start | bytes 519176 | tf_op jit(solution)/shard_map/ppermute | solution.py:356
  51.4 2.5 %collective-permute-start.15 = (bf16[208,256]{1,0:T(8,128)(2,1)S(1)}, bf16[208,256]{1,0:T(8,128)(2,1)S(1)}, u32[]{:S(2)}, u32[]{:S(2)}) collective-permute-start(bf16[208,256]{1,0:T(8,128)(2,1)S(1)} %collective-permute-done.12.refs_1_), channel_id=1, source_target_pairs={{0,1},{1,0},{2,3},{3,2},{4,5},{5,4},{6,7},{7,6},{8,9},{9,8},{10,11... | collective-permute-start | bytes 319496 | tf_op jit(solution)/shard_map/ppermute | solution.py:356
  53.9 1.3 %collective-permute-start.16 = (bf16[208,256]{1,0:T(8,128)(2,1)S(1)}, bf16[208,256]{1,0:T(8,128)(2,1)S(1)}, u32[]{:S(2)}, u32[]{:S(2)}) collective-permute-start(bf16[208,256]{1,0:T(8,128)(2,1)S(1)} %collective-permute-done.13.refs_2_), channel_id=1, source_target_pairs={{0,1},{1,0},{2,3},{3,2},{4,5},{5,4},{6,7},{7,6},{8,9},{9,8},{10,11... | collective-permute-start | bytes 319496 | tf_op jit(solution)/shard_map/ppermute | solution.py:356
  56.1 5.4 %collective-permute-start.17 = (bf16[2,208,128]{2,1,0:T(8,128)(2,1)S(1)}, bf16[2,208,128]{2,1,0:T(8,128)(2,1)S(1)}, u32[]{:S(2)}, u32[]{:S(2)}) collective-permute-start(bf16[2,208,128]{2,1,0:T(8,128)(2,1)S(1)} %get-tuple-element.58), channel_id=1, source_target_pairs={{0,2},{2,0},{4,6},{6,4},{8,10},{10,8},{12,14},{14,12},{16,18},{18,... | collective-permute-start | bytes 319496 | tf_op jit(solution)/shard_map/ppermute | solution.py:359
  57.3 5.6 %collective-permute-start.18 = (bf16[2,208,128]{2,1,0:T(8,128)(2,1)S(1)}, bf16[2,208,128]{2,1,0:T(8,128)(2,1)S(1)}, u32[]{:S(2)}, u32[]{:S(2)}) collective-permute-start(bf16[2,208,128]{2,1,0:T(8,128)(2,1)S(1)} %get-tuple-element.59), channel_id=1, source_target_pairs={{0,4},{2,6},{4,0},{6,2},{8,12},{10,14},{12,8},{14,10},{16,20},{18,... | collective-permute-start | bytes 319496 | tf_op jit(solution)/shard_map/ppermute | solution.py:359
  58.3 6.1 %collective-permute-start.19 = (bf16[2,208,128]{2,1,0:T(8,128)(2,1)S(1)}, bf16[2,208,128]{2,1,0:T(8,128)(2,1)S(1)}, u32[]{:S(2)}, u32[]{:S(2)}) collective-permute-start(bf16[2,208,128]{2,1,0:T(8,128)(2,1)S(1)} %get-tuple-element.60), channel_id=1, source_target_pairs={{0,6},{2,4},{4,2},{6,0},{8,14},{10,12},{12,10},{14,8},{16,22},{18,... | collective-permute-start | bytes 319496 | tf_op jit(solution)/shard_map/ppermute | solution.py:359

commit v4 on v3

--- a/solution.py
+++ b/solution.py
@@ -108,9 +108,19 @@
     return pl.ds(first_row, rows), pl.ds(near_row, 8)
 
 
-def prepare_kernel(small, own, t_high, t_low, pid, space, ok, own_high, own_low):
+def prepare_kernel(
+    small, whole, whole_rows, traces, t_high, t_low, pid, space, ok, own_high, own_low, own_near,
+    main_rows, near_rows, sems,
+):
     _, core, _ = my_place()
     plane = lax.axis_index("chan") // PLANE
+    main, near = tile_rows(traces, core)
+    copies = [
+        pltpu.make_async_copy(traces.at[main], main_rows, sems.at[0]),
+        pltpu.make_async_copy(traces.at[near], near_rows, sems.at[1]),
+    ]
+    for copy in copies:
+        copy.start()
     t_high[...] = jnp.zeros(t_high.shape, BF16)
     t_low[...] = jnp.zeros(t_low.shape, BF16)
     shift = SEG // 2 - (TAPS - 1) // 2
@@ -120,43 +130,43 @@
     )
     band = jnp.zeros((height, 128), F32)
     for j in range(TAPS):
-        band = jnp.where(tap == j, small[j], band)
+        band = jnp.where(tap == j, small[0, j], band)
     high, low = split_terms(band)
     for lanes in range(SEG // 128):
         at = (slice(lanes * 128 + shift, lanes * 128 + shift + height), slice(lanes * 128, lanes * 128 + 128))
         t_high[at] = high
         t_low[at] = low
     row = lax.broadcasted_iota(jnp.int32, space.shape, 0)
-    taps = jnp.zeros(space.shape, F32)
+    value = jnp.zeros(space.shape, F32)
     for j in range(STAPS):
-        taps = jnp.where(row == j, small[TAPS + j], taps)
-    space[...] = taps
+        value = jnp.where(row == j, small[1, j], value)
+    space[...] = value
     slot = lax.broadcasted_iota(jnp.int32, pid.shape, 1) >> 4
     upper = lax.broadcasted_iota(jnp.int32, pid.shape, 0) < 8
     ids = jnp.zeros(pid.shape, jnp.int32)
     for s in range(SLOTS):
-        left = small[TAPS + STAPS + s].astype(jnp.int32)
-        right = small[TAPS + STAPS + SLOTS + s].astype(jnp.int32)
-        one, two = pair_ids(left, right, plane)
+        one, two = pair_ids(whole[0, s], whole[1, s], plane)
         ids = jnp.where(slot == s, jnp.where(upper, one, two), ids)
     pid[...] = ids.astype(F32).astype(BF16)
-    at = lax.broadcasted_iota(jnp.int32, ok.shape, 0)
-    values = jnp.zeros(ok.shape, F32)
-    for k in range(ok.shape[0]):
-        values = jnp.where(at == k, small[TAPS + STAPS + 2 * SLOTS + k], values)
-    ok[...] = values
-    main, near = tile_rows(own, core)
-    own_high[...], own_low[...] = split_terms(own[main, :] * ok[main, 0:1])
+    width = ok.shape[0]
+    diagonal = lax.broadcasted_iota(jnp.int32, (width, width), 0) == lax.broadcasted_iota(
+        jnp.int32, (width, width), 1
+    )
+    spread = jnp.where(diagonal, whole_rows[2:3, :width].astype(F32), 0.0)
+    ok[...] = jnp.broadcast_to(jnp.sum(spread, axis=1, keepdims=True), ok.shape)
+    for copy in copies:
+        copy.wait()
+    own_high[...], own_low[...] = split_terms(main_rows[...] * ok[main, 0:1])
+    own_near[...] = near_rows[...] * ok[near, 0:1]
 
 
 def filter_kernel(
-    own, own_high, own_low, other, halos, space, ok, t_high, t_low, pid,
+    own_near, own_high, own_low, other, halos, space, ok, t_high, t_low, pid,
     out_first, out_second, out_1, out_2, out_3, x_high, x_low, edge, white,
 ):
     member, core, odd = my_place()
-    half = own.shape[1]
-    rows = own_high.shape[0]
-    main, near = tile_rows(own, core)
+    rows, half = own_high.shape
+    main, near = tile_rows(other, core)
     pad = SEG // 2
     total = 2 * half
     zeros = jnp.zeros((rows + 16, pad), BF16)
@@ -168,11 +178,10 @@
     x_high[0:rows, own_lanes] = own_high[...]
     x_low[0:rows, own_lanes] = own_low[...]
     x_high[0:rows, other_lanes], x_low[0:rows, other_lanes] = split_terms(other[main, :] * ok[main, 0:1])
-    ok_near = ok[near, 0:1]
-    for source, halo, lanes in ((own, halos[2:4], own_lanes), (other, halos[0:2], other_lanes)):
+    other_near = other[near, :] * ok[near, 0:1]
+    for inside, halo, lanes in ((own_near[...], halos[2:4], own_lanes), (other_near, halos[0:2], other_lanes)):
         for k in range(4):
             edge[2 * k : 2 * k + 2, :] = halo
-        inside = source[near, :] * ok_near
         outside = edge[...]
         above = jnp.where(core == 0, outside, inside)
         below = jnp.where(core == 0, inside, outside)
@@ -213,64 +222,119 @@
         out[segs] = pid[...]
 
 
-def pair_kernel(
-    first, second, b1, b2, b3, near_0, far_0, near_12, far_12, near_3, far_3, table, l_high, l_low,
-    out, out_first, out_second, spec, spec_z, cross,
-):
-    member, _, odd = my_place()
-    segs = spec.shape[1]
-    part = segs // 2
-
-    def transform(block):
-        value = mxu(block.reshape(block.shape[0] * QG, SEG), table[...])
-        return value.astype(BF16).astype(F32).reshape(block.shape[0], QG, 2 * SEG)
-
-    spec[member, pl.ds((1 - odd) * part, part)] = transform(first[...])
-    spec[member, pl.ds(odd * part, part)] = transform(second[...])
-    for rel, ref in ((1, b1), (2, b2), (3, b3)):
-        spec[member ^ rel] = transform(ref[0:segs])
-    for side, refs in ((odd, (near_0, near_12, near_3)), (1 - odd, (far_0, far_12, far_3))):
-        spec_z[side, member] = transform(refs[0][...])
-        spec_z[side, member ^ 1] = transform(refs[1][0])
-        spec_z[side, member ^ 2] = transform(refs[1][1])
-        spec_z[side, member ^ 3] = transform(refs[2][...])
+def transform(block, table):
+    value = mxu(block.reshape(block.shape[0] * QG, SEG), table[...])
+    return value.astype(BF16).astype(F32).reshape(block.shape[0], QG, 2 * SEG)
+
+
+def bin_parts():
     for q8 in range(QG // 8):
         for lanes in range(SEG // 128):
             rows = slice(q8 * 8, q8 * 8 + 8)
             re_lanes = slice(lanes * 128, lanes * 128 + 128)
             im_lanes = slice(SEG + lanes * 128, SEG + lanes * 128 + 128)
-
-            def add(sums, index, left, right):
-                re = sums[2 * index] + (left[0] * right[0] + left[1] * right[1])
-                im = sums[2 * index + 1] + (left[1] * right[0] - left[0] * right[1])
-                return [re, im]
-
-            def sweep(side, sums):
-                def body(seg, sums):
-                    at = seg + side * part
-                    mine = [(spec[w, at, rows, re_lanes], spec[w, at, rows, im_lanes]) for w in range(PLANE)]
-                    theirs = [
-                        (spec_z[side, w, seg, rows, re_lanes], spec_z[side, w, seg, rows, im_lanes])
-                        for w in range(PLANE)
-                    ]
+            yield q8 * 8, rows, re_lanes, im_lanes
+
+
+def add_product(sums, index, left, right):
+    re = sums[2 * index] + (left[0] * right[0] + left[1] * right[1])
+    im = sums[2 * index + 1] + (left[1] * right[0] - left[0] * right[1])
+    return [re, im]
+
+
+def store_sums(cross, first_pair, row, re_lanes, im_lanes, sums):
+    for index in range(len(sums) // 2):
+        at = slice((first_pair + index) * QG + row, (first_pair + index) * QG + row + 8)
+        cross[at, re_lanes] = sums[2 * index]
+        cross[at, im_lanes] = sums[2 * index + 1]
+
+
+def inner_kernel(first, second, b1, b2, b3, near_0, far_0, table, spec, spec_near, spec_far, inner):
+    member, _, odd = my_place()
+    segs = spec.shape[1]
+    part = segs // 2
+    spec[member, pl.ds((1 - odd) * part, part)] = transform(first[...], table)
+    spec[member, pl.ds(odd * part, part)] = transform(second[...], table)
+    for rel, ref in ((1, b1), (2, b2), (3, b3)):
+        spec[member ^ rel] = transform(ref[0:segs], table)
+    spec_near[...] = transform(near_0[...], table)
+    spec_far[...] = transform(far_0[...], table)
+    for row, rows, re_lanes, im_lanes in bin_parts():
+
+        def body(seg, sums):
+            mine = [(spec[w, seg, rows, re_lanes], spec[w, seg, rows, im_lanes]) for w in range(PLANE)]
+            result = []
+            for k, (i, j) in enumerate(INNER):
+                result += add_product(sums, k, mine[i], mine[j])
+            return tuple(result)
+
+        zero = jnp.zeros((8, 128), F32)
+        sums = lax.fori_loop(0, segs, body, (zero,) * (2 * N_IN), unroll=4)
+        store_sums(inner, 0, row, re_lanes, im_lanes, sums)
+
+
+def cross_kernel(spec, spec_near, spec_far, inner, near_12, far_12, table, cross, spec_z):
+    member, _, odd = my_place()
+    part = spec_near.shape[0]
+    for side, done, pair in ((odd, spec_near, near_12), (1 - odd, spec_far, far_12)):
+        spec_z[side, member] = done[...]
+        spec_z[side, member ^ 1] = transform(pair[0], table)
+        spec_z[side, member ^ 2] = transform(pair[1], table)
+        spec_z[side, member ^ 3] = jnp.zeros(done.shape, F32)
+    cross[N_CROSS * QG : (N_CROSS + N_IN) * QG, :] = inner[...]
+    for row, rows, re_lanes, im_lanes in bin_parts():
+        for side, first_pair in ((0, N_CROSS + N_IN), (1, 0)):
+
+            def body(seg, sums):
+                at = seg + side * part
+                mine = [(spec[w, at, rows, re_lanes], spec[w, at, rows, im_lanes]) for w in range(PLANE)]
+                theirs = [
+                    (spec_z[side, w, seg, rows, re_lanes], spec_z[side, w, seg, rows, im_lanes])
+                    for w in range(PLANE)
+                ]
+                low, high = (theirs, mine) if side else (mine, theirs)
+                result = []
+                for k, (i, j) in enumerate(CROSS):
+                    result += add_product(sums, k, low[i], high[j])
+                return tuple(result)
+
+            zero = jnp.zeros((8, 128), F32)
+            sums = lax.fori_loop(0, part, body, (zero,) * (2 * N_CROSS), unroll=4)
+            store_sums(cross, first_pair, row, re_lanes, im_lanes, sums)
+
+
+def lags_kernel(
+    spec, cross_in, near_3, far_3, table, l_high, l_low, out, out_first, out_second, last, cross
+):
+    member, _, odd = my_place()
+    part = near_3.shape[0]
+    diagonal = member ^ 3
+    last[odd] = transform(near_3[...], table)
+    last[1 - odd] = transform(far_3[...], table)
+    cross[...] = cross_in[...]
+    for row, rows, re_lanes, im_lanes in bin_parts():
+        for side in range(2):
+
+            def body(seg, sums):
+                at = seg + side * part
+                theirs = (last[side, seg, rows, re_lanes], last[side, seg, rows, im_lanes])
+                result = []
+                for w in range(PLANE):
+                    mine = (spec[w, at, rows, re_lanes], spec[w, at, rows, im_lanes])
                     low, high = (theirs, mine) if side else (mine, theirs)
-                    result = []
-                    for k, (i, j) in enumerate(INNER):
-                        result += add(sums, k, mine[i], mine[j])
-                    for k, (i, j) in enumerate(CROSS):
-                        result += add(sums, N_IN + k, low[i], high[j])
-                    return tuple(result)
-
-                return lax.fori_loop(0, part, body, sums, unroll=4)
+                    result += add_product(sums, w, low, high)
+                return tuple(result)
 
             zero = jnp.zeros((8, 128), F32)
-            up = sweep(0, (zero,) * (2 * N_SENT))
-            down = sweep(1, up[: 2 * N_IN] + (zero,) * (2 * N_CROSS))
-            order = down[2 * N_IN :] + down[: 2 * N_IN] + up[2 * N_IN :]
-            for index in range(N_OWN):
-                at = slice(index * QG + q8 * 8, index * QG + q8 * 8 + 8)
-                cross[at, re_lanes] = order[2 * index]
-                cross[at, im_lanes] = order[2 * index + 1]
+            sums = lax.fori_loop(0, part, body, (zero,) * (2 * PLANE), unroll=4)
+            for w in range(PLANE):
+                if side:
+                    valid, pair = w <= diagonal, diagonal * (diagonal + 1) // 2 + w
+                else:
+                    valid, pair = w >= diagonal, N_CROSS + N_IN + w * (w + 1) // 2 + diagonal
+                at = pl.ds(pl.multiple_of(jnp.where(valid, pair, 0) * QG + row, 8), 8)
+                cross[at, re_lanes] += jnp.where(valid, sums[2 * w], 0.0)
+                cross[at, im_lanes] += jnp.where(valid, sums[2 * w + 1], 0.0)
     high, low = split_terms(cross[...])
 
     def turned(left, right):
@@ -284,11 +348,9 @@
     out_second[...] = jnp.where(odd == 1, to_above, to_below).astype(BF16)
 
 
-def select_kernel(*refs):
-    mine, swapped, pids, outs = refs[0:3], refs[3:6], refs[6:10], refs[10:14]
-    chosen, lags = refs[14:16]
-    _, core, odd = my_place()
-    own, sent = N_OWN * QG, N_SENT * QG
+def choose_kernel(*refs):
+    pids, chosen = refs[:4], refs[4]
+    _, core, _ = my_place()
     row_id = lax.broadcasted_iota(jnp.int32, (N_ALL * QG, 128), 0)
     col_id = lax.broadcasted_iota(jnp.int32, (N_ALL * QG, 128), 1)
     row_key = jnp.where((row_id & 15) == (col_id & 15), (row_id >> 4).astype(F32), -1.0)
@@ -297,6 +359,12 @@
         ids = pid[0, :, pl.ds(lane, 128)].astype(F32)
         match = (row_key == ids[0:1, :]) | (row_key == ids[8:9, :])
         chosen[:, rel * 128 : (rel + 1) * 128] = jnp.where(match, 1.0, 0.0).astype(BF16)
+
+
+def select_kernel(chosen, *refs):
+    mine, swapped, outs, lags = refs[0:3], refs[3:6], refs[6:10], refs[10]
+    _, _, odd = my_place()
+    own, sent = N_OWN * QG, N_SENT * QG
     for side, (here, first, second) in enumerate((mine, swapped)):
         at = slice(side * LAG_ROWS, (side + 1) * LAG_ROWS)
         below = jnp.where(odd == 1, first[...].astype(F32), second[...].astype(F32)).astype(BF16)
@@ -316,15 +384,19 @@
     for rel in range(4):
         for side in range(2):
             stage[(core ^ side) * 4 + (member ^ rel)] = pieces[rel][side].astype(F32)
-    group = lax.broadcasted_iota(jnp.int32, (LAG_ROWS, 128), 1) >> 4
-    for s in range(SLOTS // 2):
-        value = jnp.zeros((LAG_ROWS, 128), F32)
-        for m in range(8):
-            shift = ((m - s) * QG) % 128
-            piece = stage[m]
-            moved = pltpu.roll(piece, shift, 1) if shift else piece
-            value = jnp.where(group == m, moved, value)
-        flat[:, s * 128 : (s + 1) * 128] = value
+    step = 16
+    group = lax.broadcasted_iota(jnp.int32, (step, 128), 1) >> 4
+    for row in range(0, LAG_ROWS, step):
+        tiles = [stage[m, row : row + step] for m in range(8)]
+        for bit in (4, 2, 1):
+            upper = (group & bit) > 0
+            for m in range(8):
+                if not m & bit:
+                    low, high = tiles[m], tiles[m | bit]
+                    tiles[m] = jnp.where(upper, pltpu.roll(high, bit * QG, 1), low)
+                    tiles[m | bit] = jnp.where(upper, high, pltpu.roll(low, 128 - bit * QG, 1))
+        for s in range(8):
+            flat[row : row + step, s * 128 : (s + 1) * 128] = tiles[s]
     back = mxu(table[...], flat[...].astype(BF16))
     for s in range(SLOTS // 2):
         lanes = slice(s * 128, (s + 1) * 128)
@@ -335,6 +407,7 @@
 
 VM = pl.BlockSpec(memory_space=pltpu.VMEM)
 SM = pl.BlockSpec(memory_space=pltpu.SMEM)
+HB = pl.BlockSpec(memory_space=pltpu.HBM)
 PARAMS = pltpu.CompilerParams(vmem_limit_bytes=VMEM_LIMIT)
 
 
@@ -366,38 +439,40 @@
                 route += [(low, high), (high, low)]
         return lax.ppermute(x, "chan", route)
 
+    rows = chan_width // 2
     head, tail = traces[0:2], traces[chan_width - 2 :]
     got = to_core(jnp.where(core == 0, tail, head))
     mine = jnp.where(core == 0, head, tail)
-    got, late, taps, space, ok, pairs = lax.optimization_barrier(
-        (got, traces, time_taps, space_taps, channel_ok, pairs)
-    )
+    got, late = lax.optimization_barrier((got, traces))
     route = []
     for c in range(n_chan - 1):
         route += [(2 * c + 1, 2 * c + 2), (2 * c + 2, 2 * c + 1)]
-    alive = jnp.where(core == 0, channel_ok[0:2], channel_ok[chan_width - 2 :]).astype(F32)[:, None]
-    halos = lax.ppermute(jnp.concatenate([mine * alive, got * alive], axis=0), BOTH, route)
+    alive = (jnp.where(core == 0, channel_ok[0:2], channel_ok[chan_width - 2 :]) > 0)[:, None]
+    edges = [jnp.where(alive, mine, 0.0), jnp.where(alive, got, 0.0)]
+    halos = lax.ppermute(jnp.concatenate(edges, axis=0), BOTH, route)
     other = to_core(late)
-    parts = (taps, space, pairs[0].astype(F32), pairs[1].astype(F32), ok.astype(F32))
-    small_size = sum(x.shape[0] for x in parts)
-    small, at = jnp.zeros((small_size,), F32), 0
-    for x in parts:
-        small = small + jnp.pad(x, (at, small_size - at - x.shape[0]))
-        at += x.shape[0]
-    rows = chan_width // 2
+    small = jnp.pad(time_taps[None, :], ((0, 7), (0, 128 - TAPS)))
+    small = small + jnp.pad(space_taps[None, :], ((1, 6), (0, 128 - STAPS)))
+    whole = jnp.pad(pairs, ((0, 6), (0, 128 - SLOTS)))
+    whole = whole + jnp.pad(channel_ok[None, :], ((2, 5), (0, 128 - chan_width)))
     table = shape((2 * SEG, SEG), BF16)
     split = shape((rows, half), BF16)
-    t_high, t_low, pid, space, ok, own_high, own_low = pl.pallas_call(
+    t_high, t_low, pid, space, ok, own_high, own_low, own_near = pl.pallas_call(
         prepare_kernel,
         out_shape=[
             table, table, shape((QG, SLOTS * QG), BF16), shape((8, SEG), F32), shape((chan_width, 128), F32),
-            split, split,
+            split, split, shape((8, half), F32),
         ],
-        in_specs=[SM, VM],
-        out_specs=[VM] * 7,
+        in_specs=[SM, SM, VM, HB],
+        out_specs=[VM] * 8,
+        scratch_shapes=[
+            pltpu.VMEM((rows, half), F32),
+            pltpu.VMEM((8, half), F32),
+            pltpu.SemaphoreType.DMA((2,)),
+        ],
         compiler_params=PARAMS,
         name="prepare",
-    )(small, late)
+    )(small, whole, whole, late)
     block = shape((segs + 1, QG, SEG), BF16)
     short = shape((part, QG, SEG), BF16)
     first, second, *sent = pl.pallas_call(
@@ -413,59 +488,79 @@
         ],
         compiler_params=PARAMS,
         name="filter_whiten",
-    )(late, own_high, own_low, other, halos, space, ok, t_high, t_low, pid)
+    )(own_near, own_high, own_low, other, halos, space, ok, t_high, t_low, pid)
     b1, b2 = in_plane(sent[0], 1), in_plane(sent[1], 2)
-    near_0, far_0 = plane_swap(first, 0), plane_swap(second, 1)
-    near_0, far_0, last = lax.optimization_barrier((near_0, far_0, sent[2]))
+    far_0, near_0 = plane_swap(second, 1), plane_swap(first, 0)
+    b1, last = lax.optimization_barrier((b1, sent[2]))
     b3 = in_plane(last, 3)
-
+    b1, b2, near_0, far_0 = lax.optimization_barrier((b1, b2, near_0, far_0))
     def halves(x):
         near = lax.dynamic_slice_in_dim(x, (1 - odd) * part, part, axis=0)
         far = lax.dynamic_slice_in_dim(x, odd * part, part, axis=0)
         return near, far
 
     (near_1, far_1), (near_2, far_2) = halves(b1), halves(b2)
+    far_12 = plane_swap(jnp.stack([far_1, far_2]), 1)
     near_12 = plane_swap(jnp.stack([near_1, near_2]), 0)
-    far_12 = plane_swap(jnp.stack([far_1, far_2]), 1)
     near_3, far_3 = halves(b3)
-    near_3, far_3 = plane_swap(near_3, 0), plane_swap(far_3, 1)
+    far_3, near_3 = plane_swap(far_3, 1), plane_swap(near_3, 0)
     scale = 1.0 / math.sqrt(segs * SEG)
     l_high, l_low = inverse_np(scale)
     sent_shape = shape((LAG_ROWS, N_SENT * QG), BF16)
+    table = jnp.asarray(forward_np())
+    short = shape((part, QG, 2 * SEG), F32)
+    spec, spec_near, spec_far, inner = pl.pallas_call(
+        inner_kernel,
+        out_shape=[shape((PLANE, segs, QG, 2 * SEG), F32), short, short, shape((N_IN * QG, 2 * SEG), F32)],
+        in_specs=[VM] * 8,
+        out_specs=[VM] * 4,
+        compiler_params=PARAMS,
+        name="inner_pairs",
+    )(first, second, b1, b2, b3, near_0, far_0, table)
+    cross = pl.pallas_call(
+        cross_kernel,
+        out_shape=shape((N_OWN * QG, 2 * SEG), F32),
+        in_specs=[VM] * 7,
+        out_specs=VM,
+        scratch_shapes=[pltpu.VMEM((2, PLANE, part, QG, 2 * SEG), F32)],
+        compiler_params=PARAMS,
+        name="cross_pairs",
+    )(spec, spec_near, spec_far, inner, near_12, far_12, table)
     lags, lags_first, lags_second = pl.pallas_call(
-        pair_kernel,
+        lags_kernel,
         out_shape=[shape((LAG_ROWS, N_OWN * QG), BF16), sent_shape, sent_shape],
-        in_specs=[VM] * 14,
+        in_specs=[VM] * 7,
         out_specs=[VM] * 3,
         scratch_shapes=[
-            pltpu.VMEM((PLANE, segs, QG, 2 * SEG), F32),
-            pltpu.VMEM((2, PLANE, part, QG, 2 * SEG), F32),
+            pltpu.VMEM((2, part, QG, 2 * SEG), F32),
             pltpu.VMEM((N_OWN * QG, 2 * SEG), F32),
         ],
         compiler_params=PARAMS,
         name="pair_lags",
-    )(
-        first, second, b1, b2, b3, near_0, far_0, near_12, far_12, near_3, far_3,
-        jnp.asarray(forward_np()), jnp.asarray(l_high), jnp.asarray(l_low),
-    )
+    )(spec, cross, near_3, far_3, table, jnp.asarray(l_high), jnp.asarray(l_low))
     from_first, from_second = plane_swap(lags_first, 0), plane_swap(lags_second, 1)
     known = [lags, from_first, from_second]
     pid_spec = pl.BlockSpec((1, QG, SEG), lambda step: (segs, 0, 0))
     own_spec = pl.BlockSpec((1, QG, SEG), lambda step: (0, 0, 0))
     slots_shape = shape((2, LAG_ROWS, 128), BF16)
+    chosen = pl.pallas_call(
+        choose_kernel,
+        grid=(1,),
+        out_shape=shape((N_ALL * QG, 512), BF16),
+        in_specs=[own_spec] + [pid_spec] * 3,
+        out_specs=VM,
+        compiler_params=PARAMS,
+        name="choose",
+    )(pid[None], b1, b2, b3)
     picked = pl.pallas_call(
         select_kernel,
-        grid=(1,),
         out_shape=[slots_shape] * 4,
-        in_specs=[VM] * 6 + [own_spec] + [pid_spec] * 3,
+        in_specs=[VM] * 7,
         out_specs=[VM] * 4,
-        scratch_shapes=[
-            pltpu.VMEM((N_ALL * QG, 512), BF16),
-            pltpu.VMEM((2 * LAG_ROWS, N_ALL * QG), BF16),
-        ],
+        scratch_shapes=[pltpu.VMEM((2 * LAG_ROWS, N_ALL * QG), BF16)],
         compiler_params=PARAMS,
         name="select_slots",
-    )(*known, *[to_core(x) for x in known], pid[None], b1, b2, b3)
+    )(chosen, *known, *[to_core(x) for x in known])
     pieces = [picked[0]] + [in_plane(x, rel + 1) for rel, x in enumerate(picked[1:])]
     out = pl.pallas_call(
         finish_kernel,

time: 68.4 us -> 66 us (0.965)
  starting transfers between devices: 26.1 us -> 24 us
  waiting for transfers between devices: 19.8 us -> 18.4 us
  Pallas kernels: 15.2 us -> 16.5 us
  other arithmetic: 4.18 us -> 3.41 us
    ppermute x8, waiting for transfers between devices: 13.2 us -> 4.13 us  [plane_swap(): return lax.ppermute(x, 'chan', route)]
    ppermute x6, waiting for transfers between devices: 4.1 us -> 12.2 us  [in_plane(): return lax.ppermute(x, 'chan', [(c, c ^ rel) for c in range(n_chan)])]
    ppermute x8, starting transfers between devices: 14.5 us -> 12.1 us  [plane_swap(): return lax.ppermute(x, 'chan', route)]
    convert_element_type x3 -> x0, other arithmetic: 2.22 us -> none  [the longest x1 0.8 us: local(): jnp.where(core == 0, channel_ok[0:2], channel_ok[chan_width - 2:])]
    pallas_call x2 -> x5, Pallas kernels: 5.57 us -> 6.76 us  [the longest x1 2.12 us: local(): pl.pallas_call(cross_kernel, out_shape=shape((N_OWN * QG, 2 * SEG), F32),...]
    select_n x0 -> x2, other arithmetic: none -> 1.13 us  [local(): edges = [jnp.where(alive, mine, 0.0), jnp.where(alive, got, 0.0)]]
    mul x2 -> x0, other arithmetic: 1.12 us -> none  [the longest x1 1.05 us: local(): mine * alive]
    gt x0 -> x1, other arithmetic: none -> 0.81 us  [local(): jnp.where(core == 0, channel_ok[0:2], channel_ok[chan_width - 2:]) > 0]
  transfers between devices with their start and end apart: 20 -> 20, of which waited for: 14 -> 10; matrix products, arithmetic and copies ran while one was open for 4% -> 2% of each run, Pallas kernels for 2% -> 9%
where the time goes in v4:
time: 66 us; the launch traced here: 65 us
  starting transfers between devices  24 us (36%)
  waiting for transfers between devices  18.4 us (28%)
  Pallas kernels  16.5 us (25%)
  other arithmetic  3.41 us (5%)
  local copies, waits for them, and re-layouts  1.68 us (3%)
  between operations  0.97 us (1%)
    ppermute x6, waiting for transfers between devices, in_plane(): return lax.ppermute(x, 'chan', [(c, c ^ rel) for c in range(n_chan)])  12.2 us
    ppermute x8, starting transfers between devices, plane_swap(): return lax.ppermute(x, 'chan', route)  12.1 us
    ppermute x6, starting transfers between devices, in_plane(): return lax.ppermute(x, 'chan', [(c, c ^ rel) for c in range(n_chan)])  7.47 us
    pallas_call x1, Pallas kernels, local(): pl.pallas_call(filter_kernel, out_shape=[short] * 2 + [block] * 3, in_spe...  4.63 us
    ppermute x1, starting transfers between devices, local(): halos = lax.ppermute(jnp.concatenate(edges, axis=0), BOTH, route)  4.19 us
    ppermute x8, waiting for transfers between devices, plane_swap(): return lax.ppermute(x, 'chan', route)  4.13 us
    pallas_call x1, Pallas kernels, local(): pl.pallas_call(finish_kernel, out_shape=shape((LAGS, SLOTS // 2, chan_wid...  3.19 us
    ppermute x5, waiting for transfers between devices, to_core(): return lax.ppermute(x, 'tm', [(0, 1), (1, 0)])  2.14 us
  transfers between devices with their start and end apart: 20, of which 10 were waited for; matrix products, arithmetic and copies ran while one was open for 2% of the time, Pallas kernels for 9%

profile of v4, /device:TPU:16, one launch (start us, length us, event | category | flops | bytes accessed | tf_op | source)
XLA Modules:
  0.0 65.0 jit_solution(1105810878964591705)
XLA Ops:
  0.0 0.8 %fusion = pred[2]{0:T(512)(128)(4,1)S(1)} fusion(pred[]{:T(512)S(6)} %eq.4, s32[128]{0:T(128)} %param.11), kind=kLoop, calls=%fused_computation.15 | loop fusion | flops 4 | bytes 19 | tf_op jit(solution)/shard_map/gt | solution.py:450
  0.8 1.0 %select_select_fusion = (f32[2,4096]{1,0:T(2,128)S(1)}, f32[2,4096]{1,0:T(2,128)S(1)}) fusion(pred[2]{0:T(512)(128)(4,1)S(1)} %fusion, pred[]{:T(512)S(6)} %eq.4, f32[128,4096]{1,0:T(8,128)} %traces), kind=kLoop, calls=%fused_computation.7 | loop fusion | flops 24576 | bytes 131075 | tf_op jit(solution)/shard_map/jit(_where)/select_n | solution.py:451
  1.9 0.1 collective-permute-start
  1.9 1.2 %collective-permute-done = f32[2,4096]{1,0:T(2,128)S(1)} collective-permute-done((f32[2,4096]{1,0:T(2,128)S(1)}, f32[2,4096]{1,0:T(2,128)S(1)}, u32[]{:S(2)}, u32[]{:S(2)}) %collective-permute-start) | collective-permute-done | bytes 32800 | tf_op jit(solution)/shard_map/ppermute | solution.py:429
  3.1 0.2 collective-permute-start.1
  3.3 0.7 %pad_add_fusion.whole.whole_rows = s32[8,128]{1,0:T(8,128)S(1)} fusion(s32[1,128]{1,0:T(1,128)} %bitcast.17, s32[2,16]{1,0:T(2,128)} %bitcast.15), kind=kLoop, calls=%fused_computation.10 | loop fusion | flops 1024 | bytes 4736 | tf_op jit(solution)/shard_map/add | solution.py:457
  4.0 0.1 broadcast_select_fusion
  4.1 4.2 %collective-permute-start.2 = (f32[4,4096]{1,0:T(4,128)S(1)}, f32[4,4096]{1,0:T(4,128)S(1)}, u32[]{:S(2)}, u32[]{:S(2)}) collective-permute-start(f32[4,4096]{1,0:T(4,128)S(1)} %pad_maximum_fusion.2), channel_id=1, source_target_pairs={{1,2},{2,1},{3,4},{4,3},{5,6},{6,5},{7,8},{8,7},{9,10},{10,9},{11,... | collective-permute-start | bytes 196616 | tf_op jit(solution)/shard_map/ppermute | solution.py:452
  8.3 0.7 %pad_add_fusion.1.small = f32[8,128]{1,0:T(8,128)S(1)} fusion(f32[1,5]{1,0:T(1,128)} %bitcast.18, f32[1,33]{1,0:T(1,128)} %bitcast.19), kind=kLoop, calls=%fused_computation.11 | loop fusion | flops 1024 | bytes 4248 | tf_op jit(solution)/shard_map/add | solution.py:455
  9.0 1.6 %copy-done.1 = f32[128,4096]{1,0:T(8,128)S(1)} copy-done((f32[128,4096]{1,0:T(8,128)S(1)}, f32[128,4096]{1,0:T(8,128)}, u32[]{:S(2)}) %copy-start.1) | copy-done | bytes 2097176
  10.6 1.9 %prepare.1 = (bf16[512,256]{1,0:T(8,128)(2,1)S(1)}, bf16[512,256]{1,0:T(8,128)(2,1)S(1)}, bf16[16,256]{1,0:T(8,128)(2,1)S(1)}, f32[8,256]{1,0:T(8,128)S(1)}, f32...) custom-call(f32[8,128]{1,0:T(8,128)S(1)} %pad_add_fusion.1.small, ...), custom_call_target="tpu_custom_call" | custom-call | tf_op jit(solution)/shard_map/prepare/pallas_call | solution.py:460
  12.5 0.0 collective-permute-done.2.halos
  12.5 4.6 %filter_whiten.1 = (bf16[16,16,256]{2,1,0:T(8,128)(2,1)S(1)}, bf16[16,16,256]{2,1,0:T(8,128)(2,1)S(1)}, bf16[33,16,256]{2,1,0:T(8,128)(2,1)S(1)}, bf16[33,16,256...) custom-call(f32[8,4096]{1,0:T(8,128)S(1)} %get-tuple-element.39.own_near, bf16[64,4096]{1,0:T(8,128)(2,1)S(1)} %get-tuple-element.40.own_high, ...), custom_call_target="tpu_custom_call" | custom-call | tf_op jit(solution)/shard_map/filter_whiten/pallas_call | solution.py:478
  17.1 0.0 copy-start
  17.2 0.1 collective-permute-start.3
  17.2 1.2 %collective-permute-start.4 = (bf16[33,16,256]{2,1,0:T(8,128)(2,1)S(1)}, bf16[33,16,256]{2,1,0:T(8,128)(2,1)S(1)}, u32[]{:S(2)}, u32[]{:S(2)}) collective-permute-start(bf16[33,16,256]{2,1,0:T(8,128)(2,1)S(1)} %get-tuple-element.50), channel_id=1, source_target_pairs={{0,4},{2,6},{4,0},{6,2},{8,12},{10,14},{12,8},{14,10},{16,20},{18,... | collective-permute-start | bytes 811016 | tf_op jit(solution)/shard_map/ppermute | solution.py:432
  18.4 1.6 %collective-permute-start.5 = (bf16[16,16,256]{2,1,0:T(8,128)(2,1)S(1)}, bf16[16,16,256]{2,1,0:T(8,128)(2,1)S(1)}, u32[]{:S(2)}, u32[]{:S(2)}) collective-permute-start(bf16[16,16,256]{2,1,0:T(8,128)(2,1)S(1)} %get-tuple-element.51.first), channel_id=1, source_target_pairs={{0,8},{8,0},{2,10},{10,2},{4,12},{12,4},{6,14},{14,6},{16,24},{24,... | collective-permute-start | bytes 393224 | tf_op jit(solution)/shard_map/ppermute | solution.py:440
  20.0 1.9 %collective-permute-start.6 = (bf16[16,16,256]{2,1,0:T(8,128)(2,1)S(1)}, bf16[16,16,256]{2,1,0:T(8,128)(2,1)S(1)}, u32[]{:S(2)}, u32[]{:S(2)}) collective-permute-start(bf16[16,16,256]{2,1,0:T(8,128)(2,1)S(1)} %get-tuple-element.52.second), channel_id=1, source_target_pairs={{8,16},{16,8},{10,18},{18,10},{12,20},{20,12},{14,22},{22,14},{9,1... | collective-permute-start | bytes 393224 | tf_op jit(solution)/shard_map/ppermute | solution.py:440
  22.0 3.0 %collective-permute-done.3.refs_1_.b1 = bf16[33,16,256]{2,1,0:T(8,128)(2,1)S(1)} collective-permute-done((bf16[33,16,256]{2,1,0:T(8,128)(2,1)S(1)}, bf16[33,16,256]{2,1,0:T(8,128)(2,1)S(1)}, u32[]{:S(2)}, u32[]{:S(2)}) %collective-permute-start.3) | collective-permute-done | bytes 270368 | tf_op jit(solution)/shard_map/ppermute | solution.py:432
  24.9 2.1 %collective-permute-start.7 = (bf16[33,16,256]{2,1,0:T(8,128)(2,1)S(1)}, bf16[33,16,256]{2,1,0:T(8,128)(2,1)S(1)}, u32[]{:S(2)}, u32[]{:S(2)}) collective-permute-start(bf16[33,16,256]{2,1,0:T(8,128)(2,1)S(1)} %get-tuple-element.55), channel_id=1, source_target_pairs={{0,6},{2,4},{4,2},{6,0},{8,14},{10,12},{12,10},{14,8},{16,22},{18,... | collective-permute-start | bytes 811016 | tf_op jit(solution)/shard_map/ppermute | solution.py:432
  27.1 0.0 collective-permute-done.4.refs_2_.b2
  27.2 2.4 %collective-permute-start.9 = (bf16[2,16,16,256]{3,2,1,0:T(8,128)(2,1)S(1)}, bf16[2,16,16,256]{3,2,1,0:T(8,128)(2,1)S(1)}, u32[]{:S(2)}, u32[]{:S(2)}) collective-permute-start(bf16[2,16,16,256]{3,2,1,0:T(8,128)(2,1)S(1)} %pad_maximum_fusion.1), channel_id=1, source_target_pairs={{8,16},{16,8},{10,18},{18,10},{12,20},{20,12},{14,22},{22,14},{9,1... | collective-permute-start | bytes 786440 | tf_op jit(solution)/shard_map/ppermute | solution.py:440
  29.6 0.1 collective-permute-start.8
  29.6 4.4 %collective-permute-done.7.refs_3_.b3 = bf16[33,16,256]{2,1,0:T(8,128)(2,1)S(1)} collective-permute-done((bf16[33,16,256]{2,1,0:T(8,128)(2,1)S(1)}, bf16[33,16,256]{2,1,0:T(8,128)(2,1)S(1)}, u32[]{:S(2)}, u32[]{:S(2)}) %collective-permute-start.7) | collective-permute-done | bytes 270368 | tf_op jit(solution)/shard_map/ppermute | solution.py:432
  34.0 0.8 %collective-permute-start.10 = (bf16[16,16,256]{2,1,0:T(8,128)(2,1)S(1)}, bf16[16,16,256]{2,1,0:T(8,128)(2,1)S(1)}, u32[]{:S(2)}, u32[]{:S(2)}) collective-permute-start(bf16[16,16,256]{2,1,0:T(8,128)(2,1)S(1)} %get-tuple-element.72), channel_id=1, source_target_pairs={{0,8},{8,0},{2,10},{10,2},{4,12},{12,4},{6,14},{14,6},{16,24},{24,... | collective-permute-start | bytes 393224 | tf_op jit(solution)/shard_map/ppermute | solution.py:440
  34.8 2.0 %collective-permute-start.11 = (bf16[16,16,256]{2,1,0:T(8,128)(2,1)S(1)}, bf16[16,16,256]{2,1,0:T(8,128)(2,1)S(1)}, u32[]{:S(2)}, u32[]{:S(2)}) collective-permute-start(bf16[16,16,256]{2,1,0:T(8,128)(2,1)S(1)} %get-tuple-element.71), channel_id=1, source_target_pairs={{8,16},{16,8},{10,18},{18,10},{12,20},{20,12},{14,22},{22,14},{9,1... | collective-permute-start | bytes 393224 | tf_op jit(solution)/shard_map/ppermute | solution.py:440
  36.9 1.8 %inner_pairs.1 = (f32[4,32,16,512]{3,2,1,0:T(8,128)S(1)}, f32[16,16,512]{2,1,0:T(8,128)S(1)}, f32[16,16,512]{2,1,0:T(8,128)S(1)}, f32[96,512]{1,0:T(8,128)S(1)}) custom-call(bf16[16,16,256]{2,1,0:T(8,128)(2,1)S(1)} %get-tuple-element.51.first, bf16[16,16,256]{2,1,0:T(8,128)(2,1)S(1)} %get-tuple-element.52.second, ...), custom_call_target="tpu_custom_call" | custom-call | tf_op jit(solution)/shard_map/inner_pairs/pallas_call | solution.py:512
  38.7 0.0 collective-permute-done.9.far_12
  38.7 0.1 collective-permute-done.8.near_12
  38.8 2.1 %cross_pairs.1.cross_in = f32[416,512]{1,0:T(8,128)S(1)} custom-call(f32[4,32,16,512]{3,2,1,0:T(8,128)S(1)} %get-tuple-element.58.spec, f32[16,16,512]{2,1,0:T(8,128)S(1)} %get-tuple-element.59.spec_near, f32[16,16,512]{2,1,0:T(8,128)S(1)} %get-tuple-element.60.spec_far, f32[96,512]{1,0:T(8,128)S(1)} %get-tuple-element.61.inner, ...), custom_call_target="tpu_custom_call" | custom-call | tf_op jit(solution)/shard_map/cross_pairs/pallas_call | solution.py:520
  41.0 0.7 %collective-permute-done.11.far_3 = bf16[16,16,256]{2,1,0:T(8,128)(2,1)S(1)} collective-permute-done((bf16[16,16,256]{2,1,0:T(8,128)(2,1)S(1)}, bf16[16,16,256]{2,1,0:T(8,128)(2,1)S(1)}, u32[]{:S(2)}, u32[]{:S(2)}) %collective-permute-start.11) | collective-permute-done | bytes 131104 | tf_op jit(solution)/shard_map/ppermute | solution.py:440
  41.7 1.9 %pair_lags.1 = (bf16[208,416]{1,0:T(8,128)(2,1)S(1)}, bf16[208,256]{1,0:T(8,128)(2,1)S(1)}, bf16[208,256]{1,0:T(8,128)(2,1)S(1)}) custom-call(f32[4,32,16,512]{3,2,1,0:T(8,128)S(1)} %get-tuple-element.58.spec, f32[416,512]{1,0:T(8,128)S(1)} %cross_pairs.1.cross_in, bf16[16,16,256]{2,1,0:T(8,128)(2,1)S(1)} %collective-permute-done.10.near_3, ...), custom_call_target="tpu_custom_call" | custom-call | tf_op jit(solution)/shard_map/pair_lags/pallas_call | solution.py:529
  43.6 0.0 copy-start.4
  43.6 0.0 copy-start.5
  43.6 0.1 collective-permute-start.12
  43.7 3.2 %collective-permute-start.13 = (bf16[208,256]{1,0:T(8,128)(2,1)S(1)}, bf16[208,256]{1,0:T(8,128)(2,1)S(1)}, u32[]{:S(2)}, u32[]{:S(2)}) collective-permute-start(bf16[208,256]{1,0:T(8,128)(2,1)S(1)} %get-tuple-element.64), channel_id=1, source_target_pairs={{8,16},{16,8},{10,18},{18,10},{12,20},{20,12},{14,22},{22,14},{9,1... | collective-permute-start | bytes 319496 | tf_op jit(solution)/shard_map/ppermute | solution.py:440
  46.9 0.1 collective-permute-start.14
  47.0 1.4 %collective-permute-done.12.refs_1_ = bf16[208,256]{1,0:T(8,128)(2,1)S(1)} collective-permute-done((bf16[208,256]{1,0:T(8,128)(2,1)S(1)}, bf16[208,256]{1,0:T(8,128)(2,1)S(1)}, u32[]{:S(2)}, u32[]{:S(2)}) %collective-permute-start.12) | collective-permute-done | bytes 106528 | tf_op jit(solution)/shard_map/ppermute | solution.py:440
  48.4 1.9 %collective-permute-done.13.refs_2_ = bf16[208,256]{1,0:T(8,128)(2,1)S(1)} collective-permute-done((bf16[208,256]{1,0:T(8,128)(2,1)S(1)}, bf16[208,256]{1,0:T(8,128)(2,1)S(1)}, u32[]{:S(2)}, u32[]{:S(2)}) %collective-permute-start.13) | collective-permute-done | bytes 106528 | tf_op jit(solution)/shard_map/ppermute | solution.py:440
  50.3 0.3 choose.1.chosen
  50.6 0.9 %collective-permute-done.16.refs_5_ = bf16[208,256]{1,0:T(8,128)(2,1)S(1)} collective-permute-done((bf16[208,256]{1,0:T(8,128)(2,1)S(1)}, bf16[208,256]{1,0:T(8,128)(2,1)S(1)}, u32[]{:S(2)}, u32[]{:S(2)}) %collective-permute-start.16) | collective-permute-done | bytes 106528 | tf_op jit(solution)/shard_map/ppermute | solution.py:429
  51.6 0.6 select_slots.1
  52.2 2.5 %collective-permute-start.17 = (bf16[2,208,128]{2,1,0:T(8,128)(2,1)S(1)}, bf16[2,208,128]{2,1,0:T(8,128)(2,1)S(1)}, u32[]{:S(2)}, u32[]{:S(2)}) collective-permute-start(bf16[2,208,128]{2,1,0:T(8,128)(2,1)S(1)} %get-tuple-element.66), channel_id=1, source_target_pairs={{0,2},{2,0},{4,6},{6,4},{8,10},{10,8},{12,14},{14,12},{16,18},{18,... | collective-permute-start | bytes 319496 | tf_op jit(solution)/shard_map/ppermute | solution.py:432
  54.8 0.0 collective-permute-start.18
  54.8 1.5 %collective-permute-start.19 = (bf16[2,208,128]{2,1,0:T(8,128)(2,1)S(1)}, bf16[2,208,128]{2,1,0:T(8,128)(2,1)S(1)}, u32[]{:S(2)}, u32[]{:S(2)}) collective-permute-start(bf16[2,208,128]{2,1,0:T(8,128)(2,1)S(1)} %get-tuple-element.68), channel_id=1, source_target_pairs={{0,6},{2,4},{4,2},{6,0},{8,14},{10,12},{12,10},{14,8},{16,22},{18,... | collective-permute-start | bytes 319496 | tf_op jit(solution)/shard_map/ppermute | solution.py:432
  56.9 1.1 %collective-permute-done.17.refs_1_ = bf16[2,208,128]{2,1,0:T(8,128)(2,1)S(1)} collective-permute-done((bf16[2,208,128]{2,1,0:T(8,128)(2,1)S(1)}, bf16[2,208,128]{2,1,0:T(8,128)(2,1)S(1)}, u32[]{:S(2)}, u32[]{:S(2)}) %collective-permute-start.17) | collective-permute-done | bytes 106528 | tf_op jit(solution)/shard_map/ppermute | solution.py:432
  58.1 3.7 %collective-permute-done.18.refs_2_ = bf16[2,208,128]{2,1,0:T(8,128)(2,1)S(1)} collective-permute-done((bf16[2,208,128]{2,1,0:T(8,128)(2,1)S(1)}, bf16[2,208,128]{2,1,0:T(8,128)(2,1)S(1)}, u32[]{:S(2)}, u32[]{:S(2)}) %collective-permute-start.18) | collective-permute-done | bytes 106528 | tf_op jit(solution)/shard_map/ppermute | solution.py:432
  61.8 3.2 %finish_slots.1 = f32[201,8,128]{2,1,0:T(8,128)} custom-call(s32[2,16]{1,0:T(2,128)S(1)} %bitcast.16, s32[1]{0:T(128)S(6)} %copy.11.count, bf16[2,208,128]{2,1,0:T(8,128)(2,1)S(1)} %get-tuple-element.65.refs_0_, bf16[2,208,128]{2,1,0:T(8,128)(2,1)S(1)} %collective-permute-done.17.refs_1_, bf16[2,208,128]{2,1,0:T(8,128)(2,1)S(1)} %collective-permute-done.18.refs_2_, ...), custom_call_target="tpu_custom_call" | custom-call | tf_op jit(solution)/shard_map/finish_slots/pallas_call | solution.py:565
  (22 shorter events, 0.2 us)
Async XLA Ops:
  1.9 1.3 %collective-permute-start = (f32[2,4096]{1,0:T(2,128)S(1)}, f32[2,4096]{1,0:T(2,128)S(1)}, u32[]{:S(2)}, u32[]{:S(2)}) collective-permute-start(f32[2,4096]{1,0:T(2,128)S(1)} %get-tuple-element.70), channel_id=1, source_target_pairs={{0,1},{1,0},{2,3},{3,2},{4,5},{5,4},{6,7},{7,6},{8,9},{9,8},{10,11... | collective-permute-start | bytes 98312 | tf_op jit(solution)/shard_map/ppermute | solution.py:429
  3.1 9.4 %collective-permute-start.1 = (f32[128,4096]{1,0:T(8,128)}, f32[128,4096]{1,0:T(8,128)S(1)}, u32[]{:S(2)}, u32[]{:S(2)}) collective-permute-start(f32[128,4096]{1,0:T(8,128)} %traces), channel_id=1, source_target_pairs={{0,1},{1,0},{2,3},{3,2},{4,5},{5,4},{6,7},{7,6},{8,9},{9,8},{10,11... | collective-permute-start | bytes 6291464 | tf_op jit(solution)/shard_map/ppermute | solution.py:429
  4.1 8.4 %collective-permute-start.2 = (f32[4,4096]{1,0:T(4,128)S(1)}, f32[4,4096]{1,0:T(4,128)S(1)}, u32[]{:S(2)}, u32[]{:S(2)}) collective-permute-start(f32[4,4096]{1,0:T(4,128)S(1)} %pad_maximum_fusion.2), channel_id=1, source_target_pairs={{1,2},{2,1},{3,4},{4,3},{5,6},{6,5},{7,8},{8,7},{9,10},{10,9},{11,... | collective-permute-start | bytes 196616 | tf_op jit(solution)/shard_map/ppermute | solution.py:452
  9.0 1.6 %copy-start.1 = (f32[128,4096]{1,0:T(8,128)S(1)}, f32[128,4096]{1,0:T(8,128)}, u32[]{:S(2)}) copy-start(f32[128,4096]{1,0:T(8,128)} %traces) | copy-start | bytes 6291460
  17.1 19.7 %copy-start = (bf16[256,512]{1,0:T(8,128)(2,1)S(1)}, bf16[256,512]{1,0:T(8,128)(2,1)}, u32[]{:S(2)}) copy-start(bf16[256,512]{1,0:T(8,128)(2,1)} %constant.52.clone.table) | copy-start | bytes 786436
  17.2 7.8 %collective-permute-start.3 = (bf16[33,16,256]{2,1,0:T(8,128)(2,1)S(1)}, bf16[33,16,256]{2,1,0:T(8,128)(2,1)S(1)}, u32[]{:S(2)}, u32[]{:S(2)}) collective-permute-start(bf16[33,16,256]{2,1,0:T(8,128)(2,1)S(1)} %get-tuple-element.47), channel_id=1, source_target_pairs={{0,2},{2,0},{4,6},{6,4},{8,10},{10,8},{12,14},{14,12},{16,18},{18,... | collective-permute-start | bytes 811016 | tf_op jit(solution)/shard_map/ppermute | solution.py:432
  17.2 9.8 %collective-permute-start.4 = (bf16[33,16,256]{2,1,0:T(8,128)(2,1)S(1)}, bf16[33,16,256]{2,1,0:T(8,128)(2,1)S(1)}, u32[]{:S(2)}, u32[]{:S(2)}) collective-permute-start(bf16[33,16,256]{2,1,0:T(8,128)(2,1)S(1)} %get-tuple-element.50), channel_id=1, source_target_pairs={{0,4},{2,6},{4,0},{6,2},{8,12},{10,14},{12,8},{14,10},{16,20},{18,... | collective-permute-start | bytes 811016 | tf_op jit(solution)/shard_map/ppermute | solution.py:432
  18.4 8.6 %collective-permute-start.5 = (bf16[16,16,256]{2,1,0:T(8,128)(2,1)S(1)}, bf16[16,16,256]{2,1,0:T(8,128)(2,1)S(1)}, u32[]{:S(2)}, u32[]{:S(2)}) collective-permute-start(bf16[16,16,256]{2,1,0:T(8,128)(2,1)S(1)} %get-tuple-element.51.first), channel_id=1, source_target_pairs={{0,8},{8,0},{2,10},{10,2},{4,12},{12,4},{6,14},{14,6},{16,24},{24,... | collective-permute-start | bytes 393224 | tf_op jit(solution)/shard_map/ppermute | solution.py:440
  20.0 7.1 %collective-permute-start.6 = (bf16[16,16,256]{2,1,0:T(8,128)(2,1)S(1)}, bf16[16,16,256]{2,1,0:T(8,128)(2,1)S(1)}, u32[]{:S(2)}, u32[]{:S(2)}) collective-permute-start(bf16[16,16,256]{2,1,0:T(8,128)(2,1)S(1)} %get-tuple-element.52.second), channel_id=1, source_target_pairs={{8,16},{16,8},{10,18},{18,10},{12,20},{20,12},{14,22},{22,14},{9,1... | collective-permute-start | bytes 393224 | tf_op jit(solution)/shard_map/ppermute | solution.py:440
  24.9 9.1 %collective-permute-start.7 = (bf16[33,16,256]{2,1,0:T(8,128)(2,1)S(1)}, bf16[33,16,256]{2,1,0:T(8,128)(2,1)S(1)}, u32[]{:S(2)}, u32[]{:S(2)}) collective-permute-start(bf16[33,16,256]{2,1,0:T(8,128)(2,1)S(1)} %get-tuple-element.55), channel_id=1, source_target_pairs={{0,6},{2,4},{4,2},{6,0},{8,14},{10,12},{12,10},{14,8},{16,22},{18,... | collective-permute-start | bytes 811016 | tf_op jit(solution)/shard_map/ppermute | solution.py:432
  27.2 11.6 %collective-permute-start.9 = (bf16[2,16,16,256]{3,2,1,0:T(8,128)(2,1)S(1)}, bf16[2,16,16,256]{3,2,1,0:T(8,128)(2,1)S(1)}, u32[]{:S(2)}, u32[]{:S(2)}) collective-permute-start(bf16[2,16,16,256]{3,2,1,0:T(8,128)(2,1)S(1)} %pad_maximum_fusion.1), channel_id=1, source_target_pairs={{8,16},{16,8},{10,18},{18,10},{12,20},{20,12},{14,22},{22,14},{9,1... | collective-permute-start | bytes 786440 | tf_op jit(solution)/shard_map/ppermute | solution.py:440
  29.6 9.3 %collective-permute-start.8 = (bf16[2,16,16,256]{3,2,1,0:T(8,128)(2,1)S(1)}, bf16[2,16,16,256]{3,2,1,0:T(8,128)(2,1)S(1)}, u32[]{:S(2)}, u32[]{:S(2)}) collective-permute-start(bf16[2,16,16,256]{3,2,1,0:T(8,128)(2,1)S(1)} %pad_maximum_fusion), channel_id=1, source_target_pairs={{0,8},{8,0},{2,10},{10,2},{4,12},{12,4},{6,14},{14,6},{16,24},{24,... | collective-permute-start | bytes 786440 | tf_op jit(solution)/shard_map/ppermute | solution.py:440
  34.0 7.0 %collective-permute-start.10 = (bf16[16,16,256]{2,1,0:T(8,128)(2,1)S(1)}, bf16[16,16,256]{2,1,0:T(8,128)(2,1)S(1)}, u32[]{:S(2)}, u32[]{:S(2)}) collective-permute-start(bf16[16,16,256]{2,1,0:T(8,128)(2,1)S(1)} %get-tuple-element.72), channel_id=1, source_target_pairs={{0,8},{8,0},{2,10},{10,2},{4,12},{12,4},{6,14},{14,6},{16,24},{24,... | collective-permute-start | bytes 393224 | tf_op jit(solution)/shard_map/ppermute | solution.py:440
  34.8 6.8 %collective-permute-start.11 = (bf16[16,16,256]{2,1,0:T(8,128)(2,1)S(1)}, bf16[16,16,256]{2,1,0:T(8,128)(2,1)S(1)}, u32[]{:S(2)}, u32[]{:S(2)}) collective-permute-start(bf16[16,16,256]{2,1,0:T(8,128)(2,1)S(1)} %get-tuple-element.71), channel_id=1, source_target_pairs={{8,16},{16,8},{10,18},{18,10},{12,20},{20,12},{14,22},{22,14},{9,1... | collective-permute-start | bytes 393224 | tf_op jit(solution)/shard_map/ppermute | solution.py:440
  38.8 2.9 %copy-start.2 = (bf16[208,512]{1,0:T(8,128)(2,1)S(1)}, bf16[208,512]{1,0:T(8,128)(2,1)}, u32[]{:S(2)}) copy-start(bf16[208,512]{1,0:T(8,128)(2,1)} %constant.53.clone.l_high) | copy-start | bytes 638980
  38.8 2.9 %copy-start.3 = (bf16[208,512]{1,0:T(8,128)(2,1)S(1)}, bf16[208,512]{1,0:T(8,128)(2,1)}, u32[]{:S(2)}) copy-start(bf16[208,512]{1,0:T(8,128)(2,1)} %constant.54.clone.l_low) | copy-start | bytes 638980
  43.6 18.2 %copy-start.4 = (bf16[208,208]{1,0:T(8,128)(2,1)S(1)}, bf16[208,208]{1,0:T(8,128)(2,1)}, u32[]{:S(2)}) copy-start(bf16[208,208]{1,0:T(8,128)(2,1)} %constant.55.clone.refs_4_) | copy-start | bytes 259588
  43.6 18.2 %copy-start.5 = (s32[16,2]{0,1:T(2,128)S(1)}, s32[16,2]{0,1:T(2,128)}, u32[]{:S(2)}) copy-start(s32[16,2]{0,1:T(2,128)} %param.14) | copy-start | bytes 388
  43.6 4.8 %collective-permute-start.12 = (bf16[208,256]{1,0:T(8,128)(2,1)S(1)}, bf16[208,256]{1,0:T(8,128)(2,1)S(1)}, u32[]{:S(2)}, u32[]{:S(2)}) collective-permute-start(bf16[208,256]{1,0:T(8,128)(2,1)S(1)} %get-tuple-element.63), channel_id=1, source_target_pairs={{0,8},{8,0},{2,10},{10,2},{4,12},{12,4},{6,14},{14,6},{16,24},{24,... | collective-permute-start | bytes 319496 | tf_op jit(solution)/shard_map/ppermute | solution.py:440
  43.7 6.6 %collective-permute-start.13 = (bf16[208,256]{1,0:T(8,128)(2,1)S(1)}, bf16[208,256]{1,0:T(8,128)(2,1)S(1)}, u32[]{:S(2)}, u32[]{:S(2)}) collective-permute-start(bf16[208,256]{1,0:T(8,128)(2,1)S(1)} %get-tuple-element.64), channel_id=1, source_target_pairs={{8,16},{16,8},{10,18},{18,10},{12,20},{20,12},{14,22},{22,14},{9,1... | collective-permute-start | bytes 319496 | tf_op jit(solution)/shard_map/ppermute | solution.py:440
  46.9 3.7 %collective-permute-start.14 = (bf16[208,416]{1,0:T(8,128)(2,1)S(1)}, bf16[208,416]{1,0:T(8,128)(2,1)S(1)}, u32[]{:S(2)}, u32[]{:S(2)}) collective-permute-start(bf16[208,416]{1,0:T(8,128)(2,1)S(1)} %get-tuple-element.62.refs_0_), channel_id=1, source_target_pairs={{0,1},{1,0},{2,3},{3,2},{4,5},{5,4},{6,7},{7,6},{8,9},{9,8},{10,11... | collective-permute-start | bytes 519176 | tf_op jit(solution)/shard_map/ppermute | solution.py:429
  48.4 2.3 %collective-permute-start.15 = (bf16[208,256]{1,0:T(8,128)(2,1)S(1)}, bf16[208,256]{1,0:T(8,128)(2,1)S(1)}, u32[]{:S(2)}, u32[]{:S(2)}) collective-permute-start(bf16[208,256]{1,0:T(8,128)(2,1)S(1)} %collective-permute-done.12.refs_1_), channel_id=1, source_target_pairs={{0,1},{1,0},{2,3},{3,2},{4,5},{5,4},{6,7},{7,6},{8,9},{9,8},{10,11... | collective-permute-start | bytes 319496 | tf_op jit(solution)/shard_map/ppermute | solution.py:429
  50.3 1.3 %collective-permute-start.16 = (bf16[208,256]{1,0:T(8,128)(2,1)S(1)}, bf16[208,256]{1,0:T(8,128)(2,1)S(1)}, u32[]{:S(2)}, u32[]{:S(2)}) collective-permute-start(bf16[208,256]{1,0:T(8,128)(2,1)S(1)} %collective-permute-done.13.refs_2_), channel_id=1, source_target_pairs={{0,1},{1,0},{2,3},{3,2},{4,5},{5,4},{6,7},{7,6},{8,9},{9,8},{10,11... | collective-permute-start | bytes 319496 | tf_op jit(solution)/shard_map/ppermute | solution.py:429
  52.2 5.9 %collective-permute-start.17 = (bf16[2,208,128]{2,1,0:T(8,128)(2,1)S(1)}, bf16[2,208,128]{2,1,0:T(8,128)(2,1)S(1)}, u32[]{:S(2)}, u32[]{:S(2)}) collective-permute-start(bf16[2,208,128]{2,1,0:T(8,128)(2,1)S(1)} %get-tuple-element.66), channel_id=1, source_target_pairs={{0,2},{2,0},{4,6},{6,4},{8,10},{10,8},{12,14},{14,12},{16,18},{18,... | collective-permute-start | bytes 319496 | tf_op jit(solution)/shard_map/ppermute | solution.py:432
  54.8 7.0 %collective-permute-start.18 = (bf16[2,208,128]{2,1,0:T(8,128)(2,1)S(1)}, bf16[2,208,128]{2,1,0:T(8,128)(2,1)S(1)}, u32[]{:S(2)}, u32[]{:S(2)}) collective-permute-start(bf16[2,208,128]{2,1,0:T(8,128)(2,1)S(1)} %get-tuple-element.67), channel_id=1, source_target_pairs={{0,4},{2,6},{4,0},{6,2},{8,12},{10,14},{12,8},{14,10},{16,20},{18,... | collective-permute-start | bytes 319496 | tf_op jit(solution)/shard_map/ppermute | solution.py:432
  54.8 7.0 %collective-permute-start.19 = (bf16[2,208,128]{2,1,0:T(8,128)(2,1)S(1)}, bf16[2,208,128]{2,1,0:T(8,128)(2,1)S(1)}, u32[]{:S(2)}, u32[]{:S(2)}) collective-permute-start(bf16[2,208,128]{2,1,0:T(8,128)(2,1)S(1)} %get-tuple-element.68), channel_id=1, source_target_pairs={{0,6},{2,4},{4,2},{6,0},{8,14},{10,12},{12,10},{14,8},{16,22},{18,... | collective-permute-start | bytes 319496 | tf_op jit(solution)/shard_map/ppermute | solution.py:432

commit v5 on v4

--- a/solution.py
+++ b/solution.py
@@ -110,17 +110,10 @@
 
 def prepare_kernel(
     small, whole, whole_rows, traces, t_high, t_low, pid, space, ok, own_high, own_low, own_near,
-    main_rows, near_rows, sems,
 ):
     _, core, _ = my_place()
     plane = lax.axis_index("chan") // PLANE
     main, near = tile_rows(traces, core)
-    copies = [
-        pltpu.make_async_copy(traces.at[main], main_rows, sems.at[0]),
-        pltpu.make_async_copy(traces.at[near], near_rows, sems.at[1]),
-    ]
-    for copy in copies:
-        copy.start()
     t_high[...] = jnp.zeros(t_high.shape, BF16)
     t_low[...] = jnp.zeros(t_low.shape, BF16)
     shift = SEG // 2 - (TAPS - 1) // 2
@@ -154,10 +147,8 @@
     )
     spread = jnp.where(diagonal, whole_rows[2:3, :width].astype(F32), 0.0)
     ok[...] = jnp.broadcast_to(jnp.sum(spread, axis=1, keepdims=True), ok.shape)
-    for copy in copies:
-        copy.wait()
-    own_high[...], own_low[...] = split_terms(main_rows[...] * ok[main, 0:1])
-    own_near[...] = near_rows[...] * ok[near, 0:1]
+    own_high[...], own_low[...] = split_terms(traces[main, :] * ok[main, 0:1])
+    own_near[...] = traces[near, :] * ok[near, 0:1]
 
 
 def filter_kernel(
@@ -407,7 +398,6 @@
 
 VM = pl.BlockSpec(memory_space=pltpu.VMEM)
 SM = pl.BlockSpec(memory_space=pltpu.SMEM)
-HB = pl.BlockSpec(memory_space=pltpu.HBM)
 PARAMS = pltpu.CompilerParams(vmem_limit_bytes=VMEM_LIMIT)
 
 
@@ -441,20 +431,26 @@
 
     rows = chan_width // 2
     head, tail = traces[0:2], traces[chan_width - 2 :]
-    got = to_core(jnp.where(core == 0, tail, head))
+    give = jnp.where(core == 0, tail, head)
     mine = jnp.where(core == 0, head, tail)
-    got, late = lax.optimization_barrier((got, traces))
-    route = []
-    for c in range(n_chan - 1):
-        route += [(2 * c + 1, 2 * c + 2), (2 * c + 2, 2 * c + 1)]
+    give, mine, time_taps, space_taps, channel_ok, pairs = lax.optimization_barrier(
+        (give, mine, time_taps, space_taps, channel_ok, pairs)
+    )
+    got = to_core(give)
     alive = (jnp.where(core == 0, channel_ok[0:2], channel_ok[chan_width - 2 :]) > 0)[:, None]
-    edges = [jnp.where(alive, mine, 0.0), jnp.where(alive, got, 0.0)]
-    halos = lax.ppermute(jnp.concatenate(edges, axis=0), BOTH, route)
-    other = to_core(late)
+    mine = jnp.where(alive, mine, 0.0)
     small = jnp.pad(time_taps[None, :], ((0, 7), (0, 128 - TAPS)))
     small = small + jnp.pad(space_taps[None, :], ((1, 6), (0, 128 - STAPS)))
     whole = jnp.pad(pairs, ((0, 6), (0, 128 - SLOTS)))
     whole = whole + jnp.pad(channel_ok[None, :], ((2, 5), (0, 128 - chan_width)))
+    got, mine, small, whole = lax.optimization_barrier((got, mine, small, whole))
+    route = []
+    for c in range(n_chan - 1):
+        route += [(2 * c + 1, 2 * c + 2), (2 * c + 2, 2 * c + 1)]
+    edges = jnp.concatenate([mine, jnp.where(alive, got, 0.0)], axis=0)
+    edges, late = lax.optimization_barrier((edges, traces))
+    halos = lax.ppermute(edges, BOTH, route)
+    other = to_core(late)
     table = shape((2 * SEG, SEG), BF16)
     split = shape((rows, half), BF16)
     t_high, t_low, pid, space, ok, own_high, own_low, own_near = pl.pallas_call(
@@ -463,13 +459,8 @@
             table, table, shape((QG, SLOTS * QG), BF16), shape((8, SEG), F32), shape((chan_width, 128), F32),
             split, split, shape((8, half), F32),
         ],
-        in_specs=[SM, SM, VM, HB],
+        in_specs=[SM, SM, VM, VM],
         out_specs=[VM] * 8,
-        scratch_shapes=[
-            pltpu.VMEM((rows, half), F32),
-            pltpu.VMEM((8, half), F32),
-            pltpu.SemaphoreType.DMA((2,)),
-        ],
         compiler_params=PARAMS,
         name="prepare",
     )(small, whole, whole, late)
@@ -491,7 +482,7 @@
     )(own_near, own_high, own_low, other, halos, space, ok, t_high, t_low, pid)
     b1, b2 = in_plane(sent[0], 1), in_plane(sent[1], 2)
     far_0, near_0 = plane_swap(second, 1), plane_swap(first, 0)
-    b1, last = lax.optimization_barrier((b1, sent[2]))
+    near_0, last = lax.optimization_barrier((near_0, sent[2]))
     b3 = in_plane(last, 3)
     b1, b2, near_0, far_0 = lax.optimization_barrier((b1, b2, near_0, far_0))
     def halves(x):

time: 66 us -> 63.6 us (0.964); the launches traced: 65 us -> 63.3 us
  starting transfers between devices: 24 us -> 22.8 us
    ppermute x8, waiting for transfers between devices: 4.13 us -> 7.44 us  [plane_swap(): return lax.ppermute(x, 'chan', route)]
    ppermute x6, waiting for transfers between devices: 12.2 us -> 9.5 us  [in_plane(): return lax.ppermute(x, 'chan', [(c, c ^ rel) for c in range(n_chan)])]
    ppermute x6, starting transfers between devices: 7.47 us -> 6.25 us  [in_plane(): return lax.ppermute(x, 'chan', [(c, c ^ rel) for c in range(n_chan)])]
    ppermute x5, waiting for transfers between devices: 2.14 us -> 0.95 us  [to_core(): return lax.ppermute(x, 'tm', [(0, 1), (1, 0)])]
  transfers between devices with their start and end apart: 20 -> 20, of which waited for: 10 -> 11; matrix products, arithmetic and copies ran while one was open for 2% -> 4% of each run, Pallas kernels for 9% -> 9%
where the time goes in v5:
time: 63.6 us; the launch traced here: 63.3 us
  starting transfers between devices  22.8 us (36%)
  waiting for transfers between devices  18.2 us (29%)
  Pallas kernels  16.2 us (25%)
  other arithmetic  3.44 us (5%)
  local copies, waits for them, and re-layouts  1.67 us (3%)
  between operations  0.99 us (2%)
    ppermute x8, starting transfers between devices, plane_swap(): return lax.ppermute(x, 'chan', route)  12 us
    ppermute x6, waiting for transfers between devices, in_plane(): return lax.ppermute(x, 'chan', [(c, c ^ rel) for c in range(n_chan)])  9.5 us
    ppermute x8, waiting for transfers between devices, plane_swap(): return lax.ppermute(x, 'chan', route)  7.44 us
    ppermute x6, starting transfers between devices, in_plane(): return lax.ppermute(x, 'chan', [(c, c ^ rel) for c in range(n_chan)])  6.25 us
    pallas_call x1, Pallas kernels, local(): pl.pallas_call(filter_kernel, out_shape=[short] * 2 + [block] * 3, in_spe...  4.63 us
    ppermute x1, starting transfers between devices, local(): halos = lax.ppermute(edges, BOTH, route)  3.86 us
    pallas_call x1, Pallas kernels, local(): pl.pallas_call(finish_kernel, out_shape=shape((LAGS, SLOTS // 2, chan_wid...  3.19 us
    pallas_call x1, Pallas kernels, local(): pl.pallas_call(cross_kernel, out_shape=shape((N_OWN * QG, 2 * SEG), F32),...  2.12 us
  transfers between devices with their start and end apart: 20, of which 11 were waited for; matrix products, arithmetic and copies ran while one was open for 4% of the time, Pallas kernels for 9%

profile of v5, /device:TPU:16, one launch (start us, length us, event | category | flops | bytes accessed | tf_op | source)
XLA Modules:
  0.0 63.3 jit_solution(13873378997437927087)
XLA Ops:
  0.0 1.0 %broadcast_select_fusion.2 = (f32[2,4096]{1,0:T(2,128)S(1)}, f32[2,4096]{1,0:T(2,128)S(1)}) fusion(pred[]{:T(512)S(6)} %eq.4, f32[128,4096]{1,0:T(8,128)} %traces), kind=kLoop, calls=%fused_computation.9 | loop fusion | flops 16384 | bytes 131073 | tf_op jit(solution)/shard_map/jit(_where)/select_n | solution.py:435
  1.0 0.1 collective-permute-start
  1.1 0.8 %fusion = pred[2]{0:T(512)(128)(4,1)S(1)} fusion(pred[]{:T(512)S(6)} %eq.4, s32[128]{0:T(128)} %param.11), kind=kLoop, calls=%fused_computation.16 | loop fusion | flops 4 | bytes 19 | tf_op jit(solution)/shard_map/gt | solution.py:440
  1.9 0.1 broadcast_select_fusion.1
  2.0 0.7 %pad_add_fusion.whole.whole_rows = s32[8,128]{1,0:T(8,128)S(1)} fusion(s32[1,128]{1,0:T(1,128)} %bitcast.17, s32[2,16]{1,0:T(2,128)} %bitcast.15), kind=kLoop, calls=%fused_computation.11 | loop fusion | flops 1024 | bytes 4736 | tf_op jit(solution)/shard_map/add | solution.py:445
  2.7 0.7 %pad_add_fusion.1.small = f32[8,128]{1,0:T(8,128)S(1)} fusion(f32[1,5]{1,0:T(1,128)} %bitcast.18, f32[1,33]{1,0:T(1,128)} %bitcast.19), kind=kLoop, calls=%fused_computation.12 | loop fusion | flops 1024 | bytes 4248 | tf_op jit(solution)/shard_map/add | solution.py:443
  3.4 0.1 broadcast_select_fusion
  3.5 0.6 collective-permute-start.1
  4.0 3.9 %collective-permute-start.2 = (f32[4,4096]{1,0:T(4,128)S(1)}, f32[4,4096]{1,0:T(4,128)S(1)}, u32[]{:S(2)}, u32[]{:S(2)}) collective-permute-start(f32[4,4096]{1,0:T(4,128)S(1)} %pad_maximum_fusion.2), channel_id=1, source_target_pairs={{1,2},{2,1},{3,4},{4,3},{5,6},{6,5},{7,8},{8,7},{9,10},{10,9},{11,... | collective-permute-start | bytes 196616 | tf_op jit(solution)/shard_map/ppermute | solution.py:452
  7.9 0.0 copy-start.1
  7.9 1.6 %copy-done.1 = f32[128,4096]{1,0:T(8,128)S(1)} copy-done((f32[128,4096]{1,0:T(8,128)S(1)}, f32[128,4096]{1,0:T(8,128)}, u32[]{:S(2)}) %copy-start.1) | copy-done | bytes 2097176
  9.5 1.6 %prepare.1 = (bf16[512,256]{1,0:T(8,128)(2,1)S(1)}, bf16[512,256]{1,0:T(8,128)(2,1)S(1)}, bf16[16,256]{1,0:T(8,128)(2,1)S(1)}, f32[8,256]{1,0:T(8,128)S(1)}, f32...) custom-call(f32[8,128]{1,0:T(8,128)S(1)} %pad_add_fusion.1.small, ...), custom_call_target="tpu_custom_call" | custom-call | tf_op jit(solution)/shard_map/prepare/pallas_call | solution.py:456
  11.1 0.4 collective-permute-done.2.halos
  11.5 4.6 %filter_whiten.1 = (bf16[16,16,256]{2,1,0:T(8,128)(2,1)S(1)}, bf16[16,16,256]{2,1,0:T(8,128)(2,1)S(1)}, bf16[33,16,256]{2,1,0:T(8,128)(2,1)S(1)}, bf16[33,16,256...) custom-call(f32[8,4096]{1,0:T(8,128)S(1)} %get-tuple-element.59.own_near, bf16[64,4096]{1,0:T(8,128)(2,1)S(1)} %get-tuple-element.60.own_high, ...), custom_call_target="tpu_custom_call" | custom-call | tf_op jit(solution)/shard_map/filter_whiten/pallas_call | solution.py:469
  16.1 0.0 copy-start
  16.1 0.1 collective-permute-start.3
  16.2 1.7 %collective-permute-start.4 = (bf16[33,16,256]{2,1,0:T(8,128)(2,1)S(1)}, bf16[33,16,256]{2,1,0:T(8,128)(2,1)S(1)}, u32[]{:S(2)}, u32[]{:S(2)}) collective-permute-start(bf16[33,16,256]{2,1,0:T(8,128)(2,1)S(1)} %get-tuple-element.68), channel_id=1, source_target_pairs={{0,4},{2,6},{4,0},{6,2},{8,12},{10,14},{12,8},{14,10},{16,20},{18,... | collective-permute-start | bytes 811016 | tf_op jit(solution)/shard_map/ppermute | solution.py:422
  17.9 1.6 %collective-permute-start.5 = (bf16[16,16,256]{2,1,0:T(8,128)(2,1)S(1)}, bf16[16,16,256]{2,1,0:T(8,128)(2,1)S(1)}, u32[]{:S(2)}, u32[]{:S(2)}) collective-permute-start(bf16[16,16,256]{2,1,0:T(8,128)(2,1)S(1)} %get-tuple-element.69.first), channel_id=1, source_target_pairs={{0,8},{8,0},{2,10},{10,2},{4,12},{12,4},{6,14},{14,6},{16,24},{24,... | collective-permute-start | bytes 393224 | tf_op jit(solution)/shard_map/ppermute | solution.py:430
  19.5 1.9 %collective-permute-start.6 = (bf16[16,16,256]{2,1,0:T(8,128)(2,1)S(1)}, bf16[16,16,256]{2,1,0:T(8,128)(2,1)S(1)}, u32[]{:S(2)}, u32[]{:S(2)}) collective-permute-start(bf16[16,16,256]{2,1,0:T(8,128)(2,1)S(1)} %get-tuple-element.72.second), channel_id=1, source_target_pairs={{8,16},{16,8},{10,18},{18,10},{12,20},{20,12},{14,22},{22,14},{9,1... | collective-permute-start | bytes 393224 | tf_op jit(solution)/shard_map/ppermute | solution.py:430
  21.4 2.6 %collective-permute-done.5.near_0 = bf16[16,16,256]{2,1,0:T(8,128)(2,1)S(1)} collective-permute-done((bf16[16,16,256]{2,1,0:T(8,128)(2,1)S(1)}, bf16[16,16,256]{2,1,0:T(8,128)(2,1)S(1)}, u32[]{:S(2)}, u32[]{:S(2)}) %collective-permute-start.5) | collective-permute-done | bytes 131104 | tf_op jit(solution)/shard_map/ppermute | solution.py:430
  24.0 0.6 %collective-permute-start.7 = (bf16[33,16,256]{2,1,0:T(8,128)(2,1)S(1)}, bf16[33,16,256]{2,1,0:T(8,128)(2,1)S(1)}, u32[]{:S(2)}, u32[]{:S(2)}) collective-permute-start(bf16[33,16,256]{2,1,0:T(8,128)(2,1)S(1)} %get-tuple-element.75), channel_id=1, source_target_pairs={{0,6},{2,4},{4,2},{6,0},{8,14},{10,12},{12,10},{14,8},{16,22},{18,... | collective-permute-start | bytes 811016 | tf_op jit(solution)/shard_map/ppermute | solution.py:422
  24.7 1.7 %collective-permute-done.6.far_0 = bf16[16,16,256]{2,1,0:T(8,128)(2,1)S(1)} collective-permute-done((bf16[16,16,256]{2,1,0:T(8,128)(2,1)S(1)}, bf16[16,16,256]{2,1,0:T(8,128)(2,1)S(1)}, u32[]{:S(2)}, u32[]{:S(2)}) %collective-permute-start.6) | collective-permute-done | bytes 131104 | tf_op jit(solution)/shard_map/ppermute | solution.py:430
  26.4 2.1 %collective-permute-start.9 = (bf16[2,16,16,256]{3,2,1,0:T(8,128)(2,1)S(1)}, bf16[2,16,16,256]{3,2,1,0:T(8,128)(2,1)S(1)}, u32[]{:S(2)}, u32[]{:S(2)}) collective-permute-start(bf16[2,16,16,256]{3,2,1,0:T(8,128)(2,1)S(1)} %pad_maximum_fusion.1), channel_id=1, source_target_pairs={{8,16},{16,8},{10,18},{18,10},{12,20},{20,12},{14,22},{22,14},{9,1... | collective-permute-start | bytes 786440 | tf_op jit(solution)/shard_map/ppermute | solution.py:430
  28.6 0.1 collective-permute-start.8
  28.6 4.5 %collective-permute-done.7.refs_3_.b3 = bf16[33,16,256]{2,1,0:T(8,128)(2,1)S(1)} collective-permute-done((bf16[33,16,256]{2,1,0:T(8,128)(2,1)S(1)}, bf16[33,16,256]{2,1,0:T(8,128)(2,1)S(1)}, u32[]{:S(2)}, u32[]{:S(2)}) %collective-permute-start.7) | collective-permute-done | bytes 270368 | tf_op jit(solution)/shard_map/ppermute | solution.py:422
  33.2 0.1 collective-permute-start.10
  33.3 2.8 %collective-permute-start.11 = (bf16[16,16,256]{2,1,0:T(8,128)(2,1)S(1)}, bf16[16,16,256]{2,1,0:T(8,128)(2,1)S(1)}, u32[]{:S(2)}, u32[]{:S(2)}) collective-permute-start(bf16[16,16,256]{2,1,0:T(8,128)(2,1)S(1)} %get-tuple-element.91), channel_id=1, source_target_pairs={{8,16},{16,8},{10,18},{18,10},{12,20},{20,12},{14,22},{22,14},{9,1... | collective-permute-start | bytes 393224 | tf_op jit(solution)/shard_map/ppermute | solution.py:430
  36.1 1.8 %inner_pairs.1 = (f32[4,32,16,512]{3,2,1,0:T(8,128)S(1)}, f32[16,16,512]{2,1,0:T(8,128)S(1)}, f32[16,16,512]{2,1,0:T(8,128)S(1)}, f32[96,512]{1,0:T(8,128)S(1)}) custom-call(bf16[16,16,256]{2,1,0:T(8,128)(2,1)S(1)} %get-tuple-element.69.first, bf16[16,16,256]{2,1,0:T(8,128)(2,1)S(1)} %get-tuple-element.72.second, ...), custom_call_target="tpu_custom_call" | custom-call | tf_op jit(solution)/shard_map/inner_pairs/pallas_call | solution.py:503
  37.9 0.0 copy-start.2
  37.9 0.0 copy-start.3
  37.9 2.1 %cross_pairs.1.cross_in = f32[416,512]{1,0:T(8,128)S(1)} custom-call(f32[4,32,16,512]{3,2,1,0:T(8,128)S(1)} %get-tuple-element.78.spec, f32[16,16,512]{2,1,0:T(8,128)S(1)} %get-tuple-element.79.spec_near, f32[16,16,512]{2,1,0:T(8,128)S(1)} %get-tuple-element.80.spec_far, f32[96,512]{1,0:T(8,128)S(1)} %get-tuple-element.81.inner, ...), custom_call_target="tpu_custom_call" | custom-call | tf_op jit(solution)/shard_map/cross_pairs/pallas_call | solution.py:511
  40.1 0.1 collective-permute-done.11.far_3
  40.1 1.9 %pair_lags.1 = (bf16[208,416]{1,0:T(8,128)(2,1)S(1)}, bf16[208,256]{1,0:T(8,128)(2,1)S(1)}, bf16[208,256]{1,0:T(8,128)(2,1)S(1)}) custom-call(f32[4,32,16,512]{3,2,1,0:T(8,128)S(1)} %get-tuple-element.78.spec, f32[416,512]{1,0:T(8,128)S(1)} %cross_pairs.1.cross_in, bf16[16,16,256]{2,1,0:T(8,128)(2,1)S(1)} %collective-permute-done.10.near_3, ...), custom_call_target="tpu_custom_call" | custom-call | tf_op jit(solution)/shard_map/pair_lags/pallas_call | solution.py:520
  42.0 0.0 copy-start.4
  42.0 0.1 collective-permute-start.12
  42.1 3.4 %collective-permute-start.13 = (bf16[208,256]{1,0:T(8,128)(2,1)S(1)}, bf16[208,256]{1,0:T(8,128)(2,1)S(1)}, u32[]{:S(2)}, u32[]{:S(2)}) collective-permute-start(bf16[208,256]{1,0:T(8,128)(2,1)S(1)} %get-tuple-element.84), channel_id=1, source_target_pairs={{8,16},{16,8},{10,18},{18,10},{12,20},{20,12},{14,22},{22,14},{9,1... | collective-permute-start | bytes 319496 | tf_op jit(solution)/shard_map/ppermute | solution.py:430
  45.5 0.1 collective-permute-start.14
  45.6 1.2 %collective-permute-done.12.refs_1_ = bf16[208,256]{1,0:T(8,128)(2,1)S(1)} collective-permute-done((bf16[208,256]{1,0:T(8,128)(2,1)S(1)}, bf16[208,256]{1,0:T(8,128)(2,1)S(1)}, u32[]{:S(2)}, u32[]{:S(2)}) %collective-permute-start.12) | collective-permute-done | bytes 106528 | tf_op jit(solution)/shard_map/ppermute | solution.py:430
  46.8 1.9 %collective-permute-done.13.refs_2_ = bf16[208,256]{1,0:T(8,128)(2,1)S(1)} collective-permute-done((bf16[208,256]{1,0:T(8,128)(2,1)S(1)}, bf16[208,256]{1,0:T(8,128)(2,1)S(1)}, u32[]{:S(2)}, u32[]{:S(2)}) %collective-permute-start.13) | collective-permute-done | bytes 106528 | tf_op jit(solution)/shard_map/ppermute | solution.py:430
  48.7 0.3 choose.1.chosen
  49.1 0.9 %collective-permute-done.16.refs_5_ = bf16[208,256]{1,0:T(8,128)(2,1)S(1)} collective-permute-done((bf16[208,256]{1,0:T(8,128)(2,1)S(1)}, bf16[208,256]{1,0:T(8,128)(2,1)S(1)}, u32[]{:S(2)}, u32[]{:S(2)}) %collective-permute-start.16) | collective-permute-done | bytes 106528 | tf_op jit(solution)/shard_map/ppermute | solution.py:419
  50.0 0.6 select_slots.1
  50.7 0.4 collective-permute-start.17
  51.1 3.4 %collective-permute-start.18 = (bf16[2,208,128]{2,1,0:T(8,128)(2,1)S(1)}, bf16[2,208,128]{2,1,0:T(8,128)(2,1)S(1)}, u32[]{:S(2)}, u32[]{:S(2)}) collective-permute-start(bf16[2,208,128]{2,1,0:T(8,128)(2,1)S(1)} %get-tuple-element.87), channel_id=1, source_target_pairs={{0,4},{2,6},{4,0},{6,2},{8,12},{10,14},{12,8},{14,10},{16,20},{18,... | collective-permute-start | bytes 319496 | tf_op jit(solution)/shard_map/ppermute | solution.py:422
  55.2 0.6 collective-permute-done.17.refs_1_
  55.7 3.3 %collective-permute-done.18.refs_2_ = bf16[2,208,128]{2,1,0:T(8,128)(2,1)S(1)} collective-permute-done((bf16[2,208,128]{2,1,0:T(8,128)(2,1)S(1)}, bf16[2,208,128]{2,1,0:T(8,128)(2,1)S(1)}, u32[]{:S(2)}, u32[]{:S(2)}) %collective-permute-start.18) | collective-permute-done | bytes 106528 | tf_op jit(solution)/shard_map/ppermute | solution.py:422
  59.1 1.1 %collective-permute-done.19.refs_3_ = bf16[2,208,128]{2,1,0:T(8,128)(2,1)S(1)} collective-permute-done((bf16[2,208,128]{2,1,0:T(8,128)(2,1)S(1)}, bf16[2,208,128]{2,1,0:T(8,128)(2,1)S(1)}, u32[]{:S(2)}, u32[]{:S(2)}) %collective-permute-start.19) | collective-permute-done | bytes 106528 | tf_op jit(solution)/shard_map/ppermute | solution.py:422
  60.1 3.2 %finish_slots.1 = f32[201,8,128]{2,1,0:T(8,128)} custom-call(s32[2,16]{1,0:T(2,128)S(1)} %bitcast.16, s32[1]{0:T(128)S(6)} %copy.11.count, bf16[2,208,128]{2,1,0:T(8,128)(2,1)S(1)} %get-tuple-element.85.refs_0_, bf16[2,208,128]{2,1,0:T(8,128)(2,1)S(1)} %collective-permute-done.17.refs_1_, bf16[2,208,128]{2,1,0:T(8,128)(2,1)S(1)} %collective-permute-done.18.refs_2_, ...), custom_call_target="tpu_custom_call" | custom-call | tf_op jit(solution)/shard_map/finish_slots/pallas_call | solution.py:556
  (23 shorter events, 0.2 us)
Async XLA Ops:
  1.0 2.4 %collective-permute-start = (f32[2,4096]{1,0:T(2,128)S(1)}, f32[2,4096]{1,0:T(2,128)S(1)}, u32[]{:S(2)}, u32[]{:S(2)}) collective-permute-start(f32[2,4096]{1,0:T(2,128)S(1)} %get-tuple-element.48), channel_id=1, source_target_pairs={{0,1},{1,0},{2,3},{3,2},{4,5},{5,4},{6,7},{7,6},{8,9},{9,8},{10,11... | collective-permute-start | bytes 98312 | tf_op jit(solution)/shard_map/ppermute | solution.py:419
  3.5 8.0 %collective-permute-start.1 = (f32[128,4096]{1,0:T(8,128)}, f32[128,4096]{1,0:T(8,128)S(1)}, u32[]{:S(2)}, u32[]{:S(2)}) collective-permute-start(f32[128,4096]{1,0:T(8,128)} %traces), channel_id=1, source_target_pairs={{0,1},{1,0},{2,3},{3,2},{4,5},{5,4},{6,7},{7,6},{8,9},{9,8},{10,11... | collective-permute-start | bytes 6291464 | tf_op jit(solution)/shard_map/ppermute | solution.py:419
  4.0 7.4 %collective-permute-start.2 = (f32[4,4096]{1,0:T(4,128)S(1)}, f32[4,4096]{1,0:T(4,128)S(1)}, u32[]{:S(2)}, u32[]{:S(2)}) collective-permute-start(f32[4,4096]{1,0:T(4,128)S(1)} %pad_maximum_fusion.2), channel_id=1, source_target_pairs={{1,2},{2,1},{3,4},{4,3},{5,6},{6,5},{7,8},{8,7},{9,10},{10,9},{11,... | collective-permute-start | bytes 196616 | tf_op jit(solution)/shard_map/ppermute | solution.py:452
  7.9 1.6 %copy-start.1 = (f32[128,4096]{1,0:T(8,128)S(1)}, f32[128,4096]{1,0:T(8,128)}, u32[]{:S(2)}) copy-start(f32[128,4096]{1,0:T(8,128)} %traces) | copy-start | bytes 6291460
  16.1 19.9 %copy-start = (bf16[256,512]{1,0:T(8,128)(2,1)S(1)}, bf16[256,512]{1,0:T(8,128)(2,1)}, u32[]{:S(2)}) copy-start(bf16[256,512]{1,0:T(8,128)(2,1)} %constant.52.clone.table) | copy-start | bytes 786436
  16.1 10.2 %collective-permute-start.3 = (bf16[33,16,256]{2,1,0:T(8,128)(2,1)S(1)}, bf16[33,16,256]{2,1,0:T(8,128)(2,1)S(1)}, u32[]{:S(2)}, u32[]{:S(2)}) collective-permute-start(bf16[33,16,256]{2,1,0:T(8,128)(2,1)S(1)} %get-tuple-element.67), channel_id=1, source_target_pairs={{0,2},{2,0},{4,6},{6,4},{8,10},{10,8},{12,14},{14,12},{16,18},{18,... | collective-permute-start | bytes 811016 | tf_op jit(solution)/shard_map/ppermute | solution.py:422
  16.2 10.1 %collective-permute-start.4 = (bf16[33,16,256]{2,1,0:T(8,128)(2,1)S(1)}, bf16[33,16,256]{2,1,0:T(8,128)(2,1)S(1)}, u32[]{:S(2)}, u32[]{:S(2)}) collective-permute-start(bf16[33,16,256]{2,1,0:T(8,128)(2,1)S(1)} %get-tuple-element.68), channel_id=1, source_target_pairs={{0,4},{2,6},{4,0},{6,2},{8,12},{10,14},{12,8},{14,10},{16,20},{18,... | collective-permute-start | bytes 811016 | tf_op jit(solution)/shard_map/ppermute | solution.py:422
  17.9 6.1 %collective-permute-start.5 = (bf16[16,16,256]{2,1,0:T(8,128)(2,1)S(1)}, bf16[16,16,256]{2,1,0:T(8,128)(2,1)S(1)}, u32[]{:S(2)}, u32[]{:S(2)}) collective-permute-start(bf16[16,16,256]{2,1,0:T(8,128)(2,1)S(1)} %get-tuple-element.69.first), channel_id=1, source_target_pairs={{0,8},{8,0},{2,10},{10,2},{4,12},{12,4},{6,14},{14,6},{16,24},{24,... | collective-permute-start | bytes 393224 | tf_op jit(solution)/shard_map/ppermute | solution.py:430
  19.5 6.8 %collective-permute-start.6 = (bf16[16,16,256]{2,1,0:T(8,128)(2,1)S(1)}, bf16[16,16,256]{2,1,0:T(8,128)(2,1)S(1)}, u32[]{:S(2)}, u32[]{:S(2)}) collective-permute-start(bf16[16,16,256]{2,1,0:T(8,128)(2,1)S(1)} %get-tuple-element.72.second), channel_id=1, source_target_pairs={{8,16},{16,8},{10,18},{18,10},{12,20},{20,12},{14,22},{22,14},{9,1... | collective-permute-start | bytes 393224 | tf_op jit(solution)/shard_map/ppermute | solution.py:430
  24.0 9.2 %collective-permute-start.7 = (bf16[33,16,256]{2,1,0:T(8,128)(2,1)S(1)}, bf16[33,16,256]{2,1,0:T(8,128)(2,1)S(1)}, u32[]{:S(2)}, u32[]{:S(2)}) collective-permute-start(bf16[33,16,256]{2,1,0:T(8,128)(2,1)S(1)} %get-tuple-element.75), channel_id=1, source_target_pairs={{0,6},{2,4},{4,2},{6,0},{8,14},{10,12},{12,10},{14,8},{16,22},{18,... | collective-permute-start | bytes 811016 | tf_op jit(solution)/shard_map/ppermute | solution.py:422
  26.4 11.5 %collective-permute-start.9 = (bf16[2,16,16,256]{3,2,1,0:T(8,128)(2,1)S(1)}, bf16[2,16,16,256]{3,2,1,0:T(8,128)(2,1)S(1)}, u32[]{:S(2)}, u32[]{:S(2)}) collective-permute-start(bf16[2,16,16,256]{3,2,1,0:T(8,128)(2,1)S(1)} %pad_maximum_fusion.1), channel_id=1, source_target_pairs={{8,16},{16,8},{10,18},{18,10},{12,20},{20,12},{14,22},{22,14},{9,1... | collective-permute-start | bytes 786440 | tf_op jit(solution)/shard_map/ppermute | solution.py:430
  28.6 9.3 %collective-permute-start.8 = (bf16[2,16,16,256]{3,2,1,0:T(8,128)(2,1)S(1)}, bf16[2,16,16,256]{3,2,1,0:T(8,128)(2,1)S(1)}, u32[]{:S(2)}, u32[]{:S(2)}) collective-permute-start(bf16[2,16,16,256]{3,2,1,0:T(8,128)(2,1)S(1)} %pad_maximum_fusion), channel_id=1, source_target_pairs={{0,8},{8,0},{2,10},{10,2},{4,12},{12,4},{6,14},{14,6},{16,24},{24,... | collective-permute-start | bytes 786440 | tf_op jit(solution)/shard_map/ppermute | solution.py:430
  33.2 6.9 %collective-permute-start.10 = (bf16[16,16,256]{2,1,0:T(8,128)(2,1)S(1)}, bf16[16,16,256]{2,1,0:T(8,128)(2,1)S(1)}, u32[]{:S(2)}, u32[]{:S(2)}) collective-permute-start(bf16[16,16,256]{2,1,0:T(8,128)(2,1)S(1)} %get-tuple-element.92), channel_id=1, source_target_pairs={{0,8},{8,0},{2,10},{10,2},{4,12},{12,4},{6,14},{14,6},{16,24},{24,... | collective-permute-start | bytes 393224 | tf_op jit(solution)/shard_map/ppermute | solution.py:430
  33.3 6.9 %collective-permute-start.11 = (bf16[16,16,256]{2,1,0:T(8,128)(2,1)S(1)}, bf16[16,16,256]{2,1,0:T(8,128)(2,1)S(1)}, u32[]{:S(2)}, u32[]{:S(2)}) collective-permute-start(bf16[16,16,256]{2,1,0:T(8,128)(2,1)S(1)} %get-tuple-element.91), channel_id=1, source_target_pairs={{8,16},{16,8},{10,18},{18,10},{12,20},{20,12},{14,22},{22,14},{9,1... | collective-permute-start | bytes 393224 | tf_op jit(solution)/shard_map/ppermute | solution.py:430
  37.9 2.2 %copy-start.2 = (bf16[208,512]{1,0:T(8,128)(2,1)S(1)}, bf16[208,512]{1,0:T(8,128)(2,1)}, u32[]{:S(2)}) copy-start(bf16[208,512]{1,0:T(8,128)(2,1)} %constant.53.clone.l_high) | copy-start | bytes 638980
  37.9 2.2 %copy-start.3 = (bf16[208,512]{1,0:T(8,128)(2,1)S(1)}, bf16[208,512]{1,0:T(8,128)(2,1)}, u32[]{:S(2)}) copy-start(bf16[208,512]{1,0:T(8,128)(2,1)} %constant.54.clone.l_low) | copy-start | bytes 638980
  42.0 18.1 %copy-start.4 = (bf16[208,208]{1,0:T(8,128)(2,1)S(1)}, bf16[208,208]{1,0:T(8,128)(2,1)}, u32[]{:S(2)}) copy-start(bf16[208,208]{1,0:T(8,128)(2,1)} %constant.55.clone.refs_4_) | copy-start | bytes 259588
  42.0 18.1 %copy-start.5 = (s32[16,2]{0,1:T(2,128)S(1)}, s32[16,2]{0,1:T(2,128)}, u32[]{:S(2)}) copy-start(s32[16,2]{0,1:T(2,128)} %param.14) | copy-start | bytes 388
  42.0 4.8 %collective-permute-start.12 = (bf16[208,256]{1,0:T(8,128)(2,1)S(1)}, bf16[208,256]{1,0:T(8,128)(2,1)S(1)}, u32[]{:S(2)}, u32[]{:S(2)}) collective-permute-start(bf16[208,256]{1,0:T(8,128)(2,1)S(1)} %get-tuple-element.83), channel_id=1, source_target_pairs={{0,8},{8,0},{2,10},{10,2},{4,12},{12,4},{6,14},{14,6},{16,24},{24,... | collective-permute-start | bytes 319496 | tf_op jit(solution)/shard_map/ppermute | solution.py:430
  42.1 6.6 %collective-permute-start.13 = (bf16[208,256]{1,0:T(8,128)(2,1)S(1)}, bf16[208,256]{1,0:T(8,128)(2,1)S(1)}, u32[]{:S(2)}, u32[]{:S(2)}) collective-permute-start(bf16[208,256]{1,0:T(8,128)(2,1)S(1)} %get-tuple-element.84), channel_id=1, source_target_pairs={{8,16},{16,8},{10,18},{18,10},{12,20},{20,12},{14,22},{22,14},{9,1... | collective-permute-start | bytes 319496 | tf_op jit(solution)/shard_map/ppermute | solution.py:430
  45.5 3.6 %collective-permute-start.14 = (bf16[208,416]{1,0:T(8,128)(2,1)S(1)}, bf16[208,416]{1,0:T(8,128)(2,1)S(1)}, u32[]{:S(2)}, u32[]{:S(2)}) collective-permute-start(bf16[208,416]{1,0:T(8,128)(2,1)S(1)} %get-tuple-element.82.refs_0_), channel_id=1, source_target_pairs={{0,1},{1,0},{2,3},{3,2},{4,5},{5,4},{6,7},{7,6},{8,9},{9,8},{10,11... | collective-permute-start | bytes 519176 | tf_op jit(solution)/shard_map/ppermute | solution.py:419
  46.8 2.3 %collective-permute-start.15 = (bf16[208,256]{1,0:T(8,128)(2,1)S(1)}, bf16[208,256]{1,0:T(8,128)(2,1)S(1)}, u32[]{:S(2)}, u32[]{:S(2)}) collective-permute-start(bf16[208,256]{1,0:T(8,128)(2,1)S(1)} %collective-permute-done.12.refs_1_), channel_id=1, source_target_pairs={{0,1},{1,0},{2,3},{3,2},{4,5},{5,4},{6,7},{7,6},{8,9},{9,8},{10,11... | collective-permute-start | bytes 319496 | tf_op jit(solution)/shard_map/ppermute | solution.py:419
  48.7 1.3 %collective-permute-start.16 = (bf16[208,256]{1,0:T(8,128)(2,1)S(1)}, bf16[208,256]{1,0:T(8,128)(2,1)S(1)}, u32[]{:S(2)}, u32[]{:S(2)}) collective-permute-start(bf16[208,256]{1,0:T(8,128)(2,1)S(1)} %collective-permute-done.13.refs_2_), channel_id=1, source_target_pairs={{0,1},{1,0},{2,3},{3,2},{4,5},{5,4},{6,7},{7,6},{8,9},{9,8},{10,11... | collective-permute-start | bytes 319496 | tf_op jit(solution)/shard_map/ppermute | solution.py:419
  50.7 5.1 %collective-permute-start.17 = (bf16[2,208,128]{2,1,0:T(8,128)(2,1)S(1)}, bf16[2,208,128]{2,1,0:T(8,128)(2,1)S(1)}, u32[]{:S(2)}, u32[]{:S(2)}) collective-permute-start(bf16[2,208,128]{2,1,0:T(8,128)(2,1)S(1)} %get-tuple-element.86), channel_id=1, source_target_pairs={{0,2},{2,0},{4,6},{6,4},{8,10},{10,8},{12,14},{14,12},{16,18},{18,... | collective-permute-start | bytes 319496 | tf_op jit(solution)/shard_map/ppermute | solution.py:422
  51.1 8.0 %collective-permute-start.18 = (bf16[2,208,128]{2,1,0:T(8,128)(2,1)S(1)}, bf16[2,208,128]{2,1,0:T(8,128)(2,1)S(1)}, u32[]{:S(2)}, u32[]{:S(2)}) collective-permute-start(bf16[2,208,128]{2,1,0:T(8,128)(2,1)S(1)} %get-tuple-element.87), channel_id=1, source_target_pairs={{0,4},{2,6},{4,0},{6,2},{8,12},{10,14},{12,8},{14,10},{16,20},{18,... | collective-permute-start | bytes 319496 | tf_op jit(solution)/shard_map/ppermute | solution.py:422
  54.5 5.6 %collective-permute-start.19 = (bf16[2,208,128]{2,1,0:T(8,128)(2,1)S(1)}, bf16[2,208,128]{2,1,0:T(8,128)(2,1)S(1)}, u32[]{:S(2)}, u32[]{:S(2)}) collective-permute-start(bf16[2,208,128]{2,1,0:T(8,128)(2,1)S(1)} %get-tuple-element.88), channel_id=1, source_target_pairs={{0,6},{2,4},{4,2},{6,0},{8,14},{10,12},{12,10},{14,8},{16,22},{18,... | collective-permute-start | bytes 319496 | tf_op jit(solution)/shard_map/ppermute | solution.py:422

commit v6 on v5

--- a/solution.py
+++ b/solution.py
@@ -109,7 +109,7 @@
 
 
 def prepare_kernel(
-    small, whole, whole_rows, traces, t_high, t_low, pid, space, ok, own_high, own_low, own_near,
+    small, whole, whole_rows, traces, t_high, t_low, pid, space, ok, flags, own_high, own_low, own_near,
 ):
     _, core, _ = my_place()
     plane = lax.axis_index("chan") // PLANE
@@ -141,6 +141,12 @@
         one, two = pair_ids(whole[0, s], whole[1, s], plane)
         ids = jnp.where(slot == s, jnp.where(upper, one, two), ids)
     pid[...] = ids.astype(F32).astype(BF16)
+    row = lax.broadcasted_iota(jnp.int32, flags.shape, 0)
+    value = jnp.zeros(flags.shape, F32)
+    for s in range(SLOTS // 2):
+        slot = core * (SLOTS // 2) + s
+        value = jnp.where(row == s, (whole[0, slot] > whole[1, slot]).astype(F32), value)
+    flags[...] = value
     width = ok.shape[0]
     diagonal = lax.broadcasted_iota(jnp.int32, (width, width), 0) == lax.broadcasted_iota(
         jnp.int32, (width, width), 1
@@ -369,8 +375,8 @@
             outs[rel][side] = picked[side * LAG_ROWS : (side + 1) * LAG_ROWS, rel * 128 : (rel + 1) * 128]
 
 
-def finish_kernel(pairs, count, *refs):
-    pieces, table, out, stage, flat = refs[:4], *refs[4:8]
+def finish_kernel(count, flags, *refs):
+    pieces, table, out, stage, flat, done, sems = refs[:4], *refs[4:10]
     member, core, _ = my_place()
     for rel in range(4):
         for side in range(2):
@@ -388,12 +394,20 @@
                     tiles[m | bit] = jnp.where(upper, high, pltpu.roll(low, 128 - bit * QG, 1))
         for s in range(8):
             flat[row : row + step, s * 128 : (s + 1) * 128] = tiles[s]
-    back = mxu(table[...], flat[...].astype(BF16))
-    for s in range(SLOTS // 2):
-        lanes = slice(s * 128, (s + 1) * 128)
-        slot = core * (SLOTS // 2) + s
-        value = jnp.where(pairs[0, slot] > pairs[1, slot], back[:, lanes], flat[:, lanes])
-        out[:, s, :] = jnp.where(slot < count[0], value, 0.0)[0:LAGS]
+    flat_low = flat[...].astype(BF16)
+    copies = []
+    for k, (start, stop) in enumerate(((0, 64), (64, 128), (128, LAGS))):
+        end = min(start + 80, LAG_ROWS) if stop == LAGS else stop
+        back = mxu(table[start:end, :], flat_low)
+        for s in range(SLOTS // 2):
+            lanes = slice(s * 128, (s + 1) * 128)
+            turned, alive = flags[s : s + 1, :] > 0.0, core * (SLOTS // 2) + s < count[0]
+            value = jnp.where(turned, back[:, lanes], flat[start:end, lanes])
+            done[start:stop, s, :] = jnp.where(alive, value, 0.0)[0 : stop - start]
+        copies.append(pltpu.make_async_copy(done.at[start:stop], out.at[start:stop], sems.at[k]))
+        copies[-1].start()
+    for copy in copies:
+        copy.wait()
 
 
 VM = pl.BlockSpec(memory_space=pltpu.VMEM)
@@ -453,14 +467,14 @@
     other = to_core(late)
     table = shape((2 * SEG, SEG), BF16)
     split = shape((rows, half), BF16)
-    t_high, t_low, pid, space, ok, own_high, own_low, own_near = pl.pallas_call(
+    t_high, t_low, pid, space, ok, flags, own_high, own_low, own_near = pl.pallas_call(
         prepare_kernel,
         out_shape=[
             table, table, shape((QG, SLOTS * QG), BF16), shape((8, SEG), F32), shape((chan_width, 128), F32),
-            split, split, shape((8, half), F32),
+            shape((8, 128), F32), split, split, shape((8, half), F32),
         ],
         in_specs=[SM, SM, VM, VM],
-        out_specs=[VM] * 8,
+        out_specs=[VM] * 9,
         compiler_params=PARAMS,
         name="prepare",
     )(small, whole, whole, late)
@@ -556,15 +570,17 @@
     out = pl.pallas_call(
         finish_kernel,
         out_shape=shape((LAGS, SLOTS // 2, chan_width), F32),
-        in_specs=[SM] * 2 + [VM] * 5,
-        out_specs=VM,
+        in_specs=[SM] + [VM] * 6,
+        out_specs=pl.BlockSpec(memory_space=pl.ANY),
         scratch_shapes=[
             pltpu.VMEM((8, LAG_ROWS, 128), F32),
             pltpu.VMEM((LAG_ROWS, SLOTS // 2 * 128), F32),
+            pltpu.VMEM((LAGS, SLOTS // 2, 128), F32),
+            pltpu.SemaphoreType.DMA((3,)),
         ],
         compiler_params=PARAMS,
         name="finish_slots",
-    )(pairs, pair_count, *pieces, jnp.asarray(reverse_np()))
+    )(pair_count, flags, *pieces, jnp.asarray(reverse_np()))
     return jnp.transpose(out, (1, 0, 2))
 
 

time: 63.6 us -> 63.1 us (level)
  Pallas kernels: 16.2 us -> 15.5 us
    pallas_call x1, Pallas kernels: 3.19 us -> 2.44 us  [local(): pl.pallas_call(finish_kernel, out_shape=shape((LAGS, SLOTS // 2, chan_wid...]
    unnamed x12 -> x10, local copies, waits for them, and re-layouts: 1.62 us -> 1.61 us
  transfers between devices with their start and end apart: 20 -> 20, of which waited for: 11 -> 10; matrix products, arithmetic and copies ran while one was open for 4% -> 4% of each run, Pallas kernels for 9% -> 9%
where the time goes in v6:
time: 63.1 us; the launch traced here: 62.8 us
  starting transfers between devices  22.9 us (36%)
  waiting for transfers between devices  18.2 us (29%)
  Pallas kernels  15.5 us (25%)
  other arithmetic  3.44 us (5%)
  local copies, waits for them, and re-layouts  1.67 us (3%)
  between operations  1.14 us (2%)
    ppermute x8, starting transfers between devices, plane_swap(): return lax.ppermute(x, 'chan', route)  12 us
    ppermute x6, waiting for transfers between devices, in_plane(): return lax.ppermute(x, 'chan', [(c, c ^ rel) for c in range(n_chan)])  9.49 us
    ppermute x8, waiting for transfers between devices, plane_swap(): return lax.ppermute(x, 'chan', route)  7.42 us
    ppermute x6, starting transfers between devices, in_plane(): return lax.ppermute(x, 'chan', [(c, c ^ rel) for c in range(n_chan)])  6.32 us
    pallas_call x1, Pallas kernels, local(): pl.pallas_call(filter_kernel, out_shape=[short] * 2 + [block] * 3, in_spe...  4.64 us
    ppermute x1, starting transfers between devices, local(): halos = lax.ppermute(edges, BOTH, route)  3.86 us
    pallas_call x1, Pallas kernels, local(): pl.pallas_call(finish_kernel, out_shape=shape((LAGS, SLOTS // 2, chan_wid...  2.44 us
    pallas_call x1, Pallas kernels, local(): pl.pallas_call(cross_kernel, out_shape=shape((N_OWN * QG, 2 * SEG), F32),...  2.12 us
  transfers between devices with their start and end apart: 20, of which 10 were waited for; matrix products, arithmetic and copies ran while one was open for 4% of the time, Pallas kernels for 9%

profile of v6, /device:TPU:16, one launch (start us, length us, event | category | flops | bytes accessed | tf_op | source)
XLA Modules:
  0.0 62.8 jit_solution(6341441564370966897)
XLA Ops:
  0.0 1.0 %broadcast_select_fusion.2 = (f32[2,4096]{1,0:T(2,128)S(1)}, f32[2,4096]{1,0:T(2,128)S(1)}) fusion(pred[]{:T(512)S(6)} %eq.4, f32[128,4096]{1,0:T(8,128)} %traces), kind=kLoop, calls=%fused_computation.9 | loop fusion | flops 16384 | bytes 131073 | tf_op jit(solution)/shard_map/jit(_where)/select_n | solution.py:449
  1.0 0.1 collective-permute-start
  1.1 0.8 %fusion = pred[2]{0:T(512)(128)(4,1)S(1)} fusion(pred[]{:T(512)S(6)} %eq.4, s32[128]{0:T(128)} %param.11), kind=kLoop, calls=%fused_computation.16 | loop fusion | flops 4 | bytes 19 | tf_op jit(solution)/shard_map/gt | solution.py:454
  1.9 0.1 broadcast_select_fusion.1
  2.0 0.7 %pad_add_fusion.whole.whole_rows = s32[8,128]{1,0:T(8,128)S(1)} fusion(s32[1,128]{1,0:T(1,128)} %bitcast.15, s32[2,16]{1,0:T(2,128)} %bitcast.16), kind=kLoop, calls=%fused_computation.11 | loop fusion | flops 1024 | bytes 4736 | tf_op jit(solution)/shard_map/add | solution.py:459
  2.7 0.7 %pad_add_fusion.1.small = f32[8,128]{1,0:T(8,128)S(1)} fusion(f32[1,5]{1,0:T(1,128)} %bitcast.17, f32[1,33]{1,0:T(1,128)} %bitcast.18), kind=kLoop, calls=%fused_computation.12 | loop fusion | flops 1024 | bytes 4248 | tf_op jit(solution)/shard_map/add | solution.py:457
  3.4 0.1 broadcast_select_fusion
  3.5 0.6 collective-permute-start.1
  4.0 3.9 %collective-permute-start.2 = (f32[4,4096]{1,0:T(4,128)S(1)}, f32[4,4096]{1,0:T(4,128)S(1)}, u32[]{:S(2)}, u32[]{:S(2)}) collective-permute-start(f32[4,4096]{1,0:T(4,128)S(1)} %pad_maximum_fusion.2), channel_id=1, source_target_pairs={{1,2},{2,1},{3,4},{4,3},{5,6},{6,5},{7,8},{8,7},{9,10},{10,9},{11,... | collective-permute-start | bytes 196616 | tf_op jit(solution)/shard_map/ppermute | solution.py:466
  7.9 0.0 copy-start.1
  7.9 1.6 %copy-done.1 = f32[128,4096]{1,0:T(8,128)S(1)} copy-done((f32[128,4096]{1,0:T(8,128)S(1)}, f32[128,4096]{1,0:T(8,128)}, u32[]{:S(2)}) %copy-start.1) | copy-done | bytes 2097176
  9.5 1.7 %prepare.1 = (bf16[512,256]{1,0:T(8,128)(2,1)S(1)}, bf16[512,256]{1,0:T(8,128)(2,1)S(1)}, bf16[16,256]{1,0:T(8,128)(2,1)S(1)}, f32[8,256]{1,0:T(8,128)S(1)}, f32...) custom-call(f32[8,128]{1,0:T(8,128)S(1)} %pad_add_fusion.1.small, ...), custom_call_target="tpu_custom_call" | custom-call | tf_op jit(solution)/shard_map/prepare/pallas_call | solution.py:470
  11.2 0.3 collective-permute-done.2.halos
  11.5 4.6 %filter_whiten.1 = (bf16[16,16,256]{2,1,0:T(8,128)(2,1)S(1)}, bf16[16,16,256]{2,1,0:T(8,128)(2,1)S(1)}, bf16[33,16,256]{2,1,0:T(8,128)(2,1)S(1)}, bf16[33,16,256...) custom-call(f32[8,4096]{1,0:T(8,128)S(1)} %get-tuple-element.61.own_near, bf16[64,4096]{1,0:T(8,128)(2,1)S(1)} %get-tuple-element.62.own_high, ...), custom_call_target="tpu_custom_call" | custom-call | tf_op jit(solution)/shard_map/filter_whiten/pallas_call | solution.py:483
  16.1 0.0 copy-start
  16.1 0.1 collective-permute-start.3
  16.2 1.7 %collective-permute-start.4 = (bf16[33,16,256]{2,1,0:T(8,128)(2,1)S(1)}, bf16[33,16,256]{2,1,0:T(8,128)(2,1)S(1)}, u32[]{:S(2)}, u32[]{:S(2)}) collective-permute-start(bf16[33,16,256]{2,1,0:T(8,128)(2,1)S(1)} %get-tuple-element.70), channel_id=1, source_target_pairs={{0,4},{2,6},{4,0},{6,2},{8,12},{10,14},{12,8},{14,10},{16,20},{18,... | collective-permute-start | bytes 811016 | tf_op jit(solution)/shard_map/ppermute | solution.py:436
  17.9 1.6 %collective-permute-start.5 = (bf16[16,16,256]{2,1,0:T(8,128)(2,1)S(1)}, bf16[16,16,256]{2,1,0:T(8,128)(2,1)S(1)}, u32[]{:S(2)}, u32[]{:S(2)}) collective-permute-start(bf16[16,16,256]{2,1,0:T(8,128)(2,1)S(1)} %get-tuple-element.71.first), channel_id=1, source_target_pairs={{0,8},{8,0},{2,10},{10,2},{4,12},{12,4},{6,14},{14,6},{16,24},{24,... | collective-permute-start | bytes 393224 | tf_op jit(solution)/shard_map/ppermute | solution.py:444
  19.5 1.9 %collective-permute-start.6 = (bf16[16,16,256]{2,1,0:T(8,128)(2,1)S(1)}, bf16[16,16,256]{2,1,0:T(8,128)(2,1)S(1)}, u32[]{:S(2)}, u32[]{:S(2)}) collective-permute-start(bf16[16,16,256]{2,1,0:T(8,128)(2,1)S(1)} %get-tuple-element.74.second), channel_id=1, source_target_pairs={{8,16},{16,8},{10,18},{18,10},{12,20},{20,12},{14,22},{22,14},{9,1... | collective-permute-start | bytes 393224 | tf_op jit(solution)/shard_map/ppermute | solution.py:444
  21.4 2.6 %collective-permute-done.5.near_0 = bf16[16,16,256]{2,1,0:T(8,128)(2,1)S(1)} collective-permute-done((bf16[16,16,256]{2,1,0:T(8,128)(2,1)S(1)}, bf16[16,16,256]{2,1,0:T(8,128)(2,1)S(1)}, u32[]{:S(2)}, u32[]{:S(2)}) %collective-permute-start.5) | collective-permute-done | bytes 131104 | tf_op jit(solution)/shard_map/ppermute | solution.py:444
  24.0 0.6 %collective-permute-start.7 = (bf16[33,16,256]{2,1,0:T(8,128)(2,1)S(1)}, bf16[33,16,256]{2,1,0:T(8,128)(2,1)S(1)}, u32[]{:S(2)}, u32[]{:S(2)}) collective-permute-start(bf16[33,16,256]{2,1,0:T(8,128)(2,1)S(1)} %get-tuple-element.77), channel_id=1, source_target_pairs={{0,6},{2,4},{4,2},{6,0},{8,14},{10,12},{12,10},{14,8},{16,22},{18,... | collective-permute-start | bytes 811016 | tf_op jit(solution)/shard_map/ppermute | solution.py:436
  24.7 1.7 %collective-permute-done.6.far_0 = bf16[16,16,256]{2,1,0:T(8,128)(2,1)S(1)} collective-permute-done((bf16[16,16,256]{2,1,0:T(8,128)(2,1)S(1)}, bf16[16,16,256]{2,1,0:T(8,128)(2,1)S(1)}, u32[]{:S(2)}, u32[]{:S(2)}) %collective-permute-start.6) | collective-permute-done | bytes 131104 | tf_op jit(solution)/shard_map/ppermute | solution.py:444
  26.4 2.1 %collective-permute-start.9 = (bf16[2,16,16,256]{3,2,1,0:T(8,128)(2,1)S(1)}, bf16[2,16,16,256]{3,2,1,0:T(8,128)(2,1)S(1)}, u32[]{:S(2)}, u32[]{:S(2)}) collective-permute-start(bf16[2,16,16,256]{3,2,1,0:T(8,128)(2,1)S(1)} %pad_maximum_fusion.1), channel_id=1, source_target_pairs={{8,16},{16,8},{10,18},{18,10},{12,20},{20,12},{14,22},{22,14},{9,1... | collective-permute-start | bytes 786440 | tf_op jit(solution)/shard_map/ppermute | solution.py:444
  28.6 0.1 collective-permute-start.8
  28.6 4.5 %collective-permute-done.7.refs_3_.b3 = bf16[33,16,256]{2,1,0:T(8,128)(2,1)S(1)} collective-permute-done((bf16[33,16,256]{2,1,0:T(8,128)(2,1)S(1)}, bf16[33,16,256]{2,1,0:T(8,128)(2,1)S(1)}, u32[]{:S(2)}, u32[]{:S(2)}) %collective-permute-start.7) | collective-permute-done | bytes 270368 | tf_op jit(solution)/shard_map/ppermute | solution.py:436
  33.2 0.1 collective-permute-start.10
  33.3 2.8 %collective-permute-start.11 = (bf16[16,16,256]{2,1,0:T(8,128)(2,1)S(1)}, bf16[16,16,256]{2,1,0:T(8,128)(2,1)S(1)}, u32[]{:S(2)}, u32[]{:S(2)}) collective-permute-start(bf16[16,16,256]{2,1,0:T(8,128)(2,1)S(1)} %get-tuple-element.93), channel_id=1, source_target_pairs={{8,16},{16,8},{10,18},{18,10},{12,20},{20,12},{14,22},{22,14},{9,1... | collective-permute-start | bytes 393224 | tf_op jit(solution)/shard_map/ppermute | solution.py:444
  36.1 1.8 %inner_pairs.1 = (f32[4,32,16,512]{3,2,1,0:T(8,128)S(1)}, f32[16,16,512]{2,1,0:T(8,128)S(1)}, f32[16,16,512]{2,1,0:T(8,128)S(1)}, f32[96,512]{1,0:T(8,128)S(1)}) custom-call(bf16[16,16,256]{2,1,0:T(8,128)(2,1)S(1)} %get-tuple-element.71.first, bf16[16,16,256]{2,1,0:T(8,128)(2,1)S(1)} %get-tuple-element.74.second, ...), custom_call_target="tpu_custom_call" | custom-call | tf_op jit(solution)/shard_map/inner_pairs/pallas_call | solution.py:517
  37.9 0.0 copy-start.2
  37.9 0.0 copy-start.3
  38.0 2.1 %cross_pairs.1.cross_in = f32[416,512]{1,0:T(8,128)S(1)} custom-call(f32[4,32,16,512]{3,2,1,0:T(8,128)S(1)} %get-tuple-element.80.spec, f32[16,16,512]{2,1,0:T(8,128)S(1)} %get-tuple-element.81.spec_near, f32[16,16,512]{2,1,0:T(8,128)S(1)} %get-tuple-element.82.spec_far, f32[96,512]{1,0:T(8,128)S(1)} %get-tuple-element.83.inner, ...), custom_call_target="tpu_custom_call" | custom-call | tf_op jit(solution)/shard_map/cross_pairs/pallas_call | solution.py:525
  40.1 0.0 collective-permute-done.11.far_3
  40.1 1.9 %pair_lags.1 = (bf16[208,416]{1,0:T(8,128)(2,1)S(1)}, bf16[208,256]{1,0:T(8,128)(2,1)S(1)}, bf16[208,256]{1,0:T(8,128)(2,1)S(1)}) custom-call(f32[4,32,16,512]{3,2,1,0:T(8,128)S(1)} %get-tuple-element.80.spec, f32[416,512]{1,0:T(8,128)S(1)} %cross_pairs.1.cross_in, bf16[16,16,256]{2,1,0:T(8,128)(2,1)S(1)} %collective-permute-done.10.near_3, ...), custom_call_target="tpu_custom_call" | custom-call | tf_op jit(solution)/shard_map/pair_lags/pallas_call | solution.py:534
  42.0 0.0 copy-start.4
  42.0 0.1 collective-permute-start.12
  42.1 3.4 %collective-permute-start.13 = (bf16[208,256]{1,0:T(8,128)(2,1)S(1)}, bf16[208,256]{1,0:T(8,128)(2,1)S(1)}, u32[]{:S(2)}, u32[]{:S(2)}) collective-permute-start(bf16[208,256]{1,0:T(8,128)(2,1)S(1)} %get-tuple-element.86), channel_id=1, source_target_pairs={{8,16},{16,8},{10,18},{18,10},{12,20},{20,12},{14,22},{22,14},{9,1... | collective-permute-start | bytes 319496 | tf_op jit(solution)/shard_map/ppermute | solution.py:444
  45.5 0.1 collective-permute-start.14
  45.6 1.2 %collective-permute-done.12.refs_1_ = bf16[208,256]{1,0:T(8,128)(2,1)S(1)} collective-permute-done((bf16[208,256]{1,0:T(8,128)(2,1)S(1)}, bf16[208,256]{1,0:T(8,128)(2,1)S(1)}, u32[]{:S(2)}, u32[]{:S(2)}) %collective-permute-start.12) | collective-permute-done | bytes 106528 | tf_op jit(solution)/shard_map/ppermute | solution.py:444
  46.8 1.9 %collective-permute-done.13.refs_2_ = bf16[208,256]{1,0:T(8,128)(2,1)S(1)} collective-permute-done((bf16[208,256]{1,0:T(8,128)(2,1)S(1)}, bf16[208,256]{1,0:T(8,128)(2,1)S(1)}, u32[]{:S(2)}, u32[]{:S(2)}) %collective-permute-start.13) | collective-permute-done | bytes 106528 | tf_op jit(solution)/shard_map/ppermute | solution.py:444
  48.7 0.3 choose.1.chosen
  49.1 0.9 %collective-permute-done.16.refs_5_ = bf16[208,256]{1,0:T(8,128)(2,1)S(1)} collective-permute-done((bf16[208,256]{1,0:T(8,128)(2,1)S(1)}, bf16[208,256]{1,0:T(8,128)(2,1)S(1)}, u32[]{:S(2)}, u32[]{:S(2)}) %collective-permute-start.16) | collective-permute-done | bytes 106528 | tf_op jit(solution)/shard_map/ppermute | solution.py:433
  50.0 0.6 select_slots.1
  50.7 0.6 collective-permute-start.17
  51.2 3.4 %collective-permute-start.18 = (bf16[2,208,128]{2,1,0:T(8,128)(2,1)S(1)}, bf16[2,208,128]{2,1,0:T(8,128)(2,1)S(1)}, u32[]{:S(2)}, u32[]{:S(2)}) collective-permute-start(bf16[2,208,128]{2,1,0:T(8,128)(2,1)S(1)} %get-tuple-element.89), channel_id=1, source_target_pairs={{0,4},{2,6},{4,0},{6,2},{8,12},{10,14},{12,8},{14,10},{16,20},{18,... | collective-permute-start | bytes 319496 | tf_op jit(solution)/shard_map/ppermute | solution.py:436
  55.2 0.5 collective-permute-done.17.refs_1_
  55.7 3.4 %collective-permute-done.18.refs_2_ = bf16[2,208,128]{2,1,0:T(8,128)(2,1)S(1)} collective-permute-done((bf16[2,208,128]{2,1,0:T(8,128)(2,1)S(1)}, bf16[2,208,128]{2,1,0:T(8,128)(2,1)S(1)}, u32[]{:S(2)}, u32[]{:S(2)}) %collective-permute-start.18) | collective-permute-done | bytes 106528 | tf_op jit(solution)/shard_map/ppermute | solution.py:436
  59.1 1.1 %collective-permute-done.19.refs_3_ = bf16[2,208,128]{2,1,0:T(8,128)(2,1)S(1)} collective-permute-done((bf16[2,208,128]{2,1,0:T(8,128)(2,1)S(1)}, bf16[2,208,128]{2,1,0:T(8,128)(2,1)S(1)}, u32[]{:S(2)}, u32[]{:S(2)}) %collective-permute-start.19) | collective-permute-done | bytes 106528 | tf_op jit(solution)/shard_map/ppermute | solution.py:436
  60.2 2.4 %finish_slots.1 = f32[201,8,128]{2,1,0:T(8,128)} custom-call(s32[1]{0:T(128)S(6)} %copy.11.count, f32[8,128]{1,0:T(8,128)S(1)} %get-tuple-element.59.flags, bf16[2,208,128]{2,1,0:T(8,128)(2,1)S(1)} %get-tuple-element.87.refs_0_, bf16[2,208,128]{2,1,0:T(8,128)(2,1)S(1)} %collective-permute-done.17.refs_1_, ...), custom_call_target="tpu_custom_call" | custom-call | tf_op jit(solution)/shard_map/finish_slots/pallas_call | solution.py:570
  (21 shorter events, 0.2 us)
Async XLA Ops:
  1.0 2.4 %collective-permute-start = (f32[2,4096]{1,0:T(2,128)S(1)}, f32[2,4096]{1,0:T(2,128)S(1)}, u32[]{:S(2)}, u32[]{:S(2)}) collective-permute-start(f32[2,4096]{1,0:T(2,128)S(1)} %get-tuple-element.48), channel_id=1, source_target_pairs={{0,1},{1,0},{2,3},{3,2},{4,5},{5,4},{6,7},{7,6},{8,9},{9,8},{10,11... | collective-permute-start | bytes 98312 | tf_op jit(solution)/shard_map/ppermute | solution.py:433
  3.5 8.0 %collective-permute-start.1 = (f32[128,4096]{1,0:T(8,128)}, f32[128,4096]{1,0:T(8,128)S(1)}, u32[]{:S(2)}, u32[]{:S(2)}) collective-permute-start(f32[128,4096]{1,0:T(8,128)} %traces), channel_id=1, source_target_pairs={{0,1},{1,0},{2,3},{3,2},{4,5},{5,4},{6,7},{7,6},{8,9},{9,8},{10,11... | collective-permute-start | bytes 6291464 | tf_op jit(solution)/shard_map/ppermute | solution.py:433
  4.0 7.4 %collective-permute-start.2 = (f32[4,4096]{1,0:T(4,128)S(1)}, f32[4,4096]{1,0:T(4,128)S(1)}, u32[]{:S(2)}, u32[]{:S(2)}) collective-permute-start(f32[4,4096]{1,0:T(4,128)S(1)} %pad_maximum_fusion.2), channel_id=1, source_target_pairs={{1,2},{2,1},{3,4},{4,3},{5,6},{6,5},{7,8},{8,7},{9,10},{10,9},{11,... | collective-permute-start | bytes 196616 | tf_op jit(solution)/shard_map/ppermute | solution.py:466
  7.9 1.6 %copy-start.1 = (f32[128,4096]{1,0:T(8,128)S(1)}, f32[128,4096]{1,0:T(8,128)}, u32[]{:S(2)}) copy-start(f32[128,4096]{1,0:T(8,128)} %traces) | copy-start | bytes 6291460
  16.1 19.9 %copy-start = (bf16[256,512]{1,0:T(8,128)(2,1)S(1)}, bf16[256,512]{1,0:T(8,128)(2,1)}, u32[]{:S(2)}) copy-start(bf16[256,512]{1,0:T(8,128)(2,1)} %constant.52.clone.table) | copy-start | bytes 786436
  16.1 10.2 %collective-permute-start.3 = (bf16[33,16,256]{2,1,0:T(8,128)(2,1)S(1)}, bf16[33,16,256]{2,1,0:T(8,128)(2,1)S(1)}, u32[]{:S(2)}, u32[]{:S(2)}) collective-permute-start(bf16[33,16,256]{2,1,0:T(8,128)(2,1)S(1)} %get-tuple-element.69), channel_id=1, source_target_pairs={{0,2},{2,0},{4,6},{6,4},{8,10},{10,8},{12,14},{14,12},{16,18},{18,... | collective-permute-start | bytes 811016 | tf_op jit(solution)/shard_map/ppermute | solution.py:436
  16.2 10.1 %collective-permute-start.4 = (bf16[33,16,256]{2,1,0:T(8,128)(2,1)S(1)}, bf16[33,16,256]{2,1,0:T(8,128)(2,1)S(1)}, u32[]{:S(2)}, u32[]{:S(2)}) collective-permute-start(bf16[33,16,256]{2,1,0:T(8,128)(2,1)S(1)} %get-tuple-element.70), channel_id=1, source_target_pairs={{0,4},{2,6},{4,0},{6,2},{8,12},{10,14},{12,8},{14,10},{16,20},{18,... | collective-permute-start | bytes 811016 | tf_op jit(solution)/shard_map/ppermute | solution.py:436
  17.9 6.1 %collective-permute-start.5 = (bf16[16,16,256]{2,1,0:T(8,128)(2,1)S(1)}, bf16[16,16,256]{2,1,0:T(8,128)(2,1)S(1)}, u32[]{:S(2)}, u32[]{:S(2)}) collective-permute-start(bf16[16,16,256]{2,1,0:T(8,128)(2,1)S(1)} %get-tuple-element.71.first), channel_id=1, source_target_pairs={{0,8},{8,0},{2,10},{10,2},{4,12},{12,4},{6,14},{14,6},{16,24},{24,... | collective-permute-start | bytes 393224 | tf_op jit(solution)/shard_map/ppermute | solution.py:444
  19.5 6.8 %collective-permute-start.6 = (bf16[16,16,256]{2,1,0:T(8,128)(2,1)S(1)}, bf16[16,16,256]{2,1,0:T(8,128)(2,1)S(1)}, u32[]{:S(2)}, u32[]{:S(2)}) collective-permute-start(bf16[16,16,256]{2,1,0:T(8,128)(2,1)S(1)} %get-tuple-element.74.second), channel_id=1, source_target_pairs={{8,16},{16,8},{10,18},{18,10},{12,20},{20,12},{14,22},{22,14},{9,1... | collective-permute-start | bytes 393224 | tf_op jit(solution)/shard_map/ppermute | solution.py:444
  24.0 9.2 %collective-permute-start.7 = (bf16[33,16,256]{2,1,0:T(8,128)(2,1)S(1)}, bf16[33,16,256]{2,1,0:T(8,128)(2,1)S(1)}, u32[]{:S(2)}, u32[]{:S(2)}) collective-permute-start(bf16[33,16,256]{2,1,0:T(8,128)(2,1)S(1)} %get-tuple-element.77), channel_id=1, source_target_pairs={{0,6},{2,4},{4,2},{6,0},{8,14},{10,12},{12,10},{14,8},{16,22},{18,... | collective-permute-start | bytes 811016 | tf_op jit(solution)/shard_map/ppermute | solution.py:436
  26.4 11.5 %collective-permute-start.9 = (bf16[2,16,16,256]{3,2,1,0:T(8,128)(2,1)S(1)}, bf16[2,16,16,256]{3,2,1,0:T(8,128)(2,1)S(1)}, u32[]{:S(2)}, u32[]{:S(2)}) collective-permute-start(bf16[2,16,16,256]{3,2,1,0:T(8,128)(2,1)S(1)} %pad_maximum_fusion.1), channel_id=1, source_target_pairs={{8,16},{16,8},{10,18},{18,10},{12,20},{20,12},{14,22},{22,14},{9,1... | collective-permute-start | bytes 786440 | tf_op jit(solution)/shard_map/ppermute | solution.py:444
  28.6 9.4 %collective-permute-start.8 = (bf16[2,16,16,256]{3,2,1,0:T(8,128)(2,1)S(1)}, bf16[2,16,16,256]{3,2,1,0:T(8,128)(2,1)S(1)}, u32[]{:S(2)}, u32[]{:S(2)}) collective-permute-start(bf16[2,16,16,256]{3,2,1,0:T(8,128)(2,1)S(1)} %pad_maximum_fusion), channel_id=1, source_target_pairs={{0,8},{8,0},{2,10},{10,2},{4,12},{12,4},{6,14},{14,6},{16,24},{24,... | collective-permute-start | bytes 786440 | tf_op jit(solution)/shard_map/ppermute | solution.py:444
  33.2 6.9 %collective-permute-start.10 = (bf16[16,16,256]{2,1,0:T(8,128)(2,1)S(1)}, bf16[16,16,256]{2,1,0:T(8,128)(2,1)S(1)}, u32[]{:S(2)}, u32[]{:S(2)}) collective-permute-start(bf16[16,16,256]{2,1,0:T(8,128)(2,1)S(1)} %get-tuple-element.94), channel_id=1, source_target_pairs={{0,8},{8,0},{2,10},{10,2},{4,12},{12,4},{6,14},{14,6},{16,24},{24,... | collective-permute-start | bytes 393224 | tf_op jit(solution)/shard_map/ppermute | solution.py:444
  33.3 6.9 %collective-permute-start.11 = (bf16[16,16,256]{2,1,0:T(8,128)(2,1)S(1)}, bf16[16,16,256]{2,1,0:T(8,128)(2,1)S(1)}, u32[]{:S(2)}, u32[]{:S(2)}) collective-permute-start(bf16[16,16,256]{2,1,0:T(8,128)(2,1)S(1)} %get-tuple-element.93), channel_id=1, source_target_pairs={{8,16},{16,8},{10,18},{18,10},{12,20},{20,12},{14,22},{22,14},{9,1... | collective-permute-start | bytes 393224 | tf_op jit(solution)/shard_map/ppermute | solution.py:444
  37.9 2.2 %copy-start.2 = (bf16[208,512]{1,0:T(8,128)(2,1)S(1)}, bf16[208,512]{1,0:T(8,128)(2,1)}, u32[]{:S(2)}) copy-start(bf16[208,512]{1,0:T(8,128)(2,1)} %constant.53.clone.l_high) | copy-start | bytes 638980
  37.9 2.2 %copy-start.3 = (bf16[208,512]{1,0:T(8,128)(2,1)S(1)}, bf16[208,512]{1,0:T(8,128)(2,1)}, u32[]{:S(2)}) copy-start(bf16[208,512]{1,0:T(8,128)(2,1)} %constant.54.clone.l_low) | copy-start | bytes 638980
  42.0 18.2 %copy-start.4 = (bf16[208,208]{1,0:T(8,128)(2,1)S(1)}, bf16[208,208]{1,0:T(8,128)(2,1)}, u32[]{:S(2)}) copy-start(bf16[208,208]{1,0:T(8,128)(2,1)} %constant.55.clone.refs_4_) | copy-start | bytes 259588
  42.0 4.8 %collective-permute-start.12 = (bf16[208,256]{1,0:T(8,128)(2,1)S(1)}, bf16[208,256]{1,0:T(8,128)(2,1)S(1)}, u32[]{:S(2)}, u32[]{:S(2)}) collective-permute-start(bf16[208,256]{1,0:T(8,128)(2,1)S(1)} %get-tuple-element.85), channel_id=1, source_target_pairs={{0,8},{8,0},{2,10},{10,2},{4,12},{12,4},{6,14},{14,6},{16,24},{24,... | collective-permute-start | bytes 319496 | tf_op jit(solution)/shard_map/ppermute | solution.py:444
  42.1 6.6 %collective-permute-start.13 = (bf16[208,256]{1,0:T(8,128)(2,1)S(1)}, bf16[208,256]{1,0:T(8,128)(2,1)S(1)}, u32[]{:S(2)}, u32[]{:S(2)}) collective-permute-start(bf16[208,256]{1,0:T(8,128)(2,1)S(1)} %get-tuple-element.86), channel_id=1, source_target_pairs={{8,16},{16,8},{10,18},{18,10},{12,20},{20,12},{14,22},{22,14},{9,1... | collective-permute-start | bytes 319496 | tf_op jit(solution)/shard_map/ppermute | solution.py:444
  45.5 3.6 %collective-permute-start.14 = (bf16[208,416]{1,0:T(8,128)(2,1)S(1)}, bf16[208,416]{1,0:T(8,128)(2,1)S(1)}, u32[]{:S(2)}, u32[]{:S(2)}) collective-permute-start(bf16[208,416]{1,0:T(8,128)(2,1)S(1)} %get-tuple-element.84.refs_0_), channel_id=1, source_target_pairs={{0,1},{1,0},{2,3},{3,2},{4,5},{5,4},{6,7},{7,6},{8,9},{9,8},{10,11... | collective-permute-start | bytes 519176 | tf_op jit(solution)/shard_map/ppermute | solution.py:433
  46.8 2.3 %collective-permute-start.15 = (bf16[208,256]{1,0:T(8,128)(2,1)S(1)}, bf16[208,256]{1,0:T(8,128)(2,1)S(1)}, u32[]{:S(2)}, u32[]{:S(2)}) collective-permute-start(bf16[208,256]{1,0:T(8,128)(2,1)S(1)} %collective-permute-done.12.refs_1_), channel_id=1, source_target_pairs={{0,1},{1,0},{2,3},{3,2},{4,5},{5,4},{6,7},{7,6},{8,9},{9,8},{10,11... | collective-permute-start | bytes 319496 | tf_op jit(solution)/shard_map/ppermute | solution.py:433
  48.7 1.3 %collective-permute-start.16 = (bf16[208,256]{1,0:T(8,128)(2,1)S(1)}, bf16[208,256]{1,0:T(8,128)(2,1)S(1)}, u32[]{:S(2)}, u32[]{:S(2)}) collective-permute-start(bf16[208,256]{1,0:T(8,128)(2,1)S(1)} %collective-permute-done.13.refs_2_), channel_id=1, source_target_pairs={{0,1},{1,0},{2,3},{3,2},{4,5},{5,4},{6,7},{7,6},{8,9},{9,8},{10,11... | collective-permute-start | bytes 319496 | tf_op jit(solution)/shard_map/ppermute | solution.py:433
  50.7 5.1 %collective-permute-start.17 = (bf16[2,208,128]{2,1,0:T(8,128)(2,1)S(1)}, bf16[2,208,128]{2,1,0:T(8,128)(2,1)S(1)}, u32[]{:S(2)}, u32[]{:S(2)}) collective-permute-start(bf16[2,208,128]{2,1,0:T(8,128)(2,1)S(1)} %get-tuple-element.88), channel_id=1, source_target_pairs={{0,2},{2,0},{4,6},{6,4},{8,10},{10,8},{12,14},{14,12},{16,18},{18,... | collective-permute-start | bytes 319496 | tf_op jit(solution)/shard_map/ppermute | solution.py:436
  51.2 7.9 %collective-permute-start.18 = (bf16[2,208,128]{2,1,0:T(8,128)(2,1)S(1)}, bf16[2,208,128]{2,1,0:T(8,128)(2,1)S(1)}, u32[]{:S(2)}, u32[]{:S(2)}) collective-permute-start(bf16[2,208,128]{2,1,0:T(8,128)(2,1)S(1)} %get-tuple-element.89), channel_id=1, source_target_pairs={{0,4},{2,6},{4,0},{6,2},{8,12},{10,14},{12,8},{14,10},{16,20},{18,... | collective-permute-start | bytes 319496 | tf_op jit(solution)/shard_map/ppermute | solution.py:436
  54.6 5.6 %collective-permute-start.19 = (bf16[2,208,128]{2,1,0:T(8,128)(2,1)S(1)}, bf16[2,208,128]{2,1,0:T(8,128)(2,1)S(1)}, u32[]{:S(2)}, u32[]{:S(2)}) collective-permute-start(bf16[2,208,128]{2,1,0:T(8,128)(2,1)S(1)} %get-tuple-element.90), channel_id=1, source_target_pairs={{0,6},{2,4},{4,2},{6,0},{8,14},{10,12},{12,10},{14,8},{16,22},{18,... | collective-permute-start | bytes 319496 | tf_op jit(solution)/shard_map/ppermute | solution.py:436

commit v7 on v6

--- a/solution.py
+++ b/solution.py
@@ -189,13 +189,14 @@
     chunk = 8
     height = rows + 16
     taps = [space[j : j + 1, :] for j in range(STAPS)]
+    t_all = jnp.concatenate([t_high[...], t_high[...], t_low[...]], axis=0)
 
     def body(step, carry):
         seg0 = step * chunk
         spans = [pl.ds(pl.multiple_of((seg0 + s) * SEG, SEG), 2 * SEG) for s in range(chunk)]
         high = jnp.concatenate([x_high[:, span] for span in spans], axis=0)
         low = jnp.concatenate([x_low[:, span] for span in spans], axis=0)
-        y = mxu(high, t_high[...]) + mxu(low, t_high[...]) + mxu(high, t_low[...])
+        y = mxu(jnp.concatenate([high, low, high], axis=1), t_all)
         for s in range(chunk):
             block = y[s * height : (s + 1) * height]
             ext = jnp.concatenate(

time: 63.1 us -> 62.2 us (0.986)
  Pallas kernels: 15.5 us -> 14.8 us
    pallas_call x1, Pallas kernels: 4.64 us -> 3.9 us  [local(): pl.pallas_call(filter_kernel, out_shape=[short] * 2 + [block] * 3, in_spe...]
  transfers between devices with their start and end apart: 20 -> 20, of which waited for: 10 -> 11; matrix products, arithmetic and copies ran while one was open for 4% -> 4% of each run, Pallas kernels for 9% -> 10%
where the time goes in v7:
time: 62.2 us; the launch traced here: 61.9 us
  starting transfers between devices  22.7 us (36%)
  waiting for transfers between devices  18.4 us (30%)
  Pallas kernels  14.8 us (24%)
  other arithmetic  3.44 us (6%)
  local copies, waits for them, and re-layouts  1.67 us (3%)
  between operations  0.98 us (2%)
    ppermute x8, starting transfers between devices, plane_swap(): return lax.ppermute(x, 'chan', route)  11.8 us
    ppermute x6, waiting for transfers between devices, in_plane(): return lax.ppermute(x, 'chan', [(c, c ^ rel) for c in range(n_chan)])  9.49 us
    ppermute x8, waiting for transfers between devices, plane_swap(): return lax.ppermute(x, 'chan', route)  7.61 us
    ppermute x6, starting transfers between devices, in_plane(): return lax.ppermute(x, 'chan', [(c, c ^ rel) for c in range(n_chan)])  6.32 us
    pallas_call x1, Pallas kernels, local(): pl.pallas_call(filter_kernel, out_shape=[short] * 2 + [block] * 3, in_spe...  3.9 us
    ppermute x1, starting transfers between devices, local(): halos = lax.ppermute(edges, BOTH, route)  3.86 us
    pallas_call x1, Pallas kernels, local(): pl.pallas_call(finish_kernel, out_shape=shape((LAGS, SLOTS // 2, chan_wid...  2.44 us
    pallas_call x1, Pallas kernels, local(): pl.pallas_call(cross_kernel, out_shape=shape((N_OWN * QG, 2 * SEG), F32),...  2.12 us
  transfers between devices with their start and end apart: 20, of which 11 were waited for; matrix products, arithmetic and copies ran while one was open for 4% of the time, Pallas kernels for 10%

profile of v7, /device:TPU:16, one launch (start us, length us, event | category | flops | bytes accessed | tf_op | source)
XLA Modules:
  0.0 61.9 jit_solution(5396184032508564860)
XLA Ops:
  0.0 1.0 %broadcast_select_fusion.2 = (f32[2,4096]{1,0:T(2,128)S(1)}, f32[2,4096]{1,0:T(2,128)S(1)}) fusion(pred[]{:T(512)S(6)} %eq.4, f32[128,4096]{1,0:T(8,128)} %traces), kind=kLoop, calls=%fused_computation.9 | loop fusion | flops 16384 | bytes 131073 | tf_op jit(solution)/shard_map/jit(_where)/select_n | solution.py:450
  1.0 0.1 collective-permute-start
  1.1 0.8 %fusion = pred[2]{0:T(512)(128)(4,1)S(1)} fusion(pred[]{:T(512)S(6)} %eq.4, s32[128]{0:T(128)} %param.11), kind=kLoop, calls=%fused_computation.16 | loop fusion | flops 4 | bytes 19 | tf_op jit(solution)/shard_map/gt | solution.py:455
  1.9 0.1 broadcast_select_fusion.1
  2.0 0.7 %pad_add_fusion.whole.whole_rows = s32[8,128]{1,0:T(8,128)S(1)} fusion(s32[1,128]{1,0:T(1,128)} %bitcast.15, s32[2,16]{1,0:T(2,128)} %bitcast.16), kind=kLoop, calls=%fused_computation.11 | loop fusion | flops 1024 | bytes 4736 | tf_op jit(solution)/shard_map/add | solution.py:460
  2.7 0.7 %pad_add_fusion.1.small = f32[8,128]{1,0:T(8,128)S(1)} fusion(f32[1,5]{1,0:T(1,128)} %bitcast.17, f32[1,33]{1,0:T(1,128)} %bitcast.18), kind=kLoop, calls=%fused_computation.12 | loop fusion | flops 1024 | bytes 4248 | tf_op jit(solution)/shard_map/add | solution.py:458
  3.4 0.1 broadcast_select_fusion
  3.5 0.6 collective-permute-start.1
  4.0 3.9 %collective-permute-start.2 = (f32[4,4096]{1,0:T(4,128)S(1)}, f32[4,4096]{1,0:T(4,128)S(1)}, u32[]{:S(2)}, u32[]{:S(2)}) collective-permute-start(f32[4,4096]{1,0:T(4,128)S(1)} %pad_maximum_fusion.2), channel_id=1, source_target_pairs={{1,2},{2,1},{3,4},{4,3},{5,6},{6,5},{7,8},{8,7},{9,10},{10,9},{11,... | collective-permute-start | bytes 196616 | tf_op jit(solution)/shard_map/ppermute | solution.py:467
  7.9 0.0 copy-start.1
  7.9 1.6 %copy-done.1 = f32[128,4096]{1,0:T(8,128)S(1)} copy-done((f32[128,4096]{1,0:T(8,128)S(1)}, f32[128,4096]{1,0:T(8,128)}, u32[]{:S(2)}) %copy-start.1) | copy-done | bytes 2097176
  9.5 1.7 %prepare.1 = (bf16[512,256]{1,0:T(8,128)(2,1)S(1)}, bf16[512,256]{1,0:T(8,128)(2,1)S(1)}, bf16[16,256]{1,0:T(8,128)(2,1)S(1)}, f32[8,256]{1,0:T(8,128)S(1)}, f32...) custom-call(f32[8,128]{1,0:T(8,128)S(1)} %pad_add_fusion.1.small, ...), custom_call_target="tpu_custom_call" | custom-call | tf_op jit(solution)/shard_map/prepare/pallas_call | solution.py:471
  11.2 0.3 collective-permute-done.2.halos
  11.5 3.9 %filter_whiten.1 = (bf16[16,16,256]{2,1,0:T(8,128)(2,1)S(1)}, bf16[16,16,256]{2,1,0:T(8,128)(2,1)S(1)}, bf16[33,16,256]{2,1,0:T(8,128)(2,1)S(1)}, bf16[33,16,256...) custom-call(f32[8,4096]{1,0:T(8,128)S(1)} %get-tuple-element.61.own_near, bf16[64,4096]{1,0:T(8,128)(2,1)S(1)} %get-tuple-element.62.own_high, ...), custom_call_target="tpu_custom_call" | custom-call | tf_op jit(solution)/shard_map/filter_whiten/pallas_call | solution.py:484
  15.4 0.0 copy-start
  15.4 0.1 collective-permute-start.3
  15.5 1.7 %collective-permute-start.4 = (bf16[33,16,256]{2,1,0:T(8,128)(2,1)S(1)}, bf16[33,16,256]{2,1,0:T(8,128)(2,1)S(1)}, u32[]{:S(2)}, u32[]{:S(2)}) collective-permute-start(bf16[33,16,256]{2,1,0:T(8,128)(2,1)S(1)} %get-tuple-element.70), channel_id=1, source_target_pairs={{0,4},{2,6},{4,0},{6,2},{8,12},{10,14},{12,8},{14,10},{16,20},{18,... | collective-permute-start | bytes 811016 | tf_op jit(solution)/shard_map/ppermute | solution.py:437
  17.2 1.6 %collective-permute-start.5 = (bf16[16,16,256]{2,1,0:T(8,128)(2,1)S(1)}, bf16[16,16,256]{2,1,0:T(8,128)(2,1)S(1)}, u32[]{:S(2)}, u32[]{:S(2)}) collective-permute-start(bf16[16,16,256]{2,1,0:T(8,128)(2,1)S(1)} %get-tuple-element.71.first), channel_id=1, source_target_pairs={{0,8},{8,0},{2,10},{10,2},{4,12},{12,4},{6,14},{14,6},{16,24},{24,... | collective-permute-start | bytes 393224 | tf_op jit(solution)/shard_map/ppermute | solution.py:445
  18.7 1.9 %collective-permute-start.6 = (bf16[16,16,256]{2,1,0:T(8,128)(2,1)S(1)}, bf16[16,16,256]{2,1,0:T(8,128)(2,1)S(1)}, u32[]{:S(2)}, u32[]{:S(2)}) collective-permute-start(bf16[16,16,256]{2,1,0:T(8,128)(2,1)S(1)} %get-tuple-element.74.second), channel_id=1, source_target_pairs={{8,16},{16,8},{10,18},{18,10},{12,20},{20,12},{14,22},{22,14},{9,1... | collective-permute-start | bytes 393224 | tf_op jit(solution)/shard_map/ppermute | solution.py:445
  20.7 2.6 %collective-permute-done.5.near_0 = bf16[16,16,256]{2,1,0:T(8,128)(2,1)S(1)} collective-permute-done((bf16[16,16,256]{2,1,0:T(8,128)(2,1)S(1)}, bf16[16,16,256]{2,1,0:T(8,128)(2,1)S(1)}, u32[]{:S(2)}, u32[]{:S(2)}) %collective-permute-start.5) | collective-permute-done | bytes 131104 | tf_op jit(solution)/shard_map/ppermute | solution.py:445
  23.3 0.6 %collective-permute-start.7 = (bf16[33,16,256]{2,1,0:T(8,128)(2,1)S(1)}, bf16[33,16,256]{2,1,0:T(8,128)(2,1)S(1)}, u32[]{:S(2)}, u32[]{:S(2)}) collective-permute-start(bf16[33,16,256]{2,1,0:T(8,128)(2,1)S(1)} %get-tuple-element.77), channel_id=1, source_target_pairs={{0,6},{2,4},{4,2},{6,0},{8,14},{10,12},{12,10},{14,8},{16,22},{18,... | collective-permute-start | bytes 811016 | tf_op jit(solution)/shard_map/ppermute | solution.py:437
  23.9 1.7 %collective-permute-done.6.far_0 = bf16[16,16,256]{2,1,0:T(8,128)(2,1)S(1)} collective-permute-done((bf16[16,16,256]{2,1,0:T(8,128)(2,1)S(1)}, bf16[16,16,256]{2,1,0:T(8,128)(2,1)S(1)}, u32[]{:S(2)}, u32[]{:S(2)}) %collective-permute-start.6) | collective-permute-done | bytes 131104 | tf_op jit(solution)/shard_map/ppermute | solution.py:445
  25.7 2.1 %collective-permute-start.9 = (bf16[2,16,16,256]{3,2,1,0:T(8,128)(2,1)S(1)}, bf16[2,16,16,256]{3,2,1,0:T(8,128)(2,1)S(1)}, u32[]{:S(2)}, u32[]{:S(2)}) collective-permute-start(bf16[2,16,16,256]{3,2,1,0:T(8,128)(2,1)S(1)} %pad_maximum_fusion.1), channel_id=1, source_target_pairs={{8,16},{16,8},{10,18},{18,10},{12,20},{20,12},{14,22},{22,14},{9,1... | collective-permute-start | bytes 786440 | tf_op jit(solution)/shard_map/ppermute | solution.py:445
  27.8 0.1 collective-permute-start.8
  27.9 4.5 %collective-permute-done.7.refs_3_.b3 = bf16[33,16,256]{2,1,0:T(8,128)(2,1)S(1)} collective-permute-done((bf16[33,16,256]{2,1,0:T(8,128)(2,1)S(1)}, bf16[33,16,256]{2,1,0:T(8,128)(2,1)S(1)}, u32[]{:S(2)}, u32[]{:S(2)}) %collective-permute-start.7) | collective-permute-done | bytes 270368 | tf_op jit(solution)/shard_map/ppermute | solution.py:437
  32.5 0.1 collective-permute-start.10
  32.5 2.8 %collective-permute-start.11 = (bf16[16,16,256]{2,1,0:T(8,128)(2,1)S(1)}, bf16[16,16,256]{2,1,0:T(8,128)(2,1)S(1)}, u32[]{:S(2)}, u32[]{:S(2)}) collective-permute-start(bf16[16,16,256]{2,1,0:T(8,128)(2,1)S(1)} %get-tuple-element.93), channel_id=1, source_target_pairs={{8,16},{16,8},{10,18},{18,10},{12,20},{20,12},{14,22},{22,14},{9,1... | collective-permute-start | bytes 393224 | tf_op jit(solution)/shard_map/ppermute | solution.py:445
  35.3 1.8 %inner_pairs.1 = (f32[4,32,16,512]{3,2,1,0:T(8,128)S(1)}, f32[16,16,512]{2,1,0:T(8,128)S(1)}, f32[16,16,512]{2,1,0:T(8,128)S(1)}, f32[96,512]{1,0:T(8,128)S(1)}) custom-call(bf16[16,16,256]{2,1,0:T(8,128)(2,1)S(1)} %get-tuple-element.71.first, bf16[16,16,256]{2,1,0:T(8,128)(2,1)S(1)} %get-tuple-element.74.second, ...), custom_call_target="tpu_custom_call" | custom-call | tf_op jit(solution)/shard_map/inner_pairs/pallas_call | solution.py:518
  37.2 0.0 copy-start.2
  37.2 0.0 copy-start.3
  37.2 2.1 %cross_pairs.1.cross_in = f32[416,512]{1,0:T(8,128)S(1)} custom-call(f32[4,32,16,512]{3,2,1,0:T(8,128)S(1)} %get-tuple-element.80.spec, f32[16,16,512]{2,1,0:T(8,128)S(1)} %get-tuple-element.81.spec_near, f32[16,16,512]{2,1,0:T(8,128)S(1)} %get-tuple-element.82.spec_far, f32[96,512]{1,0:T(8,128)S(1)} %get-tuple-element.83.inner, ...), custom_call_target="tpu_custom_call" | custom-call | tf_op jit(solution)/shard_map/cross_pairs/pallas_call | solution.py:526
  39.3 0.1 collective-permute-done.11.far_3
  39.4 1.9 %pair_lags.1 = (bf16[208,416]{1,0:T(8,128)(2,1)S(1)}, bf16[208,256]{1,0:T(8,128)(2,1)S(1)}, bf16[208,256]{1,0:T(8,128)(2,1)S(1)}) custom-call(f32[4,32,16,512]{3,2,1,0:T(8,128)S(1)} %get-tuple-element.80.spec, f32[416,512]{1,0:T(8,128)S(1)} %cross_pairs.1.cross_in, bf16[16,16,256]{2,1,0:T(8,128)(2,1)S(1)} %collective-permute-done.10.near_3, ...), custom_call_target="tpu_custom_call" | custom-call | tf_op jit(solution)/shard_map/pair_lags/pallas_call | solution.py:535
  41.3 0.0 copy-start.4
  41.3 0.1 collective-permute-start.12
  41.4 3.2 %collective-permute-start.13 = (bf16[208,256]{1,0:T(8,128)(2,1)S(1)}, bf16[208,256]{1,0:T(8,128)(2,1)S(1)}, u32[]{:S(2)}, u32[]{:S(2)}) collective-permute-start(bf16[208,256]{1,0:T(8,128)(2,1)S(1)} %get-tuple-element.86), channel_id=1, source_target_pairs={{8,16},{16,8},{10,18},{18,10},{12,20},{20,12},{14,22},{22,14},{9,1... | collective-permute-start | bytes 319496 | tf_op jit(solution)/shard_map/ppermute | solution.py:445
  44.6 0.1 collective-permute-start.14
  44.7 1.4 %collective-permute-done.12.refs_1_ = bf16[208,256]{1,0:T(8,128)(2,1)S(1)} collective-permute-done((bf16[208,256]{1,0:T(8,128)(2,1)S(1)}, bf16[208,256]{1,0:T(8,128)(2,1)S(1)}, u32[]{:S(2)}, u32[]{:S(2)}) %collective-permute-start.12) | collective-permute-done | bytes 106528 | tf_op jit(solution)/shard_map/ppermute | solution.py:445
  46.1 1.9 %collective-permute-done.13.refs_2_ = bf16[208,256]{1,0:T(8,128)(2,1)S(1)} collective-permute-done((bf16[208,256]{1,0:T(8,128)(2,1)S(1)}, bf16[208,256]{1,0:T(8,128)(2,1)S(1)}, u32[]{:S(2)}, u32[]{:S(2)}) %collective-permute-start.13) | collective-permute-done | bytes 106528 | tf_op jit(solution)/shard_map/ppermute | solution.py:445
  48.0 0.3 choose.1.chosen
  48.3 0.9 %collective-permute-done.16.refs_5_ = bf16[208,256]{1,0:T(8,128)(2,1)S(1)} collective-permute-done((bf16[208,256]{1,0:T(8,128)(2,1)S(1)}, bf16[208,256]{1,0:T(8,128)(2,1)S(1)}, u32[]{:S(2)}, u32[]{:S(2)}) %collective-permute-start.16) | collective-permute-done | bytes 106528 | tf_op jit(solution)/shard_map/ppermute | solution.py:434
  49.3 0.6 %select_slots.1 = (bf16[2,208,128]{2,1,0:T(8,128)(2,1)S(1)}, bf16[2,208,128]{2,1,0:T(8,128)(2,1)S(1)}, bf16[2,208,128]{2,1,0:T(8,128)(2,1)S(1)}, bf16[2,208,128]{2,1,0:T(8,128)(2,1)S(1)}) custom-call(bf16[928,512]{1,0:T(8,128)(2,1)S(1)} %choose.1.chosen, bf16[208,416]{1,0:T(8,128)(2,1)S(1)} %get-tuple-element.84.refs_0_, ...), custom_call_target="tpu_custom_call" | custom-call | tf_op jit(solution)/shard_map/select_slots/pallas_call | solution.py:561
  49.9 0.6 collective-permute-start.17
  50.5 3.4 %collective-permute-start.18 = (bf16[2,208,128]{2,1,0:T(8,128)(2,1)S(1)}, bf16[2,208,128]{2,1,0:T(8,128)(2,1)S(1)}, u32[]{:S(2)}, u32[]{:S(2)}) collective-permute-start(bf16[2,208,128]{2,1,0:T(8,128)(2,1)S(1)} %get-tuple-element.89), channel_id=1, source_target_pairs={{0,4},{2,6},{4,0},{6,2},{8,12},{10,14},{12,8},{14,10},{16,20},{18,... | collective-permute-start | bytes 319496 | tf_op jit(solution)/shard_map/ppermute | solution.py:437
  54.5 0.5 collective-permute-done.17.refs_1_
  55.0 3.4 %collective-permute-done.18.refs_2_ = bf16[2,208,128]{2,1,0:T(8,128)(2,1)S(1)} collective-permute-done((bf16[2,208,128]{2,1,0:T(8,128)(2,1)S(1)}, bf16[2,208,128]{2,1,0:T(8,128)(2,1)S(1)}, u32[]{:S(2)}, u32[]{:S(2)}) %collective-permute-start.18) | collective-permute-done | bytes 106528 | tf_op jit(solution)/shard_map/ppermute | solution.py:437
  58.4 1.1 %collective-permute-done.19.refs_3_ = bf16[2,208,128]{2,1,0:T(8,128)(2,1)S(1)} collective-permute-done((bf16[2,208,128]{2,1,0:T(8,128)(2,1)S(1)}, bf16[2,208,128]{2,1,0:T(8,128)(2,1)S(1)}, u32[]{:S(2)}, u32[]{:S(2)}) %collective-permute-start.19) | collective-permute-done | bytes 106528 | tf_op jit(solution)/shard_map/ppermute | solution.py:437
  59.4 2.4 %finish_slots.1 = f32[201,8,128]{2,1,0:T(8,128)} custom-call(s32[1]{0:T(128)S(6)} %copy.11.count, f32[8,128]{1,0:T(8,128)S(1)} %get-tuple-element.59.flags, bf16[2,208,128]{2,1,0:T(8,128)(2,1)S(1)} %get-tuple-element.87.refs_0_, bf16[2,208,128]{2,1,0:T(8,128)(2,1)S(1)} %collective-permute-done.17.refs_1_, ...), custom_call_target="tpu_custom_call" | custom-call | tf_op jit(solution)/shard_map/finish_slots/pallas_call | solution.py:571
  (21 shorter events, 0.2 us)
Async XLA Ops:
  1.0 2.4 %collective-permute-start = (f32[2,4096]{1,0:T(2,128)S(1)}, f32[2,4096]{1,0:T(2,128)S(1)}, u32[]{:S(2)}, u32[]{:S(2)}) collective-permute-start(f32[2,4096]{1,0:T(2,128)S(1)} %get-tuple-element.48), channel_id=1, source_target_pairs={{0,1},{1,0},{2,3},{3,2},{4,5},{5,4},{6,7},{7,6},{8,9},{9,8},{10,11... | collective-permute-start | bytes 98312 | tf_op jit(solution)/shard_map/ppermute | solution.py:434
  3.5 8.0 %collective-permute-start.1 = (f32[128,4096]{1,0:T(8,128)}, f32[128,4096]{1,0:T(8,128)S(1)}, u32[]{:S(2)}, u32[]{:S(2)}) collective-permute-start(f32[128,4096]{1,0:T(8,128)} %traces), channel_id=1, source_target_pairs={{0,1},{1,0},{2,3},{3,2},{4,5},{5,4},{6,7},{7,6},{8,9},{9,8},{10,11... | collective-permute-start | bytes 6291464 | tf_op jit(solution)/shard_map/ppermute | solution.py:434
  4.0 7.4 %collective-permute-start.2 = (f32[4,4096]{1,0:T(4,128)S(1)}, f32[4,4096]{1,0:T(4,128)S(1)}, u32[]{:S(2)}, u32[]{:S(2)}) collective-permute-start(f32[4,4096]{1,0:T(4,128)S(1)} %pad_maximum_fusion.2), channel_id=1, source_target_pairs={{1,2},{2,1},{3,4},{4,3},{5,6},{6,5},{7,8},{8,7},{9,10},{10,9},{11,... | collective-permute-start | bytes 196616 | tf_op jit(solution)/shard_map/ppermute | solution.py:467
  7.9 1.6 %copy-start.1 = (f32[128,4096]{1,0:T(8,128)S(1)}, f32[128,4096]{1,0:T(8,128)}, u32[]{:S(2)}) copy-start(f32[128,4096]{1,0:T(8,128)} %traces) | copy-start | bytes 6291460
  15.4 19.9 %copy-start = (bf16[256,512]{1,0:T(8,128)(2,1)S(1)}, bf16[256,512]{1,0:T(8,128)(2,1)}, u32[]{:S(2)}) copy-start(bf16[256,512]{1,0:T(8,128)(2,1)} %constant.52.clone.table) | copy-start | bytes 786436
  15.4 10.2 %collective-permute-start.3 = (bf16[33,16,256]{2,1,0:T(8,128)(2,1)S(1)}, bf16[33,16,256]{2,1,0:T(8,128)(2,1)S(1)}, u32[]{:S(2)}, u32[]{:S(2)}) collective-permute-start(bf16[33,16,256]{2,1,0:T(8,128)(2,1)S(1)} %get-tuple-element.69), channel_id=1, source_target_pairs={{0,2},{2,0},{4,6},{6,4},{8,10},{10,8},{12,14},{14,12},{16,18},{18,... | collective-permute-start | bytes 811016 | tf_op jit(solution)/shard_map/ppermute | solution.py:437
  15.5 10.1 %collective-permute-start.4 = (bf16[33,16,256]{2,1,0:T(8,128)(2,1)S(1)}, bf16[33,16,256]{2,1,0:T(8,128)(2,1)S(1)}, u32[]{:S(2)}, u32[]{:S(2)}) collective-permute-start(bf16[33,16,256]{2,1,0:T(8,128)(2,1)S(1)} %get-tuple-element.70), channel_id=1, source_target_pairs={{0,4},{2,6},{4,0},{6,2},{8,12},{10,14},{12,8},{14,10},{16,20},{18,... | collective-permute-start | bytes 811016 | tf_op jit(solution)/shard_map/ppermute | solution.py:437
  17.2 6.1 %collective-permute-start.5 = (bf16[16,16,256]{2,1,0:T(8,128)(2,1)S(1)}, bf16[16,16,256]{2,1,0:T(8,128)(2,1)S(1)}, u32[]{:S(2)}, u32[]{:S(2)}) collective-permute-start(bf16[16,16,256]{2,1,0:T(8,128)(2,1)S(1)} %get-tuple-element.71.first), channel_id=1, source_target_pairs={{0,8},{8,0},{2,10},{10,2},{4,12},{12,4},{6,14},{14,6},{16,24},{24,... | collective-permute-start | bytes 393224 | tf_op jit(solution)/shard_map/ppermute | solution.py:445
  18.7 6.8 %collective-permute-start.6 = (bf16[16,16,256]{2,1,0:T(8,128)(2,1)S(1)}, bf16[16,16,256]{2,1,0:T(8,128)(2,1)S(1)}, u32[]{:S(2)}, u32[]{:S(2)}) collective-permute-start(bf16[16,16,256]{2,1,0:T(8,128)(2,1)S(1)} %get-tuple-element.74.second), channel_id=1, source_target_pairs={{8,16},{16,8},{10,18},{18,10},{12,20},{20,12},{14,22},{22,14},{9,1... | collective-permute-start | bytes 393224 | tf_op jit(solution)/shard_map/ppermute | solution.py:445
  23.3 9.1 %collective-permute-start.7 = (bf16[33,16,256]{2,1,0:T(8,128)(2,1)S(1)}, bf16[33,16,256]{2,1,0:T(8,128)(2,1)S(1)}, u32[]{:S(2)}, u32[]{:S(2)}) collective-permute-start(bf16[33,16,256]{2,1,0:T(8,128)(2,1)S(1)} %get-tuple-element.77), channel_id=1, source_target_pairs={{0,6},{2,4},{4,2},{6,0},{8,14},{10,12},{12,10},{14,8},{16,22},{18,... | collective-permute-start | bytes 811016 | tf_op jit(solution)/shard_map/ppermute | solution.py:437
  25.7 11.5 %collective-permute-start.9 = (bf16[2,16,16,256]{3,2,1,0:T(8,128)(2,1)S(1)}, bf16[2,16,16,256]{3,2,1,0:T(8,128)(2,1)S(1)}, u32[]{:S(2)}, u32[]{:S(2)}) collective-permute-start(bf16[2,16,16,256]{3,2,1,0:T(8,128)(2,1)S(1)} %pad_maximum_fusion.1), channel_id=1, source_target_pairs={{8,16},{16,8},{10,18},{18,10},{12,20},{20,12},{14,22},{22,14},{9,1... | collective-permute-start | bytes 786440 | tf_op jit(solution)/shard_map/ppermute | solution.py:445
  27.8 9.3 %collective-permute-start.8 = (bf16[2,16,16,256]{3,2,1,0:T(8,128)(2,1)S(1)}, bf16[2,16,16,256]{3,2,1,0:T(8,128)(2,1)S(1)}, u32[]{:S(2)}, u32[]{:S(2)}) collective-permute-start(bf16[2,16,16,256]{3,2,1,0:T(8,128)(2,1)S(1)} %pad_maximum_fusion), channel_id=1, source_target_pairs={{0,8},{8,0},{2,10},{10,2},{4,12},{12,4},{6,14},{14,6},{16,24},{24,... | collective-permute-start | bytes 786440 | tf_op jit(solution)/shard_map/ppermute | solution.py:445
  32.5 6.9 %collective-permute-start.10 = (bf16[16,16,256]{2,1,0:T(8,128)(2,1)S(1)}, bf16[16,16,256]{2,1,0:T(8,128)(2,1)S(1)}, u32[]{:S(2)}, u32[]{:S(2)}) collective-permute-start(bf16[16,16,256]{2,1,0:T(8,128)(2,1)S(1)} %get-tuple-element.94), channel_id=1, source_target_pairs={{0,8},{8,0},{2,10},{10,2},{4,12},{12,4},{6,14},{14,6},{16,24},{24,... | collective-permute-start | bytes 393224 | tf_op jit(solution)/shard_map/ppermute | solution.py:445
  32.5 6.9 %collective-permute-start.11 = (bf16[16,16,256]{2,1,0:T(8,128)(2,1)S(1)}, bf16[16,16,256]{2,1,0:T(8,128)(2,1)S(1)}, u32[]{:S(2)}, u32[]{:S(2)}) collective-permute-start(bf16[16,16,256]{2,1,0:T(8,128)(2,1)S(1)} %get-tuple-element.93), channel_id=1, source_target_pairs={{8,16},{16,8},{10,18},{18,10},{12,20},{20,12},{14,22},{22,14},{9,1... | collective-permute-start | bytes 393224 | tf_op jit(solution)/shard_map/ppermute | solution.py:445
  37.2 2.2 %copy-start.2 = (bf16[208,512]{1,0:T(8,128)(2,1)S(1)}, bf16[208,512]{1,0:T(8,128)(2,1)}, u32[]{:S(2)}) copy-start(bf16[208,512]{1,0:T(8,128)(2,1)} %constant.53.clone.l_high) | copy-start | bytes 638980
  37.2 2.2 %copy-start.3 = (bf16[208,512]{1,0:T(8,128)(2,1)S(1)}, bf16[208,512]{1,0:T(8,128)(2,1)}, u32[]{:S(2)}) copy-start(bf16[208,512]{1,0:T(8,128)(2,1)} %constant.54.clone.l_low) | copy-start | bytes 638980
  41.3 18.2 %copy-start.4 = (bf16[208,208]{1,0:T(8,128)(2,1)S(1)}, bf16[208,208]{1,0:T(8,128)(2,1)}, u32[]{:S(2)}) copy-start(bf16[208,208]{1,0:T(8,128)(2,1)} %constant.55.clone.refs_4_) | copy-start | bytes 259588
  41.3 4.8 %collective-permute-start.12 = (bf16[208,256]{1,0:T(8,128)(2,1)S(1)}, bf16[208,256]{1,0:T(8,128)(2,1)S(1)}, u32[]{:S(2)}, u32[]{:S(2)}) collective-permute-start(bf16[208,256]{1,0:T(8,128)(2,1)S(1)} %get-tuple-element.85), channel_id=1, source_target_pairs={{0,8},{8,0},{2,10},{10,2},{4,12},{12,4},{6,14},{14,6},{16,24},{24,... | collective-permute-start | bytes 319496 | tf_op jit(solution)/shard_map/ppermute | solution.py:445
  41.4 6.6 %collective-permute-start.13 = (bf16[208,256]{1,0:T(8,128)(2,1)S(1)}, bf16[208,256]{1,0:T(8,128)(2,1)S(1)}, u32[]{:S(2)}, u32[]{:S(2)}) collective-permute-start(bf16[208,256]{1,0:T(8,128)(2,1)S(1)} %get-tuple-element.86), channel_id=1, source_target_pairs={{8,16},{16,8},{10,18},{18,10},{12,20},{20,12},{14,22},{22,14},{9,1... | collective-permute-start | bytes 319496 | tf_op jit(solution)/shard_map/ppermute | solution.py:445
  44.6 3.7 %collective-permute-start.14 = (bf16[208,416]{1,0:T(8,128)(2,1)S(1)}, bf16[208,416]{1,0:T(8,128)(2,1)S(1)}, u32[]{:S(2)}, u32[]{:S(2)}) collective-permute-start(bf16[208,416]{1,0:T(8,128)(2,1)S(1)} %get-tuple-element.84.refs_0_), channel_id=1, source_target_pairs={{0,1},{1,0},{2,3},{3,2},{4,5},{5,4},{6,7},{7,6},{8,9},{9,8},{10,11... | collective-permute-start | bytes 519176 | tf_op jit(solution)/shard_map/ppermute | solution.py:434
  46.1 2.3 %collective-permute-start.15 = (bf16[208,256]{1,0:T(8,128)(2,1)S(1)}, bf16[208,256]{1,0:T(8,128)(2,1)S(1)}, u32[]{:S(2)}, u32[]{:S(2)}) collective-permute-start(bf16[208,256]{1,0:T(8,128)(2,1)S(1)} %collective-permute-done.12.refs_1_), channel_id=1, source_target_pairs={{0,1},{1,0},{2,3},{3,2},{4,5},{5,4},{6,7},{7,6},{8,9},{9,8},{10,11... | collective-permute-start | bytes 319496 | tf_op jit(solution)/shard_map/ppermute | solution.py:434
  48.0 1.3 %collective-permute-start.16 = (bf16[208,256]{1,0:T(8,128)(2,1)S(1)}, bf16[208,256]{1,0:T(8,128)(2,1)S(1)}, u32[]{:S(2)}, u32[]{:S(2)}) collective-permute-start(bf16[208,256]{1,0:T(8,128)(2,1)S(1)} %collective-permute-done.13.refs_2_), channel_id=1, source_target_pairs={{0,1},{1,0},{2,3},{3,2},{4,5},{5,4},{6,7},{7,6},{8,9},{9,8},{10,11... | collective-permute-start | bytes 319496 | tf_op jit(solution)/shard_map/ppermute | solution.py:434
  49.9 5.1 %collective-permute-start.17 = (bf16[2,208,128]{2,1,0:T(8,128)(2,1)S(1)}, bf16[2,208,128]{2,1,0:T(8,128)(2,1)S(1)}, u32[]{:S(2)}, u32[]{:S(2)}) collective-permute-start(bf16[2,208,128]{2,1,0:T(8,128)(2,1)S(1)} %get-tuple-element.88), channel_id=1, source_target_pairs={{0,2},{2,0},{4,6},{6,4},{8,10},{10,8},{12,14},{14,12},{16,18},{18,... | collective-permute-start | bytes 319496 | tf_op jit(solution)/shard_map/ppermute | solution.py:437
  50.5 7.9 %collective-permute-start.18 = (bf16[2,208,128]{2,1,0:T(8,128)(2,1)S(1)}, bf16[2,208,128]{2,1,0:T(8,128)(2,1)S(1)}, u32[]{:S(2)}, u32[]{:S(2)}) collective-permute-start(bf16[2,208,128]{2,1,0:T(8,128)(2,1)S(1)} %get-tuple-element.89), channel_id=1, source_target_pairs={{0,4},{2,6},{4,0},{6,2},{8,12},{10,14},{12,8},{14,10},{16,20},{18,... | collective-permute-start | bytes 319496 | tf_op jit(solution)/shard_map/ppermute | solution.py:437
  53.8 5.6 %collective-permute-start.19 = (bf16[2,208,128]{2,1,0:T(8,128)(2,1)S(1)}, bf16[2,208,128]{2,1,0:T(8,128)(2,1)S(1)}, u32[]{:S(2)}, u32[]{:S(2)}) collective-permute-start(bf16[2,208,128]{2,1,0:T(8,128)(2,1)S(1)} %get-tuple-element.90), channel_id=1, source_target_pairs={{0,6},{2,4},{4,2},{6,0},{8,14},{10,12},{12,10},{14,8},{16,22},{18,... | collective-permute-start | bytes 319496 | tf_op jit(solution)/shard_map/ppermute | solution.py:437

commit v8 on v7

--- a/solution.py
+++ b/solution.py
@@ -186,7 +186,7 @@
         x_high[rows : rows + 16, lanes] = high
         x_low[rows : rows + 16, lanes] = low
     segs = total // SEG
-    chunk = 8
+    chunk = 4
     height = rows + 16
     taps = [space[j : j + 1, :] for j in range(STAPS)]
     t_all = jnp.concatenate([t_high[...], t_high[...], t_low[...]], axis=0)

time: 62.2 us -> 61.8 us (level)
  no operation moved by 1% of the time
where the time goes in v8:
time: 61.8 us; the launch traced here: 61.5 us
  starting transfers between devices  22.7 us (37%)
  waiting for transfers between devices  18.4 us (30%)
  Pallas kernels  14.4 us (23%)
  other arithmetic  3.44 us (6%)
  local copies, waits for them, and re-layouts  1.67 us (3%)
  between operations  0.98 us (2%)
    ppermute x8, starting transfers between devices, plane_swap(): return lax.ppermute(x, 'chan', route)  11.8 us
    ppermute x6, waiting for transfers between devices, in_plane(): return lax.ppermute(x, 'chan', [(c, c ^ rel) for c in range(n_chan)])  9.49 us
    ppermute x8, waiting for transfers between devices, plane_swap(): return lax.ppermute(x, 'chan', route)  7.62 us
    ppermute x6, starting transfers between devices, in_plane(): return lax.ppermute(x, 'chan', [(c, c ^ rel) for c in range(n_chan)])  6.32 us
    ppermute x1, starting transfers between devices, local(): halos = lax.ppermute(edges, BOTH, route)  3.86 us
    pallas_call x1, Pallas kernels, local(): pl.pallas_call(filter_kernel, out_shape=[short] * 2 + [block] * 3, in_spe...  3.54 us
    pallas_call x1, Pallas kernels, local(): pl.pallas_call(finish_kernel, out_shape=shape((LAGS, SLOTS // 2, chan_wid...  2.44 us
    pallas_call x1, Pallas kernels, local(): pl.pallas_call(cross_kernel, out_shape=shape((N_OWN * QG, 2 * SEG), F32),...  2.12 us
  transfers between devices with their start and end apart: 20, of which 11 were waited for; matrix products, arithmetic and copies ran while one was open for 4% of the time, Pallas kernels for 10%

profile of v8, /device:TPU:16, one launch (start us, length us, event | category | flops | bytes accessed | tf_op | source)
XLA Modules:
  0.0 61.5 jit_solution(9540773842985743161)
XLA Ops:
  0.0 1.0 %broadcast_select_fusion.2 = (f32[2,4096]{1,0:T(2,128)S(1)}, f32[2,4096]{1,0:T(2,128)S(1)}) fusion(pred[]{:T(512)S(6)} %eq.4, f32[128,4096]{1,0:T(8,128)} %traces), kind=kLoop, calls=%fused_computation.9 | loop fusion | flops 16384 | bytes 131073 | tf_op jit(solution)/shard_map/jit(_where)/select_n | solution.py:450
  1.0 0.1 collective-permute-start
  1.1 0.8 %fusion = pred[2]{0:T(512)(128)(4,1)S(1)} fusion(pred[]{:T(512)S(6)} %eq.4, s32[128]{0:T(128)} %param.11), kind=kLoop, calls=%fused_computation.16 | loop fusion | flops 4 | bytes 19 | tf_op jit(solution)/shard_map/gt | solution.py:455
  1.9 0.1 broadcast_select_fusion.1
  2.0 0.7 %pad_add_fusion.whole.whole_rows = s32[8,128]{1,0:T(8,128)S(1)} fusion(s32[1,128]{1,0:T(1,128)} %bitcast.15, s32[2,16]{1,0:T(2,128)} %bitcast.16), kind=kLoop, calls=%fused_computation.11 | loop fusion | flops 1024 | bytes 4736 | tf_op jit(solution)/shard_map/add | solution.py:460
  2.7 0.7 %pad_add_fusion.1.small = f32[8,128]{1,0:T(8,128)S(1)} fusion(f32[1,5]{1,0:T(1,128)} %bitcast.17, f32[1,33]{1,0:T(1,128)} %bitcast.18), kind=kLoop, calls=%fused_computation.12 | loop fusion | flops 1024 | bytes 4248 | tf_op jit(solution)/shard_map/add | solution.py:458
  3.4 0.1 broadcast_select_fusion
  3.5 0.6 collective-permute-start.1
  4.0 3.9 %collective-permute-start.2 = (f32[4,4096]{1,0:T(4,128)S(1)}, f32[4,4096]{1,0:T(4,128)S(1)}, u32[]{:S(2)}, u32[]{:S(2)}) collective-permute-start(f32[4,4096]{1,0:T(4,128)S(1)} %pad_maximum_fusion.2), channel_id=1, source_target_pairs={{1,2},{2,1},{3,4},{4,3},{5,6},{6,5},{7,8},{8,7},{9,10},{10,9},{11,... | collective-permute-start | bytes 196616 | tf_op jit(solution)/shard_map/ppermute | solution.py:467
  7.9 0.0 copy-start.1
  7.9 1.6 %copy-done.1 = f32[128,4096]{1,0:T(8,128)S(1)} copy-done((f32[128,4096]{1,0:T(8,128)S(1)}, f32[128,4096]{1,0:T(8,128)}, u32[]{:S(2)}) %copy-start.1) | copy-done | bytes 2097176
  9.5 1.7 %prepare.1 = (bf16[512,256]{1,0:T(8,128)(2,1)S(1)}, bf16[512,256]{1,0:T(8,128)(2,1)S(1)}, bf16[16,256]{1,0:T(8,128)(2,1)S(1)}, f32[8,256]{1,0:T(8,128)S(1)}, f32...) custom-call(f32[8,128]{1,0:T(8,128)S(1)} %pad_add_fusion.1.small, ...), custom_call_target="tpu_custom_call" | custom-call | tf_op jit(solution)/shard_map/prepare/pallas_call | solution.py:471
  11.2 0.3 collective-permute-done.2.halos
  11.5 3.5 %filter_whiten.1 = (bf16[16,16,256]{2,1,0:T(8,128)(2,1)S(1)}, bf16[16,16,256]{2,1,0:T(8,128)(2,1)S(1)}, bf16[33,16,256]{2,1,0:T(8,128)(2,1)S(1)}, bf16[33,16,256...) custom-call(f32[8,4096]{1,0:T(8,128)S(1)} %get-tuple-element.61.own_near, bf16[64,4096]{1,0:T(8,128)(2,1)S(1)} %get-tuple-element.62.own_high, ...), custom_call_target="tpu_custom_call" | custom-call | tf_op jit(solution)/shard_map/filter_whiten/pallas_call | solution.py:484
  15.0 0.0 copy-start
  15.0 0.1 collective-permute-start.3
  15.1 1.7 %collective-permute-start.4 = (bf16[33,16,256]{2,1,0:T(8,128)(2,1)S(1)}, bf16[33,16,256]{2,1,0:T(8,128)(2,1)S(1)}, u32[]{:S(2)}, u32[]{:S(2)}) collective-permute-start(bf16[33,16,256]{2,1,0:T(8,128)(2,1)S(1)} %get-tuple-element.70), channel_id=1, source_target_pairs={{0,4},{2,6},{4,0},{6,2},{8,12},{10,14},{12,8},{14,10},{16,20},{18,... | collective-permute-start | bytes 811016 | tf_op jit(solution)/shard_map/ppermute | solution.py:437
  16.8 1.6 %collective-permute-start.5 = (bf16[16,16,256]{2,1,0:T(8,128)(2,1)S(1)}, bf16[16,16,256]{2,1,0:T(8,128)(2,1)S(1)}, u32[]{:S(2)}, u32[]{:S(2)}) collective-permute-start(bf16[16,16,256]{2,1,0:T(8,128)(2,1)S(1)} %get-tuple-element.71.first), channel_id=1, source_target_pairs={{0,8},{8,0},{2,10},{10,2},{4,12},{12,4},{6,14},{14,6},{16,24},{24,... | collective-permute-start | bytes 393224 | tf_op jit(solution)/shard_map/ppermute | solution.py:445
  18.4 1.9 %collective-permute-start.6 = (bf16[16,16,256]{2,1,0:T(8,128)(2,1)S(1)}, bf16[16,16,256]{2,1,0:T(8,128)(2,1)S(1)}, u32[]{:S(2)}, u32[]{:S(2)}) collective-permute-start(bf16[16,16,256]{2,1,0:T(8,128)(2,1)S(1)} %get-tuple-element.74.second), channel_id=1, source_target_pairs={{8,16},{16,8},{10,18},{18,10},{12,20},{20,12},{14,22},{22,14},{9,1... | collective-permute-start | bytes 393224 | tf_op jit(solution)/shard_map/ppermute | solution.py:445
  20.3 2.6 %collective-permute-done.5.near_0 = bf16[16,16,256]{2,1,0:T(8,128)(2,1)S(1)} collective-permute-done((bf16[16,16,256]{2,1,0:T(8,128)(2,1)S(1)}, bf16[16,16,256]{2,1,0:T(8,128)(2,1)S(1)}, u32[]{:S(2)}, u32[]{:S(2)}) %collective-permute-start.5) | collective-permute-done | bytes 131104 | tf_op jit(solution)/shard_map/ppermute | solution.py:445
  22.9 0.6 %collective-permute-start.7 = (bf16[33,16,256]{2,1,0:T(8,128)(2,1)S(1)}, bf16[33,16,256]{2,1,0:T(8,128)(2,1)S(1)}, u32[]{:S(2)}, u32[]{:S(2)}) collective-permute-start(bf16[33,16,256]{2,1,0:T(8,128)(2,1)S(1)} %get-tuple-element.77), channel_id=1, source_target_pairs={{0,6},{2,4},{4,2},{6,0},{8,14},{10,12},{12,10},{14,8},{16,22},{18,... | collective-permute-start | bytes 811016 | tf_op jit(solution)/shard_map/ppermute | solution.py:437
  23.6 1.7 %collective-permute-done.6.far_0 = bf16[16,16,256]{2,1,0:T(8,128)(2,1)S(1)} collective-permute-done((bf16[16,16,256]{2,1,0:T(8,128)(2,1)S(1)}, bf16[16,16,256]{2,1,0:T(8,128)(2,1)S(1)}, u32[]{:S(2)}, u32[]{:S(2)}) %collective-permute-start.6) | collective-permute-done | bytes 131104 | tf_op jit(solution)/shard_map/ppermute | solution.py:445
  25.3 2.1 %collective-permute-start.9 = (bf16[2,16,16,256]{3,2,1,0:T(8,128)(2,1)S(1)}, bf16[2,16,16,256]{3,2,1,0:T(8,128)(2,1)S(1)}, u32[]{:S(2)}, u32[]{:S(2)}) collective-permute-start(bf16[2,16,16,256]{3,2,1,0:T(8,128)(2,1)S(1)} %pad_maximum_fusion.1), channel_id=1, source_target_pairs={{8,16},{16,8},{10,18},{18,10},{12,20},{20,12},{14,22},{22,14},{9,1... | collective-permute-start | bytes 786440 | tf_op jit(solution)/shard_map/ppermute | solution.py:445
  27.5 0.1 collective-permute-start.8
  27.5 4.5 %collective-permute-done.7.refs_3_.b3 = bf16[33,16,256]{2,1,0:T(8,128)(2,1)S(1)} collective-permute-done((bf16[33,16,256]{2,1,0:T(8,128)(2,1)S(1)}, bf16[33,16,256]{2,1,0:T(8,128)(2,1)S(1)}, u32[]{:S(2)}, u32[]{:S(2)}) %collective-permute-start.7) | collective-permute-done | bytes 270368 | tf_op jit(solution)/shard_map/ppermute | solution.py:437
  32.1 0.1 collective-permute-start.10
  32.2 2.8 %collective-permute-start.11 = (bf16[16,16,256]{2,1,0:T(8,128)(2,1)S(1)}, bf16[16,16,256]{2,1,0:T(8,128)(2,1)S(1)}, u32[]{:S(2)}, u32[]{:S(2)}) collective-permute-start(bf16[16,16,256]{2,1,0:T(8,128)(2,1)S(1)} %get-tuple-element.93), channel_id=1, source_target_pairs={{8,16},{16,8},{10,18},{18,10},{12,20},{20,12},{14,22},{22,14},{9,1... | collective-permute-start | bytes 393224 | tf_op jit(solution)/shard_map/ppermute | solution.py:445
  35.0 1.8 %inner_pairs.1 = (f32[4,32,16,512]{3,2,1,0:T(8,128)S(1)}, f32[16,16,512]{2,1,0:T(8,128)S(1)}, f32[16,16,512]{2,1,0:T(8,128)S(1)}, f32[96,512]{1,0:T(8,128)S(1)}) custom-call(bf16[16,16,256]{2,1,0:T(8,128)(2,1)S(1)} %get-tuple-element.71.first, bf16[16,16,256]{2,1,0:T(8,128)(2,1)S(1)} %get-tuple-element.74.second, ...), custom_call_target="tpu_custom_call" | custom-call | tf_op jit(solution)/shard_map/inner_pairs/pallas_call | solution.py:518
  36.8 0.0 copy-start.2
  36.8 0.0 copy-start.3
  36.8 2.1 %cross_pairs.1.cross_in = f32[416,512]{1,0:T(8,128)S(1)} custom-call(f32[4,32,16,512]{3,2,1,0:T(8,128)S(1)} %get-tuple-element.80.spec, f32[16,16,512]{2,1,0:T(8,128)S(1)} %get-tuple-element.81.spec_near, f32[16,16,512]{2,1,0:T(8,128)S(1)} %get-tuple-element.82.spec_far, f32[96,512]{1,0:T(8,128)S(1)} %get-tuple-element.83.inner, ...), custom_call_target="tpu_custom_call" | custom-call | tf_op jit(solution)/shard_map/cross_pairs/pallas_call | solution.py:526
  39.0 0.1 collective-permute-done.11.far_3
  39.0 1.9 %pair_lags.1 = (bf16[208,416]{1,0:T(8,128)(2,1)S(1)}, bf16[208,256]{1,0:T(8,128)(2,1)S(1)}, bf16[208,256]{1,0:T(8,128)(2,1)S(1)}) custom-call(f32[4,32,16,512]{3,2,1,0:T(8,128)S(1)} %get-tuple-element.80.spec, f32[416,512]{1,0:T(8,128)S(1)} %cross_pairs.1.cross_in, bf16[16,16,256]{2,1,0:T(8,128)(2,1)S(1)} %collective-permute-done.10.near_3, ...), custom_call_target="tpu_custom_call" | custom-call | tf_op jit(solution)/shard_map/pair_lags/pallas_call | solution.py:535
  40.9 0.0 copy-start.4
  40.9 0.1 collective-permute-start.12
  41.0 3.2 %collective-permute-start.13 = (bf16[208,256]{1,0:T(8,128)(2,1)S(1)}, bf16[208,256]{1,0:T(8,128)(2,1)S(1)}, u32[]{:S(2)}, u32[]{:S(2)}) collective-permute-start(bf16[208,256]{1,0:T(8,128)(2,1)S(1)} %get-tuple-element.86), channel_id=1, source_target_pairs={{8,16},{16,8},{10,18},{18,10},{12,20},{20,12},{14,22},{22,14},{9,1... | collective-permute-start | bytes 319496 | tf_op jit(solution)/shard_map/ppermute | solution.py:445
  44.2 0.1 collective-permute-start.14
  44.3 1.4 %collective-permute-done.12.refs_1_ = bf16[208,256]{1,0:T(8,128)(2,1)S(1)} collective-permute-done((bf16[208,256]{1,0:T(8,128)(2,1)S(1)}, bf16[208,256]{1,0:T(8,128)(2,1)S(1)}, u32[]{:S(2)}, u32[]{:S(2)}) %collective-permute-start.12) | collective-permute-done | bytes 106528 | tf_op jit(solution)/shard_map/ppermute | solution.py:445
  45.7 1.9 %collective-permute-done.13.refs_2_ = bf16[208,256]{1,0:T(8,128)(2,1)S(1)} collective-permute-done((bf16[208,256]{1,0:T(8,128)(2,1)S(1)}, bf16[208,256]{1,0:T(8,128)(2,1)S(1)}, u32[]{:S(2)}, u32[]{:S(2)}) %collective-permute-start.13) | collective-permute-done | bytes 106528 | tf_op jit(solution)/shard_map/ppermute | solution.py:445
  47.6 0.3 choose.1.chosen
  48.0 0.9 %collective-permute-done.16.refs_5_ = bf16[208,256]{1,0:T(8,128)(2,1)S(1)} collective-permute-done((bf16[208,256]{1,0:T(8,128)(2,1)S(1)}, bf16[208,256]{1,0:T(8,128)(2,1)S(1)}, u32[]{:S(2)}, u32[]{:S(2)}) %collective-permute-start.16) | collective-permute-done | bytes 106528 | tf_op jit(solution)/shard_map/ppermute | solution.py:434
  48.9 0.6 %select_slots.1 = (bf16[2,208,128]{2,1,0:T(8,128)(2,1)S(1)}, bf16[2,208,128]{2,1,0:T(8,128)(2,1)S(1)}, bf16[2,208,128]{2,1,0:T(8,128)(2,1)S(1)}, bf16[2,208,128]{2,1,0:T(8,128)(2,1)S(1)}) custom-call(bf16[928,512]{1,0:T(8,128)(2,1)S(1)} %choose.1.chosen, bf16[208,416]{1,0:T(8,128)(2,1)S(1)} %get-tuple-element.84.refs_0_, ...), custom_call_target="tpu_custom_call" | custom-call | tf_op jit(solution)/shard_map/select_slots/pallas_call | solution.py:561
  49.6 0.6 collective-permute-start.17
  50.1 3.4 %collective-permute-start.18 = (bf16[2,208,128]{2,1,0:T(8,128)(2,1)S(1)}, bf16[2,208,128]{2,1,0:T(8,128)(2,1)S(1)}, u32[]{:S(2)}, u32[]{:S(2)}) collective-permute-start(bf16[2,208,128]{2,1,0:T(8,128)(2,1)S(1)} %get-tuple-element.89), channel_id=1, source_target_pairs={{0,4},{2,6},{4,0},{6,2},{8,12},{10,14},{12,8},{14,10},{16,20},{18,... | collective-permute-start | bytes 319496 | tf_op jit(solution)/shard_map/ppermute | solution.py:437
  54.1 0.5 collective-permute-done.17.refs_1_
  54.6 3.4 %collective-permute-done.18.refs_2_ = bf16[2,208,128]{2,1,0:T(8,128)(2,1)S(1)} collective-permute-done((bf16[2,208,128]{2,1,0:T(8,128)(2,1)S(1)}, bf16[2,208,128]{2,1,0:T(8,128)(2,1)S(1)}, u32[]{:S(2)}, u32[]{:S(2)}) %collective-permute-start.18) | collective-permute-done | bytes 106528 | tf_op jit(solution)/shard_map/ppermute | solution.py:437
  58.0 1.1 %collective-permute-done.19.refs_3_ = bf16[2,208,128]{2,1,0:T(8,128)(2,1)S(1)} collective-permute-done((bf16[2,208,128]{2,1,0:T(8,128)(2,1)S(1)}, bf16[2,208,128]{2,1,0:T(8,128)(2,1)S(1)}, u32[]{:S(2)}, u32[]{:S(2)}) %collective-permute-start.19) | collective-permute-done | bytes 106528 | tf_op jit(solution)/shard_map/ppermute | solution.py:437
  59.1 2.4 %finish_slots.1 = f32[201,8,128]{2,1,0:T(8,128)} custom-call(s32[1]{0:T(128)S(6)} %copy.11.count, f32[8,128]{1,0:T(8,128)S(1)} %get-tuple-element.59.flags, bf16[2,208,128]{2,1,0:T(8,128)(2,1)S(1)} %get-tuple-element.87.refs_0_, bf16[2,208,128]{2,1,0:T(8,128)(2,1)S(1)} %collective-permute-done.17.refs_1_, ...), custom_call_target="tpu_custom_call" | custom-call | tf_op jit(solution)/shard_map/finish_slots/pallas_call | solution.py:571
  (21 shorter events, 0.2 us)
Async XLA Ops:
  1.0 2.4 %collective-permute-start = (f32[2,4096]{1,0:T(2,128)S(1)}, f32[2,4096]{1,0:T(2,128)S(1)}, u32[]{:S(2)}, u32[]{:S(2)}) collective-permute-start(f32[2,4096]{1,0:T(2,128)S(1)} %get-tuple-element.48), channel_id=1, source_target_pairs={{0,1},{1,0},{2,3},{3,2},{4,5},{5,4},{6,7},{7,6},{8,9},{9,8},{10,11... | collective-permute-start | bytes 98312 | tf_op jit(solution)/shard_map/ppermute | solution.py:434
  3.5 8.0 %collective-permute-start.1 = (f32[128,4096]{1,0:T(8,128)}, f32[128,4096]{1,0:T(8,128)S(1)}, u32[]{:S(2)}, u32[]{:S(2)}) collective-permute-start(f32[128,4096]{1,0:T(8,128)} %traces), channel_id=1, source_target_pairs={{0,1},{1,0},{2,3},{3,2},{4,5},{5,4},{6,7},{7,6},{8,9},{9,8},{10,11... | collective-permute-start | bytes 6291464 | tf_op jit(solution)/shard_map/ppermute | solution.py:434
  4.0 7.4 %collective-permute-start.2 = (f32[4,4096]{1,0:T(4,128)S(1)}, f32[4,4096]{1,0:T(4,128)S(1)}, u32[]{:S(2)}, u32[]{:S(2)}) collective-permute-start(f32[4,4096]{1,0:T(4,128)S(1)} %pad_maximum_fusion.2), channel_id=1, source_target_pairs={{1,2},{2,1},{3,4},{4,3},{5,6},{6,5},{7,8},{8,7},{9,10},{10,9},{11,... | collective-permute-start | bytes 196616 | tf_op jit(solution)/shard_map/ppermute | solution.py:467
  7.9 1.6 %copy-start.1 = (f32[128,4096]{1,0:T(8,128)S(1)}, f32[128,4096]{1,0:T(8,128)}, u32[]{:S(2)}) copy-start(f32[128,4096]{1,0:T(8,128)} %traces) | copy-start | bytes 6291460
  15.0 19.9 %copy-start = (bf16[256,512]{1,0:T(8,128)(2,1)S(1)}, bf16[256,512]{1,0:T(8,128)(2,1)}, u32[]{:S(2)}) copy-start(bf16[256,512]{1,0:T(8,128)(2,1)} %constant.52.clone.table) | copy-start | bytes 786436
  15.0 10.2 %collective-permute-start.3 = (bf16[33,16,256]{2,1,0:T(8,128)(2,1)S(1)}, bf16[33,16,256]{2,1,0:T(8,128)(2,1)S(1)}, u32[]{:S(2)}, u32[]{:S(2)}) collective-permute-start(bf16[33,16,256]{2,1,0:T(8,128)(2,1)S(1)} %get-tuple-element.69), channel_id=1, source_target_pairs={{0,2},{2,0},{4,6},{6,4},{8,10},{10,8},{12,14},{14,12},{16,18},{18,... | collective-permute-start | bytes 811016 | tf_op jit(solution)/shard_map/ppermute | solution.py:437
  15.1 10.1 %collective-permute-start.4 = (bf16[33,16,256]{2,1,0:T(8,128)(2,1)S(1)}, bf16[33,16,256]{2,1,0:T(8,128)(2,1)S(1)}, u32[]{:S(2)}, u32[]{:S(2)}) collective-permute-start(bf16[33,16,256]{2,1,0:T(8,128)(2,1)S(1)} %get-tuple-element.70), channel_id=1, source_target_pairs={{0,4},{2,6},{4,0},{6,2},{8,12},{10,14},{12,8},{14,10},{16,20},{18,... | collective-permute-start | bytes 811016 | tf_op jit(solution)/shard_map/ppermute | solution.py:437
  16.8 6.1 %collective-permute-start.5 = (bf16[16,16,256]{2,1,0:T(8,128)(2,1)S(1)}, bf16[16,16,256]{2,1,0:T(8,128)(2,1)S(1)}, u32[]{:S(2)}, u32[]{:S(2)}) collective-permute-start(bf16[16,16,256]{2,1,0:T(8,128)(2,1)S(1)} %get-tuple-element.71.first), channel_id=1, source_target_pairs={{0,8},{8,0},{2,10},{10,2},{4,12},{12,4},{6,14},{14,6},{16,24},{24,... | collective-permute-start | bytes 393224 | tf_op jit(solution)/shard_map/ppermute | solution.py:445
  18.4 6.8 %collective-permute-start.6 = (bf16[16,16,256]{2,1,0:T(8,128)(2,1)S(1)}, bf16[16,16,256]{2,1,0:T(8,128)(2,1)S(1)}, u32[]{:S(2)}, u32[]{:S(2)}) collective-permute-start(bf16[16,16,256]{2,1,0:T(8,128)(2,1)S(1)} %get-tuple-element.74.second), channel_id=1, source_target_pairs={{8,16},{16,8},{10,18},{18,10},{12,20},{20,12},{14,22},{22,14},{9,1... | collective-permute-start | bytes 393224 | tf_op jit(solution)/shard_map/ppermute | solution.py:445
  22.9 9.1 %collective-permute-start.7 = (bf16[33,16,256]{2,1,0:T(8,128)(2,1)S(1)}, bf16[33,16,256]{2,1,0:T(8,128)(2,1)S(1)}, u32[]{:S(2)}, u32[]{:S(2)}) collective-permute-start(bf16[33,16,256]{2,1,0:T(8,128)(2,1)S(1)} %get-tuple-element.77), channel_id=1, source_target_pairs={{0,6},{2,4},{4,2},{6,0},{8,14},{10,12},{12,10},{14,8},{16,22},{18,... | collective-permute-start | bytes 811016 | tf_op jit(solution)/shard_map/ppermute | solution.py:437
  25.3 11.5 %collective-permute-start.9 = (bf16[2,16,16,256]{3,2,1,0:T(8,128)(2,1)S(1)}, bf16[2,16,16,256]{3,2,1,0:T(8,128)(2,1)S(1)}, u32[]{:S(2)}, u32[]{:S(2)}) collective-permute-start(bf16[2,16,16,256]{3,2,1,0:T(8,128)(2,1)S(1)} %pad_maximum_fusion.1), channel_id=1, source_target_pairs={{8,16},{16,8},{10,18},{18,10},{12,20},{20,12},{14,22},{22,14},{9,1... | collective-permute-start | bytes 786440 | tf_op jit(solution)/shard_map/ppermute | solution.py:445
  27.5 9.3 %collective-permute-start.8 = (bf16[2,16,16,256]{3,2,1,0:T(8,128)(2,1)S(1)}, bf16[2,16,16,256]{3,2,1,0:T(8,128)(2,1)S(1)}, u32[]{:S(2)}, u32[]{:S(2)}) collective-permute-start(bf16[2,16,16,256]{3,2,1,0:T(8,128)(2,1)S(1)} %pad_maximum_fusion), channel_id=1, source_target_pairs={{0,8},{8,0},{2,10},{10,2},{4,12},{12,4},{6,14},{14,6},{16,24},{24,... | collective-permute-start | bytes 786440 | tf_op jit(solution)/shard_map/ppermute | solution.py:445
  32.1 6.9 %collective-permute-start.10 = (bf16[16,16,256]{2,1,0:T(8,128)(2,1)S(1)}, bf16[16,16,256]{2,1,0:T(8,128)(2,1)S(1)}, u32[]{:S(2)}, u32[]{:S(2)}) collective-permute-start(bf16[16,16,256]{2,1,0:T(8,128)(2,1)S(1)} %get-tuple-element.94), channel_id=1, source_target_pairs={{0,8},{8,0},{2,10},{10,2},{4,12},{12,4},{6,14},{14,6},{16,24},{24,... | collective-permute-start | bytes 393224 | tf_op jit(solution)/shard_map/ppermute | solution.py:445
  32.2 6.9 %collective-permute-start.11 = (bf16[16,16,256]{2,1,0:T(8,128)(2,1)S(1)}, bf16[16,16,256]{2,1,0:T(8,128)(2,1)S(1)}, u32[]{:S(2)}, u32[]{:S(2)}) collective-permute-start(bf16[16,16,256]{2,1,0:T(8,128)(2,1)S(1)} %get-tuple-element.93), channel_id=1, source_target_pairs={{8,16},{16,8},{10,18},{18,10},{12,20},{20,12},{14,22},{22,14},{9,1... | collective-permute-start | bytes 393224 | tf_op jit(solution)/shard_map/ppermute | solution.py:445
  36.8 2.2 %copy-start.2 = (bf16[208,512]{1,0:T(8,128)(2,1)S(1)}, bf16[208,512]{1,0:T(8,128)(2,1)}, u32[]{:S(2)}) copy-start(bf16[208,512]{1,0:T(8,128)(2,1)} %constant.53.clone.l_high) | copy-start | bytes 638980
  36.8 2.2 %copy-start.3 = (bf16[208,512]{1,0:T(8,128)(2,1)S(1)}, bf16[208,512]{1,0:T(8,128)(2,1)}, u32[]{:S(2)}) copy-start(bf16[208,512]{1,0:T(8,128)(2,1)} %constant.54.clone.l_low) | copy-start | bytes 638980
  40.9 18.2 %copy-start.4 = (bf16[208,208]{1,0:T(8,128)(2,1)S(1)}, bf16[208,208]{1,0:T(8,128)(2,1)}, u32[]{:S(2)}) copy-start(bf16[208,208]{1,0:T(8,128)(2,1)} %constant.55.clone.refs_4_) | copy-start | bytes 259588
  40.9 4.8 %collective-permute-start.12 = (bf16[208,256]{1,0:T(8,128)(2,1)S(1)}, bf16[208,256]{1,0:T(8,128)(2,1)S(1)}, u32[]{:S(2)}, u32[]{:S(2)}) collective-permute-start(bf16[208,256]{1,0:T(8,128)(2,1)S(1)} %get-tuple-element.85), channel_id=1, source_target_pairs={{0,8},{8,0},{2,10},{10,2},{4,12},{12,4},{6,14},{14,6},{16,24},{24,... | collective-permute-start | bytes 319496 | tf_op jit(solution)/shard_map/ppermute | solution.py:445
  41.0 6.6 %collective-permute-start.13 = (bf16[208,256]{1,0:T(8,128)(2,1)S(1)}, bf16[208,256]{1,0:T(8,128)(2,1)S(1)}, u32[]{:S(2)}, u32[]{:S(2)}) collective-permute-start(bf16[208,256]{1,0:T(8,128)(2,1)S(1)} %get-tuple-element.86), channel_id=1, source_target_pairs={{8,16},{16,8},{10,18},{18,10},{12,20},{20,12},{14,22},{22,14},{9,1... | collective-permute-start | bytes 319496 | tf_op jit(solution)/shard_map/ppermute | solution.py:445
  44.2 3.7 %collective-permute-start.14 = (bf16[208,416]{1,0:T(8,128)(2,1)S(1)}, bf16[208,416]{1,0:T(8,128)(2,1)S(1)}, u32[]{:S(2)}, u32[]{:S(2)}) collective-permute-start(bf16[208,416]{1,0:T(8,128)(2,1)S(1)} %get-tuple-element.84.refs_0_), channel_id=1, source_target_pairs={{0,1},{1,0},{2,3},{3,2},{4,5},{5,4},{6,7},{7,6},{8,9},{9,8},{10,11... | collective-permute-start | bytes 519176 | tf_op jit(solution)/shard_map/ppermute | solution.py:434
  45.7 2.3 %collective-permute-start.15 = (bf16[208,256]{1,0:T(8,128)(2,1)S(1)}, bf16[208,256]{1,0:T(8,128)(2,1)S(1)}, u32[]{:S(2)}, u32[]{:S(2)}) collective-permute-start(bf16[208,256]{1,0:T(8,128)(2,1)S(1)} %collective-permute-done.12.refs_1_), channel_id=1, source_target_pairs={{0,1},{1,0},{2,3},{3,2},{4,5},{5,4},{6,7},{7,6},{8,9},{9,8},{10,11... | collective-permute-start | bytes 319496 | tf_op jit(solution)/shard_map/ppermute | solution.py:434
  47.6 1.3 %collective-permute-start.16 = (bf16[208,256]{1,0:T(8,128)(2,1)S(1)}, bf16[208,256]{1,0:T(8,128)(2,1)S(1)}, u32[]{:S(2)}, u32[]{:S(2)}) collective-permute-start(bf16[208,256]{1,0:T(8,128)(2,1)S(1)} %collective-permute-done.13.refs_2_), channel_id=1, source_target_pairs={{0,1},{1,0},{2,3},{3,2},{4,5},{5,4},{6,7},{7,6},{8,9},{9,8},{10,11... | collective-permute-start | bytes 319496 | tf_op jit(solution)/shard_map/ppermute | solution.py:434
  49.6 5.1 %collective-permute-start.17 = (bf16[2,208,128]{2,1,0:T(8,128)(2,1)S(1)}, bf16[2,208,128]{2,1,0:T(8,128)(2,1)S(1)}, u32[]{:S(2)}, u32[]{:S(2)}) collective-permute-start(bf16[2,208,128]{2,1,0:T(8,128)(2,1)S(1)} %get-tuple-element.88), channel_id=1, source_target_pairs={{0,2},{2,0},{4,6},{6,4},{8,10},{10,8},{12,14},{14,12},{16,18},{18,... | collective-permute-start | bytes 319496 | tf_op jit(solution)/shard_map/ppermute | solution.py:437
  50.1 7.9 %collective-permute-start.18 = (bf16[2,208,128]{2,1,0:T(8,128)(2,1)S(1)}, bf16[2,208,128]{2,1,0:T(8,128)(2,1)S(1)}, u32[]{:S(2)}, u32[]{:S(2)}) collective-permute-start(bf16[2,208,128]{2,1,0:T(8,128)(2,1)S(1)} %get-tuple-element.89), channel_id=1, source_target_pairs={{0,4},{2,6},{4,0},{6,2},{8,12},{10,14},{12,8},{14,10},{16,20},{18,... | collective-permute-start | bytes 319496 | tf_op jit(solution)/shard_map/ppermute | solution.py:437
  53.5 5.6 %collective-permute-start.19 = (bf16[2,208,128]{2,1,0:T(8,128)(2,1)S(1)}, bf16[2,208,128]{2,1,0:T(8,128)(2,1)S(1)}, u32[]{:S(2)}, u32[]{:S(2)}) collective-permute-start(bf16[2,208,128]{2,1,0:T(8,128)(2,1)S(1)} %get-tuple-element.90), channel_id=1, source_target_pairs={{0,6},{2,4},{4,2},{6,0},{8,14},{10,12},{12,10},{14,8},{16,22},{18,... | collective-permute-start | bytes 319496 | tf_op jit(solution)/shard_map/ppermute | solution.py:437
